TPU v7x, 32 devices: a whole 2x2x4 slice. The times are simulated.
32 devices in a mesh: grp: 8 (over z, y), blk: 4 (over x, core).
Axes of the slice: x: 2, y: 2, z: 4, core: 2. Of those that a mesh axis runs over, the one named last changes fastest.
Arguments:
- dec_in: bfloat16 [20480, 768], P(('grp', 'blk')), may hold values from -6 to 6
- encodings: bfloat16 [16384, 768], P(('grp', 'blk')), may hold values from -6 to 6
- answer_len: int32 [1024], P(('grp', 'blk')), may hold values from 1 to 20
- answer_question: int32 [1024], P('grp'), may hold values from 0 to 3, as said below
- question_rows: int32 [8, 4], P('grp'), may hold values from 250 to 1048, as said below
- bucket_table: int32 [20], replicated, may hold values from 0 to 31, as said below
- gain_self: float32 [768], replicated, may hold values from 0.5 to 1.5
- w_qkv: bfloat16 [768, 2304], replicated, may hold values from -0.21875 to 0.21875
- w_self_out: bfloat16 [768, 768], replicated, may hold values from -0.4375 to 0.4375
- rel_bias: float32 [32, 12], replicated, may hold values from -4 to 4
- gain_cross: float32 [768], replicated, may hold values from 0.5 to 1.5
- w_cross_q: bfloat16 [768, 768], replicated, may hold values from -0.21875 to 0.21875
- w_cross_kv: bfloat16 [768, 1536], replicated, may hold values from -0.21875 to 0.21875
- w_cross_out: bfloat16 [768, 768], replicated, may hold values from -6 to 6
- gain_ffn: float32 [768], replicated, may hold values from 0.5 to 1.5
- w_in: bfloat16 [768, 3072], replicated, may hold values from -0.21875 to 0.21875
- w_out: bfloat16 [3072, 768], replicated, may hold values from -0.21875 to 0.21875
- cotangent: bfloat16 [20480, 768], P(('grp', 'blk')), may hold values from -6 to 6
Outputs:
- layer_out: bfloat16 [20480, 768], P(('grp', 'blk'))
- d_dec_in: float32 [20480, 768], P(('grp', 'blk'))
- d_encodings: float32 [16384, 768], P(('grp', 'blk'))
- d_gain_self: float32 [768], P('blk')
- d_w_qkv: float32 [768, 2304], P('blk')
- d_w_self_out: float32 [768, 768], P('blk')
- d_rel_bias: float32 [32, 12], P('blk')
- d_gain_cross: float32 [768], P('blk')
- d_w_cross_q: float32 [768, 768], P('blk')
- d_w_cross_kv: float32 [768, 1536], P('blk')
- d_w_cross_out: float32 [768, 768], P('blk')
- d_gain_ffn: float32 [768], P('blk')
- d_w_in: float32 [768, 3072], P('blk')
- d_w_out: float32 [3072, 768], P('blk')
Inputs may be any that keep to these rules, and one draw needn't show every extreme that they name: `question_rows`: in each group, in an order drawn for that group, the 4 questions hold 4, 2, 1 and 1 times (1) whole passages of 250 rows, and the largest also holds the rows left over, so that they add up to 2048. `answer_question`: answers choose a question of their group with a chance proportional to its passages. `bucket_table`: entry 0 is 0, entries never fall as the distance grows, and the last entry is 31.
All inputs are finite; a program needn't handle non-finite values.
Results may differ from a plain program's by a relative error of at most 0.02.
Values may be sent and summed in bfloat16 or wider, within the bound.
A program may use at most 256 MiB of HBM per device.

v0:
```python
import math

import jax
import jax.numpy as jnp
from jax import lax
from jax.sharding import PartitionSpec as P

EPSILON = 1e-06
NEGATIVE = -1e30
MASKED = -1000000000.0


def norm_rows(rows_in, gain_vec):
    inverse = lax.rsqrt(jnp.mean(rows_in * rows_in, axis=-1, keepdims=True) + EPSILON)
    return (rows_in * inverse * gain_vec, inverse)


def norm_back(rows_in, inverse, gain_vec, grad_in):
    scaled = grad_in * gain_vec
    mean_term = jnp.mean(rows_in * scaled, axis=-1, keepdims=True)
    return (
        inverse * scaled - rows_in * inverse * inverse * inverse * mean_term,
        jnp.sum(grad_in * rows_in * inverse, axis=0),
    )


def matmul(left_arg, right_arg):
    return jnp.dot(left_arg, right_arg, preferred_element_type=jnp.float32)


def matmul_tn(left_arg, right_arg):
    return lax.dot_general(
        left_arg, right_arg, (((0,), (0,)), ((), ())), preferred_element_type=jnp.float32
    )


def matmul_nt(left_arg, right_arg):
    return lax.dot_general(
        left_arg, right_arg, (((1,), (1,)), ((), ())), preferred_element_type=jnp.float32
    )


def segment_ids(row_index, row_ends):
    return jnp.sum((row_index[:, None] >= row_ends[None, :]).astype(jnp.int32), axis=1)


def score_block(query_block, key_block, query_ids, key_ids, score_scale):
    raw_scores = (
        jnp.einsum("ihd,jhd->ihj", query_block, key_block, preferred_element_type=jnp.float32)
        * score_scale
    )
    return (raw_scores, (query_ids[:, None] == key_ids[None, :])[:, None, :])


def block_grads(
    query_block,
    grad_block,
    lse_block,
    delta_block,
    query_ids,
    key_block,
    value_block,
    key_ids,
    score_scale,
):
    raw_scores, key_mask = score_block(query_block, key_block, query_ids, key_ids, score_scale)
    probs = jnp.where(key_mask, jnp.exp(raw_scores - lse_block[..., None]), 0.0)
    d_probs = jnp.einsum(
        "ihd,jhd->ihj", grad_block, value_block, preferred_element_type=jnp.float32
    )
    d_scores = (probs * (d_probs - delta_block[..., None])).astype(jnp.bfloat16)
    grad_values = jnp.einsum(
        "ihj,ihd->jhd", probs.astype(jnp.bfloat16), grad_block, preferred_element_type=jnp.float32
    )
    grad_keys = (
        jnp.einsum("ihj,ihd->jhd", d_scores, query_block, preferred_element_type=jnp.float32)
        * score_scale
    )
    d_query = (
        jnp.einsum("ihj,jhd->ihd", d_scores, key_block, preferred_element_type=jnp.float32)
        * score_scale
    )
    return (grad_keys, grad_values, d_query)


def body(
    dec_in,
    encodings,
    answer_len,
    answer_question,
    question_rows,
    bucket_table,
    gain_self,
    w_qkv,
    w_self_out,
    rel_bias,
    gain_cross,
    w_cross_q,
    w_cross_kv,
    w_cross_out,
    gain_ffn,
    w_in,
    w_out,
    cotangent,
):
    answer_count = answer_len.shape[0]
    length = bucket_table.shape[0]
    tok_rows = dec_in.shape[0]
    model_width = dec_in.shape[1]
    head_count = rel_bias.shape[1]
    bucket_count = rel_bias.shape[0]
    head_size = model_width // head_count
    score_scale = 1.0 / math.sqrt(head_size)
    enc_rows = encodings.shape[0]
    blocks = lax.axis_size("blk")
    blk_index = lax.axis_index("blk")
    start_x = dec_in.astype(jnp.float32)
    normed_one, inverse_one = norm_rows(start_x, gain_self)
    normed_one_low = normed_one.astype(jnp.bfloat16)
    projected = (
        matmul(normed_one_low, w_qkv)
        .astype(jnp.bfloat16)
        .reshape(answer_count, length, 3, head_count, head_size)
    )
    self_q = projected[:, :, 0]
    self_k = projected[:, :, 1]
    self_v = projected[:, :, 2]
    position = jnp.arange(length)
    distance = jnp.maximum(position[:, None] - position[None, :], 0)
    onehot = (bucket_table[distance][..., None] == jnp.arange(bucket_count)[None, None, :]).astype(
        jnp.float32
    )
    bias_full = jnp.einsum("ijb,bh->hij", onehot, rel_bias, precision=lax.Precision.HIGHEST)
    self_valid = (position[None, :] <= position[:, None])[None] & (
        position[None, None, :] < answer_len[:, None, None]
    )
    raw_self = (
        jnp.einsum("aihd,ajhd->ahij", self_q, self_k, preferred_element_type=jnp.float32)
        * score_scale
    )
    self_prob = jax.nn.softmax(
        jnp.where(self_valid[:, None], raw_self + bias_full[None], MASKED), axis=-1
    )
    self_out = jnp.einsum(
        "ahij,ajhd->aihd", self_prob, self_v.astype(jnp.float32), precision=lax.Precision.HIGHEST
    )
    self_out_low = self_out.reshape(tok_rows, model_width).astype(jnp.bfloat16)
    mid_x = start_x + matmul(self_out_low, w_self_out)
    normed_two, inverse_two = norm_rows(mid_x, gain_cross)
    normed_two_low = normed_two.astype(jnp.bfloat16)
    cross_q = matmul(normed_two_low, w_cross_q).astype(jnp.bfloat16)
    query_heads = cross_q.reshape(tok_rows, head_count, head_size)
    paired = matmul(encodings, w_cross_kv).astype(jnp.bfloat16)
    local_keys = paired[:, :model_width].reshape(enc_rows, head_count, head_size)
    local_values = paired[:, model_width:].reshape(enc_rows, head_count, head_size)
    row_ends = jnp.cumsum(question_rows[0])
    local_seg = segment_ids(blk_index * enc_rows + jnp.arange(enc_rows), row_ends)
    group_qid = jnp.repeat(answer_question, length)
    own_qid = lax.dynamic_slice_in_dim(group_qid, blk_index * tok_rows, tok_rows, 0)
    start_state = (
        jnp.full((tok_rows, head_count), NEGATIVE, jnp.float32),
        jnp.zeros((tok_rows, head_count), jnp.float32),
        jnp.zeros((tok_rows, head_count, head_size), jnp.float32),
    )
    shard_piece = lax.all_gather(
        paired.reshape(enc_rows, 2, head_count, head_size).reshape(enc_rows, 2 * model_width),
        "blk",
        axis=0,
        tiled=True,
    )
    piece_blocks = shard_piece.reshape(
        shard_piece.shape[0] // enc_rows, enc_rows, 2, head_count, head_size
    )
    first_rows = enc_rows * jnp.arange(piece_blocks.shape[0])

    def scan_inner(fold_state, scan_item):
        key_block, first_row = scan_item
        run_peak, run_total, summed = fold_state
        key_ids = segment_ids(first_row + jnp.arange(enc_rows), row_ends)
        raw_scores, key_mask = score_block(
            query_heads, key_block[:, 0], own_qid, key_ids, score_scale
        )
        new_peak = jnp.maximum(
            run_peak, jnp.max(jnp.where(key_mask, raw_scores, NEGATIVE), axis=-1)
        )
        weights = jnp.where(key_mask, jnp.exp(raw_scores - new_peak[..., None]), 0.0)
        decay_rate = jnp.exp(run_peak - new_peak)
        run_total = run_total * decay_rate + jnp.sum(weights, axis=-1)
        summed = summed * decay_rate[..., None] + jnp.einsum(
            "ihj,jhd->ihd",
            weights.astype(jnp.bfloat16),
            key_block[:, 1],
            preferred_element_type=jnp.float32,
        )
        return ((new_peak, run_total, summed), None)

    fold_state, unused = lax.scan(scan_inner, start_state, (piece_blocks, first_rows))
    run_peak, run_total, summed = fold_state
    cross_out = summed / run_total[..., None]
    log_total = run_peak + jnp.log(run_total)
    cross_flat = cross_out.reshape(tok_rows, model_width)
    cross_low = cross_flat.astype(jnp.bfloat16)
    late_x = mid_x + matmul(cross_low, w_cross_out)
    normed_three, inverse_three = norm_rows(late_x, gain_ffn)
    normed_three_low = normed_three.astype(jnp.bfloat16)
    hidden_pre = matmul(normed_three_low, w_in)
    hidden_act, gelu_back = jax.vjp(jax.nn.gelu, hidden_pre)
    hidden_low = hidden_act.astype(jnp.bfloat16)
    layer_out = (late_x + matmul(hidden_low, w_out)).astype(jnp.bfloat16)
    grad_top = cotangent.astype(jnp.float32)
    d_w_out = matmul_tn(hidden_low, cotangent)
    d_hidden = gelu_back(matmul_nt(cotangent, w_out))[0].astype(jnp.bfloat16)
    d_w_in = matmul_tn(normed_three_low, d_hidden)
    d_x_three, d_gain_ffn = norm_back(late_x, inverse_three, gain_ffn, matmul_nt(d_hidden, w_in))
    grad_late = grad_top + d_x_three
    d_cross_branch = grad_late.astype(jnp.bfloat16)
    d_w_cross_out = matmul_tn(cross_low, d_cross_branch)
    d_cross_att = matmul_nt(d_cross_branch, w_cross_out).astype(jnp.bfloat16)
    delta = jnp.sum(
        (d_cross_att.astype(jnp.float32) * cross_flat).reshape(tok_rows, head_count, head_size),
        axis=-1,
    )
    all_q, all_grad = (
        lax.all_gather(cross_q, "blk", axis=0, tiled=True),
        lax.all_gather(d_cross_att, "blk", axis=0, tiled=True),
    )
    all_lse, all_delta = (
        lax.all_gather(log_total, "blk", axis=0, tiled=True),
        lax.all_gather(delta, "blk", axis=0, tiled=True),
    )

    def back_step(grad_state, scan_item):
        grad_keys, grad_values = grad_state
        query_block, grad_block, lse_block, delta_block, id_block = scan_item
        step_keys, step_values, d_query = block_grads(
            query_block,
            grad_block,
            lse_block,
            delta_block,
            id_block,
            local_keys,
            local_values,
            local_seg,
            score_scale,
        )
        return (
            (grad_keys + step_keys, grad_values + step_values),
            d_query.reshape(tok_rows, model_width),
        )

    zero_kv = jnp.zeros((enc_rows, head_count, head_size), jnp.float32)
    back_items = (
        all_q.reshape(blocks, tok_rows, head_count, head_size),
        all_grad.reshape(blocks, tok_rows, head_count, head_size),
        all_lse.reshape(blocks, tok_rows, head_count),
        all_delta.reshape(blocks, tok_rows, head_count),
        group_qid.reshape(blocks, tok_rows),
    )
    grad_kv, d_query_all = lax.scan(back_step, (zero_kv, zero_kv), back_items)
    own_d_query = lax.psum_scatter(
        d_query_all.reshape(blocks * tok_rows, model_width), "blk", scatter_dimension=0, tiled=True
    ).astype(jnp.bfloat16)
    d_paired = jnp.concatenate(
        [grad_kv[0].reshape(enc_rows, model_width), grad_kv[1].reshape(enc_rows, model_width)],
        axis=1,
    ).astype(jnp.bfloat16)
    d_w_cross_kv = matmul_tn(encodings, d_paired)
    d_encodings = matmul_nt(d_paired, w_cross_kv)
    d_w_cross_q = matmul_tn(normed_two_low, own_d_query)
    d_x_two, d_gain_cross = norm_back(
        mid_x, inverse_two, gain_cross, matmul_nt(own_d_query, w_cross_q)
    )
    grad_mid = grad_late + d_x_two
    d_self_branch = grad_mid.astype(jnp.bfloat16)
    d_w_self_out = matmul_tn(self_out_low, d_self_branch)
    d_self_att = (
        matmul_nt(d_self_branch, w_self_out)
        .astype(jnp.bfloat16)
        .reshape(answer_count, length, head_count, head_size)
    )
    d_self_att_wide = d_self_att.astype(jnp.float32)
    d_self_prob = jnp.einsum(
        "aihd,ajhd->ahij", d_self_att, self_v, preferred_element_type=jnp.float32
    )
    d_self_scores = self_prob * (
        d_self_prob - jnp.sum(self_prob * d_self_prob, axis=-1, keepdims=True)
    )
    d_rel_bias = jnp.einsum(
        "hij,ijb->bh", jnp.sum(d_self_scores, axis=0), onehot, precision=lax.Precision.HIGHEST
    )
    d_self_v = jnp.einsum(
        "ahij,aihd->ajhd", self_prob, d_self_att_wide, precision=lax.Precision.HIGHEST
    )
    d_self_q = (
        jnp.einsum(
            "ahij,ajhd->aihd",
            d_self_scores,
            self_k.astype(jnp.float32),
            precision=lax.Precision.HIGHEST,
        )
        * score_scale
    )
    d_self_k = (
        jnp.einsum(
            "ahij,aihd->ajhd",
            d_self_scores,
            self_q.astype(jnp.float32),
            precision=lax.Precision.HIGHEST,
        )
        * score_scale
    )
    d_projected = (
        jnp.stack([d_self_q, d_self_k, d_self_v], axis=2)
        .reshape(tok_rows, 3 * model_width)
        .astype(jnp.bfloat16)
    )
    d_w_qkv = matmul_tn(normed_one_low, d_projected)
    d_x_one, d_gain_self = norm_back(start_x, inverse_one, gain_self, matmul_nt(d_projected, w_qkv))
    d_dec_in = grad_mid + d_x_one
    shared = (
        lax.psum_scatter(d_gain_self, "blk", scatter_dimension=0, tiled=True),
        lax.psum_scatter(d_w_qkv, "blk", scatter_dimension=0, tiled=True),
        lax.psum_scatter(d_w_self_out, "blk", scatter_dimension=0, tiled=True),
        lax.psum_scatter(d_rel_bias, "blk", scatter_dimension=0, tiled=True),
        lax.psum_scatter(d_gain_cross, "blk", scatter_dimension=0, tiled=True),
        lax.psum_scatter(d_w_cross_q, "blk", scatter_dimension=0, tiled=True),
        lax.psum_scatter(d_w_cross_kv, "blk", scatter_dimension=0, tiled=True),
        lax.psum_scatter(d_w_cross_out, "blk", scatter_dimension=0, tiled=True),
        lax.psum_scatter(d_gain_ffn, "blk", scatter_dimension=0, tiled=True),
        lax.psum_scatter(d_w_in, "blk", scatter_dimension=0, tiled=True),
        lax.psum_scatter(d_w_out, "blk", scatter_dimension=0, tiled=True),
    )
    totals = lax.psum(
        (
            shared[0],
            shared[1],
            shared[2],
            shared[3],
            shared[4],
            shared[5],
            shared[6],
            shared[7],
            shared[8],
            shared[9],
            shared[10],
        ),
        "grp",
    )
    return (
        layer_out,
        d_dec_in,
        d_encodings,
        totals[0],
        totals[1],
        totals[2],
        totals[3],
        totals[4],
        totals[5],
        totals[6],
        totals[7],
        totals[8],
        totals[9],
        totals[10],
    )


def solution(mesh):
    return jax.shard_map(
        body,
        mesh=mesh,
        in_specs=(
            P(("grp", "blk"), None),
            P(("grp", "blk"), None),
            P(("grp", "blk")),
            P("grp"),
            P("grp", None),
            P(),
            P(),
            P(),
            P(),
            P(),
            P(),
            P(),
            P(),
            P(),
            P(),
            P(),
            P(),
            P(("grp", "blk"), None),
        ),
        out_specs=(
            P(("grp", "blk"), None),
            P(("grp", "blk"), None),
            P(("grp", "blk"), None),
            P("blk"),
            P("blk", None),
            P("blk", None),
            P("blk", None),
            P("blk"),
            P("blk", None),
            P("blk", None),
            P("blk", None),
            P("blk"),
            P("blk", None),
            P("blk", None),
        ),
        check_vma=False,
    )
```

profile of v0, /device:TPU:0, one launch (start us, length us, event | category | flops | bytes accessed | tf_op | source)
XLA Modules:
  0.0 1272.3 jit_solution(13762273808762924329)
XLA Ops:
  23.1 5.6 convolution_convert_fusion
  28.7 9.9 reshape.273
  47.8 5.7 convert_bitcast_fusion.1
  71.3 8.9 fusion.97
  80.3 8.6 copy.109
  88.9 11.2 reshape.277
  100.0 7.0 copy.111
  107.1 114.1 %while.30 = (s32[]{:T(128)}, f32[640,12]{0,1:T(8,128)}, f32[640,12]{0,1:T(8,128)}, f32[640,12,64]{0,2,1:T(8,128)}, s32[640]{0:T(1024)S(1)}, /*index=5*/s32[4]{0:...) while((s32[]{:T(128)}, f32[640,12]{0,1:T(8,128)}, ...), condition=%wide.region_9.10_spmd.clone, body=%wide.region_5.0_spmd.clone.sunk | while | flops 1051733504 | bytes 62954256 | solution.py:197
  110.3 6.8 fusion.150
  117.1 8.7 fusion.151
  125.9 8.7 bitcast_add_fusion.6
  138.4 6.8 fusion.150
  145.2 8.7 fusion.151
  154.0 9.3 bitcast_add_fusion.6
  167.0 6.8 fusion.150
  173.9 8.7 fusion.151
  182.7 9.3 bitcast_add_fusion.6
  195.7 6.8 fusion.150
  202.6 8.7 fusion.151
  211.3 9.3 bitcast_add_fusion.6
  231.0 13.8 %fusion.45 = (bf16[640,3072]{1,0:T(8,128)(2,1)S(1)}, f32[640,3072]{1,0:T(8,128)}) fusion(f32[640,3072]{1,0:T(8,128)} %fusion.97, bf16[768,3072]{1,0:T(8,128)(2,1)} %param.37, f32[640,768]{1,0:T(8,128)S(1)} %get-tuple-element.423, f32[768]{0:T(1024)S(1)} %copy-done.50, f32[640]{0:T(1024)S(1)} %add_rsqrt_fusion), kind=kOutput, calls=%fused_computation.67 | convolution fusion | flops 3060695040 | bytes 26351104 | tf_op jit(solution)/shard_map/dot_general | solution.py:28
  263.2 6.4 copy.112
  269.6 7.7 reshape.280
  277.3 4.8 copy.118
  282.2 8.0 all_gather.17
  296.9 7.0 all_gather.19
  305.5 6.4 copy.114
  311.9 7.6 reshape.283
  319.5 4.9 copy.120
  324.4 152.2 %while.31 = (s32[]{:T(128)}, f32[512,12,64]{0,2,1:T(8,128)}, f32[512,12,64]{0,2,1:T(8,128)}, f32[4,640,768]{2,1,0:T(8,128)}, bf16[4,640,12,64]{1,3,2,0:T(8,128)(...) while((s32[]{:T(128)}, f32[512,12,64]{0,2,1:T(8,128)}, ...), condition=%wide.region_15.16_spmd.clone, body=%wide.region_14.15_spmd.clone.sunk | while | flops 2558689280 | bytes 176312128 | solution.py:259
  329.4 5.4 copy-done.2
  334.8 5.8 bitcast_add_fusion.8
  340.6 9.2 fusion.164
  367.3 5.4 copy-done.2
  372.7 6.0 bitcast_add_fusion.8
  378.7 9.2 fusion.164
  405.4 5.4 copy-done.2
  410.8 6.0 bitcast_add_fusion.8
  416.8 9.2 fusion.164
  443.5 5.4 copy-done.2
  448.9 6.0 bitcast_add_fusion.8
  454.9 9.2 fusion.164
  484.8 6.8 copy.132
  491.7 4.8 fusion.74
  496.6 12.2 fusion.91
  509.5 10.2 fusion.89
  520.0 25.9 %reduce-scatter.11.cloned.1.call-done = f32[640,768]{1,0:T(8,128)} async-done(((f32[2560,768]{1,0:T(8,128)}), f32[640,768]{1,0:T(8,128)}) %reduce-scatter.11.cloned.1.call-update) | async-done | bytes 1966096 | tf_op jit(solution)/shard_map/reduce_scatter | solution.py:260
  567.8 7.4 multiply_reduce_fusion
  575.2 5.0 fusion.94
  589.0 5.2 convert_bitcast_fusion
  596.1 5.0 copy.126
  601.0 10.8 convert_element_type.110
  611.9 8.1 fusion.79
  623.0 8.9 reduce-scatter.19.cloned.1.call-done
  631.8 81.2 %reduce-scatter.23.cloned.1.call-done = f32[768,768]{1,0:T(8,128)} async-done(((f32[3072,768]{1,0:T(8,128)}), f32[768,768]{1,0:T(8,128)}) %reduce-scatter.23.cloned.1.call-update) | async-done | bytes 2359312 | tf_op jit(solution)/shard_map/reduce_scatter | solution.py:331
  713.1 81.2 %reduce-scatter.21.cloned.1.call-done = f32[192,3072]{1,0:T(8,128)} async-done(((f32[768,3072]{1,0:T(8,128)}), f32[192,3072]{1,0:T(8,128)}) %reduce-scatter.21.cloned.1.call-update) | async-done | bytes 2359312 | tf_op jit(solution)/shard_map/reduce_scatter | solution.py:330
  794.3 36.4 %reduce-scatter.17.cloned.1.call-done = f32[192,768]{1,0:T(8,128)} async-done(((f32[768,768]{1,0:T(8,128)}), f32[192,768]{1,0:T(8,128)}) %reduce-scatter.17.cloned.1.call-update) | async-done | bytes 589840 | tf_op jit(solution)/shard_map/reduce_scatter | solution.py:326
  830.7 36.0 %reduce-scatter.15.cloned.1.call-done = f32[192,768]{1,0:T(8,128)} async-done(((f32[768,768]{1,0:T(8,128)}), f32[192,768]{1,0:T(8,128)}) %reduce-scatter.15.cloned.1.call-update) | async-done | bytes 589840 | tf_op jit(solution)/shard_map/reduce_scatter | solution.py:323
  866.7 66.5 %reduce-scatter.13.cloned.1.call-done = f32[192,2304]{1,0:T(8,128)} async-done(((f32[768,2304]{1,0:T(8,128)}), f32[192,2304]{1,0:T(8,128)}) %reduce-scatter.13.cloned.1.call-update) | async-done | bytes 1769488 | tf_op jit(solution)/shard_map/reduce_scatter | solution.py:322
  935.7 10.9 add_convert_fusion
  952.6 6.6 fusion.61
  959.2 12.2 all-reduce.6
  974.3 24.0 %all-reduce.4 = (f32[192]{0:T(256)}, f32[8,12]{1,0:T(8,128)}, f32[192]{0:T(256)}, f32[192]{0:T(256)}) all-reduce(f32[192]{0:T(256)S(1)} %dynamic-slice.1, f32[8,12]{1,0:T(8,128)S(1)} %constant_dynamic-slice_fusion.2, f32[192]{0:T(256)S(1)} %dynamic-slice.5, f32[192]{0:T(256)S(1)} %dynamic-slice.7), channel_id=1, replica_groups=mesh['grp'=8,'blk'=4] {'grp'}, use_global_device_ids=true, to_apply=%region_22.23 | all-reduce | flops 672 | bytes 5376 | tf_op jit(solution)/shard_map/psum | solution.py:333
  1003.5 249.3 %all-reduce.9.cloned.1.call-done = (f32[192,2304]{1,0:T(8,128)}, f32[192,768]{1,0:T(8,128)}, f32[192,768]{1,0:T(8,128)}, f32[192,1536]{0,1:T(8,128)}, f32[192,76...) async-done(((f32[192,2304]{1,0:T(8,128)}, f32[192,768]{1,0:T(8,128)}, f32[192,768]{1,0:T(8,128)}, f32[192,1536]{0,1:T(8,128)}, f32[192,768]{1,0:T(8,128)}, ...) | async-done | bytes 9437200 | tf_op jit(solution)/shard_map/psum | solution.py:333
  (385 shorter events, 235.5 us)
Async XLA Ops:
  7.2 15.9 %copy-start = (bf16[768,2304]{1,0:T(8,128)(2,1)S(1)}, bf16[768,2304]{1,0:T(8,128)(2,1)}, u32[]{:S(2)}) copy-start(bf16[768,2304]{1,0:T(8,128)(2,1)} %param.29) | copy-start | bytes 10616836
  7.2 73.1 %all-gather.4.cloned.1.call-start = ((), (), s32[]{:S(2)}) async-start(), calls=%async_computation.8 | async-start | bytes 7864320 | tf_op jit(solution)/shard_map/all_gather | solution.py:165
  11.9 251.3 %all-gather.6.cloned.1.call-start = ((), (), s32[]{:S(2)}) async-start(), calls=%async_computation.9 | async-start | bytes 4915200 | tf_op jit(solution)/shard_map/all_gather | solution.py:224
  13.3 9.8 copy-start.59
  28.7 9.9 copy-start.63
  38.9 8.9 copy-start.38
  47.7 5.7 copy-start.35
  66.1 239.4 %all-gather.8.cloned.1.call-start = ((), (), s32[]{:S(2)}) async-start(), calls=%async_computation.10 | async-start | bytes 4915200 | tf_op jit(solution)/shard_map/all_gather | solution.py:225
  100.0 7.0 copy-start.56
  100.0 7.0 copy-start.69
  110.2 6.9 copy-start.19
  117.1 8.7 copy-start.27
  125.9 8.7 copy-start.28
  138.4 6.9 copy-start.19
  145.2 8.7 copy-start.27
  154.0 9.3 copy-start.28
  167.0 6.9 copy-start.19
  173.9 8.7 copy-start.27
  182.7 9.3 copy-start.28
  195.7 6.9 copy-start.19
  202.6 8.7 copy-start.27
  211.3 9.3 copy-start.28
  227.2 17.6 %slice-start.2 = ((s8[4718592]{0:T(1024)(128)(4,1)}), s8[4194304]{0:T(1024)(128)(4,1)S(1)}, s32[]{:S(2)}) async-start(s8[4718592]{0:T(1024)(128)(4,1)} %bitcast.241), calls=%async_computation.22 | async-start | bytes 8388608
  231.0 17.9 %copy-start.12 = (f32[640,768]{1,0:T(8,128)}, f32[640,768]{1,0:T(8,128)S(1)}, u32[]{:S(2)}) copy-start(f32[640,768]{1,0:T(8,128)S(1)} %get-tuple-element.423) | copy-start | bytes 5898244
  231.0 17.9 %copy-start.48 = (f32[640]{0:T(1024)}, f32[640]{0:T(1024)S(1)}, u32[]{:S(2)}) copy-start(f32[640]{0:T(1024)S(1)} %add_rsqrt_fusion) | copy-start | bytes 7684
  231.0 13.8 %slice-start.3 = ((s8[4718592]{0:T(1024)(128)(4,1)}), s8[524288]{0:T(1024)(128)(4,1)S(1)}, s32[]{:S(2)}) async-start(s8[4718592]{0:T(1024)(128)(4,1)} %bitcast.241), calls=%async_computation.23 | async-start | bytes 1048576
  253.4 292.5 %reduce-scatter.11.cloned.1.call-start = ((), (), s32[]{:S(2)}) async-start(), calls=%async_computation.11 | async-start | bytes 9830400 | tf_op jit(solution)/shard_map/reduce_scatter | solution.py:260
  277.3 4.8 copy-start.20
  277.3 4.8 copy-start.29
  329.4 5.4 copy-start.2
  334.8 5.8 copy-start.40
  340.6 9.3 copy-start.3
  367.3 5.4 copy-start.2
  372.7 6.0 copy-start.40
  378.7 9.2 copy-start.3
  405.4 5.4 copy-start.2
  410.8 6.0 copy-start.40
  416.8 9.3 copy-start.3
  443.5 5.4 copy-start.2
  448.9 6.0 copy-start.40
  454.9 9.3 copy-start.3
  476.6 143.5 %reduce-scatter.25.cloned.1.call-start = ((), (), s32[]{:S(2)}) async-start(), calls=%async_computation.18 | async-start | bytes 5898240
  491.7 140.2 %reduce-scatter.19.cloned.1.call-start = ((), (), s32[]{:S(2)}) async-start(), calls=%async_computation.15 | async-start | bytes 2949120 | tf_op jit(solution)/shard_map/reduce_scatter | solution.py:328
  496.6 216.5 %reduce-scatter.23.cloned.1.call-start = ((), (), s32[]{:S(2)}) async-start(), calls=%async_computation.17 | async-start | bytes 11796480 | tf_op jit(solution)/shard_map/reduce_scatter | solution.py:331
  508.9 285.4 %reduce-scatter.21.cloned.1.call-start = ((), (), s32[]{:S(2)}) async-start(), calls=%async_computation.16 | async-start | bytes 11796480 | tf_op jit(solution)/shard_map/reduce_scatter | solution.py:330
  519.8 26.2 %copy-start.53 = (f32[640]{0:T(1024)S(1)}, f32[640]{0:T(1024)}, u32[]{:S(2)}) copy-start(f32[640]{0:T(1024)} %copy-done.52) | copy-start | bytes 7684
  519.8 26.2 %copy-start.55 = (f32[768]{0:T(1024)S(1)}, f32[768]{0:T(1024)}, u32[]{:S(2)}) copy-start(f32[768]{0:T(1024)} %param.32) | copy-start | bytes 9220
  519.8 310.9 %reduce-scatter.17.cloned.1.call-start = ((), (), s32[]{:S(2)}) async-start(), calls=%async_computation.14 | async-start | bytes 2949120 | tf_op jit(solution)/shard_map/reduce_scatter | solution.py:326
  550.8 315.9 %reduce-scatter.15.cloned.1.call-start = ((), (), s32[]{:S(2)}) async-start(), calls=%async_computation.13 | async-start | bytes 2949120 | tf_op jit(solution)/shard_map/reduce_scatter | solution.py:323
  567.7 365.5 %reduce-scatter.13.cloned.1.call-start = ((), (), s32[]{:S(2)}) async-start(), calls=%async_computation.12 | async-start | bytes 8847360 | tf_op jit(solution)/shard_map/reduce_scatter | solution.py:322
  567.7 7.4 copy-start.31
  567.7 7.4 copy-start.34
  567.8 7.4 copy-start.36
  567.8 7.4 copy-start.39
  575.2 5.0 copy-start.17
  580.3 8.7 slice-start
  584.4 4.6 slice-start.1
  584.4 4.6 copy-start.23
  601.0 10.8 copy-start.58
  601.0 10.8 copy-start.60
  620.0 632.8 %all-reduce.9.cloned.1.call-start = ((), (), s32[]{:S(2)}) async-start(), calls=%async_computation.19 | async-start | bytes 19660800 | tf_op jit(solution)/shard_map/psum | solution.py:333
  935.7 11.0 copy-start.42
  935.7 11.0 copy-start.44
  935.7 10.9 copy-start.64
  (49 other events, 138.6 us)
Sparse Core Ops, SparseCore 0:
  12.0 49.0 all-gather.3
  66.2 35.7 all-gather.5
  253.5 36.5 all-gather.7
  476.7 69.2 reduce-scatter.10
  548.5 47.8 reduce-scatter.24
  598.8 33.0 reduce-scatter.18
  634.6 78.4 reduce-scatter.22
  715.8 78.4 reduce-scatter.20
  797.6 33.0 reduce-scatter.16
  833.6 33.0 reduce-scatter.14
  869.4 63.7 reduce-scatter.12
  939.0 313.7 all-reduce.8
where the time goes:
time: 1290 us; the launch traced here: 1270 us
  waiting for transfers between devices  586 us (45%)
  matrix products  321 us (25%)
  local copies, waits for them, and re-layouts  227 us (18%)
  other arithmetic  68.4 us (5%)
  blocking collectives  51.2 us (4%)
  between operations  16.7 us (1%)
    psum x1, waiting for transfers between devices, body(): lax.psum((shared[0], shared[1], shared[2], shared[3], shared[4], shared[5...  249 us
    reduce_scatter x1, waiting for transfers between devices, body(): lax.psum_scatter(d_w_out, 'blk', scatter_dimension=0, tiled=True)  81.2 us
    reduce_scatter x1, waiting for transfers between devices, body(): lax.psum_scatter(d_w_in, 'blk', scatter_dimension=0, tiled=True)  81.2 us
    reduce_scatter x1, waiting for transfers between devices, body(): lax.psum_scatter(d_w_qkv, 'blk', scatter_dimension=0, tiled=True)  66.5 us
    unnamed x147, local copies, waits for them, and re-layouts  48.8 us
    dot_general x7, matrix products, matmul_tn(): lax.dot_general(left_arg, right_arg, (((0,), (0,)), ((), ())), preferred_...  48.1 us
    dot_general x7, matrix products, matmul(): return jnp.dot(left_arg, right_arg, preferred_element_type=jnp.float32)  43.6 us
    dot_general x8, matrix products, score_block(): jnp.einsum('ihd,jhd->ihj', query_block, key_block, preferred_element_type...  42.1 us
  transfers between devices with their start and end apart: 12, of which 8 were waited for; matrix products, arithmetic and copies ran while one was open for 33% of the time, Pallas kernels for 0%

commit v1 on v0

v1 whole, which is shorter than its diff:
```python
import functools
import math

import jax
import jax.numpy as jnp
from jax import lax
from jax.experimental import pallas as pl
from jax.experimental.pallas import tpu as pltpu
from jax.sharding import PartitionSpec as P

EPSILON = 1e-06
NEG = -1e30
MASKED = -1e9
TQ = 64
TK = 256
WIN = 128
F32 = jnp.float32
BF = jnp.bfloat16
VM = pl.BlockSpec(memory_space=pltpu.VMEM)
SM = pl.BlockSpec(memory_space=pltpu.SMEM)
LIMIT = 60 << 20


def dot(a, b):
    return jnp.dot(a, b, preferred_element_type=F32)


def dot_tn(a, b):
    return lax.dot_general(a, b, (((0,), (0,)), ((), ())), preferred_element_type=F32)


def dot_nt(a, b):
    return lax.dot_general(a, b, (((1,), (1,)), ((), ())), preferred_element_type=F32)


def stack4(t):
    lane = lax.broadcasted_iota(jnp.int32, t.shape, 1) // 64
    return jnp.concatenate([jnp.where(lane == a, t, jnp.zeros_like(t)) for a in range(4)], axis=0)


def unstack4(s):
    n = s.shape[0] // 4
    lane = lax.broadcasted_iota(jnp.int32, (n, 256), 1) // 64
    out = s[:n]
    for a in range(1, 4):
        out = jnp.where(lane == a, s[a * n : (a + 1) * n], out)
    return out


def range_mask(base, rows, start, size):
    idx = lax.broadcasted_iota(jnp.int32, (rows, start.shape[1]), 0)
    rel = idx - (start - base)
    return (rel >= 0) & (rel < size)


def red(x, op):
    return op(x.reshape(x.shape[0] // 8, 8, x.shape[1]), axis=0)


def cross_fwd_kernel(
    lo_ref, hi_ref, start_ref, size_ref, q_ref, k_ref, vt_ref, o_ref, lse_ref, qst, s_scr, m_scr, l_scr, acc, *, nq, tiles
):
    def tile(t, _):
        st = start_ref[t]
        sz = size_ref[t]
        lo = lo_ref[t]
        hi = hi_ref[t]
        row = pl.ds(pl.multiple_of(t * TQ, TQ), TQ)
        for c in range(nq):
            qst[c] = stack4(q_ref[row, c * 256 : (c + 1) * 256]).T
            m_scr[c] = jnp.full((8, 256), NEG, F32)
            l_scr[c] = jnp.zeros((8, 256), F32)
            acc[c] = jnp.zeros((256, 256), F32)

        def scores(j, _):
            kr = pl.ds(pl.multiple_of(j * TK, TK), TK)
            mask = range_mask(j * TK, TK, st, sz)
            for c in range(nq):
                s = dot(k_ref[kr, c * 256 : (c + 1) * 256], qst[c])
                s = jnp.where(mask, s, NEG)
                s_scr[c, kr, :] = s
                m_scr[c] = jnp.maximum(m_scr[c], red(s, jnp.max))
            return 0

        lax.fori_loop(lo, hi, scores, 0)
        for c in range(nq):
            m_scr[c] = jnp.broadcast_to(jnp.max(m_scr[c], axis=0, keepdims=True), (8, 256))

        def mix(j, _):
            kr = pl.ds(pl.multiple_of(j * TK, TK), TK)
            for c in range(nq):
                p = jnp.exp(s_scr[c, kr, :] - m_scr[c][0:1])
                l_scr[c] += red(p, jnp.sum)
                acc[c] += dot(vt_ref[c * 256 : (c + 1) * 256, kr], p.astype(BF))
            return 0

        lax.fori_loop(lo, hi, mix, 0)
        for c in range(nq):
            l = jnp.sum(l_scr[c], axis=0, keepdims=True)
            lse_ref[t, c] = m_scr[c][0:1] + jnp.log(l)
            o_ref[row, c * 256 : (c + 1) * 256] = unstack4((acc[c] * (1.0 / l)).T)
        return 0

    lax.fori_loop(0, tiles, tile, 0)


def quads_per_step(nq, keys):
    return nq if keys <= 2048 else 1


def cross_fwd(lo, hi, start, size, q, k, vt):
    rows, width = q.shape
    tiles, keys = rows // TQ, k.shape[0]
    nq = quads_per_step(width // 256, keys)
    full = pl.BlockSpec(start.shape, lambda g: (0, 0, 0))
    return pl.pallas_call(
        functools.partial(cross_fwd_kernel, nq=nq, tiles=tiles),
        grid=(width // 256 // nq,),
        out_shape=(
            jax.ShapeDtypeStruct(q.shape, F32),
            jax.ShapeDtypeStruct((tiles, width // 256, 1, 256), F32),
        ),
        in_specs=[
            SM,
            SM,
            full,
            full,
            pl.BlockSpec((rows, nq * 256), lambda g: (0, g)),
            pl.BlockSpec((keys, nq * 256), lambda g: (0, g)),
            pl.BlockSpec((nq * 256, keys), lambda g: (g, 0)),
        ],
        out_specs=(
            pl.BlockSpec((rows, nq * 256), lambda g: (0, g)),
            pl.BlockSpec((tiles, nq, 1, 256), lambda g: (0, g, 0, 0)),
        ),
        scratch_shapes=[
            pltpu.VMEM((nq, 256, 256), BF),
            pltpu.VMEM((nq, keys, 256), F32),
            pltpu.VMEM((nq, 8, 256), F32),
            pltpu.VMEM((nq, 8, 256), F32),
            pltpu.VMEM((nq, 256, 256), F32),
        ],
        compiler_params=pltpu.CompilerParams(vmem_limit_bytes=LIMIT),
        name="cross_fwd",
    )(lo, hi, start, size, q, k, vt)


def cross_bwd_kernel(
    lo_ref,
    hi_ref,
    start_ref,
    size_ref,
    q_ref,
    do_ref,
    o_ref,
    lse_ref,
    k_ref,
    v_ref,
    kt_ref,
    dq_ref,
    dk_ref,
    dv_ref,
    qs,
    qst,
    dos,
    dost,
    del_scr,
    dka,
    dva,
    dqt,
    *,
    nq,
    tiles,
    scale,
):
    dka[...] = jnp.zeros_like(dka)
    dva[...] = jnp.zeros_like(dva)

    def tile(t, _):
        st = start_ref[t]
        sz = size_ref[t]
        row = pl.ds(pl.multiple_of(t * TQ, TQ), TQ)
        for c in range(nq):
            cs = slice(c * 256, (c + 1) * 256)
            a = stack4(q_ref[row, cs])
            qs[c] = a
            qst[c] = a.T
            b = stack4(do_ref[row, cs])
            dos[c] = b
            dost[c] = b.T
            product = do_ref[row, cs].astype(F32) * o_ref[row, cs]
            total = jnp.sum(red(stack4(product).T, jnp.sum), axis=0, keepdims=True)
            del_scr[c] = jnp.broadcast_to(total, (8, 256))
            dqt[c] = jnp.zeros((256, 256), F32)

        def step(j, _):
            kr = pl.ds(pl.multiple_of(j * TK, TK), TK)
            mask = range_mask(j * TK, TK, st, sz)
            for c in range(nq):
                cs = slice(c * 256, (c + 1) * 256)
                s = dot(k_ref[kr, cs], qst[c])
                p = jnp.where(mask, jnp.exp(s - lse_ref[t, c]), 0.0)
                dp = dot(v_ref[kr, cs], dost[c])
                ds = (p * (dp - del_scr[c][0:1])).astype(BF)
                dva[kr, cs] += dot(p.astype(BF), dos[c])
                dka[kr, cs] += dot(ds, qs[c])
                dqt[c] += dot(kt_ref[cs, kr], ds)
            return 0

        lax.fori_loop(lo_ref[t], hi_ref[t], step, 0)
        for c in range(nq):
            cs = slice(c * 256, (c + 1) * 256)
            dq_ref[row, cs] = (unstack4(dqt[c].T) * scale).astype(BF)
        return 0

    lax.fori_loop(0, tiles, tile, 0)
    dk_ref[...] = dka[...].astype(BF)
    dv_ref[...] = dva[...].astype(BF)


def cross_bwd(lo, hi, start, size, q, do, o, lse, k, v, kt, scale):
    rows, width = q.shape
    tiles, keys = rows // TQ, k.shape[0]
    nq = quads_per_step(width // 256, keys)
    full = pl.BlockSpec(start.shape, lambda g: (0, 0, 0))
    own = pl.BlockSpec((rows, nq * 256), lambda g: (0, g))
    held = pl.BlockSpec((keys, nq * 256), lambda g: (0, g), pipeline_mode=pl.Buffered(1))
    out_kv = pl.BlockSpec((keys, nq * 256), lambda g: (0, g), pipeline_mode=pl.Buffered(1))
    return pl.pallas_call(
        functools.partial(cross_bwd_kernel, nq=nq, tiles=tiles, scale=scale),
        grid=(width // 256 // nq,),
        out_shape=(
            jax.ShapeDtypeStruct(q.shape, BF),
            jax.ShapeDtypeStruct(k.shape, BF),
            jax.ShapeDtypeStruct(k.shape, BF),
        ),
        in_specs=[
            SM,
            SM,
            full,
            full,
            own,
            own,
            own,
            pl.BlockSpec((tiles, nq, 1, 256), lambda g: (0, g, 0, 0)),
            held,
            held,
            pl.BlockSpec((nq * 256, keys), lambda g: (g, 0), pipeline_mode=pl.Buffered(1)),
        ],
        out_specs=(own, out_kv, out_kv),
        scratch_shapes=[pltpu.VMEM((nq, 256, 256), BF)] * 4
        + [
            pltpu.VMEM((nq, 8, 256), F32),
            pltpu.VMEM((keys, nq * 256), F32),
            pltpu.VMEM((keys, nq * 256), F32),
            pltpu.VMEM((nq, 256, 256), F32),
        ],
        compiler_params=pltpu.CompilerParams(vmem_limit_bytes=LIMIT),
        name="cross_bwd",
    )(lo, hi, start, size, q, do, o, lse, k, v, kt)


def distances():
    j = lax.broadcasted_iota(jnp.int32, (WIN, 256), 0)
    i = lax.broadcasted_iota(jnp.int32, (WIN, 256), 1) % 64
    return WIN - TQ + i - j


def fill_window(proj_ref, kp, vp, width):
    kp[0:64, :] = jnp.zeros((64, width), BF)
    vp[0:64, :] = jnp.zeros((64, width), BF)
    kp[64:, :] = proj_ref[:, width : 2 * width]
    vp[64:, :] = proj_ref[:, 2 * width : 3 * width]


def fill_bias(brow_ref, bias, nq):
    dist = distances()
    for c in range(nq):
        cs = slice(c * 256, (c + 1) * 256)

        def add(d, held):
            return jnp.where(dist == d, brow_ref[pl.ds(d, 1), cs], held)

        bias[c] = lax.fori_loop(0, brow_ref.shape[0], add, jnp.full((WIN, 256), MASKED, F32))


def self_fwd_kernel(start_ref, size_ref, brow_ref, proj_ref, o_ref, lse_ref, kp, vp, bias, *, nq, tiles, scale):
    width = nq * 256
    fill_window(proj_ref, kp, vp, width)
    fill_bias(brow_ref, bias, nq)

    def tile(t, _):
        row = pl.ds(pl.multiple_of(t * TQ, TQ), TQ)
        win = pl.ds(pl.multiple_of(t * TQ, TQ), WIN)
        mask = range_mask(t * TQ - 64, WIN, start_ref[t], size_ref[t])
        for c in range(nq):
            cs = slice(c * 256, (c + 1) * 256)
            qst = stack4(proj_ref[row, cs] * jnp.asarray(scale, BF)).T
            s = jnp.where(mask, dot(kp[win, cs], qst) + bias[c], MASKED)
            m = jnp.max(red(s, jnp.max), axis=0, keepdims=True)
            p = jnp.exp(s - m)
            l = jnp.sum(red(p, jnp.sum), axis=0, keepdims=True)
            p = (p * (1.0 / l)).astype(BF)
            o_ref[row, cs] = unstack4(dot_tn(p, vp[win, cs])).astype(BF)
            lse_ref[t, c] = m + jnp.log(l)
        return 0

    lax.fori_loop(0, tiles, tile, 0)


def self_fwd(start, size, brow, proj, scale):
    rows, width = proj.shape[0], proj.shape[1] // 3
    nq, tiles = width // 256, rows // TQ
    return pl.pallas_call(
        functools.partial(self_fwd_kernel, nq=nq, tiles=tiles, scale=scale),
        out_shape=(
            jax.ShapeDtypeStruct((rows, width), BF),
            jax.ShapeDtypeStruct((tiles, nq, 1, 256), F32),
        ),
        in_specs=[VM] * 4,
        out_specs=(VM, VM),
        scratch_shapes=[
            pltpu.VMEM((rows + 64, width), BF),
            pltpu.VMEM((rows + 64, width), BF),
            pltpu.VMEM((nq, WIN, 256), F32),
        ],
        compiler_params=pltpu.CompilerParams(vmem_limit_bytes=LIMIT),
        name="self_fwd",
    )(start, size, brow, proj)


def self_bwd_kernel(
    start_ref,
    size_ref,
    brow_ref,
    proj_ref,
    do_ref,
    lse_ref,
    dproj_ref,
    dbrow_ref,
    kp,
    vp,
    bias,
    dka,
    dva,
    dsum,
    *,
    nq,
    tiles,
    scale,
):
    width = nq * 256
    fill_window(proj_ref, kp, vp, width)
    fill_bias(brow_ref, bias, nq)
    dka[...] = jnp.zeros_like(dka)
    dva[...] = jnp.zeros_like(dva)
    dsum[...] = jnp.zeros_like(dsum)

    def tile(t, _):
        row = pl.ds(pl.multiple_of(t * TQ, TQ), TQ)
        win = pl.ds(pl.multiple_of(t * TQ, TQ), WIN)
        mask = range_mask(t * TQ - 64, WIN, start_ref[t], size_ref[t])
        for c in range(nq):
            cs = slice(c * 256, (c + 1) * 256)
            qs = stack4(proj_ref[row, cs] * jnp.asarray(scale, BF))
            dos = stack4(do_ref[row, cs])
            s = dot(kp[win, cs], qs.T) + bias[c]
            p = jnp.where(mask, jnp.exp(s - lse_ref[t, c]), 0.0)
            dp = dot(vp[win, cs], dos.T)
            delta = jnp.sum(red(p * dp, jnp.sum), axis=0, keepdims=True)
            ds = p * (dp - delta)
            dsum[c] += ds
            ds = ds.astype(BF)
            dva[win, cs] += dot(p.astype(BF), dos)
            dka[win, cs] += dot(ds, qs)
            dproj_ref[row, cs] = (unstack4(dot_tn(ds, kp[win, cs])) * scale).astype(BF)
        return 0

    lax.fori_loop(0, tiles, tile, 0)
    dproj_ref[:, width : 2 * width] = dka[64:, :].astype(BF)
    dproj_ref[:, 2 * width : 3 * width] = dva[64:, :].astype(BF)
    dist = distances()
    for c in range(nq):
        cs = slice(c * 256, (c + 1) * 256)

        def one(d, _):
            x = jnp.where(dist == d, dsum[c], 0.0)
            dbrow_ref[pl.ds(d, 1), cs] = jnp.sum(red(x, jnp.sum), axis=0, keepdims=True)
            return 0

        lax.fori_loop(0, brow_ref.shape[0], one, 0)


def self_bwd(start, size, brow, proj, do, lse, scale):
    rows, width = proj.shape[0], proj.shape[1] // 3
    nq, tiles = width // 256, rows // TQ
    return pl.pallas_call(
        functools.partial(self_bwd_kernel, nq=nq, tiles=tiles, scale=scale),
        out_shape=(jax.ShapeDtypeStruct((rows, 3 * width), BF), jax.ShapeDtypeStruct(brow.shape, F32)),
        in_specs=[VM] * 6,
        out_specs=(VM, VM),
        scratch_shapes=[
            pltpu.VMEM((rows + 64, width), BF),
            pltpu.VMEM((rows + 64, width), BF),
            pltpu.VMEM((nq, WIN, 256), F32),
            pltpu.VMEM((rows + 64, width), F32),
            pltpu.VMEM((rows + 64, width), F32),
            pltpu.VMEM((nq, WIN, 256), F32),
        ],
        compiler_params=pltpu.CompilerParams(vmem_limit_bytes=LIMIT),
        name="self_bwd",
    )(start, size, brow, proj, do, lse)


def norm_rows(x, gain):
    inverse = lax.rsqrt(jnp.mean(x * x, axis=-1, keepdims=True) + EPSILON)
    return x * inverse * gain, inverse


def norm_back(x, inverse, gain, grad):
    scaled = grad * gain
    mean = jnp.mean(x * scaled, axis=-1, keepdims=True)
    return inverse * scaled - x * inverse * inverse * inverse * mean, jnp.sum(grad * x * inverse, axis=0)


def swap(x, axis, bit):
    size = lax.axis_size(axis)
    return lax.ppermute(x, axis, [(i, i ^ bit) for i in range(size)])


def bits_of(axis):
    size = lax.axis_size(axis)
    return [1 << b for b in range(size.bit_length() - 1)]


def gather_parts(x, axis):
    parts = {0: x}
    for bit in reversed(bits_of(axis)):
        for r in list(parts):
            parts[r ^ bit] = swap(parts[r], axis, bit)
    return parts


def add_low(a, b):
    return (a.astype(F32) + b.astype(F32)).astype(BF)


def scatter_sum(x, axis, order):
    size = x.shape[0]
    live = list(range(size))
    block = x
    for bit in order:
        keep = [r for r in live if not r & bit]
        send = [r for r in live if r & bit]
        k = jnp.stack([block[live.index(r)] for r in keep])
        s = jnp.stack([block[live.index(r)] for r in send])
        block = add_low(k, swap(s, axis, bit))
        live = keep
    return block[0]


def gather_sum(x, axis, order):
    parts = [0]
    block = x[None]
    for bit in order:
        block = jnp.concatenate([block, swap(block, axis, bit)], axis=0)
        parts = parts + [r ^ bit for r in parts]
    inverse = [parts.index(r) for r in range(len(parts))]
    return block, inverse


def relative(x, axis):
    size = lax.axis_size(axis)
    me = lax.axis_index(axis)
    return jnp.stack([lax.dynamic_index_in_dim(x, me ^ r, 0, keepdims=False) for r in range(size)])


def reduce_all(x):
    blocks, rows, width = x.shape
    groups = lax.axis_size("grp")
    part = scatter_sum(relative(x, "blk"), "blk", bits_of("blk"))
    part = relative(part.reshape(groups, rows // groups, width), "grp")
    part = scatter_sum(part, "grp", bits_of("grp"))
    whole, inverse = gather_sum(part, "grp", list(reversed(bits_of("grp"))))
    me = lax.axis_index("grp")
    index = jnp.asarray(inverse, jnp.int32)[jnp.arange(groups) ^ me]
    return jnp.take(whole, index, axis=0).reshape(rows, width)


def sum_everywhere(x):
    for axis in ("blk", "grp"):
        for bit in bits_of(axis):
            x = x + swap(x, axis, bit)
    return x


def pack(grads, blocks):
    out = []
    for g in grads:
        k, n = g.shape
        r = g.reshape(blocks, k // blocks, n // 768, 768).transpose(0, 2, 1, 3)
        out.append(r.reshape(blocks, -1, 768))
    return jnp.concatenate(out, axis=1)


def unpack(rows, shapes, blocks):
    out, at = [], 0
    for k, n in shapes:
        count = k // blocks * (n // 768)
        piece = rows[at : at + count].reshape(n // 768, k // blocks, 768)
        out.append(piece.transpose(1, 0, 2).reshape(k // blocks, n).astype(F32))
        at += count
    return out


def body(
    dec_in,
    encodings,
    answer_len,
    answer_question,
    question_rows,
    bucket_table,
    gain_self,
    w_qkv,
    w_self_out,
    rel_bias,
    gain_cross,
    w_cross_q,
    w_cross_kv,
    w_cross_out,
    gain_ffn,
    w_in,
    w_out,
    cotangent,
):
    answers = answer_len.shape[0]
    length = bucket_table.shape[0]
    rows, width = dec_in.shape
    heads = rel_bias.shape[1]
    buckets = rel_bias.shape[0]
    scale = 1.0 / math.sqrt(width // heads)
    enc_rows = encodings.shape[0]
    blocks = lax.axis_size("blk")
    me = lax.axis_index("blk")
    tiles = rows // TQ
    nq = width // 256

    enc_parts = gather_parts(encodings, "blk")

    own_q = lax.dynamic_slice_in_dim(answer_question, me * answers, answers, 0)
    a_index = jnp.arange(answers)
    before = (own_q[None, :] < own_q[:, None]) | (
        (own_q[None, :] == own_q[:, None]) & (a_index[None, :] < a_index[:, None])
    )
    rank = jnp.sum(before.astype(jnp.int32), axis=1)
    target = (rank[:, None] * length + jnp.arange(length)[None, :]).reshape(rows)
    forward_perm = (jnp.arange(rows)[:, None] == target[None, :]).astype(BF)
    sorted_len = jnp.sum(jnp.where(rank[:, None] == a_index[None, :], answer_len[:, None], 0), axis=0)
    ends_q = jnp.cumsum(question_rows[0])
    starts_q = ends_q - question_rows[0]
    sorted_q = jnp.sum(jnp.where(rank[:, None] == a_index[None, :], own_q[:, None], 0), axis=0)
    token_q = jnp.repeat(sorted_q, length)
    pick = token_q[:, None] == jnp.arange(question_rows.shape[1])[None, :]
    token_start = jnp.sum(jnp.where(pick, starts_q[None, :], 0), axis=1)
    token_size = jnp.sum(jnp.where(pick, question_rows[0][None, :], 0), axis=1)

    def stacked(v):
        return jnp.tile(v.reshape(tiles, 1, TQ), (1, 1, 4)).astype(jnp.int32)

    c_start, c_size = stacked(token_start), stacked(token_size)
    lo = (token_start.reshape(tiles, TQ)[:, 0] // TK).astype(jnp.int32)
    hi = ((token_start + token_size).reshape(tiles, TQ)[:, -1] + TK - 1) // TK
    hi = hi.astype(jnp.int32)
    s_start = stacked(jnp.arange(rows) // length * length)
    s_size = stacked(jnp.repeat(sorted_len, length))

    bucket_hot = (bucket_table[:, None] == jnp.arange(buckets)[None, :]).astype(F32)
    brow = jnp.repeat(
        jnp.dot(bucket_hot, rel_bias, precision=lax.Precision.HIGHEST), width // heads, axis=1
    )

    x0 = dot(forward_perm, dec_in)
    grad_top = dot(forward_perm, cotangent)
    grad_low = grad_top.astype(BF)
    n1, r1 = norm_rows(x0, gain_self)
    h1 = n1.astype(BF)
    proj = dot(h1, w_qkv).astype(BF)
    o_self, lse_self = self_fwd(s_start, s_size, brow, proj, scale)
    x1 = x0 + dot(o_self, w_self_out)
    n2, r2 = norm_rows(x1, gain_cross)
    h2 = n2.astype(BF)
    qc = (dot(h2, w_cross_q).astype(BF) * jnp.asarray(scale, BF)).astype(BF)

    enc_rel = jnp.stack([enc_parts[r] for r in range(blocks)])
    enc_all = relative(enc_rel, "blk").reshape(blocks * enc_rows, width)
    kv = dot(enc_all, w_cross_kv).astype(BF)
    k_all, v_all = kv[:, :width], kv[:, width:]
    kvt = lax.dot_general(w_cross_kv, enc_all, (((0,), (1,)), ((), ())), preferred_element_type=F32).astype(BF)
    kt_all, vt_all = kvt[:width], kvt[width:]

    o_cross, lse_cross = cross_fwd(lo, hi, c_start, c_size, qc, k_all, vt_all)
    oc = o_cross.astype(BF)
    x2 = x1 + dot(oc, w_cross_out)
    n3, r3 = norm_rows(x2, gain_ffn)
    h3 = n3.astype(BF)
    hidden, gelu_back = jax.vjp(jax.nn.gelu, dot(h3, w_in))
    u = hidden.astype(BF)
    out = (x2 + dot(u, w_out)).astype(BF)
    layer_out = dot_tn(forward_perm, out).astype(BF)

    d_w_out = dot_tn(u, grad_low).astype(BF)
    da = gelu_back(dot_nt(grad_low, w_out))[0].astype(BF)
    d_w_in = dot_tn(h3, da).astype(BF)
    sums_out = reduce_all(pack([d_w_out], blocks))
    sums_in = reduce_all(pack([d_w_in], blocks))
    dx3, d_gain_ffn = norm_back(x2, r3, gain_ffn, dot_nt(da, w_in))
    dx2 = grad_top + dx3
    dyc = dx2.astype(BF)
    d_w_cross_out = dot_tn(oc, dyc).astype(BF)
    d_o = dot_nt(dyc, w_cross_out).astype(BF)
    dqc, dk, dv = cross_bwd(
        lo, hi, c_start, c_size, qc, d_o, o_cross, lse_cross, k_all, v_all, kt_all, scale
    )

    dkv = jnp.concatenate([dk, dv], axis=1).reshape(blocks, enc_rows, 2 * width)
    dkv = relative(dkv, "blk")
    dkv = add_low(dkv[0::2], swap(dkv[1::2], "blk", 1))
    enc_half = enc_rel[0::2]
    dkv_flat = dkv.reshape(-1, 2 * width)
    d_w_cross_kv = dot_tn(enc_half.reshape(-1, width), dkv_flat).astype(BF)
    d_enc = dot_nt(dkv_flat, w_cross_kv).reshape(blocks // 2, enc_rows, width)
    d_enc_parts = {2 * r: d_enc[r] for r in range(blocks // 2)}
    for bit in reversed(bits_of("blk")[1:]):
        for r in [r for r in d_enc_parts if r & bit]:
            came = swap(d_enc_parts.pop(r).astype(BF), "blk", bit)
            d_enc_parts[r ^ bit] = d_enc_parts[r ^ bit] + came.astype(F32)
    d_encodings = d_enc_parts[0]

    d_w_cross_q = dot_tn(h2, dqc).astype(BF)
    sums_cross = reduce_all(pack([d_w_cross_out, d_w_cross_q, d_w_cross_kv], blocks))
    dx_two, d_gain_cross = norm_back(x1, r2, gain_cross, dot_nt(dqc, w_cross_q))
    dx1 = dx2 + dx_two
    dy1 = dx1.astype(BF)
    d_w_self_out = dot_tn(o_self, dy1).astype(BF)
    d_os = dot_nt(dy1, w_self_out).astype(BF)
    dproj, dbrow = self_bwd(s_start, s_size, brow, proj, d_os, lse_self, scale)
    d_w_qkv = dot_tn(h1, dproj).astype(BF)
    sums_self = reduce_all(pack([d_w_qkv, d_w_self_out], blocks))
    dx_one, d_gain_self = norm_back(x0, r1, gain_self, dot_nt(dproj, w_qkv))
    d_rel = jnp.dot(
        bucket_hot.T, jnp.sum(dbrow.reshape(length, heads, -1), axis=2), precision=lax.Precision.HIGHEST
    )
    d_x0 = dx1 + dx_one
    high = d_x0.astype(BF)
    low = (d_x0 - high.astype(F32)).astype(BF)
    d_dec_in = dot_tn(forward_perm, high) + dot_tn(forward_perm, low)

    small = jnp.concatenate([d_gain_self, d_gain_cross, d_gain_ffn, d_rel.reshape(-1)])
    small = sum_everywhere(small.reshape(-1, 128)).reshape(-1)

    def own(v):
        return lax.dynamic_slice_in_dim(v, me * (v.shape[0] // blocks), v.shape[0] // blocks, 0)

    g_self, g_cross, g_ffn = (own(small[i * width : (i + 1) * width]) for i in range(3))
    g_rel = own(small[3 * width :].reshape(buckets, heads))
    (o_wout,) = unpack(sums_out, [w_out.shape], blocks)
    (o_win,) = unpack(sums_in, [w_in.shape], blocks)
    o_wco, o_wcq, o_wckv = unpack(sums_cross, [w_cross_out.shape, w_cross_q.shape, w_cross_kv.shape], blocks)
    o_wqkv, o_wso = unpack(sums_self, [w_qkv.shape, w_self_out.shape], blocks)
    return (
        layer_out,
        d_dec_in,
        d_encodings,
        g_self,
        o_wqkv,
        o_wso,
        g_rel,
        g_cross,
        o_wcq,
        o_wckv,
        o_wco,
        g_ffn,
        o_win,
        o_wout,
    )


def solution(mesh):
    rows = P(("grp", "blk"), None)
    return jax.shard_map(
        body,
        mesh=mesh,
        in_specs=(rows, rows, P(("grp", "blk")), P("grp"), P("grp", None)) + (P(),) * 12 + (rows,),
        out_specs=(rows, rows, rows, P("blk"))
        + (P("blk", None),) * 3
        + (P("blk"),)
        + (P("blk", None),) * 3
        + (P("blk"),)
        + (P("blk", None),) * 2,
        check_vma=False,
    )
```

time: 1290 us -> 641 us (0.50)
  waiting for transfers between devices: 586 us -> 152 us
  matrix products: 321 us -> 120 us
  Pallas kernels: 0 us -> 135 us
  local copies, waits for them, and re-layouts: 227 us -> 117 us
  blocking collectives: 51.2 us -> 0 us
  starting transfers between devices: 1.07 us -> 41.8 us
  between operations: 16.7 us -> 2.23 us
    reduce_scatter x7 -> x0, waiting for transfers between devices: 336 us -> none  [the longest x1 81.2 us: body(): lax.psum_scatter(d_w_out, 'blk', scatter_dimension=0, tiled=True)]
    psum x1 -> x0, waiting for transfers between devices: 249 us -> none  [body(): lax.psum((shared[0], shared[1], shared[2], shared[3], shared[4], shared[5...]
    dot_general x57 -> x27, matrix products: 321 us -> 120 us  [the longest x10 42.2 us: dot_tn(): lax.dot_general(a, b, (((0,), (0,)), ((), ())), preferred_element_type=F32)]
    ppermute x0 -> x42, waiting for transfers between devices: none -> 152 us  [swap(): return lax.ppermute(x, axis, [(i, i ^ bit) for i in range(size)])]
    pallas_call x0 -> x4, Pallas kernels: none -> 135 us  [the longest x1 65.6 us: cross_bwd(): pl.pallas_call(functools.partial(cross_bwd_kernel, nq=nq, tiles=tiles, sc...]
    reduce_sum x13 -> x4, other arithmetic: 46.9 us -> 3.85 us  [the longest x1 1.63 us: body(): jnp.sum(dbrow.reshape(length, heads, -1), axis=2)]
    ppermute x0 -> x42, starting transfers between devices: none -> 41.8 us  [swap(): return lax.ppermute(x, axis, [(i, i ^ bit) for i in range(size)])]
    unnamed x147 -> x174, local copies, waits for them, and re-layouts: 48.8 us -> 21.1 us
  transfers between devices with their start and end apart: 12 -> 42, of which waited for: 8 -> 23; matrix products, arithmetic and copies ran while one was open for 33% -> 20% of each run, Pallas kernels for 0% -> 2%
where the time goes in v1:
time: 641 us; the launch traced here: 634 us
  waiting for transfers between devices  152 us (24%)
  Pallas kernels  135 us (21%)
  matrix products  120 us (19%)
  local copies, waits for them, and re-layouts  117 us (18%)
  other arithmetic  66.7 us (10%)
  starting transfers between devices  41.8 us (7%)
    ppermute x42, waiting for transfers between devices, swap(): return lax.ppermute(x, axis, [(i, i ^ bit) for i in range(size)])  152 us
    pallas_call x1, Pallas kernels, cross_bwd(): pl.pallas_call(functools.partial(cross_bwd_kernel, nq=nq, tiles=tiles, sc...  65.6 us
    dot_general x10, matrix products, dot_tn(): lax.dot_general(a, b, (((0,), (0,)), ((), ())), preferred_element_type=F32)  42.2 us
    ppermute x42, starting transfers between devices, swap(): return lax.ppermute(x, axis, [(i, i ^ bit) for i in range(size)])  41.8 us
    dot_general x8, matrix products, dot(): return jnp.dot(a, b, preferred_element_type=F32)  38 us
    pallas_call x1, Pallas kernels, cross_fwd(): pl.pallas_call(functools.partial(cross_fwd_kernel, nq=nq, tiles=tiles), g...  38 us
    dot_general x7, matrix products, dot_nt(): lax.dot_general(a, b, (((1,), (1,)), ((), ())), preferred_element_type=F32)  37.2 us
    reshape x5, local copies, waits for them, and re-layouts, pack(): r = g.reshape(blocks, k // blocks, n // 768, 768).transpose(0, 2, 1, 3)  23.6 us
  transfers between devices with their start and end apart: 42, of which 23 were waited for; matrix products, arithmetic and copies ran while one was open for 20% of the time, Pallas kernels for 2%

profile of v1, /device:TPU:0, one launch (start us, length us, event | category | flops | bytes accessed | tf_op | source)
XLA Modules:
  0.0 634.0 jit_solution(4671299123411235194)
XLA Ops:
  0.7 2.4 copy.79
  3.1 2.9 collective-permute-start.1
  27.3 3.4 multiply_reduce_fusion.8
  34.0 5.7 convolution_convert_fusion.4.proj_ref
  39.7 13.2 %self_fwd.1 = (bf16[640,768]{1,0:T(8,128)(2,1)}, f32[10,3,1,256]{3,2,1,0:T(1,128)}) custom-call(s32[10,1,256]{2,1,0:T(1,128)} %tile.39.start_ref, s32[10,1,256]{2,1,0:T(1,128)} %tile.42.size_ref, f32[20,768]{1,0:T(8,128)} %reshape.255.brow_ref, bf16[640,2304]{1,0:T(8,128)(2,1)} %convolution_convert_fusion.4.proj_ref), custom_call_target="tpu_custom_call" | custom-call | tf_op jit(solution)/shard_map/self_fwd/pallas_call | solution.py:314
  53.4 4.5 multiply_reduce_fusion.7
  65.2 3.4 fusion.9
  75.9 4.7 copy.82
  80.6 7.5 %convolution_convert_fusion = bf16[2048,1536]{0,1:T(8,128)(2,1)S(1)} fusion(bf16[2048,768]{1,0:T(8,128)(2,1)} %bitcast.127, bf16[768,1536]{1,0:T(8,128)(2,1)} %param.36), kind=kOutput, calls=%fused_computation.19 | convolution fusion | flops 4834983936 | bytes 11796480 | tf_op jit(solution)/shard_map/dot_general | solution.py:25
  88.1 3.2 fusion.51
  91.3 3.3 fusion.50
  94.6 4.7 copy.84.k_ref
  99.2 38.0 %cross_fwd.1 = (f32[640,768]{1,0:T(8,128)}, f32[10,3,1,256]{3,2,1,0:T(1,128)}) custom-call(s32[10]{0:T(128)} %get-tuple-element.140.lo_ref, s32[10]{0:T(128)} %get-tuple-element.139.hi_ref, s32[10,1,256]{2,1,0:T(1,128)} %tile.44.start_ref, s32[10,1,256]{2,1,0:T(1,128)} %tile.46.size_ref, bf16[640,768]{1,0:T(8,128)(2,1)} %fusion.15.q_ref, ...), custom_call_target="tpu_custom_call" | custom-call | tf_op jit(solution)/shard_map/cross_fwd/pallas_call | solution.py:116
  137.2 3.5 multiply_reduce_fusion.6
  142.0 8.0 %fusion.49 = f32[640,3072]{1,0:T(8,128)} fusion(bf16[768,3072]{1,0:T(8,128)(2,1)} %param.39, f32[640,768]{1,0:T(8,128)S(1)} %get-tuple-element.135, f32[768]{0:T(1024)S(1)} %copy-done.69, f32[640]{0:T(1024)S(1)} %add_rsqrt_fusion), kind=kOutput, calls=%fused_computation.252 | convolution fusion | flops 3021373440 | bytes 14554624 | tf_op jit(solution)/shard_map/dot_general | solution.py:25
  150.0 12.1 %fusion.14 = bf16[640,768]{1,0:T(8,128)(2,1)} fusion(f32[640,768]{1,0:T(8,128)} %copy-done.19, bf16[3072,768]{1,0:T(8,128)(2,1)} %param.40, s32[640]{0:T(1024)S(1)} %add.299, f32[640,3072]{1,0:T(8,128)} %fusion.49), kind=kOutput, calls=%fused_computation.81 | convolution fusion | flops 3668623360 | bytes 15534592 | tf_op jit(solution)/shard_map/dot_general | solution.py:29
  162.1 10.9 %fusion.6 = bf16[640,3072]{1,0:T(8,128)(2,1)S(1)} fusion(f32[640,3072]{1,0:T(8,128)} %fusion.49, bf16[3072,768]{1,0:T(8,128)(2,1)} %param.40, f32[640,768]{1,0:T(8,128)} %fusion.9), kind=kOutput, calls=%fused_computation.17 | convolution fusion | flops 3059712000 | bytes 18481152 | tf_op jit(solution)/shard_map/dot_general | solution.py:33
  173.0 7.1 %convolution_convert_fusion.1 = bf16[3072,768]{1,0:T(8,128)(2,1)} fusion(f32[640,768]{1,0:T(8,128)S(1)} %copy-done.44, f32[640,3072]{1,0:T(8,128)S(1)} %copy-done.81), kind=kOutput, calls=%fused_computation.23 | convolution fusion | flops 3040444416 | bytes 14548992 | tf_op jit(solution)/shard_map/dot_general | solution.py:29
  180.1 7.6 %multiply_reduce_fusion = (f32[768]{0:T(1024)S(1)}, f32[640]{0:T(1024)}, f32[640,768]{1,0:T(8,128)}) fusion(f32[640,768]{1,0:T(8,128)S(1)} %copy-done.20, f32[640]{0:T(1024)S(1)} %add_rsqrt_fusion, f32[768]{0:T(1024)S(1)} %copy-done.69, bf16[640,3072]{1,0:T(8,128)(2,1)S(1)} %fusion.6, bf16[768,3072]{1,0:T(8,128)(2,1)} %param.39), kind=kOutput, calls=%fused_computation.48 | convolution fusion | flops 3022846464 | bytes 12594176 | tf_op jit(solution)/shard_map/dot_general | solution.py:33
  187.7 5.8 convolution_convert_fusion.2
  193.6 4.7 copy.86.v_ref
  199.0 3.4 subtract_add_fusion.2
  204.3 65.6 %cross_bwd.1 = (bf16[640,768]{1,0:T(8,128)(2,1)}, bf16[2048,768]{1,0:T(8,128)(2,1)}, bf16[2048,768]{1,0:T(8,128)(2,1)}) custom-call(s32[10]{0:T(128)} %get-tuple-element.140.lo_ref, s32[10]{0:T(128)} %get-tuple-element.139.hi_ref, s32[10,1,256]{2,1,0:T(1,128)} %tile.44.start_ref, s32[10,1,256]{2,1,0:T(1,128)} %tile.46.size_ref, ...), custom_call_target="tpu_custom_call" | custom-call | tf_op jit(solution)/shard_map/cross_bwd/pallas_call | solution.py:229
  270.0 3.5 multiply_reduce_fusion.1
  278.8 18.3 %self_bwd.1 = (bf16[640,2304]{1,0:T(8,128)(2,1)}, f32[20,768]{1,0:T(8,128)}) custom-call(s32[10,1,256]{2,1,0:T(1,128)} %tile.39.start_ref, s32[10,1,256]{2,1,0:T(1,128)} %tile.42.size_ref, f32[20,768]{1,0:T(8,128)} %reshape.255.brow_ref, bf16[640,2304]{1,0:T(8,128)(2,1)} %convolution_convert_fusion.4.proj_ref, ...), custom_call_target="tpu_custom_call" | custom-call | tf_op jit(solution)/shard_map/self_bwd/pallas_call | solution.py:397
  297.1 7.0 %multiply_reduce_fusion.2 = (f32[768]{0:T(1024)S(1)}, f32[640]{0:T(1024)}, f32[640,768]{1,0:T(8,128)}) fusion(f32[640,768]{1,0:T(8,128)} %get-tuple-element.131, f32[640]{0:T(1024)S(1)} %copy-done.65, f32[768]{0:T(1024)S(1)} %copy-done.70, bf16[640,2304]{1,0:T(8,128)(2,1)} %get-tuple-element.29, bf16[768,2304]{1,0:T(8,128)(2,1)S(1)} %copy-done), kind=kOutput, calls=%fused_computation.50 | convolution fusion | flops 2267871744 | bytes 10431488 | tf_op jit(solution)/shard_map/dot_general | solution.py:33
  304.2 3.4 convolution_convert_fusion.3
  309.9 9.7 %reshape.268 = bf16[4,192,4,768]{3,2,1,0:T(4,128)(2,1)} reshape(bf16[768,3072]{1,0:T(8,128)(2,1)} %convolution_convert_fusion.2) | data formatting | bytes 9437184 | tf_op jit(solution)/shard_map/reshape | solution.py:501
  319.6 3.2 copy.92
  322.8 2.5 constant_dynamic-slice_fusion.23
  328.7 2.8 constant_dynamic-slice_fusion.48
  339.2 5.4 reshape.263
  344.6 3.1 copy.88
  360.4 2.8 copy-done.3
  366.4 2.6 collective-permute-done.6
  369.1 4.8 collective-permute-start.7
  373.9 2.4 fusion.12
  387.3 2.5 add_convert_fusion.1
  392.9 2.4 add_convert_fusion.2
  398.2 2.4 add_convert_fusion.4
  404.3 2.7 add_convert_fusion
  408.7 3.8 bitcast_convert_fusion
  412.5 5.0 reshape.266
  419.3 4.4 fusion.57
  430.5 15.0 %collective-permute-done.27 = bf16[1,768,768]{2,1,0:T(8,128)(2,1)} collective-permute-done((bf16[1,768,768]{2,1,0:T(8,128)(2,1)}, bf16[1,768,768]{2,1,0:T(8,128)(2,1)}, u32[]{:S(2)}, u32[]{:S(2)}) %collective-permute-start.27) | collective-permute-done | bytes 1179680 | tf_op jit(solution)/shard_map/ppermute | solution.py:428
  448.7 22.0 %collective-permute-done.11 = bf16[1,768,768]{2,1,0:T(8,128)(2,1)} collective-permute-done((bf16[1,768,768]{2,1,0:T(8,128)(2,1)}, bf16[1,768,768]{2,1,0:T(8,128)(2,1)}, u32[]{:S(2)}, u32[]{:S(2)}) %collective-permute-start.11) | collective-permute-done | bytes 1179680 | tf_op jit(solution)/shard_map/ppermute | solution.py:428
  479.0 3.4 collective-permute-done.12
  484.0 25.3 %collective-permute-done.19 = bf16[1,768,768]{2,1,0:T(8,128)(2,1)S(1)} collective-permute-done((bf16[1,768,768]{2,1,0:T(8,128)(2,1)S(1)}, bf16[1,768,768]{2,1,0:T(8,128)(2,1)S(1)}, u32[]{:S(2)}, u32[]{:S(2)}) %collective-permute-start.19) | collective-permute-done | bytes 1179680 | tf_op jit(solution)/shard_map/ppermute | solution.py:428
  516.2 5.6 collective-permute-done.20
  524.7 5.5 collective-permute-done.30
  530.3 3.2 collective-permute-done.21
  537.0 9.3 %collective-permute-done.39 = bf16[1,96,768]{2,1,0:T(8,128)(2,1)S(1)} collective-permute-done((bf16[1,96,768]{2,1,0:T(8,128)(2,1)S(1)}, bf16[1,96,768]{2,1,0:T(8,128)(2,1)S(1)}, u32[]{:S(2)}, u32[]{:S(2)}) %collective-permute-start.39) | collective-permute-done | bytes 147488 | tf_op jit(solution)/shard_map/ppermute | solution.py:428
  546.4 6.3 collective-permute-done.22
  552.9 2.6 collective-permute-start.32
  555.6 3.5 collective-permute-done.15
  559.2 3.0 collective-permute-done.23
  562.3 3.0 collective-permute-done.40
  566.0 5.6 collective-permute-done.32
  573.1 4.8 collective-permute-done.16
  579.4 4.7 collective-permute-done.24
  587.7 6.7 %collective-permute-done.33 = bf16[4,96,768]{2,1,0:T(8,128)(2,1)} collective-permute-done((bf16[4,96,768]{2,1,0:T(8,128)(2,1)}, bf16[4,96,768]{2,1,0:T(8,128)(2,1)}, u32[]{:S(2)}, u32[]{:S(2)}) %collective-permute-start.33) | collective-permute-done | bytes 589856 | tf_op jit(solution)/shard_map/ppermute | solution.py:428
  597.3 9.7 %collective-permute-done.17 = bf16[4,96,768]{2,1,0:T(8,128)(2,1)} collective-permute-done((bf16[4,96,768]{2,1,0:T(8,128)(2,1)}, bf16[4,96,768]{2,1,0:T(8,128)(2,1)}, u32[]{:S(2)}, u32[]{:S(2)}) %collective-permute-start.17) | collective-permute-done | bytes 589856 | tf_op jit(solution)/shard_map/ppermute | solution.py:428
  609.9 8.7 %collective-permute-done.25 = bf16[4,96,768]{2,1,0:T(8,128)(2,1)} collective-permute-done((bf16[4,96,768]{2,1,0:T(8,128)(2,1)}, bf16[4,96,768]{2,1,0:T(8,128)(2,1)}, u32[]{:S(2)}, u32[]{:S(2)}) %collective-permute-start.25) | collective-permute-done | bytes 589856 | tf_op jit(solution)/shard_map/ppermute | solution.py:428
  621.4 2.5 broadcast_select_fusion
  (391 shorter events, 160.9 us)
Async XLA Ops:
  0.6 33.3 %copy-start = (bf16[768,2304]{1,0:T(8,128)(2,1)S(1)}, bf16[768,2304]{1,0:T(8,128)(2,1)}, u32[]{:S(2)}) copy-start(bf16[768,2304]{1,0:T(8,128)(2,1)} %param.31) | copy-start | bytes 10616836
  3.1 54.8 %collective-permute-start.1 = (bf16[512,768]{0,1:T(8,128)(2,1)}, bf16[512,768]{0,1:T(8,128)(2,1)}, u32[]{:S(2)}, u32[]{:S(2)}) collective-permute-start(bf16[512,768]{0,1:T(8,128)(2,1)} %copy.79), channel_id=1, source_target_pairs={{0,2},{1,3},{2,0},{3,1},{4,6},{5,7},{6,4},{7,5},{8,10},{9,11},{10,... | collective-permute-start | bytes 2359304 | tf_op jit(solution)/shard_map/ppermute | solution.py:428
  6.0 64.5 %collective-permute-start = (bf16[512,768]{0,1:T(8,128)(2,1)}, bf16[512,768]{0,1:T(8,128)(2,1)}, u32[]{:S(2)}, u32[]{:S(2)}) collective-permute-start(bf16[512,768]{0,1:T(8,128)(2,1)} %copy.79), channel_id=1, source_target_pairs={{0,1},{1,0},{2,3},{3,2},{4,5},{5,4},{6,7},{7,6},{8,9},{9,8},{10,11... | collective-permute-start | bytes 2359304 | tf_op jit(solution)/shard_map/ppermute | solution.py:428
  18.5 131.5 %copy-start.60 = (s32[640]{0:T(1024)}, s32[640]{0:T(1024)S(1)}, u32[]{:S(2)}) copy-start(s32[640]{0:T(1024)S(1)} %add.299) | copy-start | bytes 7684
  39.7 13.2 %copy-start.76 = (s32[8]{0:T(128)S(1)}, s32[8]{0:T(128)}, u32[]{:S(2)}) copy-start(s32[8]{0:T(128)} %gather_fusion) | copy-start | bytes 100
  57.9 10.6 %copy-start.62 = (f32[640]{0:T(1024)}, f32[640]{0:T(1024)S(1)}, u32[]{:S(2)}) copy-start(f32[640]{0:T(1024)S(1)} %add_rsqrt_fusion.1) | copy-start | bytes 7684
  57.9 12.6 %collective-permute-start.2 = (bf16[512,768]{0,1:T(8,128)(2,1)}, bf16[512,768]{0,1:T(8,128)(2,1)}, u32[]{:S(2)}, u32[]{:S(2)}) collective-permute-start(bf16[512,768]{0,1:T(8,128)(2,1)} %collective-permute-done.1), channel_id=1, source_target_pairs={{0,1},{1,0},{2,3},{3,2},{4,5},{5,4},{6,7},{7,6},{8,9},{9,8},{10,11... | collective-permute-start | bytes 2359304 | tf_op jit(solution)/shard_map/ppermute | solution.py:428
  59.6 9.0 %copy-start.72 = (f32[768]{0:T(1024)S(1)}, f32[768]{0:T(1024)}, u32[]{:S(2)}) copy-start(f32[768]{0:T(1024)} %param.34) | copy-start | bytes 9220
  162.1 10.9 %copy-start.44 = (f32[640,768]{1,0:T(8,128)S(1)}, f32[640,768]{1,0:T(8,128)}, u32[]{:S(2)}) copy-start(f32[640,768]{1,0:T(8,128)} %fusion.9) | copy-start | bytes 5898244
  162.1 10.9 %copy-start.81 = (f32[640,3072]{1,0:T(8,128)S(1)}, f32[640,3072]{1,0:T(8,128)}, u32[]{:S(2)}) copy-start(f32[640,3072]{1,0:T(8,128)} %fusion.49) | copy-start | bytes 23592964
  204.3 65.6 %copy-start.63 = (f32[640]{0:T(1024)S(1)}, f32[640]{0:T(1024)}, u32[]{:S(2)}) copy-start(f32[640]{0:T(1024)} %copy-done.62) | copy-start | bytes 7684
  204.3 65.6 %copy-start.73 = (f32[768]{0:T(1024)S(1)}, f32[768]{0:T(1024)}, u32[]{:S(2)}) copy-start(f32[768]{0:T(1024)} %param.34) | copy-start | bytes 9220
  273.5 65.1 %copy-start.54 = (f32[768]{0:T(1024)}, f32[768]{0:T(1024)S(1)}, u32[]{:S(2)}) copy-start(f32[768]{0:T(1024)S(1)} %get-tuple-element.35) | copy-start | bytes 9220
  278.8 18.3 %copy-start.65 = (f32[640]{0:T(1024)S(1)}, f32[640]{0:T(1024)}, u32[]{:S(2)}) copy-start(f32[640]{0:T(1024)} %add_rsqrt_fusion.2) | copy-start | bytes 7684
  278.8 18.3 %copy-start.70 = (f32[768]{0:T(1024)S(1)}, f32[768]{0:T(1024)}, u32[]{:S(2)}) copy-start(f32[768]{0:T(1024)} %param.30) | copy-start | bytes 9220
  278.8 28.8 %slice-start.2 = ((s8[4718592]{0:T(1024)(128)(4,1)}), s8[524288]{0:T(1024)(128)(4,1)S(1)}, s32[]{:S(2)}) async-start(s8[4718592]{0:T(1024)(128)(4,1)} %bitcast.117), calls=%async_computation.2 | async-start | bytes 1048576
  297.1 10.4 %slice-start.3 = ((s8[4718592]{0:T(1024)(128)(4,1)}), s8[4194304]{0:T(1024)(128)(4,1)S(1)}, s32[]{:S(2)}) async-start(s8[4718592]{0:T(1024)(128)(4,1)} %bitcast.117), calls=%async_computation.3 | async-start | bytes 8388608
  304.2 34.4 %copy-start.56 = (f32[768]{0:T(1024)}, f32[768]{0:T(1024)S(1)}, u32[]{:S(2)}) copy-start(f32[768]{0:T(1024)S(1)} %get-tuple-element.33) | copy-start | bytes 9220
  339.2 26.0 %collective-permute-start.5 = (f32[21,128]{1,0:T(8,128)}, f32[21,128]{1,0:T(8,128)S(1)}, u32[]{:S(2)}, u32[]{:S(2)}) collective-permute-start(f32[21,128]{1,0:T(8,128)} %maximum_bitcast_fusion), channel_id=1, source_target_pairs={{0,1},{1,0},{2,3},{3,2},{4,5},{5,4},{6,7},{7,6},{8,9},{9,8},{10,11... | collective-permute-start | bytes 32264 | tf_op jit(solution)/shard_map/ppermute | solution.py:428
  349.3 38.0 %collective-permute-start.34 = (bf16[2,768,768]{2,1,0:T(8,128)(2,1)}, bf16[2,768,768]{2,1,0:T(8,128)(2,1)}, u32[]{:S(2)}, u32[]{:S(2)}) collective-permute-start(bf16[2,768,768]{2,1,0:T(8,128)(2,1)} %pad_maximum_fusion.8), channel_id=1, source_target_pairs={{0,1},{1,0},{2,3},{3,2},{4,5},{5,4},{6,7},{7,6},{8,9},{9,8},{10,11... | collective-permute-start | bytes 7077896 | tf_op jit(solution)/shard_map/ppermute | solution.py:428
  351.8 41.0 %collective-permute-start.26 = (bf16[2,768,768]{2,1,0:T(8,128)(2,1)}, bf16[2,768,768]{2,1,0:T(8,128)(2,1)}, u32[]{:S(2)}, u32[]{:S(2)}) collective-permute-start(bf16[2,768,768]{2,1,0:T(8,128)(2,1)} %pad_maximum_fusion.7), channel_id=1, source_target_pairs={{0,1},{1,0},{2,3},{3,2},{4,5},{5,4},{6,7},{7,6},{8,9},{9,8},{10,11... | collective-permute-start | bytes 7077896 | tf_op jit(solution)/shard_map/ppermute | solution.py:428
  355.6 42.6 %collective-permute-start.10 = (bf16[2,768,768]{2,1,0:T(8,128)(2,1)}, bf16[2,768,768]{2,1,0:T(8,128)(2,1)}, u32[]{:S(2)}, u32[]{:S(2)}) collective-permute-start(bf16[2,768,768]{2,1,0:T(8,128)(2,1)} %pad_maximum_fusion.5), channel_id=1, source_target_pairs={{0,1},{1,0},{2,3},{3,2},{4,5},{5,4},{6,7},{7,6},{8,9},{9,8},{10,11... | collective-permute-start | bytes 7077896 | tf_op jit(solution)/shard_map/ppermute | solution.py:428
  363.2 41.1 %collective-permute-start.3 = (bf16[2,512,1536]{2,1,0:T(8,128)(2,1)}, bf16[2,512,1536]{2,1,0:T(8,128)(2,1)}, u32[]{:S(2)}, u32[]{:S(2)}) collective-permute-start(bf16[2,512,1536]{2,1,0:T(8,128)(2,1)} %slice.181), channel_id=1, source_target_pairs={{0,1},{1,0},{2,3},{3,2},{4,5},{5,4},{6,7},{7,6},{8,9},{9,8},{10,11... | collective-permute-start | bytes 9437192 | tf_op jit(solution)/shard_map/ppermute | solution.py:428
  365.3 3.8 collective-permute-start.6
  369.1 7.2 %collective-permute-start.7 = (f32[21,128]{1,0:T(8,128)S(1)}, f32[21,128]{1,0:T(8,128)S(1)}, u32[]{:S(2)}, u32[]{:S(2)}) collective-permute-start(f32[21,128]{1,0:T(8,128)S(1)} %fusion.88), channel_id=1, source_target_pairs={{0,4},{4,0},{8,12},{12,8},{16,20},{20,16},{24,28},{28,24},{1,5},{5... | collective-permute-start | bytes 32264 | tf_op jit(solution)/shard_map/ppermute | solution.py:428
  376.3 3.8 collective-permute-start.8
  380.1 4.6 collective-permute-start.9
  391.0 35.2 %collective-permute-start.35 = (bf16[1,768,768]{2,1,0:T(8,128)(2,1)}, bf16[1,768,768]{2,1,0:T(8,128)(2,1)}, u32[]{:S(2)}, u32[]{:S(2)}) collective-permute-start(bf16[1,768,768]{2,1,0:T(8,128)(2,1)} %slice.282), channel_id=1, source_target_pairs={{0,2},{1,3},{2,0},{3,1},{4,6},{5,7},{6,4},{7,5},{8,10},{9,11},{10,... | collective-permute-start | bytes 3538952 | tf_op jit(solution)/shard_map/ppermute | solution.py:428
  395.3 9.0 %slice-start = ((s8[6291456]{0:T(1024)(128)(4,1)}), s8[4194304]{0:T(1024)(128)(4,1)S(1)}, s32[]{:S(2)}) async-start(s8[6291456]{0:T(1024)(128)(4,1)} %bitcast.107), calls=%async_computation | async-start | bytes 8388608
  396.4 49.1 %collective-permute-start.27 = (bf16[1,768,768]{2,1,0:T(8,128)(2,1)}, bf16[1,768,768]{2,1,0:T(8,128)(2,1)}, u32[]{:S(2)}, u32[]{:S(2)}) collective-permute-start(bf16[1,768,768]{2,1,0:T(8,128)(2,1)} %slice.274), channel_id=1, source_target_pairs={{0,2},{1,3},{2,0},{3,1},{4,6},{5,7},{6,4},{7,5},{8,10},{9,11},{10,... | collective-permute-start | bytes 3538952 | tf_op jit(solution)/shard_map/ppermute | solution.py:428
  403.1 67.7 %collective-permute-start.11 = (bf16[1,768,768]{2,1,0:T(8,128)(2,1)}, bf16[1,768,768]{2,1,0:T(8,128)(2,1)}, u32[]{:S(2)}, u32[]{:S(2)}) collective-permute-start(bf16[1,768,768]{2,1,0:T(8,128)(2,1)} %slice.250), channel_id=1, source_target_pairs={{0,2},{1,3},{2,0},{3,1},{4,6},{5,7},{6,4},{7,5},{8,10},{9,11},{10,... | collective-permute-start | bytes 3538952 | tf_op jit(solution)/shard_map/ppermute | solution.py:428
  423.8 161.2 %collective-permute-start.4 = (bf16[512,768]{1,0:T(8,128)(2,1)S(1)}, bf16[512,768]{1,0:T(8,128)(2,1)S(1)}, u32[]{:S(2)}, u32[]{:S(2)}) collective-permute-start(bf16[512,768]{1,0:T(8,128)(2,1)S(1)} %slice.312), channel_id=1, source_target_pairs={{0,2},{1,3},{2,0},{3,1},{4,6},{5,7},{6,4},{7,5},{8,10},{9,11},{10,... | collective-permute-start | bytes 2359304 | tf_op jit(solution)/shard_map/ppermute | solution.py:428
  426.1 48.8 %collective-permute-start.18 = (bf16[2,768,768]{2,1,0:T(8,128)(2,1)S(1)}, bf16[2,768,768]{2,1,0:T(8,128)(2,1)S(1)}, u32[]{:S(2)}, u32[]{:S(2)}) collective-permute-start(bf16[2,768,768]{2,1,0:T(8,128)(2,1)S(1)} %pad_maximum_fusion.6), channel_id=1, source_target_pairs={{0,1},{1,0},{2,3},{3,2},{4,5},{5,4},{6,7},{7,6},{8,9},{9,8},{10,11... | collective-permute-start | bytes 7077896 | tf_op jit(solution)/shard_map/ppermute | solution.py:428
  429.1 16.4 %copy-start.16 = (bf16[2,768,768]{2,1,0:T(8,128)(2,1)S(1)}, bf16[2,768,768]{2,1,0:T(8,128)(2,1)}, u32[]{:S(2)}) copy-start(bf16[2,768,768]{2,1,0:T(8,128)(2,1)} %copy-done.15) | copy-start | bytes 7077892
  429.3 44.7 %collective-permute-start.36 = (bf16[4,96,768]{2,1,0:T(8,128)(2,1)S(1)}, bf16[4,96,768]{2,1,0:T(8,128)(2,1)S(1)}, u32[]{:S(2)}, u32[]{:S(2)}) collective-permute-start(bf16[4,96,768]{2,1,0:T(8,128)(2,1)S(1)} %pad_maximum_fusion.19), channel_id=1, source_target_pairs={{0,4},{4,0},{8,12},{12,8},{16,20},{20,16},{24,28},{28,24},{1,5},{5... | collective-permute-start | bytes 1769480 | tf_op jit(solution)/shard_map/ppermute | solution.py:428
  447.1 23.7 %copy-start.14 = (bf16[2,768,768]{2,1,0:T(8,128)(2,1)S(1)}, bf16[2,768,768]{2,1,0:T(8,128)(2,1)}, u32[]{:S(2)}) copy-start(bf16[2,768,768]{2,1,0:T(8,128)(2,1)} %copy-done.13) | copy-start | bytes 7077892
  447.3 30.1 %collective-permute-start.28 = (bf16[4,96,768]{2,1,0:T(8,128)(2,1)S(1)}, bf16[4,96,768]{2,1,0:T(8,128)(2,1)S(1)}, u32[]{:S(2)}, u32[]{:S(2)}) collective-permute-start(bf16[4,96,768]{2,1,0:T(8,128)(2,1)S(1)} %pad_maximum_fusion.17), channel_id=1, source_target_pairs={{0,4},{4,0},{8,12},{12,8},{16,20},{20,16},{24,28},{28,24},{1,5},{5... | collective-permute-start | bytes 1769480 | tf_op jit(solution)/shard_map/ppermute | solution.py:428
  472.5 9.9 %collective-permute-start.12 = (bf16[4,96,768]{2,1,0:T(8,128)(2,1)S(1)}, bf16[4,96,768]{2,1,0:T(8,128)(2,1)S(1)}, u32[]{:S(2)}, u32[]{:S(2)}) collective-permute-start(bf16[4,96,768]{2,1,0:T(8,128)(2,1)S(1)} %pad_maximum_fusion.13), channel_id=1, source_target_pairs={{0,4},{4,0},{8,12},{12,8},{16,20},{20,16},{24,28},{28,24},{1,5},{5... | collective-permute-start | bytes 1769480 | tf_op jit(solution)/shard_map/ppermute | solution.py:428
  474.3 37.1 %collective-permute-start.37 = (bf16[2,96,768]{2,1,0:T(8,128)(2,1)S(1)}, bf16[2,96,768]{2,1,0:T(8,128)(2,1)S(1)}, u32[]{:S(2)}, u32[]{:S(2)}) collective-permute-start(bf16[2,96,768]{2,1,0:T(8,128)(2,1)S(1)} %pad_maximum_fusion.27), channel_id=1, source_target_pairs={{0,8},{4,12},{8,0},{12,4},{16,24},{20,28},{24,16},{28,20},{1,9},{5... | collective-permute-start | bytes 884744 | tf_op jit(solution)/shard_map/ppermute | solution.py:428
  475.6 33.7 %collective-permute-start.19 = (bf16[1,768,768]{2,1,0:T(8,128)(2,1)S(1)}, bf16[1,768,768]{2,1,0:T(8,128)(2,1)S(1)}, u32[]{:S(2)}, u32[]{:S(2)}) collective-permute-start(bf16[1,768,768]{2,1,0:T(8,128)(2,1)S(1)} %slice.262), channel_id=1, source_target_pairs={{0,2},{1,3},{2,0},{3,1},{4,6},{5,7},{6,4},{7,5},{8,10},{9,11},{10,... | collective-permute-start | bytes 3538952 | tf_op jit(solution)/shard_map/ppermute | solution.py:428
  477.6 35.3 %collective-permute-start.29 = (bf16[2,96,768]{2,1,0:T(8,128)(2,1)S(1)}, bf16[2,96,768]{2,1,0:T(8,128)(2,1)S(1)}, u32[]{:S(2)}, u32[]{:S(2)}) collective-permute-start(bf16[2,96,768]{2,1,0:T(8,128)(2,1)S(1)} %pad_maximum_fusion.25), channel_id=1, source_target_pairs={{0,8},{4,12},{8,0},{12,4},{16,24},{20,28},{24,16},{28,20},{1,9},{5... | collective-permute-start | bytes 884744 | tf_op jit(solution)/shard_map/ppermute | solution.py:428
  482.7 31.9 %collective-permute-start.13 = (bf16[2,96,768]{2,1,0:T(8,128)(2,1)S(1)}, bf16[2,96,768]{2,1,0:T(8,128)(2,1)S(1)}, u32[]{:S(2)}, u32[]{:S(2)}) collective-permute-start(bf16[2,96,768]{2,1,0:T(8,128)(2,1)S(1)} %pad_maximum_fusion.21), channel_id=1, source_target_pairs={{0,8},{4,12},{8,0},{12,4},{16,24},{20,28},{24,16},{28,20},{1,9},{5... | collective-permute-start | bytes 884744 | tf_op jit(solution)/shard_map/ppermute | solution.py:428
  509.8 11.9 %collective-permute-start.20 = (bf16[4,96,768]{2,1,0:T(8,128)(2,1)S(1)}, bf16[4,96,768]{2,1,0:T(8,128)(2,1)S(1)}, u32[]{:S(2)}, u32[]{:S(2)}) collective-permute-start(bf16[4,96,768]{2,1,0:T(8,128)(2,1)S(1)} %pad_maximum_fusion.15), channel_id=1, source_target_pairs={{0,4},{4,0},{8,12},{12,8},{16,20},{20,16},{24,28},{28,24},{1,5},{5... | collective-permute-start | bytes 1769480 | tf_op jit(solution)/shard_map/ppermute | solution.py:428
  511.5 12.8 %collective-permute-start.38 = (bf16[1,96,768]{2,1,0:T(8,128)(2,1)S(1)}, bf16[1,96,768]{2,1,0:T(8,128)(2,1)S(1)}, u32[]{:S(2)}, u32[]{:S(2)}) collective-permute-start(bf16[1,96,768]{2,1,0:T(8,128)(2,1)S(1)} %slice.288), channel_id=1, source_target_pairs={{0,16},{4,20},{8,24},{12,28},{16,0},{20,4},{24,8},{28,12},{1,17},{... | collective-permute-start | bytes 442376 | tf_op jit(solution)/shard_map/ppermute | solution.py:428
  513.0 17.1 %collective-permute-start.30 = (bf16[1,96,768]{2,1,0:T(8,128)(2,1)S(1)}, bf16[1,96,768]{2,1,0:T(8,128)(2,1)S(1)}, u32[]{:S(2)}, u32[]{:S(2)}) collective-permute-start(bf16[1,96,768]{2,1,0:T(8,128)(2,1)S(1)} %slice.280), channel_id=1, source_target_pairs={{0,16},{4,20},{8,24},{12,28},{16,0},{20,4},{24,8},{28,12},{1,17},{... | collective-permute-start | bytes 442376 | tf_op jit(solution)/shard_map/ppermute | solution.py:428
  514.7 22.1 %collective-permute-start.14 = (bf16[1,96,768]{2,1,0:T(8,128)(2,1)S(1)}, bf16[1,96,768]{2,1,0:T(8,128)(2,1)S(1)}, u32[]{:S(2)}, u32[]{:S(2)}) collective-permute-start(bf16[1,96,768]{2,1,0:T(8,128)(2,1)S(1)} %slice.256), channel_id=1, source_target_pairs={{0,16},{4,20},{8,24},{12,28},{16,0},{20,4},{24,8},{28,12},{1,17},{... | collective-permute-start | bytes 442376 | tf_op jit(solution)/shard_map/ppermute | solution.py:428
  522.0 11.5 %collective-permute-start.21 = (bf16[2,96,768]{2,1,0:T(8,128)(2,1)S(1)}, bf16[2,96,768]{2,1,0:T(8,128)(2,1)S(1)}, u32[]{:S(2)}, u32[]{:S(2)}) collective-permute-start(bf16[2,96,768]{2,1,0:T(8,128)(2,1)S(1)} %pad_maximum_fusion.23), channel_id=1, source_target_pairs={{0,8},{4,12},{8,0},{12,4},{16,24},{20,28},{24,16},{28,20},{1,9},{5... | collective-permute-start | bytes 884744 | tf_op jit(solution)/shard_map/ppermute | solution.py:428
  524.3 22.1 %collective-permute-start.39 = (bf16[1,96,768]{2,1,0:T(8,128)(2,1)S(1)}, bf16[1,96,768]{2,1,0:T(8,128)(2,1)S(1)}, u32[]{:S(2)}, u32[]{:S(2)}) collective-permute-start(bf16[1,96,768]{2,1,0:T(8,128)(2,1)S(1)} %add_convert_fusion.18), channel_id=1, source_target_pairs={{0,16},{4,20},{8,24},{12,28},{16,0},{20,4},{24,8},{28,12},{1,17},{... | collective-permute-start | bytes 442376 | tf_op jit(solution)/shard_map/ppermute | solution.py:428
  530.2 22.7 %collective-permute-start.31 = (bf16[1,96,768]{2,1,0:T(8,128)(2,1)S(1)}, bf16[1,96,768]{2,1,0:T(8,128)(2,1)S(1)}, u32[]{:S(2)}, u32[]{:S(2)}) collective-permute-start(bf16[1,96,768]{2,1,0:T(8,128)(2,1)S(1)} %add_convert_fusion.19), channel_id=1, source_target_pairs={{0,16},{4,20},{8,24},{12,28},{16,0},{20,4},{24,8},{28,12},{1,17},{... | collective-permute-start | bytes 442376 | tf_op jit(solution)/shard_map/ppermute | solution.py:428
  533.6 19.2 %collective-permute-start.22 = (bf16[1,96,768]{2,1,0:T(8,128)(2,1)S(1)}, bf16[1,96,768]{2,1,0:T(8,128)(2,1)S(1)}, u32[]{:S(2)}, u32[]{:S(2)}) collective-permute-start(bf16[1,96,768]{2,1,0:T(8,128)(2,1)S(1)} %slice.268), channel_id=1, source_target_pairs={{0,16},{4,20},{8,24},{12,28},{16,0},{20,4},{24,8},{28,12},{1,17},{... | collective-permute-start | bytes 442376 | tf_op jit(solution)/shard_map/ppermute | solution.py:428
  536.9 22.2 %collective-permute-start.15 = (bf16[1,96,768]{2,1,0:T(8,128)(2,1)S(1)}, bf16[1,96,768]{2,1,0:T(8,128)(2,1)S(1)}, u32[]{:S(2)}, u32[]{:S(2)}) collective-permute-start(bf16[1,96,768]{2,1,0:T(8,128)(2,1)S(1)} %add_convert_fusion.21), channel_id=1, source_target_pairs={{0,16},{4,20},{8,24},{12,28},{16,0},{20,4},{24,8},{28,12},{1,17},{... | collective-permute-start | bytes 442376 | tf_op jit(solution)/shard_map/ppermute | solution.py:428
  546.4 18.9 %collective-permute-start.40 = (bf16[2,96,768]{2,1,0:T(8,128)(2,1)S(1)}, bf16[2,96,768]{2,1,0:T(8,128)(2,1)S(1)}, u32[]{:S(2)}, u32[]{:S(2)}) collective-permute-start(bf16[2,96,768]{2,1,0:T(8,128)(2,1)S(1)} %pad_maximum_fusion.28), channel_id=1, source_target_pairs={{0,8},{4,12},{8,0},{12,4},{16,24},{20,28},{24,16},{28,20},{1,9},{5... | collective-permute-start | bytes 884744 | tf_op jit(solution)/shard_map/ppermute | solution.py:428
  552.8 9.4 %collective-permute-start.23 = (bf16[1,96,768]{2,1,0:T(8,128)(2,1)S(1)}, bf16[1,96,768]{2,1,0:T(8,128)(2,1)S(1)}, u32[]{:S(2)}, u32[]{:S(2)}) collective-permute-start(bf16[1,96,768]{2,1,0:T(8,128)(2,1)S(1)} %add_convert_fusion.20), channel_id=1, source_target_pairs={{0,16},{4,20},{8,24},{12,28},{16,0},{20,4},{24,8},{28,12},{1,17},{... | collective-permute-start | bytes 442376 | tf_op jit(solution)/shard_map/ppermute | solution.py:428
  552.9 18.7 %collective-permute-start.32 = (bf16[2,96,768]{2,1,0:T(8,128)(2,1)S(1)}, bf16[2,96,768]{2,1,0:T(8,128)(2,1)S(1)}, u32[]{:S(2)}, u32[]{:S(2)}) collective-permute-start(bf16[2,96,768]{2,1,0:T(8,128)(2,1)S(1)} %pad_maximum_fusion.26), channel_id=1, source_target_pairs={{0,8},{4,12},{8,0},{12,4},{16,24},{20,28},{24,16},{28,20},{1,9},{5... | collective-permute-start | bytes 884744 | tf_op jit(solution)/shard_map/ppermute | solution.py:428
  559.1 18.8 %collective-permute-start.16 = (bf16[2,96,768]{2,1,0:T(8,128)(2,1)S(1)}, bf16[2,96,768]{2,1,0:T(8,128)(2,1)S(1)}, u32[]{:S(2)}, u32[]{:S(2)}) collective-permute-start(bf16[2,96,768]{2,1,0:T(8,128)(2,1)S(1)} %pad_maximum_fusion.22), channel_id=1, source_target_pairs={{0,8},{4,12},{8,0},{12,4},{16,24},{20,28},{24,16},{28,20},{1,9},{5... | collective-permute-start | bytes 884744 | tf_op jit(solution)/shard_map/ppermute | solution.py:428
  562.2 21.9 %collective-permute-start.24 = (bf16[2,96,768]{2,1,0:T(8,128)(2,1)S(1)}, bf16[2,96,768]{2,1,0:T(8,128)(2,1)S(1)}, u32[]{:S(2)}, u32[]{:S(2)}) collective-permute-start(bf16[2,96,768]{2,1,0:T(8,128)(2,1)S(1)} %pad_maximum_fusion.24), channel_id=1, source_target_pairs={{0,8},{4,12},{8,0},{12,4},{16,24},{20,28},{24,16},{28,20},{1,9},{5... | collective-permute-start | bytes 884744 | tf_op jit(solution)/shard_map/ppermute | solution.py:428
  565.3 21.0 %collective-permute-start.41 = (bf16[4,96,768]{2,1,0:T(8,128)(2,1)S(1)}, bf16[4,96,768]{2,1,0:T(8,128)(2,1)S(1)}, u32[]{:S(2)}, u32[]{:S(2)}) collective-permute-start(bf16[4,96,768]{2,1,0:T(8,128)(2,1)S(1)} %pad_maximum_fusion.20), channel_id=1, source_target_pairs={{0,4},{4,0},{8,12},{12,8},{16,20},{20,16},{24,28},{28,24},{1,5},{5... | collective-permute-start | bytes 1769480 | tf_op jit(solution)/shard_map/ppermute | solution.py:428
  571.6 14.8 %copy-start.50 = (bf16[2,96,768]{2,1,0:T(8,128)(2,1)}, bf16[2,96,768]{2,1,0:T(8,128)(2,1)S(1)}, u32[]{:S(2)}) copy-start(bf16[2,96,768]{2,1,0:T(8,128)(2,1)S(1)} %collective-permute-done.32) | copy-start | bytes 884740
  572.5 21.8 %collective-permute-start.33 = (bf16[4,96,768]{2,1,0:T(8,128)(2,1)}, bf16[4,96,768]{2,1,0:T(8,128)(2,1)}, u32[]{:S(2)}, u32[]{:S(2)}) collective-permute-start(bf16[4,96,768]{2,1,0:T(8,128)(2,1)} %pad_maximum_fusion.18), channel_id=1, source_target_pairs={{0,4},{4,0},{8,12},{12,8},{16,20},{20,16},{24,28},{28,24},{1,5},{5... | collective-permute-start | bytes 1769480 | tf_op jit(solution)/shard_map/ppermute | solution.py:428
  577.9 8.4 %copy-start.49 = (bf16[2,96,768]{2,1,0:T(8,128)(2,1)}, bf16[2,96,768]{2,1,0:T(8,128)(2,1)S(1)}, u32[]{:S(2)}) copy-start(bf16[2,96,768]{2,1,0:T(8,128)(2,1)S(1)} %collective-permute-done.16) | copy-start | bytes 884740
  578.8 28.2 %collective-permute-start.17 = (bf16[4,96,768]{2,1,0:T(8,128)(2,1)}, bf16[4,96,768]{2,1,0:T(8,128)(2,1)}, u32[]{:S(2)}, u32[]{:S(2)}) collective-permute-start(bf16[4,96,768]{2,1,0:T(8,128)(2,1)} %pad_maximum_fusion.14), channel_id=1, source_target_pairs={{0,4},{4,0},{8,12},{12,8},{16,20},{20,16},{24,28},{28,24},{1,5},{5... | collective-permute-start | bytes 1769480 | tf_op jit(solution)/shard_map/ppermute | solution.py:428
  585.1 33.5 %collective-permute-start.25 = (bf16[4,96,768]{2,1,0:T(8,128)(2,1)}, bf16[4,96,768]{2,1,0:T(8,128)(2,1)}, u32[]{:S(2)}, u32[]{:S(2)}) collective-permute-start(bf16[4,96,768]{2,1,0:T(8,128)(2,1)} %pad_maximum_fusion.16), channel_id=1, source_target_pairs={{0,4},{4,0},{8,12},{12,8},{16,20},{20,16},{24,28},{28,24},{1,5},{5... | collective-permute-start | bytes 1769480 | tf_op jit(solution)/shard_map/ppermute | solution.py:428
  597.3 21.3 %copy-start.48 = (bf16[2,96,768]{2,1,0:T(8,128)(2,1)S(1)}, bf16[2,96,768]{2,1,0:T(8,128)(2,1)}, u32[]{:S(2)}) copy-start(bf16[2,96,768]{2,1,0:T(8,128)(2,1)} %copy-done.47) | copy-start | bytes 884740
  609.9 11.5 %copy-start.75 = (pred[8]{0:T(512)(128)(4,1)S(1)}, pred[8]{0:T(512)(128)(4,1)}, u32[]{:S(2)}) copy-start(pred[8]{0:T(512)(128)(4,1)} %compare_and_fusion) | copy-start | bytes 28
  (64 other events, 240.3 us)

commit v2 on v1

--- a/solution.py
+++ b/solution.py
@@ -685,10 +685,1094 @@
     )
 
 
+def slot_of(rel):
+    return (rel & 1) * 4 + (rel & 2) + ((rel >> 2) & 1)
+
+
+def gelu_both(a):
+    c = math.sqrt(2.0 / math.pi)
+    a2 = a * a
+    t = jnp.tanh(c * (a + 0.044715 * (a2 * a)))
+    half = 0.5 * (1.0 + t)
+    return a * half, half + 0.5 * a * (1.0 - t * t) * (c * (1.0 + 3.0 * 0.044715 * a2))
+
+
+def rms(x):
+    return lax.rsqrt(jnp.mean(x * x, axis=-1, keepdims=True) + EPSILON)
+
+
+def rms_back(x, inverse, gain, grad):
+    scaled = grad * gain
+    mean = jnp.mean(x * scaled, axis=-1, keepdims=True)
+    unit = x * inverse
+    return inverse * (scaled - unit * (inverse * mean)), jnp.sum(grad * unit, axis=0, keepdims=True)
+
+
+def onehot_rows(src):
+    n = src.shape[1]
+    return (lax.broadcasted_iota(jnp.int32, (n, n), 0) == src).astype(F32).astype(BF)
+
+
+def pre_kernel(
+    me_ref,
+    aq_ref,
+    len_ref,
+    qrows_ref,
+    bucket_ref,
+    dec_ref,
+    gain1_ref,
+    rel_ref,
+    wqkv_ref,
+    src_ref,
+    cstart_ref,
+    csize_ref,
+    sstart_ref,
+    ssize_ref,
+    lo_ref,
+    hi_ref,
+    brow_ref,
+    x0_ref,
+    h1_ref,
+    proj_ref,
+    oself_ref,
+    lse_ref,
+    order,
+    qstart,
+    qcount,
+    wide,
+    kp,
+    vp,
+    bias,
+    *,
+    answers,
+    length,
+    questions,
+    scale,
+):
+    rows, width = dec_ref.shape
+    nq, tiles = width // 256, rows // TQ
+    base = me_ref[0] * answers
+    n = jnp.int32(0)
+    first_row = jnp.int32(0)
+    for c in range(questions):
+        qstart[c] = first_row
+        first_row = first_row + qrows_ref[0, c]
+        qcount[c] = n
+
+        def visit(a, n):
+            hit = aq_ref[base + a] == c
+
+            @pl.when(hit)
+            def _():
+                order[n] = a
+
+            return n + hit.astype(jnp.int32)
+
+        n = lax.fori_loop(0, answers, visit, n)
+
+    def answer_of(tok):
+        ans = jnp.zeros_like(tok)
+        for k in range(1, answers):
+            ans = ans + (tok >= k * length).astype(jnp.int32)
+        return ans
+
+    tok = lax.broadcasted_iota(jnp.int32, (1, rows), 1)
+    ans = answer_of(tok)
+    src = tok - ans * length
+    for k in range(answers):
+        src = src + jnp.where(ans == k, order[k] * length, 0)
+    src_ref[...] = src
+
+    lane = lax.broadcasted_iota(jnp.int32, (tiles, 256), 1) % TQ
+    tok = lane + TQ * lax.broadcasted_iota(jnp.int32, (tiles, 256), 0)
+    ans = answer_of(tok)
+    sstart_ref[...] = ans * length
+    size = jnp.zeros_like(ans)
+    for k in range(answers):
+        size = size + jnp.where(ans == k, len_ref[order[k]], 0)
+    ssize_ref[...] = size
+    cstart = jnp.zeros_like(ans)
+    csize = jnp.zeros_like(ans) + qrows_ref[0, 0]
+    for c in range(1, questions):
+        here = ans >= qcount[c]
+        cstart = jnp.where(here, qstart[c], cstart)
+        csize = jnp.where(here, qrows_ref[0, c], csize)
+    cstart_ref[...] = cstart
+    csize_ref[...] = csize
+    for t in range(tiles):
+        q_first = aq_ref[base + order[t * TQ // length]]
+        q_last = aq_ref[base + order[(t * TQ + TQ - 1) // length]]
+        lo_ref[t] = qstart[q_first] // TK
+        hi_ref[t] = (qstart[q_last] + qrows_ref[0, q_last] + TK - 1) // TK
+
+    for c in range(nq):
+        head = lax.broadcasted_iota(jnp.int32, (rel_ref.shape[0], 256), 1) // 64
+        held = jnp.zeros((rel_ref.shape[0], 256), F32)
+        for a in range(4):
+            h = c * 4 + a
+            held = jnp.where(head == a, rel_ref[:, h : h + 1], held)
+        wide[:, c * 256 : (c + 1) * 256] = held
+    for d in range(length):
+        brow_ref[d : d + 1, :] = wide[pl.ds(bucket_ref[d], 1), :]
+
+    x0 = dot_tn(onehot_rows(src), dec_ref[...])
+    x0_ref[...] = x0.astype(BF)
+    h1_ref[...] = (x0 * rms(x0) * gain1_ref[...]).astype(BF)
+    for i in range(3):
+        cs = slice(i * width, (i + 1) * width)
+        proj_ref[:, cs] = dot(h1_ref[...], wqkv_ref[:, cs]).astype(BF)
+    fill_window(proj_ref, kp, vp, width)
+    fill_bias(brow_ref, bias, nq)
+
+    def tile(t, _):
+        row = pl.ds(pl.multiple_of(t * TQ, TQ), TQ)
+        win = pl.ds(pl.multiple_of(t * TQ, TQ), WIN)
+        mask = range_mask(t * TQ - 64, WIN, sstart_ref[pl.ds(t, 1), :], ssize_ref[pl.ds(t, 1), :])
+        for c in range(nq):
+            cs = slice(c * 256, (c + 1) * 256)
+            qst = stack4(proj_ref[row, cs] * jnp.asarray(scale, BF)).T
+            s = jnp.where(mask, dot(kp[win, cs], qst) + bias[c], MASKED)
+            m = jnp.max(red(s, jnp.max), axis=0, keepdims=True)
+            p = jnp.exp(s - m)
+            l = jnp.sum(red(p, jnp.sum), axis=0, keepdims=True)
+            p = (p * (1.0 / l)).astype(BF)
+            oself_ref[row, cs] = unstack4(dot_tn(p, vp[win, cs])).astype(BF)
+            lse_ref[t, c] = m + jnp.log(l)
+        return 0
+
+    lax.fori_loop(0, tiles, tile, 0)
+
+
+def mid_kernel(x0_ref, oself_ref, wso_ref, gain2_ref, wcq_ref, x1_ref, h2_ref, qc_ref, *, scale):
+    x1 = x0_ref[...].astype(F32) + dot(oself_ref[...], wso_ref[...])
+    x1_ref[...] = x1
+    h2_ref[...] = (x1 * rms(x1) * gain2_ref[...]).astype(BF)
+    qc_ref[...] = dot(h2_ref[...], wcq_ref[...]).astype(BF) * jnp.asarray(scale, BF)
+
+
+def mid(x0, oself, wso, gain, wcq, scale):
+    rows, width = x0.shape
+    return call(
+        functools.partial(mid_kernel, scale=scale),
+        "mid",
+        (sds((rows, width), F32), sds((rows, width), BF), sds((rows, width), BF)),
+        [VM] * 5,
+        (VM,) * 3,
+        [],
+        (x0, oself, wso, gain, wcq),
+        us=8,
+    )
+
+
+def call(kernel, name, out_shape, in_specs, out_specs, scratch, args, us):
+    moved = sum(math.prod(a.shape) * a.dtype.itemsize for a in args)
+    moved += sum(math.prod(a.shape) * a.dtype.itemsize for a in out_shape)
+    return pl.pallas_call(
+        kernel,
+        out_shape=out_shape,
+        in_specs=in_specs,
+        out_specs=out_specs,
+        scratch_shapes=scratch,
+        compiler_params=pltpu.CompilerParams(vmem_limit_bytes=LIMIT),
+        cost_estimate=pl.CostEstimate(flops=int(us * 1e11), bytes_accessed=moved, transcendentals=0),
+        name=name,
+    )(*args)
+
+
+def sds(shape, dtype):
+    return jax.ShapeDtypeStruct(shape, dtype)
+
+
+def pre(me, aq, lens, qrows, bucket, dec, g1, rel, wqkv, scale):
+    rows, width = dec.shape
+    tiles, nq, length = rows // TQ, width // 256, bucket.shape[0]
+    i32 = jnp.int32
+    meta = sds((tiles, 256), i32)
+    out = (
+        sds((1, rows), i32),
+        meta,
+        meta,
+        meta,
+        meta,
+        sds((tiles,), i32),
+        sds((tiles,), i32),
+        sds((length, width), F32),
+        sds((rows, width), BF),
+        sds((rows, width), BF),
+        sds((rows, 3 * width), BF),
+        sds((rows, width), BF),
+        sds((tiles, nq, 1, 256), F32),
+    )
+    return call(
+        functools.partial(
+            pre_kernel, answers=lens.shape[0], length=length, questions=qrows.shape[1], scale=scale
+        ),
+        "pre",
+        out,
+        [SM] * 5 + [VM] * 4,
+        (VM,) * 5 + (SM, SM) + (VM,) * 6,
+        [
+            pltpu.SMEM((lens.shape[0],), i32),
+            pltpu.SMEM((qrows.shape[1],), i32),
+            pltpu.SMEM((qrows.shape[1],), i32),
+            pltpu.VMEM((rel.shape[0], width), F32),
+            pltpu.VMEM((rows + 64, width), BF),
+            pltpu.VMEM((rows + 64, width), BF),
+            pltpu.VMEM((nq, WIN, 256), F32),
+        ],
+        (me, aq, lens, qrows, bucket, dec, g1, rel, wqkv),
+        us=40,
+    )
+
+
+def kv_cross_kernel(
+    me_ref,
+    lo_ref,
+    hi_ref,
+    start_ref,
+    size_ref,
+    q_ref,
+    *rest,
+    pieces,
+):
+    enc = rest[:pieces]
+    wkv_ref, k_ref, v_ref, kt_ref, o_ref, lse_ref, vt, qst, s_scr, m_scr, l_scr, acc = rest[pieces:]
+    rows, width = q_ref.shape
+    nq, tiles = width // 256, rows // TQ
+    n = enc[0].shape[0]
+    for r in range(pieces):
+        at = pl.ds(pl.multiple_of((me_ref[0] ^ r) * n, n), n)
+        kk = dot(enc[r][...], wkv_ref[:, :width]).astype(BF)
+        k_ref[at, :] = kk
+        kt_ref[:, at] = kk.T
+        vv = dot(enc[r][...], wkv_ref[:, width:]).astype(BF)
+        v_ref[at, :] = vv
+        vt[:, at] = vv.T
+
+    def tile(t, _):
+        st = start_ref[pl.ds(t, 1), :]
+        sz = size_ref[pl.ds(t, 1), :]
+        lo = lo_ref[t]
+        hi = hi_ref[t]
+        row = pl.ds(pl.multiple_of(t * TQ, TQ), TQ)
+        for c in range(nq):
+            qst[c] = stack4(q_ref[row, c * 256 : (c + 1) * 256]).T
+            m_scr[c] = jnp.full((8, 256), NEG, F32)
+            l_scr[c] = jnp.zeros((8, 256), F32)
+            acc[c] = jnp.zeros((256, 256), F32)
+
+        def scores(j, _):
+            kr = pl.ds(pl.multiple_of(j * TK, TK), TK)
+            mask = range_mask(j * TK, TK, st, sz)
+            for c in range(nq):
+                s = dot(k_ref[kr, c * 256 : (c + 1) * 256], qst[c])
+                s = jnp.where(mask, s, NEG)
+                s_scr[c, kr, :] = s
+                m_scr[c] = jnp.maximum(m_scr[c], red(s, jnp.max))
+            return 0
+
+        lax.fori_loop(lo, hi, scores, 0)
+        for c in range(nq):
+            m_scr[c] = jnp.broadcast_to(jnp.max(m_scr[c], axis=0, keepdims=True), (8, 256))
+
+        def mix(j, _):
+            kr = pl.ds(pl.multiple_of(j * TK, TK), TK)
+            for c in range(nq):
+                p = jnp.exp(s_scr[c, kr, :] - m_scr[c][0:1])
+                l_scr[c] += red(p, jnp.sum)
+                acc[c] += dot(vt[c * 256 : (c + 1) * 256, kr], p.astype(BF))
+            return 0
+
+        lax.fori_loop(lo, hi, mix, 0)
+        for c in range(nq):
+            l = jnp.sum(l_scr[c], axis=0, keepdims=True)
+            lse_ref[t, c] = m_scr[c][0:1] + jnp.log(l)
+            o_ref[row, c * 256 : (c + 1) * 256] = unstack4((acc[c] * (1.0 / l)).T)
+        return 0
+
+    lax.fori_loop(0, tiles, tile, 0)
+
+
+def kv_cross(me, lo, hi, start, size, q, enc, wkv):
+    rows, width = q.shape
+    tiles, nq = rows // TQ, width // 256
+    keys = len(enc) * enc[0].shape[0]
+    return call(
+        functools.partial(kv_cross_kernel, pieces=len(enc)),
+        "kv_cross",
+        (
+            sds((keys, width), BF),
+            sds((keys, width), BF),
+            sds((width, keys), BF),
+            sds((rows, width), F32),
+            sds((tiles, nq, 1, 256), F32),
+        ),
+        [SM] * 3 + [VM] * (3 + len(enc) + 1),
+        (VM,) * 5,
+        [
+            pltpu.VMEM((width, keys), BF),
+            pltpu.VMEM((nq, 256, 256), BF),
+            pltpu.VMEM((nq, keys, 256), F32),
+            pltpu.VMEM((nq, 8, 256), F32),
+            pltpu.VMEM((nq, 8, 256), F32),
+            pltpu.VMEM((nq, 256, 256), F32),
+        ],
+        (me, lo, hi, start, size, q, *enc, wkv),
+        us=80,
+    )
+
+
+def ffn_kernel(
+    me_ref,
+    src_ref,
+    x1_ref,
+    ocross_ref,
+    gain_ref,
+    cot_ref,
+    wco_ref,
+    win_ref,
+    wout_ref,
+    keep_ref,
+    send_ref,
+    x2_ref,
+    dh_ref,
+    g_ref,
+    oc_ref,
+    out_ref,
+    h3,
+    h3t,
+    out_acc,
+    *,
+    last,
+):
+    i = pl.program_id(0)
+    me_b, me_g = me_ref[0], me_ref[1]
+    f = me_b ^ i
+    rows, width = x1_ref.shape
+    quarter = width // 4
+    half = quarter // 2
+
+    @pl.when(i == 0)
+    def _():
+        hot = onehot_rows(src_ref[...])
+        g_ref[...] = dot_tn(hot, cot_ref[...]).astype(BF)
+        oc = ocross_ref[...].astype(BF)
+        oc_ref[...] = oc
+        x2 = x1_ref[...] + dot(oc, wco_ref[...])
+        x2_ref[...] = x2
+        n = (x2 * rms(x2) * gain_ref[...]).astype(BF)
+        h3[...] = n
+        h3t[...] = n.T
+        out_acc[...] = jnp.zeros_like(out_acc)
+        dh_ref[...] = jnp.zeros_like(dh_ref)
+
+    u, slope = gelu_both(dot(h3[...], win_ref[...]))
+    u = u.astype(BF)
+    out_acc[...] += dot(u, wout_ref[...])
+    da = (slope * dot_nt(g_ref[...], wout_ref[...])).astype(BF)
+    dh_ref[...] += dot_nt(da, win_ref[...])
+    dwo = dot_tn(u, g_ref[...]).astype(BF)
+    for s in range(8):
+        at = (i >> 1) * 8 + slot_of(me_g ^ s)
+
+        @pl.when((i & 1) == 0)
+        def _():
+            keep_ref[at, half:, :] = dwo[s * half : (s + 1) * half]
+
+        @pl.when((i & 1) == 1)
+        def _():
+            send_ref[at, half:, :] = dwo[s * half : (s + 1) * half]
+
+    for r in range(4):
+        part = h3t[pl.ds(pl.multiple_of((me_b ^ r) * quarter, quarter), quarter), :]
+        dwi = dot(part, da).astype(BF)
+        target = send_ref if r & 1 else keep_ref
+        for b in range(2):
+            at = (r >> 1) * 8 + slot_of(me_g ^ (2 * f + b))
+            target[at, :half, :] = dwi[b * half : (b + 1) * half]
+
+    @pl.when(i == last)
+    def _():
+        out = (x2_ref[...] + out_acc[...]).astype(BF)
+        out_ref[...] = dot(onehot_rows(src_ref[...]), out).astype(BF)
+
+
+def ffn(me, src, x1, ocross, gain, cot, wco, win, wout):
+    rows, width = x1.shape
+    steps = win.shape[1] // width
+    half = width // 8
+    full = lambda a: pl.BlockSpec(a.shape, lambda i, m: (0,) * len(a.shape))
+    outs = (
+        sds((16, 2 * half, width), BF),
+        sds((16, 2 * half, width), BF),
+        sds((rows, width), F32),
+        sds((rows, width), F32),
+        sds((rows, width), BF),
+        sds((rows, width), BF),
+        sds((rows, width), BF),
+    )
+    ins = (src, x1, ocross, gain, cot, wco)
+    grid_spec = pltpu.PrefetchScalarGridSpec(
+        num_scalar_prefetch=1,
+        grid=(steps,),
+        in_specs=[full(a) for a in ins]
+        + [
+            pl.BlockSpec((width, width), lambda i, m: (0, m[0] ^ i)),
+            pl.BlockSpec((width, width), lambda i, m: (m[0] ^ i, 0)),
+        ],
+        out_specs=tuple(full(a) for a in outs),
+        scratch_shapes=[
+            pltpu.VMEM((rows, width), BF),
+            pltpu.VMEM((width, rows), BF),
+            pltpu.VMEM((rows, width), F32),
+        ],
+    )
+    return pl.pallas_call(
+        functools.partial(ffn_kernel, last=steps - 1),
+        out_shape=outs,
+        grid_spec=grid_spec,
+        compiler_params=pltpu.CompilerParams(vmem_limit_bytes=LIMIT),
+        cost_estimate=pl.CostEstimate(flops=60 * 10**11, bytes_accessed=30 << 20, transcendentals=0),
+        name="ffn",
+    )(me, *ins, win, wout)
+
+
+def ffn_back_kernel(x2_ref, dh_ref, g_ref, gain_ref, wco_ref, dx2_ref, dyc_ref, do_ref, dgain_ref):
+    x2 = x2_ref[...]
+    dx, dgain_ref[...] = rms_back(x2, rms(x2), gain_ref[...], dh_ref[...])
+    dx2 = g_ref[...].astype(F32) + dx
+    dx2_ref[...] = dx2
+    dyc_ref[...] = dx2.astype(BF)
+    do_ref[...] = dot_nt(dyc_ref[...], wco_ref[...]).astype(BF)
+
+
+def ffn_back(x2, dh, g, gain, wco):
+    rows, width = x2.shape
+    return call(
+        ffn_back_kernel,
+        "ffn_back",
+        (sds((rows, width), F32), sds((rows, width), BF), sds((rows, width), BF), sds((1, width), F32)),
+        [VM] * 5,
+        (VM,) * 4,
+        [],
+        (x2, dh, g, gain, wco),
+        us=30,
+    )
+
+
+def cross_back_kernel(
+    me_ref,
+    lo_ref,
+    hi_ref,
+    start_ref,
+    size_ref,
+    q_ref,
+    do_ref,
+    o_ref,
+    lse_ref,
+    k_ref,
+    v_ref,
+    kt_ref,
+    dq_ref,
+    keep_ref,
+    send_ref,
+    qs,
+    qst,
+    dos,
+    dost,
+    del_scr,
+    dka,
+    dva,
+    dqt,
+    *,
+    scale,
+):
+    rows, width = q_ref.shape
+    nq, tiles = width // 256, rows // TQ
+    dka[...] = jnp.zeros_like(dka)
+    dva[...] = jnp.zeros_like(dva)
+
+    def tile(t, _):
+        st = start_ref[pl.ds(t, 1), :]
+        sz = size_ref[pl.ds(t, 1), :]
+        row = pl.ds(pl.multiple_of(t * TQ, TQ), TQ)
+        for c in range(nq):
+            cs = slice(c * 256, (c + 1) * 256)
+            a = stack4(q_ref[row, cs])
+            qs[c] = a
+            qst[c] = a.T
+            b = stack4(do_ref[row, cs])
+            dos[c] = b
+            dost[c] = b.T
+            product = do_ref[row, cs].astype(F32) * o_ref[row, cs]
+            total = jnp.sum(red(stack4(product).T, jnp.sum), axis=0, keepdims=True)
+            del_scr[c] = jnp.broadcast_to(total, (8, 256))
+            dqt[c] = jnp.zeros((256, 256), F32)
+
+        def step(j, _):
+            kr = pl.ds(pl.multiple_of(j * TK, TK), TK)
+            mask = range_mask(j * TK, TK, st, sz)
+            for c in range(nq):
+                cs = slice(c * 256, (c + 1) * 256)
+                s = dot(k_ref[kr, cs], qst[c])
+                p = jnp.where(mask, jnp.exp(s - lse_ref[t, c]), 0.0)
+                dp = dot(v_ref[kr, cs], dost[c])
+                ds = (p * (dp - del_scr[c][0:1])).astype(BF)
+                dva[kr, cs] += dot(p.astype(BF), dos[c])
+                dka[kr, cs] += dot(ds, qs[c])
+                dqt[c] += dot(kt_ref[cs, kr], ds)
+            return 0
+
+        lax.fori_loop(lo_ref[t], hi_ref[t], step, 0)
+        for c in range(nq):
+            cs = slice(c * 256, (c + 1) * 256)
+            dq_ref[row, cs] = (unstack4(dqt[c].T) * scale).astype(BF)
+        return 0
+
+    lax.fori_loop(0, tiles, tile, 0)
+    n = keep_ref.shape[1]
+    for r in range(4):
+        at = pl.ds(pl.multiple_of((me_ref[0] ^ r) * n, n), n)
+        target = send_ref if r & 1 else keep_ref
+        target[r >> 1, :, :width] = dka[at, :].astype(BF)
+        target[r >> 1, :, width:] = dva[at, :].astype(BF)
+
+
+def cross_back(me, lo, hi, start, size, q, do, o, lse, k, v, kt, scale):
+    rows, width = q.shape
+    keys, nq = k.shape[0], width // 256
+    part = sds((2, keys // 4, 2 * width), BF)
+    return call(
+        functools.partial(cross_back_kernel, scale=scale),
+        "cross_back",
+        (sds((rows, width), BF), part, part),
+        [SM] * 3 + [VM] * 9,
+        (VM,) * 3,
+        [pltpu.VMEM((nq, 256, 256), BF)] * 4
+        + [
+            pltpu.VMEM((nq, 8, 256), F32),
+            pltpu.VMEM((keys, width), F32),
+            pltpu.VMEM((keys, width), F32),
+            pltpu.VMEM((nq, 256, 256), F32),
+        ],
+        (me, lo, hi, start, size, q, do, o, lse, k, v, kt),
+        us=150,
+    )
+
+
+def cross_in_kernel(dq_ref, x1_ref, dx2_ref, gain_ref, wcq_ref, wso_ref, dx1_ref, dy1_ref, dos_ref, dgain_ref):
+    x1 = x1_ref[...]
+    dx, dgain_ref[...] = rms_back(x1, rms(x1), gain_ref[...], dot_nt(dq_ref[...], wcq_ref[...]))
+    dx1 = dx2_ref[...] + dx
+    dx1_ref[...] = dx1
+    dy1_ref[...] = dx1.astype(BF)
+    dos_ref[...] = dot_nt(dy1_ref[...], wso_ref[...]).astype(BF)
+
+
+def cross_in(dq, x1, dx2, gain, wcq, wso):
+    rows, width = x1.shape
+    return call(
+        cross_in_kernel,
+        "cross_in",
+        (sds((rows, width), F32), sds((rows, width), BF), sds((rows, width), BF), sds((1, width), F32)),
+        [VM] * 6,
+        (VM,) * 4,
+        [],
+        (dq, x1, dx2, gain, wcq, wso),
+        us=60,
+    )
+
+
+def put_pieces(me_ref, left_t, right, block, keep_ref, send_ref):
+    width = left_t.shape[0]
+    quarter = width // 4
+    half = quarter // 2
+    for r in range(4):
+        part = left_t[pl.ds(pl.multiple_of((me_ref[0] ^ r) * quarter, quarter), quarter), :]
+        grad = dot(part, right).astype(BF)
+        target = send_ref if r & 1 else keep_ref
+        for b in range(2):
+            at = (r >> 1) * 8 + slot_of(me_ref[1] ^ (2 * block + b))
+            target[at] = grad[b * half : (b + 1) * half]
+
+
+def cross_weights_kernel(
+    me_ref, dkv_ref, came_ref, enc0_ref, enc2_ref, wkv_ref, oc_ref, dyc_ref, h2_ref, dq_ref,
+    keep_ref, send_ref, own_ref, out_ref, both, enc_t, left_t,
+):
+    n, width2 = dkv_ref.shape[1], dkv_ref.shape[2]
+    width = width2 // 2
+    for r in range(2):
+        both[r * n : (r + 1) * n, :] = (dkv_ref[r].astype(F32) + came_ref[r].astype(F32)).astype(BF)
+    out_ref[...] = dot_nt(both[n:, :], wkv_ref[...]).astype(BF)
+    own_ref[...] = dot_nt(both[:n, :], wkv_ref[...])
+    enc_t[:, :n] = enc0_ref[...].T
+    enc_t[:, n:] = enc2_ref[...].T
+    put_pieces(me_ref, enc_t, both[:, :width], 2, keep_ref, send_ref)
+    put_pieces(me_ref, enc_t, both[:, width:], 3, keep_ref, send_ref)
+    left_t[...] = oc_ref[...].T
+    put_pieces(me_ref, left_t, dyc_ref[...], 0, keep_ref, send_ref)
+    left_t[...] = h2_ref[...].T
+    put_pieces(me_ref, left_t, dq_ref[...], 1, keep_ref, send_ref)
+
+
+def cross_weights(me, dkv, came, enc0, enc2, wkv, oc, dyc, h2, dq):
+    rows, width = oc.shape
+    n = enc0.shape[0]
+    part = sds((16, width // 8, width), BF)
+    return call(
+        cross_weights_kernel,
+        "cross_weights",
+        (part, part, sds((n, width), F32), sds((n, width), BF)),
+        [SM] + [VM] * 9,
+        (VM,) * 4,
+        [pltpu.VMEM((2 * n, 2 * width), BF), pltpu.VMEM((width, 2 * n), BF), pltpu.VMEM((width, rows), BF)],
+        (me, dkv, came, enc0, enc2, wkv, oc, dyc, h2, dq),
+        us=30,
+    )
+
+
+def self_back_kernel(
+    start_ref,
+    size_ref,
+    brow_ref,
+    bucket_ref,
+    proj_ref,
+    do_ref,
+    lse_ref,
+    dproj_ref,
+    drel_ref,
+    kp,
+    vp,
+    bias,
+    dka,
+    dva,
+    dsum,
+    *,
+    scale,
+):
+    rows, width = do_ref.shape
+    nq, tiles = width // 256, rows // TQ
+    fill_window(proj_ref, kp, vp, width)
+    fill_bias(brow_ref, bias, nq)
+    dka[...] = jnp.zeros_like(dka)
+    dva[...] = jnp.zeros_like(dva)
+    dsum[...] = jnp.zeros_like(dsum)
+
+    def tile(t, _):
+        row = pl.ds(pl.multiple_of(t * TQ, TQ), TQ)
+        win = pl.ds(pl.multiple_of(t * TQ, TQ), WIN)
+        mask = range_mask(t * TQ - 64, WIN, start_ref[pl.ds(t, 1), :], size_ref[pl.ds(t, 1), :])
+        for c in range(nq):
+            cs = slice(c * 256, (c + 1) * 256)
+            qs = stack4(proj_ref[row, cs] * jnp.asarray(scale, BF))
+            dos = stack4(do_ref[row, cs])
+            s = dot(kp[win, cs], qs.T) + bias[c]
+            p = jnp.where(mask, jnp.exp(s - lse_ref[t, c]), 0.0)
+            dp = dot(vp[win, cs], dos.T)
+            delta = jnp.sum(red(p * dp, jnp.sum), axis=0, keepdims=True)
+            ds = p * (dp - delta)
+            dsum[c] += ds
+            ds = ds.astype(BF)
+            dva[win, cs] += dot(p.astype(BF), dos)
+            dka[win, cs] += dot(ds, qs)
+            dproj_ref[row, cs] = (unstack4(dot_tn(ds, kp[win, cs])) * scale).astype(BF)
+        return 0
+
+    lax.fori_loop(0, tiles, tile, 0)
+    dproj_ref[:, width : 2 * width] = dka[64:, :].astype(BF)
+    dproj_ref[:, 2 * width : 3 * width] = dva[64:, :].astype(BF)
+    dist = distances()
+    drel_ref[...] = jnp.zeros_like(drel_ref)
+    for c in range(nq):
+        cs = slice(c * 256, (c + 1) * 256)
+
+        def one(d, _):
+            x = jnp.where(dist == d, dsum[c], 0.0)
+            at = pl.ds(bucket_ref[d], 1)
+            drel_ref[at, cs] += jnp.sum(red(x, jnp.sum), axis=0, keepdims=True)
+            return 0
+
+        lax.fori_loop(0, brow_ref.shape[0], one, 0)
+
+
+def self_back(start, size, brow, bucket, proj, do, lse, buckets, scale):
+    rows, width = do.shape
+    nq = width // 256
+    return call(
+        functools.partial(self_back_kernel, scale=scale),
+        "self_back",
+        (sds((rows, 3 * width), BF), sds((buckets, width), F32)),
+        [VM] * 3 + [SM] + [VM] * 3,
+        (VM, VM),
+        [
+            pltpu.VMEM((rows + 64, width), BF),
+            pltpu.VMEM((rows + 64, width), BF),
+            pltpu.VMEM((nq, WIN, 256), F32),
+            pltpu.VMEM((rows + 64, width), F32),
+            pltpu.VMEM((rows + 64, width), F32),
+            pltpu.VMEM((nq, WIN, 256), F32),
+        ],
+        (start, size, brow, bucket, proj, do, lse),
+        us=60,
+    )
+
+
+def self_weights_kernel(me_ref, h1_ref, dproj_ref, oself_ref, dy1_ref, keep_ref, send_ref, left_t):
+    width = h1_ref.shape[1]
+    left_t[...] = h1_ref[...].T
+    for i in range(3):
+        put_pieces(me_ref, left_t, dproj_ref[:, i * width : (i + 1) * width], i, keep_ref, send_ref)
+    left_t[...] = oself_ref[...].T
+    put_pieces(me_ref, left_t, dy1_ref[...], 3, keep_ref, send_ref)
+
+
+def self_weights(me, h1, dproj, oself, dy1):
+    rows, width = h1.shape
+    part = sds((16, width // 8, width), BF)
+    return call(
+        self_weights_kernel,
+        "self_weights",
+        (part, part),
+        [SM] + [VM] * 4,
+        (VM, VM),
+        [pltpu.VMEM((width, rows), BF)],
+        (me, h1, dproj, oself, dy1),
+        us=20,
+    )
+
+
+def self_in_kernel(src_ref, dproj_ref, wqkv_ref, x0_ref, gain_ref, dx1_ref, d_ref, dgain_ref):
+    x0 = x0_ref[...].astype(F32)
+    dx, dgain_ref[...] = rms_back(x0, rms(x0), gain_ref[...], dot_nt(dproj_ref[...], wqkv_ref[...]))
+    dx0 = dx1_ref[...] + dx
+    high = dx0.astype(BF)
+    low = (dx0 - high.astype(F32)).astype(BF)
+    hot = onehot_rows(src_ref[...])
+    d_ref[...] = dot(hot, high) + dot(hot, low)
+
+
+def self_in(src, dproj, wqkv, x0, gain, dx1):
+    rows, width = x0.shape
+    return call(
+        self_in_kernel,
+        "self_in",
+        (sds((rows, width), F32), sds((1, width), F32)),
+        [VM] * 6,
+        (VM, VM),
+        [],
+        (src, dproj, wqkv, x0, gain, dx1),
+        us=20,
+    )
+
+
+def unpack_ffn_kernel(me_ref, a0, a1, a2, a3, win_ref, wout_ref):
+    half = a0.shape[1] // 2
+    for i, ref in enumerate((a0, a1, a2, a3)):
+        for z2 in range(2):
+            s = me_ref[1] ^ ((i >> 1) + 2 * (i & 1) + 4 * z2)
+            piece = ref[z2]
+            rows = pl.ds(pl.multiple_of((s & 1) * half, half), half)
+            cols = pl.ds(pl.multiple_of((s >> 1) * 768, 768), 768)
+            win_ref[rows, cols] = piece[:half].astype(F32)
+            wout_ref[pl.ds(pl.multiple_of(s * half, half), half), :] = piece[half:].astype(F32)
+
+
+def unpack_ffn(me, arrays, win_shape, wout_shape):
+    return call(
+        unpack_ffn_kernel,
+        "unpack_ffn",
+        (sds(win_shape, F32), sds(wout_shape, F32)),
+        [SM] + [VM] * 4,
+        (VM, VM),
+        [],
+        (me, *arrays),
+        us=4,
+    )
+
+
+def tail_kernel(ck, sk, cs, ss, *rest, columns):
+    outs = rest[:4]
+    q, r1, r2, r3, r4, r5, f, send_sem, recv_sem = rest[4:]
+    count, step_rows = q.shape[0], q.shape[2]
+    per = count // 2
+    g, b = lax.axis_index("grp"), lax.axis_index("blk")
+    peers = [(g, b ^ 1), (g, b ^ 2), (g ^ 1, b), (g ^ 2, b), (g ^ 4, b), (g ^ 4, b), (g ^ 2, b), (g ^ 1, b)]
+    barrier = pltpu.get_barrier_semaphore()
+    for p in peers[:5]:
+        pl.semaphore_signal(barrier, inc=1, device_id=p, device_id_type=pl.DeviceIdType.MESH)
+    pl.semaphore_wait(barrier, 5)
+
+    def copy(k, j, first=None):
+        at = pl.ds(pl.multiple_of((j % per) * step_rows, step_rows), step_rows)
+        src, dst = [
+            lambda: (first.at[:, at, :], r1.at[j]),
+            lambda: (q.at[j, pl.ds(8, 8)], r2.at[j]),
+            lambda: (q.at[j, pl.ds(4, 4)], r3.at[j]),
+            lambda: (q.at[j, pl.ds(2, 2)], r4.at[j]),
+            lambda: (q.at[j, pl.ds(1, 1)], r5.at[j]),
+            lambda: (f.at[j, pl.ds(0, 1)], f.at[j, pl.ds(1, 1)]),
+            lambda: (f.at[j, pl.ds(0, 2)], f.at[j, pl.ds(2, 2)]),
+            lambda: (f.at[j, pl.ds(0, 4)], f.at[j, pl.ds(4, 4)]),
+        ][k]()
+        return pltpu.make_async_remote_copy(
+            src_ref=src,
+            dst_ref=dst,
+            send_sem=send_sem.at[k, j],
+            recv_sem=recv_sem.at[k, j],
+            device_id=peers[k],
+            device_id_type=pl.DeviceIdType.MESH,
+        )
+
+    def start_core(j, _):
+        copy(0, j, cs).start()
+        return 0
+
+    def start_core2(j, _):
+        copy(0, j, ss).start()
+        return 0
+
+    lax.fori_loop(0, per, start_core, 0)
+    lax.fori_loop(per, count, start_core2, 0)
+
+    def add(a, c):
+        return (a.astype(F32) + c.astype(F32)).astype(BF)
+
+    def event(k, j):
+        if k == 0:
+            at = pl.ds(pl.multiple_of((j % per) * step_rows, step_rows), step_rows)
+
+            @pl.when((j >= 0) & (j < per))
+            def _():
+                copy(0, j, cs).wait()
+                q[j] = add(ck[:, at, :], r1[j])
+                copy(1, j).start()
+
+            @pl.when((j >= per) & (j < count))
+            def _():
+                copy(0, j, ss).wait()
+                q[j] = add(sk[:, at, :], r1[j])
+                copy(1, j).start()
+
+            return
+
+        @pl.when((j >= 0) & (j < count))
+        def _():
+            copy(k, j).wait()
+            if k == 1:
+                q[j, 0:8] = add(q[j, 0:8], r2[j])
+            elif k == 2:
+                q[j, 0:4] = add(q[j, 0:4], r3[j])
+            elif k == 3:
+                q[j, 0:2] = add(q[j, 0:2], r4[j])
+            elif k == 4:
+                f[j, 0:1] = add(q[j, 0:1], r5[j])
+            if k < 7:
+                copy(k + 1, j).start()
+                return
+            base = (j % per) * step_rows
+            for slot in range(8):
+                s = g ^ ((slot >> 2) + (slot & 2) + 4 * (slot & 1))
+                block, side = s >> 1, s & 1
+                at = pl.ds(pl.multiple_of(side * (per * step_rows) + base, step_rows), step_rows)
+                wide = f[j, slot].astype(F32)
+                first = 0
+                for o, (out, n) in enumerate(zip(outs, columns)):
+                    if o == 2 or o == 0:
+                        first = 0
+                    mine = (j < per) if o < 2 else (j >= per)
+
+                    @pl.when(mine & (block >= first) & (block < first + n))
+                    def _():
+                        cols = pl.ds(pl.multiple_of((block - first) * 768, 768), 768)
+                        out[at, cols] = wide
+
+                    first += n
+
+    event(0, jnp.int32(0))
+    event(0, jnp.int32(1))
+
+    def step(t, _):
+        event(0, t + 2)
+        event(1, t)
+        event(4, t - 2)
+        event(7, t - 4)
+        event(6, t - 3)
+        event(3, t - 1)
+        event(5, t - 2)
+        event(2, t)
+        return 0
+
+    lax.fori_loop(0, count + 4, step, 0)
+
+
+def tail(c_keep, s_keep, c_send, s_send):
+    slots, rows, width = c_keep.shape
+    step_rows = 16
+    count = 2 * rows // step_rows
+    columns = (2, 2, 3, 1)
+    any_spec = pl.BlockSpec(memory_space=pl.ANY)
+
+    def buf(n):
+        return pltpu.VMEM((count, n, step_rows, width), BF)
+
+    return pl.pallas_call(
+        functools.partial(tail_kernel, columns=columns),
+        out_shape=tuple(sds((2 * rows, n * width), F32) for n in columns),
+        in_specs=[VM, VM, any_spec, any_spec],
+        out_specs=(VM,) * 4,
+        scratch_shapes=[buf(16), buf(16), buf(8), buf(4), buf(2), buf(1), buf(8)]
+        + [pltpu.SemaphoreType.DMA((8, count))] * 2,
+        compiler_params=pltpu.CompilerParams(
+            vmem_limit_bytes=LIMIT, collective_id=0, has_side_effects=True
+        ),
+        cost_estimate=pl.CostEstimate(flops=10**13, bytes_accessed=30 << 20, transcendentals=0),
+        name="tail",
+    )(c_keep, s_keep, c_send, s_send)
+
+
+def hop(x, core=0, xb=0, yb=0, z1=0, z2=0):
+    b, g = core | (xb << 1), yb | (z1 << 1) | (z2 << 2)
+    groups, blocks = lax.axis_size("grp"), lax.axis_size("blk")
+    pairs = [(i * blocks + j, (i ^ g) * blocks + (j ^ b)) for i in range(groups) for j in range(blocks)]
+    return lax.ppermute(x, ("grp", "blk"), pairs)
+
+
+def total(*parts):
+    out = parts[0].astype(F32)
+    for p in parts[1:]:
+        out = out + p.astype(F32)
+    return out.astype(BF)
+
+
+def after(x, *deps):
+    return lax.optimization_barrier((x,) + deps)[0]
+
+
+def split_xy(keep, came):
+    return [total(keep[4 * j : 4 * j + 4], came[4 * j : 4 * j + 4]) for j in range(4)]
+
+
+def send_xy(q):
+    return q[0], hop(q[1], yb=1), hop(q[2], xb=1), hop(q[3], xb=1, yb=1)
+
+
+def split_z(parts):
+    return [total(*[p[j] for p in parts]) for j in range(4)]
+
+
+def send_z(q):
+    return q[0], hop(q[1], z2=1), hop(q[2], z1=1), hop(q[3], z1=1, z2=1)
+
+
+def fused_body(
+    dec_in,
+    encodings,
+    answer_len,
+    answer_question,
+    question_rows,
+    bucket_table,
+    gain_self,
+    w_qkv,
+    w_self_out,
+    rel_bias,
+    gain_cross,
+    w_cross_q,
+    w_cross_kv,
+    w_cross_out,
+    gain_ffn,
+    w_in,
+    w_out,
+    cotangent,
+):
+    rows, width = dec_in.shape
+    buckets, heads = rel_bias.shape
+    scale = 1.0 / math.sqrt(width // heads)
+    me_b, me_g = lax.axis_index("blk"), lax.axis_index("grp")
+    me = jnp.stack([me_b, me_g]).astype(jnp.int32)
+    g1, g2, g3 = (g.reshape(1, width) for g in (gain_self, gain_cross, gain_ffn))
+
+    enc2 = hop(encodings, xb=1)
+    enc1 = hop(encodings, core=1)
+    src, cstart, csize, sstart, ssize, lo, hi, brow, x0, h1, proj, oself, lse_self = pre(
+        me, answer_question, answer_len, question_rows, bucket_table, dec_in, g1, rel_bias, w_qkv, scale
+    )
+    enc2, oself = lax.optimization_barrier((enc2, oself))
+    enc3 = hop(enc2, core=1)
+    enc1 = after(enc1, x0)
+    x1, h2, qc = mid(x0, oself, w_self_out, g2, w_cross_q, scale)
+    k, v, kt, ocross, lse = kv_cross(
+        me, lo, hi, cstart, csize, qc, (encodings, enc1, enc2, enc3), w_cross_kv
+    )
+    f_keep, f_send, x2, dh3, g_low, oc, layer_out = ffn(
+        me, src, x1, ocross, g3, cotangent, w_cross_out, w_in, w_out
+    )
+    f_came = hop(f_send, core=1)
+    dx2, dyc, do, dgain3 = ffn_back(x2, dh3, g_low, g3, w_cross_out)
+    f_came = after(f_came, do)
+    f_q = split_xy(f_keep, f_came)
+    do = after(do, *f_q)
+    f_parts = send_xy(f_q)
+    dq, kv_keep, kv_send = cross_back(me, lo, hi, cstart, csize, qc, do, ocross, lse, k, v, kt, scale)
+    kv_came = hop(kv_send, core=1)
+    f_parts = [after(p, dq) for p in f_parts]
+    f_q = split_z(f_parts)
+    dq = after(dq, *f_q)
+    f_parts = send_z(f_q)
+    dx1, dy1, dos, dgain2 = cross_in(dq, x1, dx2, g2, w_cross_q, w_self_out)
+    kv_came = after(kv_came, dos)
+    c_keep, c_send, enc_own, enc_out = cross_weights(
+        me, kv_keep, kv_came, encodings, enc2, w_cross_kv, oc, dyc, h2, dq
+    )
+    enc_came = hop(enc_out, xb=1)
+    f_parts = [after(p, c_keep) for p in f_parts]
+    f_own = total(*f_parts)
+    dos = after(dos, f_own, c_keep)
+    f_came = hop(f_own, z2=1)
+    dproj, drel = self_back(sstart, ssize, brow, bucket_table, proj, dos, lse_self, buckets, scale)
+    f_came = after(f_came, dproj)
+    f_pair = jnp.stack([f_own, f_came])
+    dproj = after(dproj, f_pair, enc_came)
+    s_keep, s_send = self_weights(me, h1, dproj, oself, dy1)
+    d_dec_in, dgain1 = self_in(src, dproj, w_qkv, x0, g1, dx1)
+    f_all = [f_pair, hop(f_pair, z1=1), hop(f_pair, yb=1), hop(f_pair, yb=1, z1=1)]
+    o_win, o_wout = unpack_ffn(me, f_all, (width // 4, w_in.shape[1]), (w_out.shape[0] // 4, width))
+    d_encodings = enc_own + enc_came.astype(F32)
+
+    drel = jnp.sum(drel.reshape(buckets, heads, -1), axis=2)
+    small = jnp.concatenate([dgain1[0], dgain2[0], dgain3[0], drel.reshape(-1)])
+    small = sum_everywhere(small.reshape(-1, 128)).reshape(-1)
+    o_co_cq, o_wckv, o_wqkv, o_wso = tail(c_keep, s_keep, c_send, s_send)
+    o_wco, o_wcq = o_co_cq[:, :width], o_co_cq[:, width:]
+
+    def own(v):
+        return lax.dynamic_slice_in_dim(v, me_b * (v.shape[0] // 4), v.shape[0] // 4, 0)
+
+    g_self, g_cross, g_ffn = (own(small[i * width : (i + 1) * width]) for i in range(3))
+    g_rel = own(small[3 * width :].reshape(buckets, heads))
+    return (
+        layer_out,
+        d_dec_in,
+        d_encodings,
+        g_self,
+        o_wqkv,
+        o_wso,
+        g_rel,
+        g_cross,
+        o_wcq,
+        o_wckv,
+        o_wco,
+        g_ffn,
+        o_win,
+        o_wout,
+    )
+
+
 def solution(mesh):
     rows = P(("grp", "blk"), None)
+    fused = mesh.shape["grp"] == 8 and mesh.shape["blk"] == 4
     return jax.shard_map(
-        body,
+        fused_body if fused else body,
         mesh=mesh,
         in_specs=(rows, rows, P(("grp", "blk")), P("grp"), P("grp", None)) + (P(),) * 12 + (rows,),
         out_specs=(rows, rows, rows, P("blk"))

time: 641 us -> 425 us (0.66)
  Pallas kernels: 135 us -> 334 us
  waiting for transfers between devices: 152 us -> 2.81 us
  matrix products: 120 us -> 0 us
  local copies, waits for them, and re-layouts: 117 us -> 12.5 us
  other arithmetic: 66.7 us -> 22.4 us
  starting transfers between devices: 41.8 us -> 50.7 us
    pallas_call x4 -> x13, Pallas kernels: 135 us -> 334 us  [the longest x11 199 us: call(): pl.pallas_call(kernel, out_shape=out_shape, in_specs=in_specs, out_specs=...]
    ppermute x42 -> x5, waiting for transfers between devices: 152 us -> 1.9 us  [swap(): return lax.ppermute(x, axis, [(i, i ^ bit) for i in range(size)])]
    dot_general x27 -> x0, matrix products: 120 us -> none  [the longest x10 42.2 us: dot_tn(): lax.dot_general(a, b, (((0,), (0,)), ((), ())), preferred_element_type=F32)]
    ppermute x0 -> x16, starting transfers between devices: none -> 45.1 us  [hop(): return lax.ppermute(x, ('grp', 'blk'), pairs)]
    ppermute x42 -> x5, starting transfers between devices: 41.8 us -> 5.54 us  [swap(): return lax.ppermute(x, axis, [(i, i ^ bit) for i in range(size)])]
    reshape x10 -> x6, local copies, waits for them, and re-layouts: 27.9 us -> 4.16 us  [the longest x3 2.43 us: fused_body(): g.reshape(1, width)]
    slice x24 -> x3, local copies, waits for them, and re-layouts: 21.5 us -> 1.1 us  [the longest x1 1.09 us: fused_body(): o_wco, o_wcq = (o_co_cq[:, :width], o_co_cq[:, width:])]
    unnamed x174 -> x38, local copies, waits for them, and re-layouts: 21.1 us -> 4.7 us
  transfers between devices with their start and end apart: 42 -> 21, of which waited for: 23 -> 2; matrix products, arithmetic and copies ran while one was open for 20% -> 5% of each run, Pallas kernels for 2% -> 56%
where the time goes in v2:
time: 425 us; the launch traced here: 423 us
  Pallas kernels  334 us (79%)
  starting transfers between devices  50.7 us (12%)
  other arithmetic  22.4 us (5%)
  local copies, waits for them, and re-layouts  12.5 us (3%)
    pallas_call x11, Pallas kernels, call(): pl.pallas_call(kernel, out_shape=out_shape, in_specs=in_specs, out_specs=...  199 us
    pallas_call x1, Pallas kernels, tail(): pl.pallas_call(functools.partial(tail_kernel, columns=columns), out_shape...  96.5 us
    ppermute x16, starting transfers between devices, hop(): return lax.ppermute(x, ('grp', 'blk'), pairs)  45.1 us
    pallas_call x1, Pallas kernels, ffn(): pl.pallas_call(functools.partial(ffn_kernel, last=steps - 1), out_shape=o...  38.1 us
  transfers between devices with their start and end apart: 21, of which 2 were waited for; matrix products, arithmetic and copies ran while one was open for 5% of the time, Pallas kernels for 56%

profile of v2, /device:TPU:0, one launch (start us, length us, event | category | flops | bytes accessed | tf_op | source)
XLA Modules:
  0.0 423.3 jit_solution(14032540956974643914)
XLA Ops:
  0.6 3.0 collective-permute-start
  3.6 0.0 collective-permute-start.1
  3.7 1.3 reshape.87.gain1_ref.gain_ref
  4.9 1.4 copy.33.rel_ref
  6.3 0.6 pad_add_fusion.me_ref
  6.9 20.2 %pre.1 = (s32[1,640]{1,0:T(1,128)}, s32[10,256]{1,0:T(8,128)}, s32[10,256]{1,0:T(8,128)}, s32[10,256]{1,0:T(8,128)}, s32[10,256]{1,0:T(8,128)}, /*index=5*/s32[1...) custom-call(s32[2]{0:T(128)} %pad_add_fusion.me_ref, ...), custom_call_target="tpu_custom_call" | custom-call | flops 3999999983616 | bytes 10561336 | tf_op jit(solution)/shard_map/pre/pallas_call | solution.py:870
  27.1 0.6 reshape.88.gain2_ref.gain_ref
  27.7 0.6 reshape.89.gain_ref
  28.3 0.5 collective-permute-start.2
  28.8 5.5 %mid.1 = (f32[640,768]{1,0:T(8,128)}, bf16[640,768]{1,0:T(8,128)(2,1)}, bf16[640,768]{1,0:T(8,128)(2,1)}) custom-call(bf16[640,768]{1,0:T(8,128)(2,1)} %get-tuple-element.88.x0_ref, bf16[640,768]{1,0:T(8,128)(2,1)} %get-tuple-element.90.oself_ref, bf16[768,768]{1,0:T(8,128)(2,1)} %wso_ref.3, f32[1,768]{1,0:T(1,128)} %reshape.88.gain2_ref.gain_ref, ...), custom_call_target="tpu_custom_call" | custom-call | flops 799999983616 | bytes 8260608 | tf_op jit(solution)/shard_map/mid/pallas_call | solution.py:870
  34.3 0.0 collective-permute-done.1.rest_1_
  34.3 41.9 %kv_cross.1 = (bf16[2048,768]{1,0:T(8,128)(2,1)}, bf16[2048,768]{1,0:T(8,128)(2,1)}, bf16[768,2048]{1,0:T(8,128)(2,1)}, f32[640,768]{1,0:T(8,128)}, f32[10,3,1,256]{3,2,1,0:T(1,128)}) custom-call(s32[2]{0:T(128)} %pad_add_fusion.me_ref, s32[10]{0:T(128)} %get-tuple-element.92.lo_ref, s32[10]{0:T(128)} %get-tuple-element.93.hi_ref, ...), custom_call_target="tpu_custom_call" | custom-call | flops 7999999967232 | bytes 17942616 | tf_op jit(solution)/shard_map/kv_cross/pallas_call | solution.py:870
  76.2 38.1 %ffn.1 = (bf16[16,192,768]{2,1,0:T(8,128)(2,1)}, bf16[16,192,768]{2,1,0:T(8,128)(2,1)}, f32[640,768]{1,0:T(8,128)}, f32[640,768]{1,0:T(8,128)}, bf16[640,768]{1,...) custom-call(s32[2]{0:T(128)} %pad_add_fusion.me_ref, s32[1,640]{1,0:T(1,128)} %get-tuple-element.87.src_ref, ...), custom_call_target="tpu_custom_call" | custom-call | flops 6000000106496 | bytes 31457280 | tf_op jit(solution)/shard_map/ffn/pallas_call | solution.py:1130
  114.2 3.1 collective-permute-start.3
  117.3 5.7 %ffn_back.1 = (f32[640,768]{1,0:T(8,128)}, bf16[640,768]{1,0:T(8,128)(2,1)}, bf16[640,768]{1,0:T(8,128)(2,1)}, f32[1,768]{1,0:T(1,128)}) custom-call(f32[640,768]{1,0:T(8,128)} %get-tuple-element.105.x2_ref, f32[640,768]{1,0:T(8,128)} %get-tuple-element.106.dh_ref, bf16[640,768]{1,0:T(8,128)(2,1)} %get-tuple-element.107.g_ref, f32[1,768]{1,0:T(1,128)} %reshape.89.gain_ref, ...), custom_call_target="tpu_custom_call" | custom-call | flops 3000000053248 | bytes 10033152 | tf_op jit(solution)/shard_map/ffn_back/pallas_call | solution.py:870
  123.0 1.3 reduce.2
  124.3 0.9 collective-permute-done.3
  125.2 5.9 %add_convert_fusion = (bf16[4,192,768]{2,1,0:T(8,128)(2,1)}, bf16[4,192,768]{2,1,0:T(8,128)(2,1)}, bf16[4,192,768]{2,1,0:T(8,128)(2,1)}, bf16[4,192,768]{2,1,0:T(8,128)(2,1)}) fusion(bf16[16,192,768]{2,1,0:T(8,128)(2,1)} %collective-permute-done.3, bf16[16,192,768]{2,1,0:T(8,128)(2,1)} %get-tuple-element.109), kind=kLoop, calls=%fused_computation | loop fusion | flops 9437184 | bytes 14155776 | tf_op jit(solution)/shard_map/convert_element_type | solution.py:1645
  131.1 2.7 collective-permute-start.6
  133.9 0.6 collective-permute-start.5
  134.5 1.1 collective-permute-start.4
  135.6 60.1 %cross_back.1 = (bf16[640,768]{1,0:T(8,128)(2,1)}, bf16[2,512,1536]{2,1,0:T(8,128)(2,1)}, bf16[2,512,1536]{2,1,0:T(8,128)(2,1)}) custom-call(s32[2]{0:T(128)} %pad_add_fusion.me_ref, s32[10]{0:T(128)} %get-tuple-element.92.lo_ref, s32[10]{0:T(128)} %get-tuple-element.93.hi_ref, s32[10,256]{1,0:T(8,128)} %get-tuple-element.94.start_ref, ...), custom_call_target="tpu_custom_call" | custom-call | flops 15000000266240 | bytes 20695128 | tf_op jit(solution)/shard_map/cross_back/pallas_call | solution.py:870
  195.6 4.8 %collective-permute-start.7 = (bf16[2,512,1536]{2,1,0:T(8,128)(2,1)}, bf16[2,512,1536]{2,1,0:T(8,128)(2,1)}, u32[]{:S(2)}, u32[]{:S(2)}) collective-permute-start(bf16[2,512,1536]{2,1,0:T(8,128)(2,1)} %get-tuple-element.126), channel_id=1, source_target_pairs={{0,1},{1,0},{2,3},{3,2},{4,5},{5,4},{6,7},{7,6},{8,9},{9,8},{10,11... | collective-permute-start | bytes 9437192 | tf_op jit(solution)/shard_map/ppermute | solution.py:1638
  200.4 0.0 collective-permute-done.6
  200.4 3.4 fusion.3
  203.8 22.9 %collective-permute-start.9 = (bf16[192,768]{1,0:T(8,128)(2,1)}, bf16[192,768]{1,0:T(8,128)(2,1)}, u32[]{:S(2)}, u32[]{:S(2)}) collective-permute-start(bf16[192,768]{1,0:T(8,128)(2,1)} %get-tuple-element.165), channel_id=1, source_target_pairs={{0,8},{1,9},{2,10},{3,11},{4,12},{5,13},{6,14},{7,15},{8,0},{9,1},... | collective-permute-start | bytes 884744 | tf_op jit(solution)/shard_map/ppermute | solution.py:1638
  226.7 1.4 collective-permute-start.8
  228.1 6.9 %cross_in.1 = (f32[640,768]{1,0:T(8,128)}, bf16[640,768]{1,0:T(8,128)(2,1)}, bf16[640,768]{1,0:T(8,128)(2,1)}, f32[1,768]{1,0:T(1,128)}) custom-call(bf16[640,768]{1,0:T(8,128)(2,1)} %get-tuple-element.122.dq_ref, f32[640,768]{1,0:T(8,128)} %get-tuple-element.91.x1_ref, f32[640,768]{1,0:T(8,128)} %get-tuple-element.123.dx2_ref, ...), custom_call_target="tpu_custom_call" | custom-call | flops 6000000106496 | bytes 11212800 | tf_op jit(solution)/shard_map/cross_in/pallas_call | solution.py:870
  235.0 1.3 reduce.1
  236.3 14.8 %cross_weights.1 = (bf16[16,96,768]{2,1,0:T(8,128)(2,1)}, bf16[16,96,768]{2,1,0:T(8,128)(2,1)}, f32[512,768]{1,0:T(8,128)}, bf16[512,768]{1,0:T(8,128)(2,1)}) custom-call(s32[2]{0:T(128)} %pad_add_fusion.me_ref, bf16[2,512,1536]{2,1,0:T(8,128)(2,1)} %get-tuple-element.125.dkv_ref, bf16[2,512,1536]{2,1,0:T(8,128)(2,1)} %collective-permute-done.7.came_ref, ...), custom_call_target="tpu_custom_call" | custom-call | flops 3000000053248 | bytes 21233672 | tf_op jit(solution)/shard_map/cross_weights/pallas_call | solution.py:870
  251.1 2.0 add_convert_fusion.4
  253.1 1.5 collective-permute-start.11
  254.6 18.6 %self_back.1 = (bf16[640,2304]{1,0:T(8,128)(2,1)}, f32[32,768]{1,0:T(8,128)}) custom-call(s32[10,256]{1,0:T(8,128)} %get-tuple-element.101.start_ref, s32[10,256]{1,0:T(8,128)} %get-tuple-element.102.size_ref, f32[20,768]{1,0:T(8,128)} %get-tuple-element.103.brow_ref, s32[20]{0:T(128)} %bucket_ref.3, bf16[640,2304]{1,0:T(8,128)(2,1)} %get-tuple-element.104.proj_ref, ...), custom_call_target="tpu_custom_call" | custom-call | flops 6000000106496 | bytes 7092304 | tf_op jit(solution)/shard_map/self_back/pallas_call | solution.py:870
  273.2 1.0 reshape.90
  274.2 0.1 reduce_sum.9
  274.3 0.6 reshape.91
  275.0 1.9 pad_maximum_fusion.a0
  276.9 12.4 %self_in.1 = (f32[640,768]{1,0:T(8,128)}, f32[1,768]{1,0:T(1,128)}) custom-call(s32[1,640]{1,0:T(1,128)} %get-tuple-element.87.src_ref, bf16[640,2304]{1,0:T(8,128)(2,1)} %get-tuple-element.141.dproj_ref, bf16[768,2304]{1,0:T(8,128)(2,1)} %wqkv_ref.3, bf16[640,768]{1,0:T(8,128)(2,1)} %get-tuple-element.88.x0_ref, f32[1,768]{1,0:T(1,128)} %reshape.87.gain1_ref.gain_ref, ...), custom_call_target="tpu_custom_call" | custom-call | flops 1999999991808 | bytes 11411968 | tf_op jit(solution)/shard_map/self_in/pallas_call | solution.py:870
  289.3 0.7 reduce
  290.0 0.0 copy-start.11
  290.1 0.1 collective-permute-start.13
  290.2 0.6 collective-permute-start.18
  290.7 3.0 collective-permute-start.20
  293.7 0.6 fusion.5
  294.3 2.0 collective-permute-start.14
  296.4 8.9 %self_weights.1 = (bf16[16,96,768]{2,1,0:T(8,128)(2,1)}, bf16[16,96,768]{2,1,0:T(8,128)(2,1)}) custom-call(s32[2]{0:T(128)} %pad_add_fusion.me_ref, bf16[640,768]{1,0:T(8,128)(2,1)} %get-tuple-element.149.h1_ref, bf16[640,2304]{1,0:T(8,128)(2,1)} %get-tuple-element.141.dproj_ref, bf16[640,768]{1,0:T(8,128)(2,1)} %get-tuple-element.90.oself_ref, ...), custom_call_target="tpu_custom_call" | custom-call | flops 1999999991808 | bytes 10616840 | tf_op jit(solution)/shard_map/self_weights/pallas_call | solution.py:870
  305.3 1.3 fusion.6
  306.6 96.5 %tail.1 = (f32[192,1536]{1,0:T(8,128)}, f32[192,1536]{1,0:T(8,128)}, f32[192,2304]{1,0:T(8,128)}, f32[192,768]{1,0:T(8,128)}) custom-call(bf16[16,96,768]{2,1,0:T(8,128)(2,1)} %get-tuple-element.131.ck, bf16[16,96,768]{2,1,0:T(8,128)(2,1)} %get-tuple-element.151.sk, bf16[16,96,768]{2,1,0:T(8,128)(2,1)} %get-tuple-element.152.cs, ...), custom_call_target="tpu_custom_call" | custom-call | flops 9999999827968 | bytes 31457280 | tf_op jit(solution)/shard_map/tail/pallas_call | solution.py:1619
  403.2 0.7 add.129
  403.9 1.8 collective-permute-start.16
  405.7 2.4 convert_add_fusion
  408.2 1.6 collective-permute-start.17
  409.8 1.1 fusion.4
  410.9 1.9 collective-permute-done.17
  412.8 0.1 reshape.93
  412.9 0.6 dynamic_slice.12
  413.5 0.6 dynamic_slice.14
  414.2 0.6 dynamic_slice.15
  414.8 0.6 constant_dynamic-slice_fusion
  415.4 4.2 unpack_ffn.1
  419.6 1.2 copy.37
  420.9 0.2 copy-done.6
  421.1 0.8 copy.38
  421.9 1.0 copy.39
  (58 shorter events, 0.1 us)
Async XLA Ops:
  0.6 27.6 %collective-permute-start = (bf16[512,768]{1,0:T(8,128)(2,1)}, bf16[512,768]{1,0:T(8,128)(2,1)}, u32[]{:S(2)}, u32[]{:S(2)}) collective-permute-start(bf16[512,768]{1,0:T(8,128)(2,1)} %enc0_ref.1), channel_id=1, source_target_pairs={{0,2},{1,3},{2,0},{3,1},{4,6},{5,7},{6,4},{7,5},{8,10},{9,11},{10,... | collective-permute-start | bytes 2359304 | tf_op jit(solution)/shard_map/ppermute | solution.py:1638
  3.6 30.6 %collective-permute-start.1 = (bf16[512,768]{1,0:T(8,128)(2,1)}, bf16[512,768]{1,0:T(8,128)(2,1)}, u32[]{:S(2)}, u32[]{:S(2)}) collective-permute-start(bf16[512,768]{1,0:T(8,128)(2,1)} %enc0_ref.1), channel_id=1, source_target_pairs={{0,1},{1,0},{2,3},{3,2},{4,5},{5,4},{6,7},{7,6},{8,9},{9,8},{10,11... | collective-permute-start | bytes 2359304 | tf_op jit(solution)/shard_map/ppermute | solution.py:1638
  6.9 20.2 %copy-start.15 = (f32[768]{0:T(1024)S(1)}, f32[768]{0:T(1024)}, u32[]{:S(2)}) copy-start(f32[768]{0:T(1024)} %param.28) | copy-start | bytes 9220
  6.9 20.8 %copy-start.16 = (f32[768]{0:T(1024)S(1)}, f32[768]{0:T(1024)}, u32[]{:S(2)}) copy-start(f32[768]{0:T(1024)} %param.32) | copy-start | bytes 9220
  28.3 6.0 %collective-permute-start.2 = (bf16[512,768]{1,0:T(8,128)(2,1)}, bf16[512,768]{1,0:T(8,128)(2,1)}, u32[]{:S(2)}, u32[]{:S(2)}) collective-permute-start(bf16[512,768]{1,0:T(8,128)(2,1)} %collective-permute-done.rest_2_.enc2_ref), channel_id=1, source_target_pairs={{0,1},{1,0},{2,3},{3,2},{4,5},{5,4},{6,7},{7,6},{8,9},{9,8},{10,11... | collective-permute-start | bytes 2359304 | tf_op jit(solution)/shard_map/ppermute | solution.py:1638
  114.2 11.0 %collective-permute-start.3 = (bf16[16,192,768]{2,1,0:T(8,128)(2,1)}, bf16[16,192,768]{2,1,0:T(8,128)(2,1)}, u32[]{:S(2)}, u32[]{:S(2)}) collective-permute-start(bf16[16,192,768]{2,1,0:T(8,128)(2,1)} %get-tuple-element.110), channel_id=1, source_target_pairs={{0,1},{1,0},{2,3},{3,2},{4,5},{5,4},{6,7},{7,6},{8,9},{9,8},{10,11... | collective-permute-start | bytes 14155784 | tf_op jit(solution)/shard_map/ppermute | solution.py:1638
  131.1 69.3 %collective-permute-start.6 = (bf16[4,192,768]{2,1,0:T(8,128)(2,1)}, bf16[4,192,768]{2,1,0:T(8,128)(2,1)}, u32[]{:S(2)}, u32[]{:S(2)}) collective-permute-start(bf16[4,192,768]{2,1,0:T(8,128)(2,1)} %get-tuple-element.160), channel_id=1, source_target_pairs={{0,6},{1,7},{2,4},{3,5},{4,2},{5,3},{6,0},{7,1},{8,14},{9,15},{10,... | collective-permute-start | bytes 3538952 | tf_op jit(solution)/shard_map/ppermute | solution.py:1638
  133.9 66.5 %collective-permute-start.5 = (bf16[4,192,768]{2,1,0:T(8,128)(2,1)}, bf16[4,192,768]{2,1,0:T(8,128)(2,1)}, u32[]{:S(2)}, u32[]{:S(2)}) collective-permute-start(bf16[4,192,768]{2,1,0:T(8,128)(2,1)} %get-tuple-element.161), channel_id=1, source_target_pairs={{0,2},{1,3},{2,0},{3,1},{4,6},{5,7},{6,4},{7,5},{8,10},{9,11},{10,... | collective-permute-start | bytes 3538952 | tf_op jit(solution)/shard_map/ppermute | solution.py:1638
  134.5 65.9 %collective-permute-start.4 = (bf16[4,192,768]{2,1,0:T(8,128)(2,1)}, bf16[4,192,768]{2,1,0:T(8,128)(2,1)}, u32[]{:S(2)}, u32[]{:S(2)}) collective-permute-start(bf16[4,192,768]{2,1,0:T(8,128)(2,1)} %get-tuple-element.162), channel_id=1, source_target_pairs={{0,4},{1,5},{2,6},{3,7},{4,0},{5,1},{6,2},{7,3},{8,12},{9,13},{10,... | collective-permute-start | bytes 3538952 | tf_op jit(solution)/shard_map/ppermute | solution.py:1638
  135.6 64.8 %copy-start = (bf16[4,192,768]{2,1,0:T(8,128)(2,1)S(1)}, bf16[4,192,768]{2,1,0:T(8,128)(2,1)}, u32[]{:S(2)}) copy-start(bf16[4,192,768]{2,1,0:T(8,128)(2,1)} %get-tuple-element.118) | copy-start | bytes 3538948
  195.6 40.7 %collective-permute-start.7 = (bf16[2,512,1536]{2,1,0:T(8,128)(2,1)}, bf16[2,512,1536]{2,1,0:T(8,128)(2,1)}, u32[]{:S(2)}, u32[]{:S(2)}) collective-permute-start(bf16[2,512,1536]{2,1,0:T(8,128)(2,1)} %get-tuple-element.126), channel_id=1, source_target_pairs={{0,1},{1,0},{2,3},{3,2},{4,5},{5,4},{6,7},{7,6},{8,9},{9,8},{10,11... | collective-permute-start | bytes 9437192 | tf_op jit(solution)/shard_map/ppermute | solution.py:1638
  203.8 47.2 %collective-permute-start.10 = (bf16[192,768]{1,0:T(8,128)(2,1)}, bf16[192,768]{1,0:T(8,128)(2,1)}, u32[]{:S(2)}, u32[]{:S(2)}) collective-permute-start(bf16[192,768]{1,0:T(8,128)(2,1)} %get-tuple-element.164), channel_id=1, source_target_pairs={{0,24},{1,25},{2,26},{3,27},{4,28},{5,29},{6,30},{7,31},{8,16},{9,... | collective-permute-start | bytes 884744 | tf_op jit(solution)/shard_map/ppermute | solution.py:1638
  203.8 47.2 %collective-permute-start.9 = (bf16[192,768]{1,0:T(8,128)(2,1)}, bf16[192,768]{1,0:T(8,128)(2,1)}, u32[]{:S(2)}, u32[]{:S(2)}) collective-permute-start(bf16[192,768]{1,0:T(8,128)(2,1)} %get-tuple-element.165), channel_id=1, source_target_pairs={{0,8},{1,9},{2,10},{3,11},{4,12},{5,13},{6,14},{7,15},{8,0},{9,1},... | collective-permute-start | bytes 884744 | tf_op jit(solution)/shard_map/ppermute | solution.py:1638
  226.7 24.3 %collective-permute-start.8 = (bf16[192,768]{1,0:T(8,128)(2,1)}, bf16[192,768]{1,0:T(8,128)(2,1)}, u32[]{:S(2)}, u32[]{:S(2)}) collective-permute-start(bf16[192,768]{1,0:T(8,128)(2,1)} %get-tuple-element.166), channel_id=1, source_target_pairs={{0,16},{1,17},{2,18},{3,19},{4,20},{5,21},{6,22},{7,23},{8,24},{9,... | collective-permute-start | bytes 884744 | tf_op jit(solution)/shard_map/ppermute | solution.py:1638
  236.3 14.8 %copy-start.3 = (bf16[192,768]{1,0:T(8,128)(2,1)S(1)}, bf16[192,768]{1,0:T(8,128)(2,1)}, u32[]{:S(2)}) copy-start(bf16[192,768]{1,0:T(8,128)(2,1)} %get-tuple-element.132) | copy-start | bytes 884740
  253.1 21.9 %collective-permute-start.11 = (bf16[192,768]{1,0:T(8,128)(2,1)}, bf16[192,768]{1,0:T(8,128)(2,1)}, u32[]{:S(2)}, u32[]{:S(2)}) collective-permute-start(bf16[192,768]{1,0:T(8,128)(2,1)} %add_convert_fusion.4), channel_id=1, source_target_pairs={{0,16},{1,17},{2,18},{3,19},{4,20},{5,21},{6,22},{7,23},{8,24},{9,... | collective-permute-start | bytes 884744 | tf_op jit(solution)/shard_map/ppermute | solution.py:1638
  254.6 22.3 %collective-permute-start.12 = (bf16[512,768]{1,0:T(8,128)(2,1)}, bf16[512,768]{1,0:T(8,128)(2,1)}, u32[]{:S(2)}, u32[]{:S(2)}) collective-permute-start(bf16[512,768]{1,0:T(8,128)(2,1)} %get-tuple-element.140), channel_id=1, source_target_pairs={{0,2},{1,3},{2,0},{3,1},{4,6},{5,7},{6,4},{7,5},{8,10},{9,11},{10,... | collective-permute-start | bytes 2359304 | tf_op jit(solution)/shard_map/ppermute | solution.py:1638
  276.9 13.1 %copy-start.7 = (f32[768]{0:T(1024)S(1)}, f32[768]{0:T(1024)}, u32[]{:S(2)}) copy-start(f32[768]{0:T(1024)} %reduce.2) | copy-start | bytes 9220
  276.9 13.1 %copy-start.9 = (f32[768]{0:T(1024)S(1)}, f32[768]{0:T(1024)}, u32[]{:S(2)}) copy-start(f32[768]{0:T(1024)} %reduce.1) | copy-start | bytes 9220
  276.9 13.2 %copy-start.13 = (f32[384]{0:T(512)S(1)}, f32[384]{0:T(512)}, u32[]{:S(2)}) copy-start(f32[384]{0:T(512)} %reshape.91) | copy-start | bytes 4612
  290.0 15.2 %copy-start.11 = (f32[768]{0:T(1024)}, f32[768]{0:T(1024)S(1)}, u32[]{:S(2)}) copy-start(f32[768]{0:T(1024)S(1)} %reduce) | copy-start | bytes 9220
  290.1 3.6 collective-permute-start.13
  290.2 125.2 %collective-permute-start.18 = (bf16[2,192,768]{2,1,0:T(8,128)(2,1)}, bf16[2,192,768]{2,1,0:T(8,128)(2,1)}, u32[]{:S(2)}, u32[]{:S(2)}) collective-permute-start(bf16[2,192,768]{2,1,0:T(8,128)(2,1)} %pad_maximum_fusion.a0), channel_id=1, source_target_pairs={{0,8},{1,9},{2,10},{3,11},{4,12},{5,13},{6,14},{7,15},{8,0},{9,1},... | collective-permute-start | bytes 1769480 | tf_op jit(solution)/shard_map/ppermute | solution.py:1638
  290.7 124.7 %collective-permute-start.19 = (bf16[2,192,768]{2,1,0:T(8,128)(2,1)}, bf16[2,192,768]{2,1,0:T(8,128)(2,1)}, u32[]{:S(2)}, u32[]{:S(2)}) collective-permute-start(bf16[2,192,768]{2,1,0:T(8,128)(2,1)} %pad_maximum_fusion.a0), channel_id=1, source_target_pairs={{0,4},{1,5},{2,6},{3,7},{4,0},{5,1},{6,2},{7,3},{8,12},{9,13},{10,... | collective-permute-start | bytes 1769480 | tf_op jit(solution)/shard_map/ppermute | solution.py:1638
  290.7 124.7 %collective-permute-start.20 = (bf16[2,192,768]{2,1,0:T(8,128)(2,1)}, bf16[2,192,768]{2,1,0:T(8,128)(2,1)}, u32[]{:S(2)}, u32[]{:S(2)}) collective-permute-start(bf16[2,192,768]{2,1,0:T(8,128)(2,1)} %pad_maximum_fusion.a0), channel_id=1, source_target_pairs={{0,12},{1,13},{2,14},{3,15},{4,8},{5,9},{6,10},{7,11},{8,4},{9,5},... | collective-permute-start | bytes 1769480 | tf_op jit(solution)/shard_map/ppermute | solution.py:1638
  293.7 11.5 %copy-start.12 = (f32[21,128]{1,0:T(8,128)}, f32[21,128]{1,0:T(8,128)S(1)}, u32[]{:S(2)}) copy-start(f32[21,128]{1,0:T(8,128)S(1)} %collective-permute-done.13) | copy-start | bytes 32260
  294.3 10.9 %collective-permute-start.14 = (f32[21,128]{1,0:T(8,128)}, f32[21,128]{1,0:T(8,128)}, u32[]{:S(2)}, u32[]{:S(2)}) collective-permute-start(f32[21,128]{1,0:T(8,128)} %fusion.5), channel_id=1, source_target_pairs={{0,2},{1,3},{2,0},{3,1},{4,6},{5,7},{6,4},{7,5},{8,10},{9,11},{10,... | collective-permute-start | bytes 32264 | tf_op jit(solution)/shard_map/ppermute | solution.py:428
  296.3 8.9 %copy-start.8 = (f32[768]{0:T(1024)S(1)}, f32[768]{0:T(1024)}, u32[]{:S(2)}) copy-start(f32[768]{0:T(1024)} %reduce.2) | copy-start | bytes 9220
  296.3 8.9 %copy-start.10 = (f32[768]{0:T(1024)S(1)}, f32[768]{0:T(1024)}, u32[]{:S(2)}) copy-start(f32[768]{0:T(1024)} %reduce.1) | copy-start | bytes 9220
  296.3 8.9 %copy-start.14 = (f32[384]{0:T(512)S(1)}, f32[384]{0:T(512)}, u32[]{:S(2)}) copy-start(f32[384]{0:T(512)} %reshape.91) | copy-start | bytes 4612
  306.6 96.6 %collective-permute-start.15 = (f32[21,128]{1,0:T(8,128)}, f32[21,128]{1,0:T(8,128)}, u32[]{:S(2)}, u32[]{:S(2)}) collective-permute-start(f32[21,128]{1,0:T(8,128)} %fusion.6), channel_id=1, source_target_pairs={{0,4},{4,0},{8,12},{12,8},{16,20},{20,16},{24,28},{28,24},{1,5},{5... | collective-permute-start | bytes 32264 | tf_op jit(solution)/shard_map/ppermute | solution.py:428
  306.6 99.1 %copy-start.2 = (f32[512,768]{1,0:T(8,128)S(1)}, f32[512,768]{1,0:T(8,128)}, u32[]{:S(2)}) copy-start(f32[512,768]{1,0:T(8,128)} %get-tuple-element.144) | copy-start | bytes 4718596
  403.9 5.9 %copy-start.5 = (f32[192,1536]{1,0:T(8,128)S(1)}, f32[192,1536]{1,0:T(8,128)}, u32[]{:S(2)}) copy-start(f32[192,1536]{1,0:T(8,128)} %get-tuple-element.156) | copy-start | bytes 3538948
  403.9 4.3 %collective-permute-start.16 = (f32[21,128]{1,0:T(8,128)S(1)}, f32[21,128]{1,0:T(8,128)S(1)}, u32[]{:S(2)}, u32[]{:S(2)}) collective-permute-start(f32[21,128]{1,0:T(8,128)S(1)} %add.129), channel_id=1, source_target_pairs={{0,8},{4,12},{8,0},{12,4},{16,24},{20,28},{24,16},{28,20},{1,9},{5... | collective-permute-start | bytes 32264 | tf_op jit(solution)/shard_map/ppermute | solution.py:428
  408.2 4.6 %collective-permute-start.17 = (f32[21,128]{1,0:T(8,128)S(1)}, f32[21,128]{1,0:T(8,128)S(1)}, u32[]{:S(2)}, u32[]{:S(2)}) collective-permute-start(f32[21,128]{1,0:T(8,128)S(1)} %add.130), channel_id=1, source_target_pairs={{0,16},{4,20},{8,24},{12,28},{16,0},{20,4},{24,8},{28,12},{1,17},{... | collective-permute-start | bytes 32264 | tf_op jit(solution)/shard_map/ppermute | solution.py:428
  415.4 4.2 copy-start.1
  419.6 1.4 copy-start.6
  419.6 2.3 copy-start.4

commit v3 on v2

--- a/solution.py
+++ b/solution.py
@@ -925,6 +925,23 @@
     )
 
 
+def own_heads(x):
+    return jnp.concatenate([x[a * 64 : (a + 1) * 64, a * TQ : (a + 1) * TQ] for a in range(4)], axis=0)
+
+
+def in_pairs(lo, hi, work):
+    def two(i, _):
+        work(lo + 2 * i)
+        work(lo + 2 * i + 1)
+        return 0
+
+    lax.fori_loop(0, (hi - lo) // 2, two, 0)
+
+    @pl.when((hi - lo) % 2 == 1)
+    def _():
+        work(hi - 1)
+
+
 def kv_cross_kernel(
     me_ref,
     lo_ref,
@@ -956,38 +973,36 @@
         hi = hi_ref[t]
         row = pl.ds(pl.multiple_of(t * TQ, TQ), TQ)
         for c in range(nq):
-            qst[c] = stack4(q_ref[row, c * 256 : (c + 1) * 256]).T
+            qst[c] = stack4(q_ref[row, c * 256 : (c + 1) * 256])
             m_scr[c] = jnp.full((8, 256), NEG, F32)
             l_scr[c] = jnp.zeros((8, 256), F32)
             acc[c] = jnp.zeros((256, 256), F32)
 
-        def scores(j, _):
+        def scores(j):
             kr = pl.ds(pl.multiple_of(j * TK, TK), TK)
             mask = range_mask(j * TK, TK, st, sz)
             for c in range(nq):
-                s = dot(k_ref[kr, c * 256 : (c + 1) * 256], qst[c])
+                s = dot_nt(k_ref[kr, c * 256 : (c + 1) * 256], qst[c])
                 s = jnp.where(mask, s, NEG)
                 s_scr[c, kr, :] = s
                 m_scr[c] = jnp.maximum(m_scr[c], red(s, jnp.max))
-            return 0
-
-        lax.fori_loop(lo, hi, scores, 0)
+
+        in_pairs(lo, hi, scores)
         for c in range(nq):
             m_scr[c] = jnp.broadcast_to(jnp.max(m_scr[c], axis=0, keepdims=True), (8, 256))
 
-        def mix(j, _):
+        def mix(j):
             kr = pl.ds(pl.multiple_of(j * TK, TK), TK)
             for c in range(nq):
                 p = jnp.exp(s_scr[c, kr, :] - m_scr[c][0:1])
                 l_scr[c] += red(p, jnp.sum)
                 acc[c] += dot(vt[c * 256 : (c + 1) * 256, kr], p.astype(BF))
-            return 0
-
-        lax.fori_loop(lo, hi, mix, 0)
+
+        in_pairs(lo, hi, mix)
         for c in range(nq):
             l = jnp.sum(l_scr[c], axis=0, keepdims=True)
             lse_ref[t, c] = m_scr[c][0:1] + jnp.log(l)
-            o_ref[row, c * 256 : (c + 1) * 256] = unstack4((acc[c] * (1.0 / l)).T)
+            o_ref[row, c * 256 : (c + 1) * 256] = own_heads(acc[c] * (1.0 / l)).T
         return 0
 
     lax.fori_loop(0, tiles, tile, 0)
@@ -1088,7 +1103,8 @@
         dwi = dot(part, da).astype(BF)
         target = send_ref if r & 1 else keep_ref
         for b in range(2):
-            at = (r >> 1) * 8 + slot_of(me_g ^ (2 * f + b))
+            rel = me_g ^ (2 * f + b)
+            at = (rel & 1) * 8 + (r >> 1) * 4 + (rel & 2) + ((rel >> 2) & 1)
             target[at, :half, :] = dwi[b * half : (b + 1) * half]
 
     @pl.when(i == last)
@@ -1177,13 +1193,13 @@
     keep_ref,
     send_ref,
     qs,
-    qst,
     dos,
-    dost,
     del_scr,
     dka,
     dva,
     dqt,
+    ps,
+    dss,
     *,
     scale,
 ):
@@ -1198,35 +1214,56 @@
         row = pl.ds(pl.multiple_of(t * TQ, TQ), TQ)
         for c in range(nq):
             cs = slice(c * 256, (c + 1) * 256)
-            a = stack4(q_ref[row, cs])
-            qs[c] = a
-            qst[c] = a.T
-            b = stack4(do_ref[row, cs])
-            dos[c] = b
-            dost[c] = b.T
-            product = do_ref[row, cs].astype(F32) * o_ref[row, cs]
-            total = jnp.sum(red(stack4(product).T, jnp.sum), axis=0, keepdims=True)
+            qs[c] = stack4(q_ref[row, cs])
+            b = do_ref[row, cs]
+            dos[c] = stack4(b)
+            product = (b.astype(F32) * o_ref[row, cs]).T
+            total = jnp.concatenate(
+                [jnp.sum(product[h * 64 : (h + 1) * 64], axis=0, keepdims=True) for h in range(4)], axis=1
+            )
             del_scr[c] = jnp.broadcast_to(total, (8, 256))
             dqt[c] = jnp.zeros((256, 256), F32)
 
-        def step(j, _):
+        def probs(j, slot):
             kr = pl.ds(pl.multiple_of(j * TK, TK), TK)
             mask = range_mask(j * TK, TK, st, sz)
             for c in range(nq):
                 cs = slice(c * 256, (c + 1) * 256)
-                s = dot(k_ref[kr, cs], qst[c])
+                s = dot_nt(k_ref[kr, cs], qs[c])
                 p = jnp.where(mask, jnp.exp(s - lse_ref[t, c]), 0.0)
-                dp = dot(v_ref[kr, cs], dost[c])
-                ds = (p * (dp - del_scr[c][0:1])).astype(BF)
-                dva[kr, cs] += dot(p.astype(BF), dos[c])
+                dp = dot_nt(v_ref[kr, cs], dos[c])
+                ps[slot, c] = p.astype(BF)
+                dss[slot, c] = (p * (dp - del_scr[c][0:1])).astype(BF)
+
+        def grads(j, slot):
+            kr = pl.ds(pl.multiple_of(j * TK, TK), TK)
+            for c in range(nq):
+                cs = slice(c * 256, (c + 1) * 256)
+                ds = dss[slot, c]
+                dva[kr, cs] += dot(ps[slot, c], dos[c])
                 dka[kr, cs] += dot(ds, qs[c])
                 dqt[c] += dot(kt_ref[cs, kr], ds)
+
+        lo = lo_ref[t]
+        hi = hi_ref[t]
+
+        def two(i, _):
+            probs(lo + 2 * i, 0)
+            probs(lo + 2 * i + 1, 1)
+            grads(lo + 2 * i, 0)
+            grads(lo + 2 * i + 1, 1)
             return 0
 
-        lax.fori_loop(lo_ref[t], hi_ref[t], step, 0)
+        lax.fori_loop(0, (hi - lo) // 2, two, 0)
+
+        @pl.when((hi - lo) % 2 == 1)
+        def _():
+            probs(hi - 1, 0)
+            grads(hi - 1, 0)
+
         for c in range(nq):
             cs = slice(c * 256, (c + 1) * 256)
-            dq_ref[row, cs] = (unstack4(dqt[c].T) * scale).astype(BF)
+            dq_ref[row, cs] = (own_heads(dqt[c]).T * scale).astype(BF)
         return 0
 
     lax.fori_loop(0, tiles, tile, 0)
@@ -1238,275 +1275,207 @@
         target[r >> 1, :, width:] = dva[at, :].astype(BF)
 
 
-def cross_back(me, lo, hi, start, size, q, do, o, lse, k, v, kt, scale):
-    rows, width = q.shape
-    keys, nq = k.shape[0], width // 256
+def cross_back(me, lo, hi, start, size, q, do, o, lse, k, v, kt, scale, first, nq):
+    rows = q.shape[0]
+    keys, width = k.shape[0], nq * 256
+    tiles = rows // TQ
+    at = first // nq
     part = sds((2, keys // 4, 2 * width), BF)
-    return call(
+    cols = lambda n: pl.BlockSpec((n, width), lambda i: (0, at))
+    whole = lambda a: pl.BlockSpec(a.shape, lambda i: (0,) * len(a.shape))
+    outs = (sds((rows, width), BF), part, part)
+    return pl.pallas_call(
         functools.partial(cross_back_kernel, scale=scale),
-        "cross_back",
-        (sds((rows, width), BF), part, part),
-        [SM] * 3 + [VM] * 9,
-        (VM,) * 3,
-        [pltpu.VMEM((nq, 256, 256), BF)] * 4
+        grid=(1,),
+        out_shape=outs,
+        in_specs=[
+            SM,
+            SM,
+            SM,
+            whole(start),
+            whole(size),
+            cols(rows),
+            cols(rows),
+            cols(rows),
+            pl.BlockSpec((tiles, nq, 1, 256), lambda i: (0, at, 0, 0)),
+            cols(keys),
+            cols(keys),
+            pl.BlockSpec((width, keys), lambda i: (at, 0)),
+        ],
+        out_specs=tuple(whole(a) for a in outs),
+        scratch_shapes=[pltpu.VMEM((nq, 256, 256), BF)] * 2
         + [
             pltpu.VMEM((nq, 8, 256), F32),
             pltpu.VMEM((keys, width), F32),
             pltpu.VMEM((keys, width), F32),
             pltpu.VMEM((nq, 256, 256), F32),
+            pltpu.VMEM((2, nq, 256, 256), BF),
+            pltpu.VMEM((2, nq, 256, 256), BF),
         ],
-        (me, lo, hi, start, size, q, do, o, lse, k, v, kt),
-        us=150,
-    )
-
-
-def cross_in_kernel(dq_ref, x1_ref, dx2_ref, gain_ref, wcq_ref, wso_ref, dx1_ref, dy1_ref, dos_ref, dgain_ref):
+        compiler_params=pltpu.CompilerParams(vmem_limit_bytes=LIMIT),
+        cost_estimate=pl.CostEstimate(flops=10**13, bytes_accessed=30 << 20, transcendentals=0),
+        name="cross_back",
+    )(me, lo, hi, start, size, q, do, o, lse, k, v, kt)
+
+
+def cross_in_kernel(
+    dq0_ref, dq1_ref, x1_ref, dx2_ref, gain_ref, wcq_ref, wso_ref, dx1_ref, dy1_ref, dos_ref, dgain_ref
+):
     x1 = x1_ref[...]
-    dx, dgain_ref[...] = rms_back(x1, rms(x1), gain_ref[...], dot_nt(dq_ref[...], wcq_ref[...]))
+    cut = dq0_ref.shape[1]
+    back = dot_nt(dq0_ref[...], wcq_ref[:, :cut]) + dot_nt(dq1_ref[...], wcq_ref[:, cut:])
+    dx, dgain_ref[...] = rms_back(x1, rms(x1), gain_ref[...], back)
     dx1 = dx2_ref[...] + dx
     dx1_ref[...] = dx1
     dy1_ref[...] = dx1.astype(BF)
     dos_ref[...] = dot_nt(dy1_ref[...], wso_ref[...]).astype(BF)
 
 
-def cross_in(dq, x1, dx2, gain, wcq, wso):
+def cross_in(dq0, dq1, x1, dx2, gain, wcq, wso):
     rows, width = x1.shape
     return call(
         cross_in_kernel,
         "cross_in",
         (sds((rows, width), F32), sds((rows, width), BF), sds((rows, width), BF), sds((1, width), F32)),
-        [VM] * 6,
+        [VM] * 7,
         (VM,) * 4,
         [],
-        (dq, x1, dx2, gain, wcq, wso),
+        (dq0, dq1, x1, dx2, gain, wcq, wso),
         us=60,
     )
 
 
-def put_pieces(me_ref, left_t, right, block, keep_ref, send_ref):
+def put_pieces(me_b, me_g, left_t, right, block, keep_ref, send_ref):
     width = left_t.shape[0]
     quarter = width // 4
-    half = quarter // 2
+    tall, wide = quarter // 4, width // 2
     for r in range(4):
-        part = left_t[pl.ds(pl.multiple_of((me_ref[0] ^ r) * quarter, quarter), quarter), :]
+        part = left_t[pl.ds(pl.multiple_of((me_b ^ r) * quarter, quarter), quarter), :]
         grad = dot(part, right).astype(BF)
         target = send_ref if r & 1 else keep_ref
-        for b in range(2):
-            at = (r >> 1) * 8 + slot_of(me_ref[1] ^ (2 * block + b))
-            target[at] = grad[b * half : (b + 1) * half]
+        for s in range(8):
+            at = (r >> 1) * 8 + slot_of(me_g ^ s)
+            y, x = (s >> 1) * tall, (s & 1) * wide
+            target[at, block * tall : (block + 1) * tall, :] = grad[y : y + tall, x : x + wide]
 
 
 def cross_weights_kernel(
-    me_ref, dkv_ref, came_ref, enc0_ref, enc2_ref, wkv_ref, oc_ref, dyc_ref, h2_ref, dq_ref,
-    keep_ref, send_ref, own_ref, out_ref, both, enc_t, left_t,
+    me_ref, keep0_ref, came0_ref, keep1_ref, came1_ref, enc0_ref, enc2_ref, wkv_ref, oc_ref, dyc_ref, h2_ref,
+    dq0_ref, dq1_ref, keep_ref, send_ref, own_ref, out_ref, both, enc_t, left_t,
 ):
-    n, width2 = dkv_ref.shape[1], dkv_ref.shape[2]
-    width = width2 // 2
+    n = keep0_ref.shape[1]
+    width = oc_ref.shape[1]
+    cut = dq0_ref.shape[1]
     for r in range(2):
-        both[r * n : (r + 1) * n, :] = (dkv_ref[r].astype(F32) + came_ref[r].astype(F32)).astype(BF)
+        rows = slice(r * n, (r + 1) * n)
+        for keep, came, at, wide in ((keep0_ref, came0_ref, 0, cut), (keep1_ref, came1_ref, cut, width - cut)):
+            total = (keep[r].astype(F32) + came[r].astype(F32)).astype(BF)
+            both[rows, at : at + wide] = total[:, :wide]
+            both[rows, width + at : width + at + wide] = total[:, wide:]
     out_ref[...] = dot_nt(both[n:, :], wkv_ref[...]).astype(BF)
     own_ref[...] = dot_nt(both[:n, :], wkv_ref[...])
     enc_t[:, :n] = enc0_ref[...].T
     enc_t[:, n:] = enc2_ref[...].T
-    put_pieces(me_ref, enc_t, both[:, :width], 2, keep_ref, send_ref)
-    put_pieces(me_ref, enc_t, both[:, width:], 3, keep_ref, send_ref)
+    me_b, me_g = me_ref[0], me_ref[1]
+    put_pieces(me_b, me_g, enc_t, both[:, :width], 2, keep_ref, send_ref)
+    put_pieces(me_b, me_g, enc_t, both[:, width:], 3, keep_ref, send_ref)
     left_t[...] = oc_ref[...].T
-    put_pieces(me_ref, left_t, dyc_ref[...], 0, keep_ref, send_ref)
+    put_pieces(me_b, me_g, left_t, dyc_ref[...], 0, keep_ref, send_ref)
     left_t[...] = h2_ref[...].T
-    put_pieces(me_ref, left_t, dq_ref[...], 1, keep_ref, send_ref)
-
-
-def cross_weights(me, dkv, came, enc0, enc2, wkv, oc, dyc, h2, dq):
+    dq = jnp.concatenate([dq0_ref[...], dq1_ref[...]], axis=1)
+    put_pieces(me_b, me_g, left_t, dq, 1, keep_ref, send_ref)
+
+
+def cross_weights(me, keep0, came0, keep1, came1, enc0, enc2, wkv, oc, dyc, h2, dq0, dq1):
     rows, width = oc.shape
     n = enc0.shape[0]
-    part = sds((16, width // 8, width), BF)
+    part = sds((16, width // 4, width // 2), BF)
     return call(
         cross_weights_kernel,
         "cross_weights",
         (part, part, sds((n, width), F32), sds((n, width), BF)),
-        [SM] + [VM] * 9,
+        [SM] + [VM] * 12,
         (VM,) * 4,
         [pltpu.VMEM((2 * n, 2 * width), BF), pltpu.VMEM((width, 2 * n), BF), pltpu.VMEM((width, rows), BF)],
-        (me, dkv, came, enc0, enc2, wkv, oc, dyc, h2, dq),
+        (me, keep0, came0, keep1, came1, enc0, enc2, wkv, oc, dyc, h2, dq0, dq1),
         us=30,
     )
 
 
-def self_back_kernel(
+def late_kernel(
     start_ref,
     size_ref,
+    bucket_ref,
     brow_ref,
-    bucket_ref,
     proj_ref,
     do_ref,
     lse_ref,
-    dproj_ref,
-    drel_ref,
+    h1_ref,
+    oself_ref,
+    dy1_ref,
+    src_ref,
+    x0_ref,
+    gain_ref,
+    dx1_ref,
+    wqkv_ref,
+    dg2_ref,
+    dg3_ref,
+    ck,
+    cs,
+    d_ref,
+    small_ref,
+    f_ref,
     kp,
     vp,
     bias,
     dka,
     dva,
     dsum,
+    dproj,
+    left_t,
+    sk,
+    ss,
+    high,
+    low,
+    drow,
+    sm_in,
+    dgain,
+    q,
+    r1,
+    r2,
+    r3,
+    r4,
+    r5,
+    f,
+    send_sem,
+    recv_sem,
+    sm_send,
+    sm_recv,
     *,
     scale,
 ):
     rows, width = do_ref.shape
     nq, tiles = width // 256, rows // TQ
-    fill_window(proj_ref, kp, vp, width)
-    fill_bias(brow_ref, bias, nq)
-    dka[...] = jnp.zeros_like(dka)
-    dva[...] = jnp.zeros_like(dva)
-    dsum[...] = jnp.zeros_like(dsum)
-
-    def tile(t, _):
-        row = pl.ds(pl.multiple_of(t * TQ, TQ), TQ)
-        win = pl.ds(pl.multiple_of(t * TQ, TQ), WIN)
-        mask = range_mask(t * TQ - 64, WIN, start_ref[pl.ds(t, 1), :], size_ref[pl.ds(t, 1), :])
-        for c in range(nq):
-            cs = slice(c * 256, (c + 1) * 256)
-            qs = stack4(proj_ref[row, cs] * jnp.asarray(scale, BF))
-            dos = stack4(do_ref[row, cs])
-            s = dot(kp[win, cs], qs.T) + bias[c]
-            p = jnp.where(mask, jnp.exp(s - lse_ref[t, c]), 0.0)
-            dp = dot(vp[win, cs], dos.T)
-            delta = jnp.sum(red(p * dp, jnp.sum), axis=0, keepdims=True)
-            ds = p * (dp - delta)
-            dsum[c] += ds
-            ds = ds.astype(BF)
-            dva[win, cs] += dot(p.astype(BF), dos)
-            dka[win, cs] += dot(ds, qs)
-            dproj_ref[row, cs] = (unstack4(dot_tn(ds, kp[win, cs])) * scale).astype(BF)
-        return 0
-
-    lax.fori_loop(0, tiles, tile, 0)
-    dproj_ref[:, width : 2 * width] = dka[64:, :].astype(BF)
-    dproj_ref[:, 2 * width : 3 * width] = dva[64:, :].astype(BF)
-    dist = distances()
-    drel_ref[...] = jnp.zeros_like(drel_ref)
-    for c in range(nq):
-        cs = slice(c * 256, (c + 1) * 256)
-
-        def one(d, _):
-            x = jnp.where(dist == d, dsum[c], 0.0)
-            at = pl.ds(bucket_ref[d], 1)
-            drel_ref[at, cs] += jnp.sum(red(x, jnp.sum), axis=0, keepdims=True)
-            return 0
-
-        lax.fori_loop(0, brow_ref.shape[0], one, 0)
-
-
-def self_back(start, size, brow, bucket, proj, do, lse, buckets, scale):
-    rows, width = do.shape
-    nq = width // 256
-    return call(
-        functools.partial(self_back_kernel, scale=scale),
-        "self_back",
-        (sds((rows, 3 * width), BF), sds((buckets, width), F32)),
-        [VM] * 3 + [SM] + [VM] * 3,
-        (VM, VM),
-        [
-            pltpu.VMEM((rows + 64, width), BF),
-            pltpu.VMEM((rows + 64, width), BF),
-            pltpu.VMEM((nq, WIN, 256), F32),
-            pltpu.VMEM((rows + 64, width), F32),
-            pltpu.VMEM((rows + 64, width), F32),
-            pltpu.VMEM((nq, WIN, 256), F32),
-        ],
-        (start, size, brow, bucket, proj, do, lse),
-        us=60,
-    )
-
-
-def self_weights_kernel(me_ref, h1_ref, dproj_ref, oself_ref, dy1_ref, keep_ref, send_ref, left_t):
-    width = h1_ref.shape[1]
-    left_t[...] = h1_ref[...].T
-    for i in range(3):
-        put_pieces(me_ref, left_t, dproj_ref[:, i * width : (i + 1) * width], i, keep_ref, send_ref)
-    left_t[...] = oself_ref[...].T
-    put_pieces(me_ref, left_t, dy1_ref[...], 3, keep_ref, send_ref)
-
-
-def self_weights(me, h1, dproj, oself, dy1):
-    rows, width = h1.shape
-    part = sds((16, width // 8, width), BF)
-    return call(
-        self_weights_kernel,
-        "self_weights",
-        (part, part),
-        [SM] + [VM] * 4,
-        (VM, VM),
-        [pltpu.VMEM((width, rows), BF)],
-        (me, h1, dproj, oself, dy1),
-        us=20,
-    )
-
-
-def self_in_kernel(src_ref, dproj_ref, wqkv_ref, x0_ref, gain_ref, dx1_ref, d_ref, dgain_ref):
-    x0 = x0_ref[...].astype(F32)
-    dx, dgain_ref[...] = rms_back(x0, rms(x0), gain_ref[...], dot_nt(dproj_ref[...], wqkv_ref[...]))
-    dx0 = dx1_ref[...] + dx
-    high = dx0.astype(BF)
-    low = (dx0 - high.astype(F32)).astype(BF)
-    hot = onehot_rows(src_ref[...])
-    d_ref[...] = dot(hot, high) + dot(hot, low)
-
-
-def self_in(src, dproj, wqkv, x0, gain, dx1):
-    rows, width = x0.shape
-    return call(
-        self_in_kernel,
-        "self_in",
-        (sds((rows, width), F32), sds((1, width), F32)),
-        [VM] * 6,
-        (VM, VM),
-        [],
-        (src, dproj, wqkv, x0, gain, dx1),
-        us=20,
-    )
-
-
-def unpack_ffn_kernel(me_ref, a0, a1, a2, a3, win_ref, wout_ref):
-    half = a0.shape[1] // 2
-    for i, ref in enumerate((a0, a1, a2, a3)):
-        for z2 in range(2):
-            s = me_ref[1] ^ ((i >> 1) + 2 * (i & 1) + 4 * z2)
-            piece = ref[z2]
-            rows = pl.ds(pl.multiple_of((s & 1) * half, half), half)
-            cols = pl.ds(pl.multiple_of((s >> 1) * 768, 768), 768)
-            win_ref[rows, cols] = piece[:half].astype(F32)
-            wout_ref[pl.ds(pl.multiple_of(s * half, half), half), :] = piece[half:].astype(F32)
-
-
-def unpack_ffn(me, arrays, win_shape, wout_shape):
-    return call(
-        unpack_ffn_kernel,
-        "unpack_ffn",
-        (sds(win_shape, F32), sds(wout_shape, F32)),
-        [SM] + [VM] * 4,
-        (VM, VM),
-        [],
-        (me, *arrays),
-        us=4,
-    )
-
-
-def tail_kernel(ck, sk, cs, ss, *rest, columns):
-    outs = rest[:4]
-    q, r1, r2, r3, r4, r5, f, send_sem, recv_sem = rest[4:]
+    length, buckets = brow_ref.shape[0], 32
     count, step_rows = q.shape[0], q.shape[2]
-    per = count // 2
+    per = ck.shape[1] // step_rows
+    each = width // 16 // step_rows
+    early = per + each
     g, b = lax.axis_index("grp"), lax.axis_index("blk")
     peers = [(g, b ^ 1), (g, b ^ 2), (g ^ 1, b), (g ^ 2, b), (g ^ 4, b), (g ^ 4, b), (g ^ 2, b), (g ^ 1, b)]
+    mesh_id = pl.DeviceIdType.MESH
     barrier = pltpu.get_barrier_semaphore()
     for p in peers[:5]:
-        pl.semaphore_signal(barrier, inc=1, device_id=p, device_id_type=pl.DeviceIdType.MESH)
+        pl.semaphore_signal(barrier, inc=1, device_id=p, device_id_type=mesh_id)
     pl.semaphore_wait(barrier, 5)
 
+    def rows_of(j):
+        j = j - per * (j >= per).astype(jnp.int32) if not isinstance(j, int) else j % per
+        return pl.ds(pl.multiple_of(j * step_rows, step_rows), step_rows)
+
     def copy(k, j, first=None):
-        at = pl.ds(pl.multiple_of((j % per) * step_rows, step_rows), step_rows)
         src, dst = [
-            lambda: (first.at[:, at, :], r1.at[j]),
+            lambda: (first.at[:, rows_of(j), :], r1.at[j]),
             lambda: (q.at[j, pl.ds(8, 8)], r2.at[j]),
             lambda: (q.at[j, pl.ds(4, 4)], r3.at[j]),
             lambda: (q.at[j, pl.ds(2, 2)], r4.at[j]),
@@ -1521,38 +1490,24 @@
             send_sem=send_sem.at[k, j],
             recv_sem=recv_sem.at[k, j],
             device_id=peers[k],
-            device_id_type=pl.DeviceIdType.MESH,
+            device_id_type=mesh_id,
         )
 
-    def start_core(j, _):
-        copy(0, j, cs).start()
-        return 0
-
-    def start_core2(j, _):
-        copy(0, j, ss).start()
-        return 0
-
-    lax.fori_loop(0, per, start_core, 0)
-    lax.fori_loop(per, count, start_core2, 0)
-
-    def add(a, c):
-        return (a.astype(F32) + c.astype(F32)).astype(BF)
+    def add(x, y):
+        return (x.astype(F32) + y.astype(F32)).astype(BF)
 
     def event(k, j):
         if k == 0:
-            at = pl.ds(pl.multiple_of((j % per) * step_rows, step_rows), step_rows)
-
-            @pl.when((j >= 0) & (j < per))
-            def _():
-                copy(0, j, cs).wait()
-                q[j] = add(ck[:, at, :], r1[j])
-                copy(1, j).start()
-
-            @pl.when((j >= per) & (j < count))
-            def _():
-                copy(0, j, ss).wait()
-                q[j] = add(sk[:, at, :], r1[j])
-                copy(1, j).start()
+            for live, keep, send in (
+                ((j >= 0) & (j < per), ck, cs),
+                ((j >= per) & (j < count), sk, ss),
+            ):
+
+                @pl.when(live)
+                def _():
+                    copy(0, j, send).wait()
+                    q[j] = add(keep[:, rows_of(j), :], r1[j])
+                    copy(1, j).start()
 
             return
 
@@ -1570,65 +1525,243 @@
             if k < 7:
                 copy(k + 1, j).start()
                 return
-            base = (j % per) * step_rows
-            for slot in range(8):
-                s = g ^ ((slot >> 2) + (slot & 2) + 4 * (slot & 1))
-                block, side = s >> 1, s & 1
-                at = pl.ds(pl.multiple_of(side * (per * step_rows) + base, step_rows), step_rows)
-                wide = f[j, slot].astype(F32)
-                first = 0
-                for o, (out, n) in enumerate(zip(outs, columns)):
-                    if o == 2 or o == 0:
-                        first = 0
-                    mine = (j < per) if o < 2 else (j >= per)
-
-                    @pl.when(mine & (block >= first) & (block < first + n))
-                    def _():
-                        cols = pl.ds(pl.multiple_of((block - first) * 768, 768), 768)
-                        out[at, cols] = wide
-
-                    first += n
-
+            f_ref[j] = f[j]
+
+    def step(t):
+        t = jnp.asarray(t, jnp.int32)
+        event(0, t + 2)
+        for k in range(1, 8):
+            event(k, t + 1 - k)
+
+    def start_first(j, _):
+        copy(0, j, cs).start()
+        return 0
+
+    def start_second(j, _):
+        copy(0, j, ss).start()
+        return 0
+
+    lax.fori_loop(0, per, start_first, 0)
+    left_t[...] = oself_ref[...].T
+    put_pieces(b, g, left_t, dy1_ref[...], 0, sk, ss)
+    lax.fori_loop(per, early, start_second, 0)
+
+    fill_window(proj_ref, kp, vp, width)
+    fill_bias(brow_ref, bias, nq)
+    dka[...] = jnp.zeros_like(dka)
+    dva[...] = jnp.zeros_like(dva)
+    dsum[...] = jnp.zeros_like(dsum)
     event(0, jnp.int32(0))
     event(0, jnp.int32(1))
 
-    def step(t, _):
-        event(0, t + 2)
-        event(1, t)
-        event(4, t - 2)
-        event(7, t - 4)
-        event(6, t - 3)
-        event(3, t - 1)
-        event(5, t - 2)
-        event(2, t)
+    def tile(t):
+        row = pl.ds(pl.multiple_of(t * TQ, TQ), TQ)
+        win = pl.ds(pl.multiple_of(t * TQ, TQ), WIN)
+        mask = range_mask(t * TQ - 64, WIN, start_ref[pl.ds(t, 1), :], size_ref[pl.ds(t, 1), :])
+        for c in range(nq):
+            cols = slice(c * 256, (c + 1) * 256)
+            qs = stack4(proj_ref[row, cols] * jnp.asarray(scale, BF))
+            dos = stack4(do_ref[row, cols])
+            s = dot(kp[win, cols], qs.T) + bias[c]
+            p = jnp.where(mask, jnp.exp(s - lse_ref[t, c]), 0.0)
+            dp = dot(vp[win, cols], dos.T)
+            delta = jnp.sum(red(p * dp, jnp.sum), axis=0, keepdims=True)
+            ds = p * (dp - delta)
+            dsum[c] += ds
+            ds = ds.astype(BF)
+            dva[win, cols] += dot(p.astype(BF), dos)
+            dka[win, cols] += dot(ds, qs)
+            dproj[row, cols] = (unstack4(dot_tn(ds, kp[win, cols])) * scale).astype(BF)
+
+    def tile_and_step(t, _):
+        tile(t)
+        step(t)
         return 0
 
-    lax.fori_loop(0, count + 4, step, 0)
-
-
-def tail(c_keep, s_keep, c_send, s_send):
-    slots, rows, width = c_keep.shape
+    lax.fori_loop(0, tiles, tile_and_step, 0)
+    dproj[:, width : 2 * width] = dka[64:, :].astype(BF)
+    dproj[:, 2 * width : 3 * width] = dva[64:, :].astype(BF)
+    left_t[...] = h1_ref[...].T
+    done = tiles
+    for i in range(3):
+        put_pieces(b, g, left_t, dproj[:, i * width : (i + 1) * width], i + 1, sk, ss)
+        lax.fori_loop(early + i * each, early + (i + 1) * each, start_second, 0)
+        step(done)
+        done += 1
+    dgain[...] = jnp.zeros_like(dgain)
+    parts = 5
+    block = rows // parts
+
+    def self_in(i, _):
+        at = pl.ds(pl.multiple_of(i * block, block), block)
+        x0 = x0_ref[at, :].astype(F32)
+        dx, part = rms_back(x0, rms(x0), gain_ref[...], dot_nt(dproj[at, :], wqkv_ref[...]))
+        dgain[...] += part
+        dx0 = dx1_ref[at, :] + dx
+        top = dx0.astype(BF)
+        high[at, :] = top
+        low[at, :] = (dx0 - top.astype(F32)).astype(BF)
+        step(done + i)
+        return 0
+
+    lax.fori_loop(0, parts, self_in, 0)
+
+    dist = distances()
+    for c in range(nq):
+        cols = slice(c * 256, (c + 1) * 256)
+
+        def one(d, _):
+            x = jnp.where(dist == d, dsum[c], 0.0)
+            drow[pl.ds(d, 1), cols] = jnp.sum(red(x, jnp.sum), axis=0, keepdims=True)
+            return 0
+
+        lax.fori_loop(0, length, one, 0)
+    lane = lax.broadcasted_iota(jnp.int32, (buckets, length), 1)
+    place = jnp.zeros((buckets, length), jnp.int32)
+    for d in range(length):
+        place = jnp.where(lane == d, bucket_ref[d], place)
+    hot = (place == lax.broadcasted_iota(jnp.int32, (buckets, length), 0)).astype(F32)
+    head = (
+        lax.broadcasted_iota(jnp.int32, (width, 128), 0) // 64
+        == lax.broadcasted_iota(jnp.int32, (width, 128), 1)
+    ).astype(F32)
+    by_bucket = jnp.dot(hot, drow[...], preferred_element_type=F32, precision=lax.Precision.HIGHEST)
+    small_ref[...] = jnp.zeros_like(small_ref)
+    small_ref[24:, :] = jnp.dot(by_bucket, head, preferred_element_type=F32, precision=lax.Precision.HIGHEST)
+    for i, ref in enumerate((dgain, dg2_ref, dg3_ref)):
+        for k in range(6):
+            small_ref[6 * i + k : 6 * i + k + 1, :] = ref[0:1, k * 128 : (k + 1) * 128]
+
+    def small_copy(k):
+        return pltpu.make_async_remote_copy(
+            src_ref=small_ref if k == 0 else sm_in.at[k + 4],
+            dst_ref=sm_in.at[k],
+            send_sem=sm_send.at[k],
+            recv_sem=sm_recv.at[k],
+            device_id=peers[k],
+            device_id_type=mesh_id,
+        )
+
+    def small_sum(k):
+        small_copy(k).wait()
+        held = small_ref[...] if k == 0 else sm_in[k + 4]
+        if k < 4:
+            sm_in[k + 5] = held + sm_in[k]
+            small_copy(k + 1).start()
+        else:
+            small_ref[...] = held + sm_in[k]
+
+    small_copy(0).start()
+    done += parts
+    step(done)
+    small_sum(0)
+    hot_rows = onehot_rows(src_ref[...])
+    d_ref[...] = dot(hot_rows, high[...]) + dot(hot_rows, low[...])
+    for k in range(1, 5):
+        step(done + k)
+        small_sum(k)
+
+    def rest(t, _):
+        step(t)
+        return 0
+
+    lax.fori_loop(done + 5, count + 6, rest, 0)
+
+
+def late(start, size, bucket, brow, proj, do, lse, h1, oself, dy1, src, x0, gain, dx1, wqkv, dg2, dg3, ck, cs, scale):
+    rows, width = do.shape
+    nq = width // 256
+    slots, piece, wide = ck.shape
     step_rows = 16
-    count = 2 * rows // step_rows
-    columns = (2, 2, 3, 1)
+    count = 2 * piece // step_rows
     any_spec = pl.BlockSpec(memory_space=pl.ANY)
 
     def buf(n):
-        return pltpu.VMEM((count, n, step_rows, width), BF)
+        return pltpu.VMEM((count, n, step_rows, wide), BF)
 
     return pl.pallas_call(
-        functools.partial(tail_kernel, columns=columns),
-        out_shape=tuple(sds((2 * rows, n * width), F32) for n in columns),
-        in_specs=[VM, VM, any_spec, any_spec],
-        out_specs=(VM,) * 4,
-        scratch_shapes=[buf(16), buf(16), buf(8), buf(4), buf(2), buf(1), buf(8)]
-        + [pltpu.SemaphoreType.DMA((8, count))] * 2,
+        functools.partial(late_kernel, scale=scale),
+        out_shape=(sds((rows, width), F32), sds((56, 128), F32), sds((count, 8, step_rows, wide), BF)),
+        in_specs=[VM, VM, SM] + [VM] * 15 + [any_spec],
+        out_specs=(VM,) * 3,
+        scratch_shapes=[
+            pltpu.VMEM((rows + 64, width), BF),
+            pltpu.VMEM((rows + 64, width), BF),
+            pltpu.VMEM((nq, WIN, 256), F32),
+            pltpu.VMEM((rows + 64, width), F32),
+            pltpu.VMEM((rows + 64, width), F32),
+            pltpu.VMEM((nq, WIN, 256), F32),
+            pltpu.VMEM((rows, 3 * width), BF),
+            pltpu.VMEM((width, rows), BF),
+            pltpu.VMEM((slots, piece, wide), BF),
+            pltpu.VMEM((slots, piece, wide), BF),
+            pltpu.VMEM((rows, width), BF),
+            pltpu.VMEM((rows, width), BF),
+            pltpu.VMEM(brow.shape, F32),
+            pltpu.VMEM((9, 56, 128), F32),
+            pltpu.VMEM((1, width), F32),
+            buf(16),
+            buf(16),
+            buf(8),
+            buf(4),
+            buf(2),
+            buf(1),
+            buf(8),
+        ]
+        + [pltpu.SemaphoreType.DMA((8, count))] * 2
+        + [pltpu.SemaphoreType.DMA((5,))] * 2,
         compiler_params=pltpu.CompilerParams(
-            vmem_limit_bytes=LIMIT, collective_id=0, has_side_effects=True
+            vmem_limit_bytes=62 << 20, collective_id=0, has_side_effects=True
         ),
         cost_estimate=pl.CostEstimate(flops=10**13, bytes_accessed=30 << 20, transcendentals=0),
-        name="tail",
-    )(c_keep, s_keep, c_send, s_send)
+        name="late",
+    )(start, size, bucket, brow, proj, do, lse, h1, oself, dy1, src, x0, gain, dx1, wqkv, dg2, dg3, ck, cs)
+
+
+def last_kernel(
+    me_ref, a0, a1, a2, a3, f_ref, own_ref, came_ref, win_ref, wout_ref, co_ref, cq_ref, ckv_ref, qkv_ref, so_ref, enc_ref
+):
+    half = a0.shape[1] // 2
+    for i, ref in enumerate((a0, a1, a2, a3)):
+        for z2 in range(2):
+            s = me_ref[1] ^ ((i >> 1) + 2 * (i & 1) + 4 * z2)
+            piece = ref[z2]
+            rows = pl.ds(pl.multiple_of((s & 1) * half, half), half)
+            cols = pl.ds(pl.multiple_of((s >> 1) * 768, 768), 768)
+            win_ref[rows, cols] = piece[:half].astype(F32)
+            wout_ref[pl.ds(pl.multiple_of(s * half, half), half), :] = piece[half:].astype(F32)
+    count, _, step_rows, wide = f_ref.shape
+    width = 2 * wide
+    places = (
+        (co_ref, 0), (cq_ref, 0), (ckv_ref, 0), (ckv_ref, width),
+        (so_ref, 0), (qkv_ref, 0), (qkv_ref, width), (qkv_ref, 2 * width),
+    )
+    each = count // 8
+    tall = each * step_rows
+    for slot in range(8):
+        s = me_ref[1] ^ ((slot >> 2) + (slot & 2) + 4 * (slot & 1))
+        for n, (out, col) in enumerate(places):
+            for k in range(each):
+                at = pl.ds(pl.multiple_of((s >> 1) * tall + k * step_rows, step_rows), step_rows)
+                cols = pl.ds(pl.multiple_of(col + (s & 1) * wide, 128), wide)
+                out[at, cols] = f_ref[n * each + k, slot].astype(F32)
+    enc_ref[...] = own_ref[...] + came_ref[...].astype(F32)
+
+
+def last(me, arrays, f, own, came):
+    width = own.shape[1]
+    quarter = width // 4
+    cols = lambda n: sds((quarter, n * width), F32)
+    return call(
+        last_kernel,
+        "last",
+        (cols(4), sds((width, width), F32), cols(1), cols(1), cols(2), cols(3), cols(1), sds(own.shape, F32)),
+        [SM] + [VM] * 7,
+        (VM,) * 8,
+        [],
+        (me, *arrays, f, own, came),
+        us=8,
+    )
 
 
 def hop(x, core=0, xb=0, yb=0, z1=0, z2=0):
@@ -1647,22 +1780,6 @@
 
 def after(x, *deps):
     return lax.optimization_barrier((x,) + deps)[0]
-
-
-def split_xy(keep, came):
-    return [total(keep[4 * j : 4 * j + 4], came[4 * j : 4 * j + 4]) for j in range(4)]
-
-
-def send_xy(q):
-    return q[0], hop(q[1], yb=1), hop(q[2], xb=1), hop(q[3], xb=1, yb=1)
-
-
-def split_z(parts):
-    return [total(*[p[j] for p in parts]) for j in range(4)]
-
-
-def send_z(q):
-    return q[0], hop(q[1], z2=1), hop(q[2], z1=1), hop(q[3], z1=1, z2=1)
 
 
 def fused_body(
@@ -1710,46 +1827,74 @@
     f_came = hop(f_send, core=1)
     dx2, dyc, do, dgain3 = ffn_back(x2, dh3, g_low, g3, w_cross_out)
     f_came = after(f_came, do)
-    f_q = split_xy(f_keep, f_came)
-    do = after(do, *f_q)
-    f_parts = send_xy(f_q)
-    dq, kv_keep, kv_send = cross_back(me, lo, hi, cstart, csize, qc, do, ocross, lse, k, v, kt, scale)
-    kv_came = hop(kv_send, core=1)
-    f_parts = [after(p, dq) for p in f_parts]
-    f_q = split_z(f_parts)
-    dq = after(dq, *f_q)
-    f_parts = send_z(f_q)
-    dx1, dy1, dos, dgain2 = cross_in(dq, x1, dx2, g2, w_cross_q, w_self_out)
-    kv_came = after(kv_came, dos)
+    half = width // 8
+    i_keep, i_send, o_keep, o_send = (
+        total(f_keep[n : n + 8, rows_], f_came[n : n + 8, rows_])
+        for rows_ in (slice(0, half), slice(half, 2 * half))
+        for n in (0, 8)
+    )
+    do, o_send, i_send = lax.optimization_barrier((do, o_send, i_send))
+    i_came, o_came = hop(i_send, yb=1), hop(o_send, xb=1)
+    dq0, keep0, send0 = cross_back(
+        me, lo, hi, cstart, csize, qc, do, ocross, lse, k, v, kt, scale, 0, 2
+    )
+    came0 = hop(send0, core=1)
+    i_came, o_came, dq0 = lax.optimization_barrier((i_came, o_came, dq0))
+    i_q = [total(i_keep[2 * j : 2 * j + 2], i_came[2 * j : 2 * j + 2]) for j in range(4)]
+    o_q = [total(o_keep[2 * j : 2 * j + 2], o_came[2 * j : 2 * j + 2]) for j in range(4)]
+    z_send = jnp.concatenate([i_q[1], o_q[1]], axis=1)
+    do1, z_send, i_q[2], i_q[3], o_q[2], o_q[3] = lax.optimization_barrier(
+        (do, z_send, i_q[2], i_q[3], o_q[2], o_q[3])
+    )
+    z_came = hop(z_send, z1=1)
+    ix, ixz = hop(i_q[2], xb=1), hop(i_q[3], xb=1, z1=1)
+    oy, oyz = hop(o_q[2], yb=1), hop(o_q[3], yb=1, z1=1)
+    dq1, keep1, send1 = cross_back(
+        me, lo, hi, cstart, csize, qc, do1, ocross, lse, k, v, kt, scale, 2, 1
+    )
+    came1 = hop(send1, core=1)
+    z_came, ix, ixz, oy, oyz, dq1 = lax.optimization_barrier((z_came, ix, ixz, oy, oyz, dq1))
+
+    def line(n):
+        return jnp.concatenate(
+            [
+                total(i_q[0][n], z_came[n, :half], ix[n], ixz[n]),
+                total(o_q[0][n], z_came[n, half:], oy[n], oyz[n]),
+            ],
+            axis=0,
+        )
+
+    f_keep, f_send = line(0), line(1)
+    dq1, f_send = lax.optimization_barrier((dq1, f_send))
+    f_came = hop(f_send, z2=1)
+    dx1, dy1, dos, dgain2 = cross_in(dq0, dq1, x1, dx2, g2, w_cross_q, w_self_out)
+    f_came, came1, dos = lax.optimization_barrier((f_came, came1, dos))
+    f_own = total(f_keep, f_came)
+    came1, f_own = lax.optimization_barrier((came1, f_own))
+    f_came = hop(f_own, z2=1)
     c_keep, c_send, enc_own, enc_out = cross_weights(
-        me, kv_keep, kv_came, encodings, enc2, w_cross_kv, oc, dyc, h2, dq
+        me, keep0, came0, keep1, came1, encodings, enc2, w_cross_kv, oc, dyc, h2, dq0, dq1
     )
     enc_came = hop(enc_out, xb=1)
-    f_parts = [after(p, c_keep) for p in f_parts]
-    f_own = total(*f_parts)
-    dos = after(dos, f_own, c_keep)
-    f_came = hop(f_own, z2=1)
-    dproj, drel = self_back(sstart, ssize, brow, bucket_table, proj, dos, lse_self, buckets, scale)
-    f_came = after(f_came, dproj)
+    f_came, c_keep = lax.optimization_barrier((f_came, c_keep))
     f_pair = jnp.stack([f_own, f_came])
-    dproj = after(dproj, f_pair, enc_came)
-    s_keep, s_send = self_weights(me, h1, dproj, oself, dy1)
-    d_dec_in, dgain1 = self_in(src, dproj, w_qkv, x0, g1, dx1)
-    f_all = [f_pair, hop(f_pair, z1=1), hop(f_pair, yb=1), hop(f_pair, yb=1, z1=1)]
-    o_win, o_wout = unpack_ffn(me, f_all, (width // 4, w_in.shape[1]), (w_out.shape[0] // 4, width))
-    d_encodings = enc_own + enc_came.astype(F32)
-
-    drel = jnp.sum(drel.reshape(buckets, heads, -1), axis=2)
-    small = jnp.concatenate([dgain1[0], dgain2[0], dgain3[0], drel.reshape(-1)])
-    small = sum_everywhere(small.reshape(-1, 128)).reshape(-1)
-    o_co_cq, o_wckv, o_wqkv, o_wso = tail(c_keep, s_keep, c_send, s_send)
-    o_wco, o_wcq = o_co_cq[:, :width], o_co_cq[:, width:]
+    dos, c_keep, f_pair = lax.optimization_barrier((dos, c_keep, f_pair))
+    f_all = [hop(f_pair, z1=1), hop(f_pair, yb=1), hop(f_pair, yb=1, z1=1)]
+    d_dec_in, small, gathered = late(
+        sstart, ssize, bucket_table, brow, proj, dos, lse_self, h1, oself, dy1, src, x0, g1, dx1, w_qkv,
+        dgain2, dgain3, c_keep, c_send, scale,
+    )
+    *f_all, enc_came, gathered = lax.optimization_barrier((*f_all, enc_came, gathered))
+    o_win, o_wout, o_wco, o_wcq, o_wckv, o_wqkv, o_wso, d_encodings = last(
+        me, [f_pair, *f_all], gathered, enc_own, enc_came
+    )
 
     def own(v):
         return lax.dynamic_slice_in_dim(v, me_b * (v.shape[0] // 4), v.shape[0] // 4, 0)
 
-    g_self, g_cross, g_ffn = (own(small[i * width : (i + 1) * width]) for i in range(3))
-    g_rel = own(small[3 * width :].reshape(buckets, heads))
+    gains = small[:18].reshape(3, width)
+    g_self, g_cross, g_ffn = (own(gains[i]) for i in range(3))
+    g_rel = own(small[24:, :heads])
     return (
         layer_out,
         d_dec_in,

time: 425 us -> 386 us (0.908)
  starting transfers between devices: 50.7 us -> 18.2 us
  Pallas kernels: 334 us -> 324 us
  waiting for transfers between devices: 2.81 us -> 12.1 us
  other arithmetic: 22.4 us -> 17.5 us
    pallas_call x11 -> x7, Pallas kernels: 199 us -> 98.2 us  [call(): pl.pallas_call(kernel, out_shape=out_shape, in_specs=in_specs, out_specs=...]
    pallas_call x1 -> x3, Pallas kernels: 96.5 us -> 176 us  [the longest x1 118 us: late(): pl.pallas_call(functools.partial(late_kernel, scale=scale), out_shape=(sd...]
    ppermute x16 -> x19, starting transfers between devices: 45.1 us -> 18.2 us  [hop(): return lax.ppermute(x, ('grp', 'blk'), pairs)]
    ppermute x16 -> x19, waiting for transfers between devices: 0.91 us -> 12.1 us  [hop(): return lax.ppermute(x, ('grp', 'blk'), pairs)]
    pallas_call x1, Pallas kernels: 38.1 us -> 49 us  [ffn(): pl.pallas_call(functools.partial(ffn_kernel, last=steps - 1), out_shape=o...]
    ppermute x5 -> x0, starting transfers between devices: 5.54 us -> none  [swap(): return lax.ppermute(x, axis, [(i, i ^ bit) for i in range(size)])]
    add x6 -> x0, other arithmetic: 5.11 us -> none  [the longest x5 2.69 us: sum_everywhere(): x = x + swap(x, axis, bit)]
    convert_element_type x2 -> x3, other arithmetic: 7.94 us -> 10.9 us  [total(): return out.astype(BF)]
  transfers between devices with their start and end apart: 21 -> 19, of which waited for: 2 -> 2; matrix products, arithmetic and copies ran while one was open for 5% -> 4% of each run, Pallas kernels for 56% -> 60%
where the time goes in v3:
time: 386 us; the launch traced here: 381 us
  Pallas kernels  324 us (84%)
  starting transfers between devices  18.2 us (5%)
  other arithmetic  17.5 us (5%)
  waiting for transfers between devices  12.1 us (3%)
  local copies, waits for them, and re-layouts  9.11 us (2%)
    pallas_call x1, Pallas kernels, late(): pl.pallas_call(functools.partial(late_kernel, scale=scale), out_shape=(sd...  118 us
    pallas_call x7, Pallas kernels, call(): pl.pallas_call(kernel, out_shape=out_shape, in_specs=in_specs, out_specs=...  98.2 us
    pallas_call x2, Pallas kernels, cross_back(): pl.pallas_call(functools.partial(cross_back_kernel, scale=scale), grid=(1...  58.6 us
    pallas_call x1, Pallas kernels, ffn(): pl.pallas_call(functools.partial(ffn_kernel, last=steps - 1), out_shape=o...  49 us
    ppermute x19, starting transfers between devices, hop(): return lax.ppermute(x, ('grp', 'blk'), pairs)  18.2 us
    ppermute x19, waiting for transfers between devices, hop(): return lax.ppermute(x, ('grp', 'blk'), pairs)  12.1 us
    convert_element_type x3, other arithmetic, total(): return out.astype(BF)  10.9 us
  transfers between devices with their start and end apart: 19, of which 2 were waited for; matrix products, arithmetic and copies ran while one was open for 4% of the time, Pallas kernels for 60%

profile of v3, /device:TPU:0, one launch (start us, length us, event | category | flops | bytes accessed | tf_op | source)
XLA Modules:
  0.0 381.4 jit_solution(17307906764668237184)
XLA Ops:
  0.6 3.0 collective-permute-start
  3.6 0.0 collective-permute-start.1
  3.7 1.3 reshape.76.gain1_ref.gain_ref
  4.9 1.4 copy.32.rel_ref
  6.3 0.6 pad_add_fusion.me_ref
  6.9 20.1 %pre.1 = (s32[1,640]{1,0:T(1,128)}, s32[10,256]{1,0:T(8,128)}, s32[10,256]{1,0:T(8,128)}, s32[10,256]{1,0:T(8,128)}, s32[10,256]{1,0:T(8,128)}, /*index=5*/s32[1...) custom-call(s32[2]{0:T(128)} %pad_add_fusion.me_ref, ...), custom_call_target="tpu_custom_call" | custom-call | flops 3999999983616 | bytes 10561336 | tf_op jit(solution)/shard_map/pre/pallas_call | solution.py:870
  27.0 0.6 reshape.77.gain2_ref.gain_ref
  27.6 0.6 reshape.78.gain_ref
  28.2 0.0 collective-permute-done.rest_2_.enc2_ref
  28.2 0.5 collective-permute-start.2
  28.7 5.5 %mid.1 = (f32[640,768]{1,0:T(8,128)}, bf16[640,768]{1,0:T(8,128)(2,1)}, bf16[640,768]{1,0:T(8,128)(2,1)}) custom-call(bf16[640,768]{1,0:T(8,128)(2,1)} %get-tuple-element.111.x0_ref, bf16[640,768]{1,0:T(8,128)(2,1)} %get-tuple-element.113.oself_ref, bf16[768,768]{1,0:T(8,128)(2,1)} %wso_ref.3, f32[1,768]{1,0:T(1,128)} %reshape.77.gain2_ref.gain_ref, ...), custom_call_target="tpu_custom_call" | custom-call | flops 799999983616 | bytes 8260608 | tf_op jit(solution)/shard_map/mid/pallas_call | solution.py:870
  34.2 0.0 collective-permute-done.1.rest_1_
  34.2 0.0 collective-permute-done.2.rest_3_
  34.2 37.1 %kv_cross.1 = (bf16[2048,768]{1,0:T(8,128)(2,1)}, bf16[2048,768]{1,0:T(8,128)(2,1)}, bf16[768,2048]{1,0:T(8,128)(2,1)}, f32[640,768]{1,0:T(8,128)}, f32[10,3,1,256]{3,2,1,0:T(1,128)}) custom-call(s32[2]{0:T(128)} %pad_add_fusion.me_ref, s32[10]{0:T(128)} %get-tuple-element.115.lo_ref, s32[10]{0:T(128)} %get-tuple-element.116.hi_ref, ...), custom_call_target="tpu_custom_call" | custom-call | flops 7999999967232 | bytes 17942616 | tf_op jit(solution)/shard_map/kv_cross/pallas_call | solution.py:870
  71.3 49.0 %ffn.1 = (bf16[16,192,768]{2,1,0:T(8,128)(2,1)}, bf16[16,192,768]{2,1,0:T(8,128)(2,1)}, f32[640,768]{1,0:T(8,128)}, f32[640,768]{1,0:T(8,128)}, bf16[640,768]{1,...) custom-call(s32[2]{0:T(128)} %pad_add_fusion.me_ref, s32[1,640]{1,0:T(1,128)} %get-tuple-element.110.src_ref, ...), custom_call_target="tpu_custom_call" | custom-call | flops 6000000106496 | bytes 31457280 | tf_op jit(solution)/shard_map/ffn/pallas_call | solution.py:1146
  120.3 1.3 collective-permute-start.3
  121.5 5.7 %ffn_back.1 = (f32[640,768]{1,0:T(8,128)}, bf16[640,768]{1,0:T(8,128)(2,1)}, bf16[640,768]{1,0:T(8,128)(2,1)}, f32[1,768]{1,0:T(1,128)}) custom-call(f32[640,768]{1,0:T(8,128)} %get-tuple-element.128.x2_ref, f32[640,768]{1,0:T(8,128)} %get-tuple-element.129.dh_ref, bf16[640,768]{1,0:T(8,128)(2,1)} %get-tuple-element.130.g_ref, f32[1,768]{1,0:T(1,128)} %reshape.78.gain_ref, ...), custom_call_target="tpu_custom_call" | custom-call | flops 3000000053248 | bytes 10033152 | tf_op jit(solution)/shard_map/ffn_back/pallas_call | solution.py:870
  127.2 2.2 collective-permute-done.3
  129.4 5.9 %add_convert_fusion.1 = (bf16[8,96,768]{2,1,0:T(8,128)(2,1)}, bf16[8,96,768]{2,1,0:T(8,128)(2,1)}, bf16[8,96,768]{2,1,0:T(8,128)(2,1)}, bf16[8,96,768]{2,1,0:T(8,128)(2,1)}) fusion(bf16[16,192,768]{2,1,0:T(8,128)(2,1)} %collective-permute-done.3, bf16[16,192,768]{2,1,0:T(8,128)(2,1)} %get-tuple-element.132), kind=kLoop, calls=%fused_computation.1 | loop fusion | flops 9437184 | bytes 14155776 | tf_op jit(solution)/shard_map/convert_element_type | solution.py:1778
  135.4 2.5 collective-permute-start.4
  137.9 0.2 collective-permute-start.5
  138.1 33.9 %cross_back.2 = (bf16[640,512]{1,0:T(8,128)(2,1)}, bf16[2,512,1024]{2,1,0:T(8,128)(2,1)}, bf16[2,512,1024]{2,1,0:T(8,128)(2,1)}) custom-call(s32[2]{0:T(128)} %pad_add_fusion.me_ref, s32[10]{0:T(128)} %get-tuple-element.115.lo_ref, s32[10]{0:T(128)} %get-tuple-element.116.hi_ref, s32[10,256]{1,0:T(8,128)} %get-tuple-element.117.start_ref, ...), custom_call_target="tpu_custom_call" | custom-call | flops 9999999827968 | bytes 31457280 | tf_op jit(solution)/shard_map/cross_back/pallas_call | solution.py:1287
  172.0 0.0 collective-permute-done.4
  172.0 0.0 collective-permute-done.5
  172.0 3.2 add_convert_fusion.5
  175.2 0.9 pad_maximum_fusion
  176.1 0.0 collective-permute-start.6
  176.1 0.3 collective-permute-start.7
  176.4 3.2 collective-permute-start.8
  179.6 2.1 collective-permute-start.9
  181.6 0.1 collective-permute-start.10
  181.7 24.6 %cross_back.3 = (bf16[640,256]{1,0:T(8,128)(2,1)}, bf16[2,512,512]{2,1,0:T(8,128)(2,1)}, bf16[2,512,512]{2,1,0:T(8,128)(2,1)}) custom-call(s32[2]{0:T(128)} %pad_add_fusion.me_ref, s32[10]{0:T(128)} %get-tuple-element.115.lo_ref, s32[10]{0:T(128)} %get-tuple-element.116.hi_ref, s32[10,256]{1,0:T(8,128)} %get-tuple-element.117.start_ref, ...), custom_call_target="tpu_custom_call" | custom-call | flops 9999999827968 | bytes 31457280 | tf_op jit(solution)/shard_map/cross_back/pallas_call | solution.py:1287
  206.4 0.0 collective-permute-done.7
  206.4 1.4 collective-permute-start.14
  207.7 0.0 collective-permute-done.8
  207.7 0.1 collective-permute-start.12
  207.8 0.0 collective-permute-done.9
  207.8 0.0 collective-permute-done.10
  207.8 0.0 collective-permute-done.6
  207.8 2.5 fusion.2
  210.4 0.7 pad_maximum_fusion.2
  211.1 7.0 %cross_in.1 = (f32[640,768]{1,0:T(8,128)}, bf16[640,768]{1,0:T(8,128)(2,1)}, bf16[640,768]{1,0:T(8,128)(2,1)}, f32[1,768]{1,0:T(1,128)}) custom-call(bf16[640,512]{1,0:T(8,128)(2,1)} %get-tuple-element.160.dq0_ref, bf16[640,256]{1,0:T(8,128)(2,1)} %get-tuple-element.161.dq1_ref, f32[640,768]{1,0:T(8,128)} %get-tuple-element.114.x1_ref, ...), custom_call_target="tpu_custom_call" | custom-call | flops 6000000106496 | bytes 11212800 | tf_op jit(solution)/shard_map/cross_in/pallas_call | solution.py:870
  218.1 9.9 %collective-permute-done.11 = bf16[192,768]{1,0:T(8,128)(2,1)} collective-permute-done((bf16[192,768]{1,0:T(8,128)(2,1)}, bf16[192,768]{1,0:T(8,128)(2,1)}, u32[]{:S(2)}, u32[]{:S(2)}) %collective-permute-start.11) | collective-permute-done | bytes 294944 | tf_op jit(solution)/shard_map/ppermute | solution.py:1771
  228.0 0.0 collective-permute-done.12.came1_ref
  228.0 1.7 add_convert_fusion.4
  229.7 0.0 collective-permute-done.14.came0_ref
  229.7 14.8 %cross_weights.1 = (bf16[16,192,384]{2,1,0:T(8,128)(2,1)}, bf16[16,192,384]{2,1,0:T(8,128)(2,1)}, f32[512,768]{1,0:T(8,128)}, bf16[512,768]{1,0:T(8,128)(2,1)}) custom-call(s32[2]{0:T(128)} %pad_add_fusion.me_ref, bf16[2,512,1024]{2,1,0:T(8,128)(2,1)} %get-tuple-element.168.keep0_ref, bf16[2,512,1024]{2,1,0:T(8,128)(2,1)} %collective-permute-done.14.came0_ref, ...), custom_call_target="tpu_custom_call" | custom-call | flops 3000000053248 | bytes 21233672 | tf_op jit(solution)/shard_map/cross_weights/pallas_call | solution.py:870
  244.6 0.0 collective-permute-start.18
  244.6 1.9 pad_maximum_fusion.1.a0
  246.5 1.3 collective-permute-start.15
  247.8 2.0 collective-permute-start.16
  249.7 0.4 collective-permute-start.17
  250.1 117.8 %late.1 = (f32[640,768]{1,0:T(8,128)}, f32[56,128]{1,0:T(8,128)}, bf16[24,8,16,384]{3,2,1,0:T(8,128)(2,1)}) custom-call(s32[10,256]{1,0:T(8,128)} %get-tuple-element.124.start_ref, s32[10,256]{1,0:T(8,128)} %get-tuple-element.125.size_ref, s32[20]{0:T(128)} %bucket_ref.3, f32[20,768]{1,0:T(8,128)} %get-tuple-element.126.brow_ref, ...), custom_call_target="tpu_custom_call" | custom-call | flops 9999999827968 | bytes 31457280 | tf_op jit(solution)/shard_map/late/pallas_call | solution.py:1682
  368.0 0.7 slice.180
  368.7 0.8 slice_bitcast_fusion
  369.5 0.6 dynamic_slice.12
  370.1 0.6 dynamic_slice.14
  370.7 0.6 dynamic_slice.15
  371.4 0.6 constant_dynamic-slice_fusion
  372.0 0.0 collective-permute-done.18.came_ref
  372.0 0.0 collective-permute-done.15.a1
  372.0 0.0 collective-permute-done.16.a2
  372.0 8.0 %last.1 = (f32[192,3072]{1,0:T(8,128)}, f32[768,768]{1,0:T(8,128)}, f32[192,768]{1,0:T(8,128)}, f32[192,768]{1,0:T(8,128)}, f32[192,1536]{1,0:T(8,128)}, /*index...) custom-call(s32[2]{0:T(128)} %pad_add_fusion.me_ref, bf16[2,192,768]{2,1,0:T(8,128)(2,1)} %pad_maximum_fusion.1.a0, ...), custom_call_target="tpu_custom_call" | custom-call | flops 799999983616 | bytes 18087944 | tf_op jit(solution)/shard_map/last/pallas_call | solution.py:870
  380.0 1.3 copy.34
  (22 shorter events, 0.0 us)
Async XLA Ops:
  0.6 27.5 %collective-permute-start = (bf16[512,768]{1,0:T(8,128)(2,1)}, bf16[512,768]{1,0:T(8,128)(2,1)}, u32[]{:S(2)}, u32[]{:S(2)}) collective-permute-start(bf16[512,768]{1,0:T(8,128)(2,1)} %enc0_ref.1), channel_id=1, source_target_pairs={{0,2},{1,3},{2,0},{3,1},{4,6},{5,7},{6,4},{7,5},{8,10},{9,11},{10,... | collective-permute-start | bytes 2359304 | tf_op jit(solution)/shard_map/ppermute | solution.py:1771
  3.6 30.6 %collective-permute-start.1 = (bf16[512,768]{1,0:T(8,128)(2,1)}, bf16[512,768]{1,0:T(8,128)(2,1)}, u32[]{:S(2)}, u32[]{:S(2)}) collective-permute-start(bf16[512,768]{1,0:T(8,128)(2,1)} %enc0_ref.1), channel_id=1, source_target_pairs={{0,1},{1,0},{2,3},{3,2},{4,5},{5,4},{6,7},{7,6},{8,9},{9,8},{10,11... | collective-permute-start | bytes 2359304 | tf_op jit(solution)/shard_map/ppermute | solution.py:1771
  6.9 20.1 %copy-start.7 = (f32[768]{0:T(1024)S(1)}, f32[768]{0:T(1024)}, u32[]{:S(2)}) copy-start(f32[768]{0:T(1024)} %param.28) | copy-start | bytes 9220
  6.9 20.7 %copy-start.8 = (f32[768]{0:T(1024)S(1)}, f32[768]{0:T(1024)}, u32[]{:S(2)}) copy-start(f32[768]{0:T(1024)} %param.32) | copy-start | bytes 9220
  28.2 6.0 %collective-permute-start.2 = (bf16[512,768]{1,0:T(8,128)(2,1)}, bf16[512,768]{1,0:T(8,128)(2,1)}, u32[]{:S(2)}, u32[]{:S(2)}) collective-permute-start(bf16[512,768]{1,0:T(8,128)(2,1)} %collective-permute-done.rest_2_.enc2_ref), channel_id=1, source_target_pairs={{0,1},{1,0},{2,3},{3,2},{4,5},{5,4},{6,7},{7,6},{8,9},{9,8},{10,11... | collective-permute-start | bytes 2359304 | tf_op jit(solution)/shard_map/ppermute | solution.py:1771
  120.3 9.2 %collective-permute-start.3 = (bf16[16,192,768]{2,1,0:T(8,128)(2,1)}, bf16[16,192,768]{2,1,0:T(8,128)(2,1)}, u32[]{:S(2)}, u32[]{:S(2)}) collective-permute-start(bf16[16,192,768]{2,1,0:T(8,128)(2,1)} %get-tuple-element.133), channel_id=1, source_target_pairs={{0,1},{1,0},{2,3},{3,2},{4,5},{5,4},{6,7},{7,6},{8,9},{9,8},{10,11... | collective-permute-start | bytes 14155784 | tf_op jit(solution)/shard_map/ppermute | solution.py:1771
  135.4 36.6 %collective-permute-start.4 = (bf16[8,96,768]{2,1,0:T(8,128)(2,1)}, bf16[8,96,768]{2,1,0:T(8,128)(2,1)}, u32[]{:S(2)}, u32[]{:S(2)}) collective-permute-start(bf16[8,96,768]{2,1,0:T(8,128)(2,1)} %get-tuple-element.136), channel_id=1, source_target_pairs={{0,4},{1,5},{2,6},{3,7},{4,0},{5,1},{6,2},{7,3},{8,12},{9,13},{10,... | collective-permute-start | bytes 3538952 | tf_op jit(solution)/shard_map/ppermute | solution.py:1771
  137.9 34.1 %collective-permute-start.5 = (bf16[8,96,768]{2,1,0:T(8,128)(2,1)}, bf16[8,96,768]{2,1,0:T(8,128)(2,1)}, u32[]{:S(2)}, u32[]{:S(2)}) collective-permute-start(bf16[8,96,768]{2,1,0:T(8,128)(2,1)} %get-tuple-element.137), channel_id=1, source_target_pairs={{0,2},{1,3},{2,0},{3,1},{4,6},{5,7},{6,4},{7,5},{8,10},{9,11},{10,... | collective-permute-start | bytes 3538952 | tf_op jit(solution)/shard_map/ppermute | solution.py:1771
  138.1 33.9 %copy-start = (bf16[8,96,768]{2,1,0:T(8,128)(2,1)S(1)}, bf16[8,96,768]{2,1,0:T(8,128)(2,1)}, u32[]{:S(2)}) copy-start(bf16[8,96,768]{2,1,0:T(8,128)(2,1)} %get-tuple-element.206) | copy-start | bytes 3538948
  138.1 33.9 %copy-start.1 = (bf16[8,96,768]{2,1,0:T(8,128)(2,1)S(1)}, bf16[8,96,768]{2,1,0:T(8,128)(2,1)}, u32[]{:S(2)}) copy-start(bf16[8,96,768]{2,1,0:T(8,128)(2,1)} %get-tuple-element.207) | copy-start | bytes 3538948
  176.1 31.7 %collective-permute-start.6 = (bf16[2,192,768]{2,1,0:T(8,128)(2,1)}, bf16[2,192,768]{2,1,0:T(8,128)(2,1)}, u32[]{:S(2)}, u32[]{:S(2)}) collective-permute-start(bf16[2,192,768]{2,1,0:T(8,128)(2,1)} %pad_maximum_fusion), channel_id=1, source_target_pairs={{0,8},{1,9},{2,10},{3,11},{4,12},{5,13},{6,14},{7,15},{8,0},{9,1},... | collective-permute-start | bytes 1769480 | tf_op jit(solution)/shard_map/ppermute | solution.py:1771
  176.1 30.3 %collective-permute-start.7 = (bf16[2,96,768]{2,1,0:T(8,128)(2,1)}, bf16[2,96,768]{2,1,0:T(8,128)(2,1)}, u32[]{:S(2)}, u32[]{:S(2)}) collective-permute-start(bf16[2,96,768]{2,1,0:T(8,128)(2,1)} %get-tuple-element.146), channel_id=1, source_target_pairs={{0,2},{1,3},{2,0},{3,1},{4,6},{5,7},{6,4},{7,5},{8,10},{9,11},{10,... | collective-permute-start | bytes 884744 | tf_op jit(solution)/shard_map/ppermute | solution.py:1771
  176.4 31.3 %collective-permute-start.8 = (bf16[2,96,768]{2,1,0:T(8,128)(2,1)}, bf16[2,96,768]{2,1,0:T(8,128)(2,1)}, u32[]{:S(2)}, u32[]{:S(2)}) collective-permute-start(bf16[2,96,768]{2,1,0:T(8,128)(2,1)} %get-tuple-element.147), channel_id=1, source_target_pairs={{0,10},{1,11},{2,8},{3,9},{4,14},{5,15},{6,12},{7,13},{8,2},{9,3},... | collective-permute-start | bytes 884744 | tf_op jit(solution)/shard_map/ppermute | solution.py:1771
  179.6 28.2 %collective-permute-start.9 = (bf16[2,96,768]{2,1,0:T(8,128)(2,1)}, bf16[2,96,768]{2,1,0:T(8,128)(2,1)}, u32[]{:S(2)}, u32[]{:S(2)}) collective-permute-start(bf16[2,96,768]{2,1,0:T(8,128)(2,1)} %get-tuple-element.148), channel_id=1, source_target_pairs={{0,4},{1,5},{2,6},{3,7},{4,0},{5,1},{6,2},{7,3},{8,12},{9,13},{10,... | collective-permute-start | bytes 884744 | tf_op jit(solution)/shard_map/ppermute | solution.py:1771
  181.6 26.2 %collective-permute-start.10 = (bf16[2,96,768]{2,1,0:T(8,128)(2,1)}, bf16[2,96,768]{2,1,0:T(8,128)(2,1)}, u32[]{:S(2)}, u32[]{:S(2)}) collective-permute-start(bf16[2,96,768]{2,1,0:T(8,128)(2,1)} %get-tuple-element.149), channel_id=1, source_target_pairs={{0,12},{1,13},{2,14},{3,15},{4,8},{5,9},{6,10},{7,11},{8,4},{9,5},... | collective-permute-start | bytes 884744 | tf_op jit(solution)/shard_map/ppermute | solution.py:1771
  181.7 26.1 %copy-start.3 = (bf16[2,96,768]{2,1,0:T(8,128)(2,1)S(1)}, bf16[2,96,768]{2,1,0:T(8,128)(2,1)}, u32[]{:S(2)}) copy-start(bf16[2,96,768]{2,1,0:T(8,128)(2,1)} %get-tuple-element.214) | copy-start | bytes 884740
  181.7 26.1 %copy-start.4 = (bf16[2,96,768]{2,1,0:T(8,128)(2,1)S(1)}, bf16[2,96,768]{2,1,0:T(8,128)(2,1)}, u32[]{:S(2)}) copy-start(bf16[2,96,768]{2,1,0:T(8,128)(2,1)} %get-tuple-element.230) | copy-start | bytes 884740
  206.4 23.4 %collective-permute-start.14 = (bf16[2,512,1024]{2,1,0:T(8,128)(2,1)}, bf16[2,512,1024]{2,1,0:T(8,128)(2,1)}, u32[]{:S(2)}, u32[]{:S(2)}) collective-permute-start(bf16[2,512,1024]{2,1,0:T(8,128)(2,1)} %get-tuple-element.169), channel_id=1, source_target_pairs={{0,1},{1,0},{2,3},{3,2},{4,5},{5,4},{6,7},{7,6},{8,9},{9,8},{10,11... | collective-permute-start | bytes 6291464 | tf_op jit(solution)/shard_map/ppermute | solution.py:1771
  207.7 20.3 %collective-permute-start.12 = (bf16[2,512,512]{2,1,0:T(8,128)(2,1)}, bf16[2,512,512]{2,1,0:T(8,128)(2,1)}, u32[]{:S(2)}, u32[]{:S(2)}) collective-permute-start(bf16[2,512,512]{2,1,0:T(8,128)(2,1)} %get-tuple-element.159), channel_id=1, source_target_pairs={{0,1},{1,0},{2,3},{3,2},{4,5},{5,4},{6,7},{7,6},{8,9},{9,8},{10,11... | collective-permute-start | bytes 3145736 | tf_op jit(solution)/shard_map/ppermute | solution.py:1771
  211.1 16.9 %collective-permute-start.11 = (bf16[192,768]{1,0:T(8,128)(2,1)}, bf16[192,768]{1,0:T(8,128)(2,1)}, u32[]{:S(2)}, u32[]{:S(2)}) collective-permute-start(bf16[192,768]{1,0:T(8,128)(2,1)} %pad_maximum_fusion.2), channel_id=1, source_target_pairs={{0,16},{1,17},{2,18},{3,19},{4,20},{5,21},{6,22},{7,23},{8,24},{9,... | collective-permute-start | bytes 884744 | tf_op jit(solution)/shard_map/ppermute | solution.py:1771
  211.1 16.9 %copy-start.5 = (bf16[96,768]{1,0:T(8,128)(2,1)S(1)}, bf16[96,768]{1,0:T(8,128)(2,1)}, u32[]{:S(2)}) copy-start(bf16[96,768]{1,0:T(8,128)(2,1)} %get-tuple-element.218) | copy-start | bytes 442372
  211.1 16.9 %copy-start.6 = (bf16[96,768]{1,0:T(8,128)(2,1)S(1)}, bf16[96,768]{1,0:T(8,128)(2,1)}, u32[]{:S(2)}) copy-start(bf16[96,768]{1,0:T(8,128)(2,1)} %get-tuple-element.223) | copy-start | bytes 442372
  229.7 14.8 %collective-permute-start.13 = (bf16[192,768]{1,0:T(8,128)(2,1)}, bf16[192,768]{1,0:T(8,128)(2,1)}, u32[]{:S(2)}, u32[]{:S(2)}) collective-permute-start(bf16[192,768]{1,0:T(8,128)(2,1)} %add_convert_fusion.4), channel_id=1, source_target_pairs={{0,16},{1,17},{2,18},{3,19},{4,20},{5,21},{6,22},{7,23},{8,24},{9,... | collective-permute-start | bytes 884744 | tf_op jit(solution)/shard_map/ppermute | solution.py:1771
  244.6 127.4 %collective-permute-start.18 = (bf16[512,768]{1,0:T(8,128)(2,1)}, bf16[512,768]{1,0:T(8,128)(2,1)}, u32[]{:S(2)}, u32[]{:S(2)}) collective-permute-start(bf16[512,768]{1,0:T(8,128)(2,1)} %get-tuple-element.189), channel_id=1, source_target_pairs={{0,2},{1,3},{2,0},{3,1},{4,6},{5,7},{6,4},{7,5},{8,10},{9,11},{10,... | collective-permute-start | bytes 2359304 | tf_op jit(solution)/shard_map/ppermute | solution.py:1771
  246.5 125.5 %collective-permute-start.15 = (bf16[2,192,768]{2,1,0:T(8,128)(2,1)}, bf16[2,192,768]{2,1,0:T(8,128)(2,1)}, u32[]{:S(2)}, u32[]{:S(2)}) collective-permute-start(bf16[2,192,768]{2,1,0:T(8,128)(2,1)} %pad_maximum_fusion.1.a0), channel_id=1, source_target_pairs={{0,8},{1,9},{2,10},{3,11},{4,12},{5,13},{6,14},{7,15},{8,0},{9,1},... | collective-permute-start | bytes 1769480 | tf_op jit(solution)/shard_map/ppermute | solution.py:1771
  247.8 124.2 %collective-permute-start.16 = (bf16[2,192,768]{2,1,0:T(8,128)(2,1)}, bf16[2,192,768]{2,1,0:T(8,128)(2,1)}, u32[]{:S(2)}, u32[]{:S(2)}) collective-permute-start(bf16[2,192,768]{2,1,0:T(8,128)(2,1)} %pad_maximum_fusion.1.a0), channel_id=1, source_target_pairs={{0,4},{1,5},{2,6},{3,7},{4,0},{5,1},{6,2},{7,3},{8,12},{9,13},{10,... | collective-permute-start | bytes 1769480 | tf_op jit(solution)/shard_map/ppermute | solution.py:1771
  249.7 122.2 %collective-permute-start.17 = (bf16[2,192,768]{2,1,0:T(8,128)(2,1)}, bf16[2,192,768]{2,1,0:T(8,128)(2,1)}, u32[]{:S(2)}, u32[]{:S(2)}) collective-permute-start(bf16[2,192,768]{2,1,0:T(8,128)(2,1)} %pad_maximum_fusion.1.a0), channel_id=1, source_target_pairs={{0,12},{1,13},{2,14},{3,15},{4,8},{5,9},{6,10},{7,11},{8,4},{9,5},... | collective-permute-start | bytes 1769480 | tf_op jit(solution)/shard_map/ppermute | solution.py:1771
  372.0 8.0 %copy-start.2 = (f32[640,768]{1,0:T(8,128)S(1)}, f32[640,768]{1,0:T(8,128)}, u32[]{:S(2)}) copy-start(f32[640,768]{1,0:T(8,128)} %get-tuple-element.246) | copy-start | bytes 5898244

commit v4 on v3

--- a/solution.py
+++ b/solution.py
@@ -830,8 +830,8 @@
         mask = range_mask(t * TQ - 64, WIN, sstart_ref[pl.ds(t, 1), :], ssize_ref[pl.ds(t, 1), :])
         for c in range(nq):
             cs = slice(c * 256, (c + 1) * 256)
-            qst = stack4(proj_ref[row, cs] * jnp.asarray(scale, BF)).T
-            s = jnp.where(mask, dot(kp[win, cs], qst) + bias[c], MASKED)
+            qs = stack4(proj_ref[row, cs] * jnp.asarray(scale, BF))
+            s = jnp.where(mask, dot_nt(kp[win, cs], qs) + bias[c], MASKED)
             m = jnp.max(red(s, jnp.max), axis=0, keepdims=True)
             p = jnp.exp(s - m)
             l = jnp.sum(red(p, jnp.sum), axis=0, keepdims=True)
@@ -953,7 +953,9 @@
     pieces,
 ):
     enc = rest[:pieces]
-    wkv_ref, k_ref, v_ref, kt_ref, o_ref, lse_ref, vt, qst, s_scr, m_scr, l_scr, acc = rest[pieces:]
+    wkv_ref, k_any, v_any, kt_any, o_ref, lse_ref, vt, k_ref, v_ref, kt_ref, out_sem, qst, s_scr, m_scr, l_scr, acc = rest[
+        pieces:
+    ]
     rows, width = q_ref.shape
     nq, tiles = width // 256, rows // TQ
     n = enc[0].shape[0]
@@ -965,6 +967,12 @@
         vv = dot(enc[r][...], wkv_ref[:, width:]).astype(BF)
         v_ref[at, :] = vv
         vt[:, at] = vv.T
+    leaving = [
+        pltpu.make_async_copy(a, b, out_sem.at[i])
+        for i, (a, b) in enumerate(((k_ref, k_any), (v_ref, v_any), (kt_ref, kt_any)))
+    ]
+    for c in leaving:
+        c.start()
 
     def tile(t, _):
         st = start_ref[pl.ds(t, 1), :]
@@ -1006,6 +1014,8 @@
         return 0
 
     lax.fori_loop(0, tiles, tile, 0)
+    for c in leaving:
+        c.wait()
 
 
 def kv_cross(me, lo, hi, start, size, q, enc, wkv):
@@ -1023,9 +1033,13 @@
             sds((tiles, nq, 1, 256), F32),
         ),
         [SM] * 3 + [VM] * (3 + len(enc) + 1),
-        (VM,) * 5,
+        (pl.BlockSpec(memory_space=pl.ANY),) * 3 + (VM, VM),
         [
             pltpu.VMEM((width, keys), BF),
+            pltpu.VMEM((keys, width), BF),
+            pltpu.VMEM((keys, width), BF),
+            pltpu.VMEM((width, keys), BF),
+            pltpu.SemaphoreType.DMA((3,)),
             pltpu.VMEM((nq, 256, 256), BF),
             pltpu.VMEM((nq, keys, 256), F32),
             pltpu.VMEM((nq, 8, 256), F32),
@@ -1345,266 +1359,350 @@
     )
 
 
-def put_pieces(me_b, me_g, left_t, right, block, keep_ref, send_ref):
-    width = left_t.shape[0]
-    quarter = width // 4
-    tall, wide = quarter // 4, width // 2
-    for r in range(4):
-        part = left_t[pl.ds(pl.multiple_of((me_b ^ r) * quarter, quarter), quarter), :]
-        grad = dot(part, right).astype(BF)
-        target = send_ref if r & 1 else keep_ref
-        for s in range(8):
-            at = (r >> 1) * 8 + slot_of(me_g ^ s)
-            y, x = (s >> 1) * tall, (s & 1) * wide
-            target[at, block * tall : (block + 1) * tall, :] = grad[y : y + tall, x : x + wide]
-
-
-def cross_weights_kernel(
-    me_ref, keep0_ref, came0_ref, keep1_ref, came1_ref, enc0_ref, enc2_ref, wkv_ref, oc_ref, dyc_ref, h2_ref,
-    dq0_ref, dq1_ref, keep_ref, send_ref, own_ref, out_ref, both, enc_t, left_t,
-):
-    n = keep0_ref.shape[1]
-    width = oc_ref.shape[1]
-    cut = dq0_ref.shape[1]
-    for r in range(2):
-        rows = slice(r * n, (r + 1) * n)
-        for keep, came, at, wide in ((keep0_ref, came0_ref, 0, cut), (keep1_ref, came1_ref, cut, width - cut)):
-            total = (keep[r].astype(F32) + came[r].astype(F32)).astype(BF)
-            both[rows, at : at + wide] = total[:, :wide]
-            both[rows, width + at : width + at + wide] = total[:, wide:]
-    out_ref[...] = dot_nt(both[n:, :], wkv_ref[...]).astype(BF)
-    own_ref[...] = dot_nt(both[:n, :], wkv_ref[...])
-    enc_t[:, :n] = enc0_ref[...].T
-    enc_t[:, n:] = enc2_ref[...].T
-    me_b, me_g = me_ref[0], me_ref[1]
-    put_pieces(me_b, me_g, enc_t, both[:, :width], 2, keep_ref, send_ref)
-    put_pieces(me_b, me_g, enc_t, both[:, width:], 3, keep_ref, send_ref)
-    left_t[...] = oc_ref[...].T
-    put_pieces(me_b, me_g, left_t, dyc_ref[...], 0, keep_ref, send_ref)
-    left_t[...] = h2_ref[...].T
-    dq = jnp.concatenate([dq0_ref[...], dq1_ref[...]], axis=1)
-    put_pieces(me_b, me_g, left_t, dq, 1, keep_ref, send_ref)
-
-
-def cross_weights(me, keep0, came0, keep1, came1, enc0, enc2, wkv, oc, dyc, h2, dq0, dq1):
-    rows, width = oc.shape
-    n = enc0.shape[0]
-    part = sds((16, width // 4, width // 2), BF)
-    return call(
-        cross_weights_kernel,
-        "cross_weights",
-        (part, part, sds((n, width), F32), sds((n, width), BF)),
-        [SM] + [VM] * 12,
-        (VM,) * 4,
-        [pltpu.VMEM((2 * n, 2 * width), BF), pltpu.VMEM((width, 2 * n), BF), pltpu.VMEM((width, rows), BF)],
-        (me, keep0, came0, keep1, came1, enc0, enc2, wkv, oc, dyc, h2, dq0, dq1),
-        us=30,
-    )
-
-
 def late_kernel(
     start_ref,
     size_ref,
     bucket_ref,
     brow_ref,
-    proj_ref,
-    do_ref,
+    proj_any,
+    do_any,
     lse_ref,
-    h1_ref,
-    oself_ref,
-    dy1_ref,
+    h1_any,
+    oself_any,
+    dy1_any,
     src_ref,
-    x0_ref,
+    x0_any,
     gain_ref,
-    dx1_ref,
-    wqkv_ref,
+    dx1_any,
+    wqkv_any,
     dg2_ref,
     dg3_ref,
-    ck,
-    cs,
+    keep0_any,
+    came0_any,
+    keep1_any,
+    came1_any,
+    enc0_any,
+    enc2_any,
+    wkv_any,
+    oc_ref,
+    dyc_ref,
+    h2_ref,
+    dq0_ref,
+    dq1_ref,
+    fkeep_ref,
+    fsend_any,
     d_ref,
     small_ref,
-    f_ref,
-    kp,
-    vp,
+    f,
+    own_ref,
+    came_any,
+    ffn_any,
+    projs,
+    wbuf,
+    both,
+    stage,
+    enc_t,
+    enc_out,
     bias,
     dka,
     dva,
     dsum,
-    dproj,
     left_t,
-    sk,
     ss,
-    high,
-    low,
     drow,
     sm_in,
     dgain,
+    fown,
+    frecv,
     q,
     r1,
     r2,
     r3,
     r4,
     r5,
-    f,
+    do_ref,
+    h1_ref,
+    oself_ref,
+    dy1_ref,
+    x0_ref,
+    dx1_ref,
+    enc0_ref,
+    enc2_ref,
     send_sem,
     recv_sem,
     sm_send,
     sm_recv,
+    x_send,
+    x_recv,
+    f_send,
+    f_recv,
+    loc,
     *,
     scale,
 ):
     rows, width = do_ref.shape
     nq, tiles = width // 256, rows // TQ
     length, buckets = brow_ref.shape[0], 32
-    count, step_rows = q.shape[0], q.shape[2]
-    per = ck.shape[1] // step_rows
-    each = width // 16 // step_rows
-    early = per + each
+    count, step_rows, wide = q.shape[0], q.shape[2], q.shape[3]
+    each = count // 8
+    quarter = width // 4
+    tall = quarter // 4
+    n = enc0_ref.shape[0]
+    cut = dq0_ref.shape[1]
     g, b = lax.axis_index("grp"), lax.axis_index("blk")
-    peers = [(g, b ^ 1), (g, b ^ 2), (g ^ 1, b), (g ^ 2, b), (g ^ 4, b), (g ^ 4, b), (g ^ 2, b), (g ^ 1, b)]
+    peers = [(g, b ^ 1), (g, b ^ 2), (g ^ 1, b), (g ^ 2, b), (g ^ 4, b), (g ^ 2, b), (g ^ 1, b)]
     mesh_id = pl.DeviceIdType.MESH
+
+    def local(src, dst, k):
+        return pltpu.make_async_copy(src, dst, loc.at[k])
+
+    def remote(src, dst, send, recv, k):
+        return pltpu.make_async_remote_copy(
+            src_ref=src, dst_ref=dst, send_sem=send, recv_sem=recv, device_id=peers[k], device_id_type=mesh_id
+        )
+
+    proj_in = local(proj_any, projs.at[pl.ds(64, rows), :], 0)
+    wkv_in = local(wkv_any, wbuf.at[:, pl.ds(0, 2 * width)], 1)
+    held_in = [
+        local(src, dst, 20 + i)
+        for i, (src, dst) in enumerate(
+            (
+                (oself_any, oself_ref),
+                (dy1_any, dy1_ref),
+                (enc0_any, enc0_ref),
+                (enc2_any, enc2_ref),
+                (do_any, do_ref),
+                (h1_any, h1_ref),
+                (x0_any, x0_ref),
+                (dx1_any, dx1_ref),
+            )
+        )
+    ]
+    wqkv_in = local(wqkv_any, wbuf, 2)
+    dkv_in = []
+    for r in range(2):
+        for i, (keep, came, at, w) in enumerate(
+            ((keep0_any, came0_any, 0, cut), (keep1_any, came1_any, cut, width - cut))
+        ):
+            for half in range(2):
+                from_, to = pl.ds(half * w, w), pl.ds(half * width + at, w)
+                k = 3 + 8 * r + 4 * i + 2 * half
+                dkv_in.append((r, local(keep.at[r, :, from_], both.at[pl.ds(r * n, n), to], k)))
+                dkv_in.append((r, local(came.at[r, :, from_], stage.at[:, to], k + 1)))
+    for r, c in dkv_in:
+        if r == 0:
+            c.start()
+    for c in held_in[:4] + [wkv_in, proj_in] + held_in[4:]:
+        c.start()
+
     barrier = pltpu.get_barrier_semaphore()
     for p in peers[:5]:
         pl.semaphore_signal(barrier, inc=1, device_id=p, device_id_type=mesh_id)
     pl.semaphore_wait(barrier, 5)
 
-    def rows_of(j):
-        j = j - per * (j >= per).astype(jnp.int32) if not isinstance(j, int) else j % per
-        return pl.ds(pl.multiple_of(j * step_rows, step_rows), step_rows)
-
-    def copy(k, j, first=None):
+    f_first = remote(fsend_any, frecv, f_send.at[0], f_recv.at[0], 4)
+    f_second = remote(fown, ffn_any.at[1], f_send.at[1], f_recv.at[1], 4)
+    f_third = remote(ffn_any.at[pl.ds(0, 2)], ffn_any.at[pl.ds(2, 2)], f_send.at[2], f_recv.at[2], 3)
+    f_local = local(fown, ffn_any.at[0], 19)
+    f_slices = fown.shape[0] // step_rows
+    f_first.start()
+
+    def f_copy(i):
+        at = pl.ds(pl.multiple_of(i * step_rows, step_rows), step_rows)
+        src, dst = ffn_any.at[pl.ds(0, 4), at, :], ffn_any.at[pl.ds(4, 4), at, :]
+        return remote(src, dst, f_send.at[3 + i], f_recv.at[3 + i], 2)
+
+    enc_copy = remote(enc_out, came_any, x_send, x_recv, 1)
+
+    def add(x, y):
+        return (x.astype(F32) + y.astype(F32)).astype(BF)
+
+    def core_copy(j):
+        at = pl.ds(pl.multiple_of(j * step_rows, step_rows), step_rows)
+        return remote(ss.at[:, at, :], r1.at[j], send_sem.at[0, j], recv_sem.at[0, j], 0)
+
+    def copy(k, j):
         src, dst = [
-            lambda: (first.at[:, rows_of(j), :], r1.at[j]),
             lambda: (q.at[j, pl.ds(8, 8)], r2.at[j]),
             lambda: (q.at[j, pl.ds(4, 4)], r3.at[j]),
             lambda: (q.at[j, pl.ds(2, 2)], r4.at[j]),
-            lambda: (q.at[j, pl.ds(1, 1)], r5.at[j]),
-            lambda: (f.at[j, pl.ds(0, 1)], f.at[j, pl.ds(1, 1)]),
+            lambda: (q.at[j, pl.ds(0, 2)], r5.at[j]),
             lambda: (f.at[j, pl.ds(0, 2)], f.at[j, pl.ds(2, 2)]),
             lambda: (f.at[j, pl.ds(0, 4)], f.at[j, pl.ds(4, 4)]),
-        ][k]()
-        return pltpu.make_async_remote_copy(
-            src_ref=src,
-            dst_ref=dst,
-            send_sem=send_sem.at[k, j],
-            recv_sem=recv_sem.at[k, j],
-            device_id=peers[k],
-            device_id_type=mesh_id,
-        )
-
-    def add(x, y):
-        return (x.astype(F32) + y.astype(F32)).astype(BF)
+        ][k - 1]()
+        return remote(src, dst, send_sem.at[k, j], recv_sem.at[k, j], k)
 
     def event(k, j):
-        if k == 0:
-            for live, keep, send in (
-                ((j >= 0) & (j < per), ck, cs),
-                ((j >= per) & (j < count), sk, ss),
-            ):
-
-                @pl.when(live)
-                def _():
-                    copy(0, j, send).wait()
-                    q[j] = add(keep[:, rows_of(j), :], r1[j])
-                    copy(1, j).start()
-
-            return
-
         @pl.when((j >= 0) & (j < count))
         def _():
-            copy(k, j).wait()
-            if k == 1:
+            (core_copy(j) if k == 0 else copy(k, j)).wait()
+            if k == 0:
+                q[j] = add(q[j], r1[j])
+            elif k == 1:
                 q[j, 0:8] = add(q[j, 0:8], r2[j])
             elif k == 2:
                 q[j, 0:4] = add(q[j, 0:4], r3[j])
             elif k == 3:
                 q[j, 0:2] = add(q[j, 0:2], r4[j])
             elif k == 4:
-                f[j, 0:1] = add(q[j, 0:1], r5[j])
-            if k < 7:
+                f[j, 0] = add(q[j, 0], r5[j, 1])
+                f[j, 1] = add(q[j, 1], r5[j, 0])
+            if k < 6:
                 copy(k + 1, j).start()
-                return
-            f_ref[j] = f[j]
 
     def step(t):
         t = jnp.asarray(t, jnp.int32)
-        event(0, t + 2)
-        for k in range(1, 8):
-            event(k, t + 1 - k)
-
-    def start_first(j, _):
-        copy(0, j, cs).start()
-        return 0
-
-    def start_second(j, _):
-        copy(0, j, ss).start()
-        return 0
-
-    lax.fori_loop(0, per, start_first, 0)
+        event(0, t + 3)
+        for k in range(1, 7):
+            event(k, t - 2 * (k - 1))
+
+    def put(right, block):
+        for r in range(4):
+            part = left_t[pl.ds(pl.multiple_of((b ^ r) * quarter, quarter), quarter), :]
+            spread(dot(part, right).astype(BF), r, block)
+        start_core(block)
+
+    def spread(grad, r, block):
+        for s in range(8):
+            at = (r >> 1) * 8 + slot_of(g ^ s)
+            y, x = (s >> 1) * tall, (s & 1) * wide
+            if r & 1:
+                ss[at, block * tall : (block + 1) * tall, :] = grad[y : y + tall, x : x + wide]
+            else:
+                for k in range(each):
+                    piece = grad[y + k * step_rows : y + (k + 1) * step_rows, x : x + wide]
+                    q[block * each + k, at] = piece
+
+    def start_core(block):
+        for k in range(each):
+            core_copy(block * each + k).start()
+
+    left_t[...] = oc_ref[...].T
+    put(dyc_ref[...], 0)
+    left_t[...] = h2_ref[...].T
+    for j in range(each):
+        event(0, jnp.int32(j))
+    put(jnp.concatenate([dq0_ref[...], dq1_ref[...]], axis=1), 1)
+    step(0)
+    held_in[0].wait()
+    held_in[1].wait()
     left_t[...] = oself_ref[...].T
-    put_pieces(b, g, left_t, dy1_ref[...], 0, sk, ss)
-    lax.fori_loop(per, early, start_second, 0)
-
-    fill_window(proj_ref, kp, vp, width)
+    for r, c in dkv_in:
+        if r == 0:
+            c.wait()
+    both[:n, :] = add(both[:n, :], stage[...])
+    for r, c in dkv_in:
+        if r == 1:
+            c.start()
+    put(dy1_ref[...], 2)
+    f_first.wait()
+    fown[...] = add(fkeep_ref[...], frecv[...])
+    f_local.start()
+    f_second.start()
+    step(1)
+
+    held_in[2].wait()
+    held_in[3].wait()
+    enc_t[:, :n] = enc0_ref[...].T
+    enc_t[:, n:] = enc2_ref[...].T
+    for r, c in dkv_in:
+        if r == 1:
+            c.wait()
+    both[n:, :] = add(both[n:, :], stage[...])
+    for i in range(2):
+        for r in range(4):
+            part = enc_t[pl.ds(pl.multiple_of((b ^ r) * quarter, quarter), quarter), :]
+            spread(dot(part, both[:, i * width : (i + 1) * width]).astype(BF), r, 3 + i)
+        start_core(3 + i)
+        step(2 + i)
+    wkv_in.wait()
+    enc_out[...] = dot_nt(both[n:, :], wbuf[:, : 2 * width]).astype(BF)
+    own_ref[...] = dot_nt(both[:n, :], wbuf[:, : 2 * width])
+    wqkv_in.start()
+
+    projs[0:64, :] = jnp.zeros((64, 3 * width), BF)
     fill_bias(brow_ref, bias, nq)
     dka[...] = jnp.zeros_like(dka)
     dva[...] = jnp.zeros_like(dva)
     dsum[...] = jnp.zeros_like(dsum)
-    event(0, jnp.int32(0))
-    event(0, jnp.int32(1))
+    proj_in.wait()
+    held_in[4].wait()
 
     def tile(t):
         row = pl.ds(pl.multiple_of(t * TQ, TQ), TQ)
+        held = pl.ds(pl.multiple_of(t * TQ + 64, TQ), TQ)
         win = pl.ds(pl.multiple_of(t * TQ, TQ), WIN)
         mask = range_mask(t * TQ - 64, WIN, start_ref[pl.ds(t, 1), :], size_ref[pl.ds(t, 1), :])
         for c in range(nq):
             cols = slice(c * 256, (c + 1) * 256)
-            qs = stack4(proj_ref[row, cols] * jnp.asarray(scale, BF))
+            kcols = slice(width + c * 256, width + (c + 1) * 256)
+            vcols = slice(2 * width + c * 256, 2 * width + (c + 1) * 256)
+            qs = stack4(projs[held, cols] * jnp.asarray(scale, BF))
             dos = stack4(do_ref[row, cols])
-            s = dot(kp[win, cols], qs.T) + bias[c]
+            s = dot_nt(projs[win, kcols], qs) + bias[c]
             p = jnp.where(mask, jnp.exp(s - lse_ref[t, c]), 0.0)
-            dp = dot(vp[win, cols], dos.T)
+            dp = dot_nt(projs[win, vcols], dos)
             delta = jnp.sum(red(p * dp, jnp.sum), axis=0, keepdims=True)
             ds = p * (dp - delta)
             dsum[c] += ds
             ds = ds.astype(BF)
             dva[win, cols] += dot(p.astype(BF), dos)
             dka[win, cols] += dot(ds, qs)
-            dproj[row, cols] = (unstack4(dot_tn(ds, kp[win, cols])) * scale).astype(BF)
+            projs[held, cols] = (unstack4(dot_tn(ds, projs[win, kcols])) * scale).astype(BF)
 
     def tile_and_step(t, _):
         tile(t)
-        step(t)
+        step(t + 4)
         return 0
 
-    lax.fori_loop(0, tiles, tile_and_step, 0)
-    dproj[:, width : 2 * width] = dka[64:, :].astype(BF)
-    dproj[:, 2 * width : 3 * width] = dva[64:, :].astype(BF)
+    lax.fori_loop(0, tiles - 2, tile_and_step, 0)
+
+    def tile_alone(t, _):
+        tile(t)
+        return 0
+
+    lax.fori_loop(tiles - 2, tiles, tile_alone, 0)
+    f_second.wait()
+    f_local.wait()
+    f_third.start()
+    done = tiles + 2
+    projs[64:, width : 2 * width] = dka[64:, :].astype(BF)
+    projs[64:, 2 * width : 3 * width] = dva[64:, :].astype(BF)
+    held_in[5].wait()
     left_t[...] = h1_ref[...].T
-    done = tiles
     for i in range(3):
-        put_pieces(b, g, left_t, dproj[:, i * width : (i + 1) * width], i + 1, sk, ss)
-        lax.fori_loop(early + i * each, early + (i + 1) * each, start_second, 0)
+        put(projs[64:, i * width : (i + 1) * width], 5 + i)
         step(done)
-        done += 1
+        step(done + 1)
+        done += 2
+
     dgain[...] = jnp.zeros_like(dgain)
     parts = 5
     block = rows // parts
+    wqkv_in.wait()
+    held_in[6].wait()
+    held_in[7].wait()
 
     def self_in(i, _):
         at = pl.ds(pl.multiple_of(i * block, block), block)
+        held = pl.ds(pl.multiple_of(i * block + 64, 64), block)
         x0 = x0_ref[at, :].astype(F32)
-        dx, part = rms_back(x0, rms(x0), gain_ref[...], dot_nt(dproj[at, :], wqkv_ref[...]))
+        dx, part = rms_back(x0, rms(x0), gain_ref[...], dot_nt(projs[held, :], wbuf[...]))
         dgain[...] += part
         dx0 = dx1_ref[at, :] + dx
         top = dx0.astype(BF)
-        high[at, :] = top
-        low[at, :] = (dx0 - top.astype(F32)).astype(BF)
+        both[at, :width] = top
+        both[at, width:] = (dx0 - top.astype(F32)).astype(BF)
         step(done + i)
+
+        @pl.when(i == 2)
+        def _():
+            enc_copy.start()
+
         return 0
 
     lax.fori_loop(0, parts, self_in, 0)
+    done += parts
 
     dist = distances()
     for c in range(nq):
@@ -1633,14 +1731,8 @@
             small_ref[6 * i + k : 6 * i + k + 1, :] = ref[0:1, k * 128 : (k + 1) * 128]
 
     def small_copy(k):
-        return pltpu.make_async_remote_copy(
-            src_ref=small_ref if k == 0 else sm_in.at[k + 4],
-            dst_ref=sm_in.at[k],
-            send_sem=sm_send.at[k],
-            recv_sem=sm_recv.at[k],
-            device_id=peers[k],
-            device_id_type=mesh_id,
-        )
+        src = small_ref if k == 0 else sm_in.at[k + 4]
+        return remote(src, sm_in.at[k], sm_send.at[k], sm_recv.at[k], k)
 
     def small_sum(k):
         small_copy(k).wait()
@@ -1652,28 +1744,41 @@
             small_ref[...] = held + sm_in[k]
 
     small_copy(0).start()
-    done += parts
+    f_third.wait()
+    f_copy(0).start()
+    f_copy(1).start()
     step(done)
-    small_sum(0)
     hot_rows = onehot_rows(src_ref[...])
-    d_ref[...] = dot(hot_rows, high[...]) + dot(hot_rows, low[...])
-    for k in range(1, 5):
-        step(done + k)
+    d_ref[...] = dot(hot_rows, both[:rows, :width]) + dot(hot_rows, both[:rows, width:])
+    for k in range(5):
         small_sum(k)
+        for i in range(2):
+            f_copy(2 + 2 * k + i).start()
+            step(done + 1 + 2 * k + i)
 
     def rest(t, _):
         step(t)
         return 0
 
-    lax.fori_loop(done + 5, count + 6, rest, 0)
-
-
-def late(start, size, bucket, brow, proj, do, lse, h1, oself, dy1, src, x0, gain, dx1, wqkv, dg2, dg3, ck, cs, scale):
+    lax.fori_loop(done + 11, count + 10, rest, 0)
+
+    def f_end(i, _):
+        f_copy(i).wait()
+        return 0
+
+    lax.fori_loop(0, f_slices, f_end, 0)
+    enc_copy.wait()
+
+
+def late(
+    start, size, bucket, brow, proj, do, lse, h1, oself, dy1, src, x0, gain, dx1, wqkv, dg2, dg3,
+    keep0, came0, keep1, came1, enc0, enc2, wkv, oc, dyc, h2, dq0, dq1, fkeep, fsend, scale,
+):
     rows, width = do.shape
     nq = width // 256
-    slots, piece, wide = ck.shape
-    step_rows = 16
-    count = 2 * piece // step_rows
+    n = enc0.shape[0]
+    step_rows, wide, tall = 16, width // 2, width // 16
+    count = 8 * tall // step_rows
     any_spec = pl.BlockSpec(memory_space=pl.ANY)
 
     def buf(n):
@@ -1681,60 +1786,85 @@
 
     return pl.pallas_call(
         functools.partial(late_kernel, scale=scale),
-        out_shape=(sds((rows, width), F32), sds((56, 128), F32), sds((count, 8, step_rows, wide), BF)),
-        in_specs=[VM, VM, SM] + [VM] * 15 + [any_spec],
-        out_specs=(VM,) * 3,
+        out_shape=(
+            sds((rows, width), F32),
+            sds((56, 128), F32),
+            sds((count, 8, step_rows, wide), BF),
+            sds((n, width), F32),
+            sds((n, width), BF),
+            sds((8,) + fkeep.shape, BF),
+        ),
+        in_specs=[VM, VM, SM, VM, any_spec, any_spec, VM]
+        + [any_spec] * 3
+        + [VM, any_spec, VM, any_spec]
+        + [any_spec, VM, VM]
+        + [any_spec] * 7
+        + [VM] * 6
+        + [any_spec],
+        out_specs=(VM,) * 4 + (any_spec, any_spec),
         scratch_shapes=[
-            pltpu.VMEM((rows + 64, width), BF),
-            pltpu.VMEM((rows + 64, width), BF),
+            pltpu.VMEM((rows + 64, 3 * width), BF),
+            pltpu.VMEM((width, 3 * width), BF),
+            pltpu.VMEM((2 * n, 2 * width), BF),
+            pltpu.VMEM((n, 2 * width), BF),
+            pltpu.VMEM((width, 2 * n), BF),
+            pltpu.VMEM((n, width), BF),
             pltpu.VMEM((nq, WIN, 256), F32),
             pltpu.VMEM((rows + 64, width), F32),
             pltpu.VMEM((rows + 64, width), F32),
             pltpu.VMEM((nq, WIN, 256), F32),
-            pltpu.VMEM((rows, 3 * width), BF),
             pltpu.VMEM((width, rows), BF),
-            pltpu.VMEM((slots, piece, wide), BF),
-            pltpu.VMEM((slots, piece, wide), BF),
-            pltpu.VMEM((rows, width), BF),
-            pltpu.VMEM((rows, width), BF),
+            pltpu.VMEM((16, 8 * tall, wide), BF),
             pltpu.VMEM(brow.shape, F32),
             pltpu.VMEM((9, 56, 128), F32),
             pltpu.VMEM((1, width), F32),
+            pltpu.VMEM(fkeep.shape, BF),
+            pltpu.VMEM(fkeep.shape, BF),
             buf(16),
             buf(16),
             buf(8),
             buf(4),
             buf(2),
-            buf(1),
-            buf(8),
+            buf(2),
         ]
-        + [pltpu.SemaphoreType.DMA((8, count))] * 2
-        + [pltpu.SemaphoreType.DMA((5,))] * 2,
+        + [pltpu.VMEM(a.shape, a.dtype) for a in (do, h1, oself, dy1, x0, dx1, enc0, enc2)]
+        + [
+            pltpu.SemaphoreType.DMA((7, count)),
+            pltpu.SemaphoreType.DMA((7, count)),
+            pltpu.SemaphoreType.DMA((5,)),
+            pltpu.SemaphoreType.DMA((5,)),
+            pltpu.SemaphoreType.DMA,
+            pltpu.SemaphoreType.DMA,
+            pltpu.SemaphoreType.DMA((15,)),
+            pltpu.SemaphoreType.DMA((15,)),
+            pltpu.SemaphoreType.DMA((28,)),
+        ],
         compiler_params=pltpu.CompilerParams(
-            vmem_limit_bytes=62 << 20, collective_id=0, has_side_effects=True
+            vmem_limit_bytes=63 << 20, collective_id=0, has_side_effects=True
         ),
         cost_estimate=pl.CostEstimate(flops=10**13, bytes_accessed=30 << 20, transcendentals=0),
         name="late",
-    )(start, size, bucket, brow, proj, do, lse, h1, oself, dy1, src, x0, gain, dx1, wqkv, dg2, dg3, ck, cs)
+    )(
+        start, size, bucket, brow, proj, do, lse, h1, oself, dy1, src, x0, gain, dx1, wqkv, dg2, dg3,
+        keep0, came0, keep1, came1, enc0, enc2, wkv, oc, dyc, h2, dq0, dq1, fkeep, fsend,
+    )
 
 
 def last_kernel(
-    me_ref, a0, a1, a2, a3, f_ref, own_ref, came_ref, win_ref, wout_ref, co_ref, cq_ref, ckv_ref, qkv_ref, so_ref, enc_ref
+    me_ref, small_ref, ffn_ref, f_ref, own_ref, came_ref, win_ref, wout_ref, co_ref, cq_ref, ckv_ref, qkv_ref, so_ref, enc_ref, g1_ref, g2_ref, g3_ref, rel_ref
 ):
-    half = a0.shape[1] // 2
-    for i, ref in enumerate((a0, a1, a2, a3)):
-        for z2 in range(2):
-            s = me_ref[1] ^ ((i >> 1) + 2 * (i & 1) + 4 * z2)
-            piece = ref[z2]
-            rows = pl.ds(pl.multiple_of((s & 1) * half, half), half)
-            cols = pl.ds(pl.multiple_of((s >> 1) * 768, 768), 768)
-            win_ref[rows, cols] = piece[:half].astype(F32)
-            wout_ref[pl.ds(pl.multiple_of(s * half, half), half), :] = piece[half:].astype(F32)
+    half = ffn_ref.shape[1] // 2
+    for slot in range(8):
+        s = me_ref[1] ^ ((slot >> 2) + (slot & 2) + 4 * (slot & 1))
+        rows = pl.ds(pl.multiple_of((s & 1) * half, half), half)
+        cols = pl.ds(pl.multiple_of((s >> 1) * 768, 768), 768)
+        win_ref[rows, cols] = ffn_ref[slot, :half].astype(F32)
+        wout_ref[pl.ds(pl.multiple_of(s * half, half), half), :] = ffn_ref[slot, half:].astype(F32)
     count, _, step_rows, wide = f_ref.shape
     width = 2 * wide
     places = (
-        (co_ref, 0), (cq_ref, 0), (ckv_ref, 0), (ckv_ref, width),
-        (so_ref, 0), (qkv_ref, 0), (qkv_ref, width), (qkv_ref, 2 * width),
+        (co_ref, 0), (cq_ref, 0), (so_ref, 0), (ckv_ref, 0), (ckv_ref, width),
+        (qkv_ref, 0), (qkv_ref, width), (qkv_ref, 2 * width),
     )
     each = count // 8
     tall = each * step_rows
@@ -1746,20 +1876,33 @@
                 cols = pl.ds(pl.multiple_of(col + (s & 1) * wide, 128), wide)
                 out[at, cols] = f_ref[n * each + k, slot].astype(F32)
     enc_ref[...] = own_ref[...] + came_ref[...].astype(F32)
-
-
-def last(me, arrays, f, own, came):
+    quarter = g1_ref.shape[1]
+    for i, ref in enumerate((g1_ref, g2_ref, g3_ref)):
+        whole = jnp.concatenate([small_ref[6 * i + k : 6 * i + k + 1, :] for k in range(6)], axis=1)
+        for j in range(4):
+
+            @pl.when(me_ref[0] == j)
+            def _():
+                ref[...] = whole[:, j * quarter : (j + 1) * quarter]
+
+    part, heads = rel_ref.shape
+    rel_ref[...] = small_ref[pl.ds(pl.multiple_of(24 + me_ref[0] * part, 8), part), :heads]
+
+
+def last(me, small, ffn, f, own, came, buckets, heads):
     width = own.shape[1]
     quarter = width // 4
     cols = lambda n: sds((quarter, n * width), F32)
     return call(
         last_kernel,
         "last",
-        (cols(4), sds((width, width), F32), cols(1), cols(1), cols(2), cols(3), cols(1), sds(own.shape, F32)),
-        [SM] + [VM] * 7,
-        (VM,) * 8,
+        (cols(4), sds((width, width), F32), cols(1), cols(1), cols(2), cols(3), cols(1), sds(own.shape, F32))
+        + (sds((1, quarter), F32),) * 3
+        + (sds((buckets // 4, heads), F32),),
+        [SM] + [VM] * 5,
+        (VM,) * 12,
         [],
-        (me, *arrays, f, own, came),
+        (me, small, ffn, f, own, came),
         us=8,
     )
 
@@ -1865,36 +2008,17 @@
         )
 
     f_keep, f_send = line(0), line(1)
-    dq1, f_send = lax.optimization_barrier((dq1, f_send))
-    f_came = hop(f_send, z2=1)
     dx1, dy1, dos, dgain2 = cross_in(dq0, dq1, x1, dx2, g2, w_cross_q, w_self_out)
-    f_came, came1, dos = lax.optimization_barrier((f_came, came1, dos))
-    f_own = total(f_keep, f_came)
-    came1, f_own = lax.optimization_barrier((came1, f_own))
-    f_came = hop(f_own, z2=1)
-    c_keep, c_send, enc_own, enc_out = cross_weights(
-        me, keep0, came0, keep1, came1, encodings, enc2, w_cross_kv, oc, dyc, h2, dq0, dq1
-    )
-    enc_came = hop(enc_out, xb=1)
-    f_came, c_keep = lax.optimization_barrier((f_came, c_keep))
-    f_pair = jnp.stack([f_own, f_came])
-    dos, c_keep, f_pair = lax.optimization_barrier((dos, c_keep, f_pair))
-    f_all = [hop(f_pair, z1=1), hop(f_pair, yb=1), hop(f_pair, yb=1, z1=1)]
-    d_dec_in, small, gathered = late(
+    came0, came1, dos = lax.optimization_barrier((came0, came1, dos))
+    d_dec_in, small, gathered, enc_own, enc_came, f_all = late(
         sstart, ssize, bucket_table, brow, proj, dos, lse_self, h1, oself, dy1, src, x0, g1, dx1, w_qkv,
-        dgain2, dgain3, c_keep, c_send, scale,
-    )
-    *f_all, enc_came, gathered = lax.optimization_barrier((*f_all, enc_came, gathered))
-    o_win, o_wout, o_wco, o_wcq, o_wckv, o_wqkv, o_wso, d_encodings = last(
-        me, [f_pair, *f_all], gathered, enc_own, enc_came
-    )
-
-    def own(v):
-        return lax.dynamic_slice_in_dim(v, me_b * (v.shape[0] // 4), v.shape[0] // 4, 0)
-
-    gains = small[:18].reshape(3, width)
-    g_self, g_cross, g_ffn = (own(gains[i]) for i in range(3))
-    g_rel = own(small[24:, :heads])
+        dgain2, dgain3, keep0, came0, keep1, came1, encodings, enc2, w_cross_kv, oc, dyc, h2, dq0, dq1,
+        f_keep, f_send, scale,
+    )
+    (
+        o_win, o_wout, o_wco, o_wcq, o_wckv, o_wqkv, o_wso, d_encodings, g_self, g_cross, g_ffn, g_rel,
+    ) = last(me, small, f_all, gathered, enc_own, enc_came, buckets, heads)
+    g_self, g_cross, g_ffn = (g.reshape(-1) for g in (g_self, g_cross, g_ffn))
     return (
         layer_out,
         d_dec_in,

time: 386 us -> 353 us (0.915)
  Pallas kernels: 324 us -> 309 us
  waiting for transfers between devices: 12.1 us -> 2.61 us
  local copies, waits for them, and re-layouts: 9.11 us -> 5.12 us
    pallas_call x7 -> x6, Pallas kernels: 98.2 us -> 79.6 us  [call(): pl.pallas_call(kernel, out_shape=out_shape, in_specs=in_specs, out_specs=...]
    ppermute x19 -> x13, waiting for transfers between devices: 12.1 us -> 2.61 us  [hop(): return lax.ppermute(x, ('grp', 'blk'), pairs)]
    pallas_call x1, Pallas kernels: 118 us -> 125 us  [late(): pl.pallas_call(functools.partial(late_kernel, scale=scale), out_shape=(sd...]
    ppermute x19 -> x13, starting transfers between devices: 18.2 us -> 15.9 us  [hop(): return lax.ppermute(x, ('grp', 'blk'), pairs)]
    convert_element_type x3 -> x2, other arithmetic: 10.9 us -> 9.12 us  [total(): return out.astype(BF)]
  transfers between devices with their start and end apart: 19 -> 13, of which waited for: 2 -> 1; matrix products, arithmetic and copies ran while one was open for 4% -> 2% of each run, Pallas kernels for 60% -> 27%
where the time goes in v4:
time: 353 us; the launch traced here: 348 us
  Pallas kernels  309 us (88%)
  starting transfers between devices  15.9 us (5%)
  other arithmetic  13.9 us (4%)
  local copies, waits for them, and re-layouts  5.12 us (1%)
    pallas_call x1, Pallas kernels, late(): pl.pallas_call(functools.partial(late_kernel, scale=scale), out_shape=(sd...  125 us
    pallas_call x6, Pallas kernels, call(): pl.pallas_call(kernel, out_shape=out_shape, in_specs=in_specs, out_specs=...  79.6 us
    pallas_call x2, Pallas kernels, cross_back(): pl.pallas_call(functools.partial(cross_back_kernel, scale=scale), grid=(1...  55.5 us
    pallas_call x1, Pallas kernels, ffn(): pl.pallas_call(functools.partial(ffn_kernel, last=steps - 1), out_shape=o...  49 us
    ppermute x13, starting transfers between devices, hop(): return lax.ppermute(x, ('grp', 'blk'), pairs)  15.9 us
    convert_element_type x2, other arithmetic, total(): return out.astype(BF)  9.12 us
  transfers between devices with their start and end apart: 13, of which 1 were waited for; matrix products, arithmetic and copies ran while one was open for 2% of the time, Pallas kernels for 27%

profile of v4, /device:TPU:0, one launch (start us, length us, event | category | flops | bytes accessed | tf_op | source)
XLA Modules:
  0.0 347.5 jit_solution(7684518553607440382)
XLA Ops:
  0.6 0.5 collective-permute-start.1
  1.2 2.6 collective-permute-start
  3.7 1.3 reshape.78.gain1_ref.gain_ref
  5.0 1.4 copy.32.rel_ref
  6.4 0.6 pad_add_fusion.me_ref
  7.0 0.0 copy-start.5
  7.0 0.0 copy-start.6
  7.0 20.1 %pre.1 = (s32[1,640]{1,0:T(1,128)}, s32[10,256]{1,0:T(8,128)}, s32[10,256]{1,0:T(8,128)}, s32[10,256]{1,0:T(8,128)}, s32[10,256]{1,0:T(8,128)}, /*index=5*/s32[1...) custom-call(s32[2]{0:T(128)} %pad_add_fusion.me_ref, ...), custom_call_target="tpu_custom_call" | custom-call | flops 3999999983616 | bytes 10561336 | tf_op jit(solution)/shard_map/pre/pallas_call | solution.py:870
  27.1 0.0 copy-done.5
  27.1 0.6 reshape.79.gain2_ref.gain_ref
  27.7 0.0 copy-done.6
  27.7 0.6 reshape.80.gain_ref
  28.3 0.0 collective-permute-done.rest_2_.enc2_any
  28.3 0.2 collective-permute-start.2
  28.5 5.5 %mid.1 = (f32[640,768]{1,0:T(8,128)}, bf16[640,768]{1,0:T(8,128)(2,1)}, bf16[640,768]{1,0:T(8,128)(2,1)}) custom-call(bf16[640,768]{1,0:T(8,128)(2,1)} %get-tuple-element.100.x0_ref.x0_any, bf16[640,768]{1,0:T(8,128)(2,1)} %get-tuple-element.102.oself_ref.oself_any, bf16[768,768]{1,0:T(8,128)(2,1)} %wso_ref.3, f32[1,768]{1,0:T(1,128)} %reshape.79.gain2_ref.gain_ref, ...), custom_call_target="tpu_custom_call" | custom-call | flops 799999983616 | bytes 8260608 | tf_op jit(solution)/shard_map/mid/pallas_call | solution.py:870
  34.0 0.0 collective-permute-done.1.rest_1_
  34.0 0.0 collective-permute-done.2.rest_3_
  34.0 33.1 %kv_cross.1 = (bf16[2048,768]{1,0:T(8,128)(2,1)}, bf16[2048,768]{1,0:T(8,128)(2,1)}, bf16[768,2048]{1,0:T(8,128)(2,1)}, f32[640,768]{1,0:T(8,128)}, f32[10,3,1,256]{3,2,1,0:T(1,128)}) custom-call(s32[2]{0:T(128)} %pad_add_fusion.me_ref, s32[10]{0:T(128)} %get-tuple-element.104.lo_ref, s32[10]{0:T(128)} %get-tuple-element.105.hi_ref, ...), custom_call_target="tpu_custom_call" | custom-call | flops 7999999967232 | bytes 17942616 | tf_op jit(solution)/shard_map/kv_cross/pallas_call | solution.py:870
  67.1 49.0 %ffn.1 = (bf16[16,192,768]{2,1,0:T(8,128)(2,1)}, bf16[16,192,768]{2,1,0:T(8,128)(2,1)}, f32[640,768]{1,0:T(8,128)}, f32[640,768]{1,0:T(8,128)}, bf16[640,768]{1,...) custom-call(s32[2]{0:T(128)} %pad_add_fusion.me_ref, s32[1,640]{1,0:T(1,128)} %get-tuple-element.99.src_ref, ...), custom_call_target="tpu_custom_call" | custom-call | flops 6000000106496 | bytes 31457280 | tf_op jit(solution)/shard_map/ffn/pallas_call | solution.py:1160
  116.0 0.0 collective-permute-start.3
  116.0 5.7 %ffn_back.1 = (f32[640,768]{1,0:T(8,128)}, bf16[640,768]{1,0:T(8,128)(2,1)}, bf16[640,768]{1,0:T(8,128)(2,1)}, f32[1,768]{1,0:T(1,128)}) custom-call(f32[640,768]{1,0:T(8,128)} %get-tuple-element.117.x2_ref, f32[640,768]{1,0:T(8,128)} %get-tuple-element.118.dh_ref, bf16[640,768]{1,0:T(8,128)(2,1)} %get-tuple-element.119.g_ref, f32[1,768]{1,0:T(1,128)} %reshape.80.gain_ref, ...), custom_call_target="tpu_custom_call" | custom-call | flops 3000000053248 | bytes 10033152 | tf_op jit(solution)/shard_map/ffn_back/pallas_call | solution.py:870
  121.7 2.6 collective-permute-done.3
  124.3 5.9 %add_convert_fusion.1 = (bf16[8,96,768]{2,1,0:T(8,128)(2,1)}, bf16[8,96,768]{2,1,0:T(8,128)(2,1)}, bf16[8,96,768]{2,1,0:T(8,128)(2,1)}, bf16[8,96,768]{2,1,0:T(8,128)(2,1)}) fusion(bf16[16,192,768]{2,1,0:T(8,128)(2,1)} %collective-permute-done.3, bf16[16,192,768]{2,1,0:T(8,128)(2,1)} %get-tuple-element.121), kind=kLoop, calls=%fused_computation.1 | loop fusion | flops 9437184 | bytes 14155776 | tf_op jit(solution)/shard_map/convert_element_type | solution.py:1921
  130.2 3.2 collective-permute-start.5
  133.4 0.5 collective-permute-start.6
  133.9 0.0 copy-start
  133.9 0.0 copy-start.1
  133.9 32.0 %cross_back.2 = (bf16[640,512]{1,0:T(8,128)(2,1)}, bf16[2,512,1024]{2,1,0:T(8,128)(2,1)}, bf16[2,512,1024]{2,1,0:T(8,128)(2,1)}) custom-call(s32[2]{0:T(128)} %pad_add_fusion.me_ref, s32[10]{0:T(128)} %get-tuple-element.104.lo_ref, s32[10]{0:T(128)} %get-tuple-element.105.hi_ref, s32[10,256]{1,0:T(8,128)} %get-tuple-element.106.start_ref, ...), custom_call_target="tpu_custom_call" | custom-call | flops 9999999827968 | bytes 31457280 | tf_op jit(solution)/shard_map/cross_back/pallas_call | solution.py:1301
  165.9 0.0 collective-permute-done.5
  165.9 0.0 collective-permute-done.6
  165.9 0.0 copy-done
  165.9 0.0 copy-done.1
  165.9 3.2 add_convert_fusion.4
  169.1 0.9 pad_maximum_fusion
  170.0 0.0 collective-permute-start.9
  170.0 4.9 %collective-permute-start.10 = (bf16[2,96,768]{2,1,0:T(8,128)(2,1)}, bf16[2,96,768]{2,1,0:T(8,128)(2,1)}, u32[]{:S(2)}, u32[]{:S(2)}) collective-permute-start(bf16[2,96,768]{2,1,0:T(8,128)(2,1)} %get-tuple-element.140), channel_id=1, source_target_pairs={{0,10},{1,11},{2,8},{3,9},{4,14},{5,15},{6,12},{7,13},{8,2},{9,3},... | collective-permute-start | bytes 884744 | tf_op jit(solution)/shard_map/ppermute | solution.py:1914
  174.9 0.0 collective-permute-start.11
  174.9 1.1 collective-permute-start.12
  176.0 2.4 collective-permute-start.8
  178.4 23.5 %cross_back.3 = (bf16[640,256]{1,0:T(8,128)(2,1)}, bf16[2,512,512]{2,1,0:T(8,128)(2,1)}, bf16[2,512,512]{2,1,0:T(8,128)(2,1)}) custom-call(s32[2]{0:T(128)} %pad_add_fusion.me_ref, s32[10]{0:T(128)} %get-tuple-element.104.lo_ref, s32[10]{0:T(128)} %get-tuple-element.105.hi_ref, s32[10,256]{1,0:T(8,128)} %get-tuple-element.106.start_ref, ...), custom_call_target="tpu_custom_call" | custom-call | flops 9999999827968 | bytes 31457280 | tf_op jit(solution)/shard_map/cross_back/pallas_call | solution.py:1301
  201.9 0.0 collective-permute-done.9
  201.9 0.0 collective-permute-start.4
  201.9 0.0 collective-permute-done.10
  201.9 0.5 collective-permute-start.7
  202.4 0.0 collective-permute-done.11
  202.4 0.0 collective-permute-done.12
  202.4 0.0 collective-permute-done.8
  202.5 0.0 copy-start.3
  202.5 0.0 copy-start.4
  202.5 7.0 %cross_in.1 = (f32[640,768]{1,0:T(8,128)}, bf16[640,768]{1,0:T(8,128)(2,1)}, bf16[640,768]{1,0:T(8,128)(2,1)}, f32[1,768]{1,0:T(1,128)}) custom-call(bf16[640,512]{1,0:T(8,128)(2,1)} %get-tuple-element.137.dq0_ref, bf16[640,256]{1,0:T(8,128)(2,1)} %get-tuple-element.144.dq1_ref, f32[640,768]{1,0:T(8,128)} %get-tuple-element.103.x1_ref, ...), custom_call_target="tpu_custom_call" | custom-call | flops 6000000106496 | bytes 11212800 | tf_op jit(solution)/shard_map/cross_in/pallas_call | solution.py:870
  209.5 0.0 copy-done.3
  209.5 0.0 copy-done.4
  209.5 1.8 fusion.2
  211.3 0.7 pad_maximum_fusion.2.fsend_any
  212.0 0.7 pad_maximum_fusion.1.fkeep_ref
  212.8 0.0 collective-permute-done.4.came0_any
  212.8 0.0 collective-permute-done.7.came1_any
  212.8 125.0 %late.1 = (f32[640,768]{1,0:T(8,128)}, f32[56,128]{1,0:T(8,128)}, bf16[24,8,16,384]{3,2,1,0:T(8,128)(2,1)}, f32[512,768]{1,0:T(8,128)}, bf16[512,768]{1,0:T(8,128)(2,1)}, /*index=5*/bf16[8,192,768]{2,1,0:T(8,128)(2,1)}) custom-call(s32[10,256]{1,0:T(8,128)} %get-tuple-element.113.start_ref, s32[10,256]{1,0:T(8,128)} %get-tuple-element.114.size_ref, ...), custom_call_target="tpu_custom_call" | custom-call | flops 9999999827968 | bytes 31457280 | tf_op jit(solution)/shard_map/late/pallas_call | solution.py:1787
  337.8 0.0 copy-start.2
  337.8 8.2 %last.1 = (f32[192,3072]{1,0:T(8,128)}, f32[768,768]{1,0:T(8,128)}, f32[192,768]{1,0:T(8,128)}, f32[192,768]{1,0:T(8,128)}, f32[192,1536]{1,0:T(8,128)}, /*index...) custom-call(s32[2]{0:T(128)} %pad_add_fusion.me_ref, ...), custom_call_target="tpu_custom_call" | custom-call | flops 799999983616 | bytes 18119304 | tf_op jit(solution)/shard_map/last/pallas_call | solution.py:870
  346.0 0.0 copy-done.2
  346.0 1.3 copy.34
Async XLA Ops:
  0.6 33.4 %collective-permute-start.1 = (bf16[512,768]{1,0:T(8,128)(2,1)}, bf16[512,768]{1,0:T(8,128)(2,1)}, u32[]{:S(2)}, u32[]{:S(2)}) collective-permute-start(bf16[512,768]{1,0:T(8,128)(2,1)} %enc0_any.1), channel_id=1, source_target_pairs={{0,1},{1,0},{2,3},{3,2},{4,5},{5,4},{6,7},{7,6},{8,9},{9,8},{10,11... | collective-permute-start | bytes 2359304 | tf_op jit(solution)/shard_map/ppermute | solution.py:1914
  1.2 27.1 %collective-permute-start = (bf16[512,768]{1,0:T(8,128)(2,1)}, bf16[512,768]{1,0:T(8,128)(2,1)}, u32[]{:S(2)}, u32[]{:S(2)}) collective-permute-start(bf16[512,768]{1,0:T(8,128)(2,1)} %enc0_any.1), channel_id=1, source_target_pairs={{0,2},{1,3},{2,0},{3,1},{4,6},{5,7},{6,4},{7,5},{8,10},{9,11},{10,... | collective-permute-start | bytes 2359304 | tf_op jit(solution)/shard_map/ppermute | solution.py:1914
  7.0 20.1 %copy-start.5 = (f32[768]{0:T(1024)S(1)}, f32[768]{0:T(1024)}, u32[]{:S(2)}) copy-start(f32[768]{0:T(1024)} %param.28) | copy-start | bytes 9220
  7.0 20.7 %copy-start.6 = (f32[768]{0:T(1024)S(1)}, f32[768]{0:T(1024)}, u32[]{:S(2)}) copy-start(f32[768]{0:T(1024)} %param.32) | copy-start | bytes 9220
  28.3 5.7 %collective-permute-start.2 = (bf16[512,768]{1,0:T(8,128)(2,1)}, bf16[512,768]{1,0:T(8,128)(2,1)}, u32[]{:S(2)}, u32[]{:S(2)}) collective-permute-start(bf16[512,768]{1,0:T(8,128)(2,1)} %collective-permute-done.rest_2_.enc2_any), channel_id=1, source_target_pairs={{0,1},{1,0},{2,3},{3,2},{4,5},{5,4},{6,7},{7,6},{8,9},{9,8},{10,11... | collective-permute-start | bytes 2359304 | tf_op jit(solution)/shard_map/ppermute | solution.py:1914
  116.0 8.3 %collective-permute-start.3 = (bf16[16,192,768]{2,1,0:T(8,128)(2,1)}, bf16[16,192,768]{2,1,0:T(8,128)(2,1)}, u32[]{:S(2)}, u32[]{:S(2)}) collective-permute-start(bf16[16,192,768]{2,1,0:T(8,128)(2,1)} %get-tuple-element.122), channel_id=1, source_target_pairs={{0,1},{1,0},{2,3},{3,2},{4,5},{5,4},{6,7},{7,6},{8,9},{9,8},{10,11... | collective-permute-start | bytes 14155784 | tf_op jit(solution)/shard_map/ppermute | solution.py:1914
  130.2 35.7 %collective-permute-start.5 = (bf16[8,96,768]{2,1,0:T(8,128)(2,1)}, bf16[8,96,768]{2,1,0:T(8,128)(2,1)}, u32[]{:S(2)}, u32[]{:S(2)}) collective-permute-start(bf16[8,96,768]{2,1,0:T(8,128)(2,1)} %get-tuple-element.130), channel_id=1, source_target_pairs={{0,4},{1,5},{2,6},{3,7},{4,0},{5,1},{6,2},{7,3},{8,12},{9,13},{10,... | collective-permute-start | bytes 3538952 | tf_op jit(solution)/shard_map/ppermute | solution.py:1914
  133.4 32.5 %collective-permute-start.6 = (bf16[8,96,768]{2,1,0:T(8,128)(2,1)}, bf16[8,96,768]{2,1,0:T(8,128)(2,1)}, u32[]{:S(2)}, u32[]{:S(2)}) collective-permute-start(bf16[8,96,768]{2,1,0:T(8,128)(2,1)} %get-tuple-element.131), channel_id=1, source_target_pairs={{0,2},{1,3},{2,0},{3,1},{4,6},{5,7},{6,4},{7,5},{8,10},{9,11},{10,... | collective-permute-start | bytes 3538952 | tf_op jit(solution)/shard_map/ppermute | solution.py:1914
  133.9 32.0 %copy-start = (bf16[8,96,768]{2,1,0:T(8,128)(2,1)S(1)}, bf16[8,96,768]{2,1,0:T(8,128)(2,1)}, u32[]{:S(2)}) copy-start(bf16[8,96,768]{2,1,0:T(8,128)(2,1)} %get-tuple-element.184) | copy-start | bytes 3538948
  133.9 32.0 %copy-start.1 = (bf16[8,96,768]{2,1,0:T(8,128)(2,1)S(1)}, bf16[8,96,768]{2,1,0:T(8,128)(2,1)}, u32[]{:S(2)}) copy-start(bf16[8,96,768]{2,1,0:T(8,128)(2,1)} %get-tuple-element.185) | copy-start | bytes 3538948
  170.0 31.9 %collective-permute-start.9 = (bf16[2,96,768]{2,1,0:T(8,128)(2,1)}, bf16[2,96,768]{2,1,0:T(8,128)(2,1)}, u32[]{:S(2)}, u32[]{:S(2)}) collective-permute-start(bf16[2,96,768]{2,1,0:T(8,128)(2,1)} %get-tuple-element.139), channel_id=1, source_target_pairs={{0,2},{1,3},{2,0},{3,1},{4,6},{5,7},{6,4},{7,5},{8,10},{9,11},{10,... | collective-permute-start | bytes 884744 | tf_op jit(solution)/shard_map/ppermute | solution.py:1914
  170.0 31.9 %collective-permute-start.10 = (bf16[2,96,768]{2,1,0:T(8,128)(2,1)}, bf16[2,96,768]{2,1,0:T(8,128)(2,1)}, u32[]{:S(2)}, u32[]{:S(2)}) collective-permute-start(bf16[2,96,768]{2,1,0:T(8,128)(2,1)} %get-tuple-element.140), channel_id=1, source_target_pairs={{0,10},{1,11},{2,8},{3,9},{4,14},{5,15},{6,12},{7,13},{8,2},{9,3},... | collective-permute-start | bytes 884744 | tf_op jit(solution)/shard_map/ppermute | solution.py:1914
  174.9 27.5 %collective-permute-start.11 = (bf16[2,96,768]{2,1,0:T(8,128)(2,1)}, bf16[2,96,768]{2,1,0:T(8,128)(2,1)}, u32[]{:S(2)}, u32[]{:S(2)}) collective-permute-start(bf16[2,96,768]{2,1,0:T(8,128)(2,1)} %get-tuple-element.141), channel_id=1, source_target_pairs={{0,4},{1,5},{2,6},{3,7},{4,0},{5,1},{6,2},{7,3},{8,12},{9,13},{10,... | collective-permute-start | bytes 884744 | tf_op jit(solution)/shard_map/ppermute | solution.py:1914
  174.9 27.5 %collective-permute-start.12 = (bf16[2,96,768]{2,1,0:T(8,128)(2,1)}, bf16[2,96,768]{2,1,0:T(8,128)(2,1)}, u32[]{:S(2)}, u32[]{:S(2)}) collective-permute-start(bf16[2,96,768]{2,1,0:T(8,128)(2,1)} %get-tuple-element.142), channel_id=1, source_target_pairs={{0,12},{1,13},{2,14},{3,15},{4,8},{5,9},{6,10},{7,11},{8,4},{9,5},... | collective-permute-start | bytes 884744 | tf_op jit(solution)/shard_map/ppermute | solution.py:1914
  176.0 26.4 %collective-permute-start.8 = (bf16[2,192,768]{2,1,0:T(8,128)(2,1)}, bf16[2,192,768]{2,1,0:T(8,128)(2,1)}, u32[]{:S(2)}, u32[]{:S(2)}) collective-permute-start(bf16[2,192,768]{2,1,0:T(8,128)(2,1)} %pad_maximum_fusion), channel_id=1, source_target_pairs={{0,8},{1,9},{2,10},{3,11},{4,12},{5,13},{6,14},{7,15},{8,0},{9,1},... | collective-permute-start | bytes 1769480 | tf_op jit(solution)/shard_map/ppermute | solution.py:1914
  201.9 10.8 %collective-permute-start.4 = (bf16[2,512,1024]{2,1,0:T(8,128)(2,1)}, bf16[2,512,1024]{2,1,0:T(8,128)(2,1)}, u32[]{:S(2)}, u32[]{:S(2)}) collective-permute-start(bf16[2,512,1024]{2,1,0:T(8,128)(2,1)} %get-tuple-element.129), channel_id=1, source_target_pairs={{0,1},{1,0},{2,3},{3,2},{4,5},{5,4},{6,7},{7,6},{8,9},{9,8},{10,11... | collective-permute-start | bytes 6291464 | tf_op jit(solution)/shard_map/ppermute | solution.py:1914
  201.9 10.8 %collective-permute-start.7 = (bf16[2,512,512]{2,1,0:T(8,128)(2,1)}, bf16[2,512,512]{2,1,0:T(8,128)(2,1)}, u32[]{:S(2)}, u32[]{:S(2)}) collective-permute-start(bf16[2,512,512]{2,1,0:T(8,128)(2,1)} %get-tuple-element.136), channel_id=1, source_target_pairs={{0,1},{1,0},{2,3},{3,2},{4,5},{5,4},{6,7},{7,6},{8,9},{9,8},{10,11... | collective-permute-start | bytes 3145736 | tf_op jit(solution)/shard_map/ppermute | solution.py:1914
  202.5 7.0 %copy-start.3 = (bf16[2,96,768]{2,1,0:T(8,128)(2,1)S(1)}, bf16[2,96,768]{2,1,0:T(8,128)(2,1)}, u32[]{:S(2)}) copy-start(bf16[2,96,768]{2,1,0:T(8,128)(2,1)} %get-tuple-element.192) | copy-start | bytes 884740
  202.5 7.0 %copy-start.4 = (bf16[2,96,768]{2,1,0:T(8,128)(2,1)S(1)}, bf16[2,96,768]{2,1,0:T(8,128)(2,1)}, u32[]{:S(2)}) copy-start(bf16[2,96,768]{2,1,0:T(8,128)(2,1)} %get-tuple-element.205) | copy-start | bytes 884740
  337.8 8.2 %copy-start.2 = (f32[640,768]{1,0:T(8,128)S(1)}, f32[640,768]{1,0:T(8,128)}, u32[]{:S(2)}) copy-start(f32[640,768]{1,0:T(8,128)} %get-tuple-element.221) | copy-start | bytes 5898244

commit v5 on v4

--- a/solution.py
+++ b/solution.py
@@ -689,6 +689,19 @@
     return (rel & 1) * 4 + (rel & 2) + ((rel >> 2) & 1)
 
 
+def fill_bias_all(brow_ref, bias, nq):
+    dist = distances()
+
+    def add(d, held):
+        here = dist == d
+        row = pl.ds(d, 1)
+        return tuple(jnp.where(here, brow_ref[row, c * 256 : (c + 1) * 256], held[c]) for c in range(nq))
+
+    held = lax.fori_loop(0, brow_ref.shape[0], add, (jnp.full((WIN, 256), MASKED, F32),) * nq)
+    for c in range(nq):
+        bias[c] = held[c]
+
+
 def gelu_both(a):
     c = math.sqrt(2.0 / math.pi)
     a2 = a * a
@@ -739,6 +752,7 @@
     order,
     qstart,
     qcount,
+    place,
     wide,
     kp,
     vp,
@@ -752,23 +766,20 @@
     rows, width = dec_ref.shape
     nq, tiles = width // 256, rows // TQ
     base = me_ref[0] * answers
+    own = [aq_ref[base + a] for a in range(answers)]
     n = jnp.int32(0)
     first_row = jnp.int32(0)
     for c in range(questions):
         qstart[c] = first_row
         first_row = first_row + qrows_ref[0, c]
         qcount[c] = n
-
-        def visit(a, n):
-            hit = aq_ref[base + a] == c
-
-            @pl.when(hit)
-            def _():
-                order[n] = a
-
-            return n + hit.astype(jnp.int32)
-
-        n = lax.fori_loop(0, answers, visit, n)
+        place[c] = n
+        for q in own:
+            n = n + (q == c).astype(jnp.int32)
+    for a, q in enumerate(own):
+        at = place[q]
+        order[at] = a
+        place[q] = at + 1
 
     def answer_of(tok):
         ans = jnp.zeros_like(tok)
@@ -822,25 +833,39 @@
         cs = slice(i * width, (i + 1) * width)
         proj_ref[:, cs] = dot(h1_ref[...], wqkv_ref[:, cs]).astype(BF)
     fill_window(proj_ref, kp, vp, width)
-    fill_bias(brow_ref, bias, nq)
-
-    def tile(t, _):
+    fill_bias_all(brow_ref, bias, nq)
+
+    def scores(t, c):
         row = pl.ds(pl.multiple_of(t * TQ, TQ), TQ)
         win = pl.ds(pl.multiple_of(t * TQ, TQ), WIN)
+        cs = slice(c * 256, (c + 1) * 256)
+        qs = stack4(proj_ref[row, cs] * jnp.asarray(scale, BF))
+        return dot_nt(kp[win, cs], qs) + bias[c]
+
+    def probs(t, c, s):
         mask = range_mask(t * TQ - 64, WIN, sstart_ref[pl.ds(t, 1), :], ssize_ref[pl.ds(t, 1), :])
-        for c in range(nq):
-            cs = slice(c * 256, (c + 1) * 256)
-            qs = stack4(proj_ref[row, cs] * jnp.asarray(scale, BF))
-            s = jnp.where(mask, dot_nt(kp[win, cs], qs) + bias[c], MASKED)
-            m = jnp.max(red(s, jnp.max), axis=0, keepdims=True)
-            p = jnp.exp(s - m)
-            l = jnp.sum(red(p, jnp.sum), axis=0, keepdims=True)
-            p = (p * (1.0 / l)).astype(BF)
-            oself_ref[row, cs] = unstack4(dot_tn(p, vp[win, cs])).astype(BF)
-            lse_ref[t, c] = m + jnp.log(l)
+        s = jnp.where(mask, s, MASKED)
+        m = jnp.max(red(s, jnp.max), axis=0, keepdims=True)
+        p = jnp.exp(s - m)
+        l = jnp.sum(red(p, jnp.sum), axis=0, keepdims=True)
+        lse_ref[t, c] = m + jnp.log(l)
+        return (p * (1.0 / l)).astype(BF)
+
+    def mix(t, c, p):
+        row = pl.ds(pl.multiple_of(t * TQ, TQ), TQ)
+        win = pl.ds(pl.multiple_of(t * TQ, TQ), WIN)
+        cs = slice(c * 256, (c + 1) * 256)
+        oself_ref[row, cs] = unstack4(dot_tn(p, vp[win, cs])).astype(BF)
+
+    def two_tiles(i, _):
+        work = [(2 * i + k, c) for k in range(2) for c in range(nq)]
+        s = [scores(t, c) for t, c in work]
+        p = [probs(t, c, x) for (t, c), x in zip(work, s)]
+        for (t, c), x in zip(work, p):
+            mix(t, c, x)
         return 0
 
-    lax.fori_loop(0, tiles, tile, 0)
+    lax.fori_loop(0, tiles // 2, two_tiles, 0)
 
 
 def mid_kernel(x0_ref, oself_ref, wso_ref, gain2_ref, wcq_ref, x1_ref, h2_ref, qc_ref, *, scale):
@@ -913,6 +938,7 @@
         (VM,) * 5 + (SM, SM) + (VM,) * 6,
         [
             pltpu.SMEM((lens.shape[0],), i32),
+            pltpu.SMEM((qrows.shape[1],), i32),
             pltpu.SMEM((qrows.shape[1],), i32),
             pltpu.SMEM((qrows.shape[1],), i32),
             pltpu.VMEM((rel.shape[0], width), F32),
@@ -1052,142 +1078,222 @@
 
 
 def ffn_kernel(
-    me_ref,
     src_ref,
     x1_ref,
     ocross_ref,
     gain_ref,
     cot_ref,
     wco_ref,
-    win_ref,
-    wout_ref,
-    keep_ref,
-    send_ref,
-    x2_ref,
-    dh_ref,
-    g_ref,
+    win_any,
+    wout_any,
+    okeep_ref,
+    osend_ref,
+    wi_ref,
     oc_ref,
     out_ref,
+    dx2_ref,
+    dyc_ref,
+    do_ref,
+    dgain_ref,
+    win,
+    wout,
     h3,
     h3t,
+    g_low,
+    dh,
     out_acc,
-    *,
-    last,
+    u_all,
+    ik,
+    ss,
+    ic,
+    iy,
+    ix,
+    even,
+    odd,
+    came,
+    w_sem,
+    send_sem,
+    recv_sem,
+    o_send,
+    o_recv,
 ):
-    i = pl.program_id(0)
-    me_b, me_g = me_ref[0], me_ref[1]
-    f = me_b ^ i
     rows, width = x1_ref.shape
+    steps = win.shape[1] // width
     quarter = width // 4
     half = quarter // 2
-
-    @pl.when(i == 0)
-    def _():
-        hot = onehot_rows(src_ref[...])
-        g_ref[...] = dot_tn(hot, cot_ref[...]).astype(BF)
-        oc = ocross_ref[...].astype(BF)
-        oc_ref[...] = oc
-        x2 = x1_ref[...] + dot(oc, wco_ref[...])
-        x2_ref[...] = x2
-        n = (x2 * rms(x2) * gain_ref[...]).astype(BF)
-        h3[...] = n
-        h3t[...] = n.T
-        out_acc[...] = jnp.zeros_like(out_acc)
-        dh_ref[...] = jnp.zeros_like(dh_ref)
-
-    u, slope = gelu_both(dot(h3[...], win_ref[...]))
-    u = u.astype(BF)
-    out_acc[...] += dot(u, wout_ref[...])
-    da = (slope * dot_nt(g_ref[...], wout_ref[...])).astype(BF)
-    dh_ref[...] += dot_nt(da, win_ref[...])
-    dwo = dot_tn(u, g_ref[...]).astype(BF)
-    for s in range(8):
-        at = (i >> 1) * 8 + slot_of(me_g ^ s)
-
-        @pl.when((i & 1) == 0)
+    g, b = lax.axis_index("grp"), lax.axis_index("blk")
+    mesh_id = pl.DeviceIdType.MESH
+    peers = [(g, b ^ 1), (g ^ 1, b), (g, b ^ 2)]
+
+    def part(f):
+        return pl.ds(pl.multiple_of(f * width, width), width)
+
+    def weights(f):
+        return (
+            pltpu.make_async_copy(win_any.at[:, part(f)], win.at[:, part(f)], w_sem.at[0, f]),
+            pltpu.make_async_copy(wout_any.at[part(f), :], wout.at[part(f), :], w_sem.at[1, f]),
+        )
+
+    for f in range(steps):
+        for c in weights(f):
+            c.start()
+    barrier = pltpu.get_barrier_semaphore()
+    for p in peers:
+        pl.semaphore_signal(barrier, inc=1, device_id=p, device_id_type=mesh_id)
+    pl.semaphore_wait(barrier, 3)
+
+    def remote(k, f):
+        src, dst = ((ss.at[f], ic.at[f]), (ik.at[f, pl.ds(2, 2)], iy.at[f]), (ik.at[f, pl.ds(1, 1)], ix.at[f]))[k]
+        return pltpu.make_async_remote_copy(
+            src_ref=src,
+            dst_ref=dst,
+            send_sem=send_sem.at[k, f],
+            recv_sem=recv_sem.at[k, f],
+            device_id=peers[k],
+            device_id_type=mesh_id,
+        )
+
+    o_copy = pltpu.make_async_remote_copy(
+        src_ref=odd, dst_ref=came, send_sem=o_send, recv_sem=o_recv, device_id=peers[0], device_id_type=mesh_id
+    )
+
+    def add(x, y):
+        return (x.astype(F32) + y.astype(F32)).astype(BF)
+
+    def event(k, f):
+        @pl.when((f >= 0) & (f < steps))
         def _():
-            keep_ref[at, half:, :] = dwo[s * half : (s + 1) * half]
-
-        @pl.when((i & 1) == 1)
-        def _():
-            send_ref[at, half:, :] = dwo[s * half : (s + 1) * half]
-
-    for r in range(4):
-        part = h3t[pl.ds(pl.multiple_of((me_b ^ r) * quarter, quarter), quarter), :]
-        dwi = dot(part, da).astype(BF)
-        target = send_ref if r & 1 else keep_ref
-        for b in range(2):
-            rel = me_g ^ (2 * f + b)
-            at = (rel & 1) * 8 + (r >> 1) * 4 + (rel & 2) + ((rel >> 2) & 1)
-            target[at, :half, :] = dwi[b * half : (b + 1) * half]
-
-    @pl.when(i == last)
-    def _():
-        out = (x2_ref[...] + out_acc[...]).astype(BF)
-        out_ref[...] = dot(onehot_rows(src_ref[...]), out).astype(BF)
-
-
-def ffn(me, src, x1, ocross, gain, cot, wco, win, wout):
+            remote(k, f).wait()
+            if k == 0:
+                ik[f] = add(ik[f], ic[f])
+            elif k == 1:
+                ik[f, 0:2] = add(ik[f, 0:2], iy[f])
+            else:
+                rel = (g >> 1) ^ f
+                wi_ref[(rel & 1) * 2 + (rel >> 1)] = add(ik[f, 0], ix[f, 0])
+            if k < 2:
+                remote(k + 1, f).start()
+
+    hot = onehot_rows(src_ref[...])
+    g_low[...] = dot_tn(hot, cot_ref[...]).astype(BF)
+    oc_ref[...] = ocross_ref[...].astype(BF)
+    x2 = x1_ref[...] + dot(oc_ref[...], wco_ref[...])
+    dx2_ref[...] = x2
+    n = (x2 * rms(x2) * gain_ref[...]).astype(BF)
+    h3[...] = n
+    h3t[...] = n.T
+    out_acc[...] = jnp.zeros_like(out_acc)
+    dh[...] = jnp.zeros_like(dh)
+
+    def hidden(f, _):
+        for c in weights(f):
+            c.wait()
+        u, slope = gelu_both(dot(h3[...], win[:, part(f)]))
+        u = u.astype(BF)
+        u_all[:, part(f)] = u
+        da = (slope * dot_nt(g_low[...], wout[part(f), :])).astype(BF)
+        for r in range(4):
+            left = h3t[pl.ds(pl.multiple_of((b ^ r) * quarter, quarter), quarter), :]
+            dwi = dot(left, da).astype(BF)
+            target = ss if r & 1 else ik
+            for i in range(2):
+                y = (g ^ (2 * f + i)) & 1
+                target[f, y * 2 + (r >> 1)] = dwi[i * half : (i + 1) * half]
+        remote(0, f).start()
+        out_acc[...] += dot(u, wout[part(f), :])
+        event(0, f)
+        dh[...] += dot_nt(da, win[:, part(f)])
+        event(1, f - 1)
+        event(2, f - 2)
+        return 0
+
+    lax.fori_loop(0, steps, hidden, 0)
+
+    def last_rows(f, _):
+        dwo = dot_tn(u_all[:, part(f)], g_low[...]).astype(BF)
+        r = b ^ f
+        for s in range(8):
+            at = (r >> 1) * 8 + slot_of(g ^ s)
+
+            @pl.when((r & 1) == 0)
+            def _():
+                even[at] = dwo[s * half : (s + 1) * half]
+
+            @pl.when((r & 1) == 1)
+            def _():
+                odd[at] = dwo[s * half : (s + 1) * half]
+
+        return 0
+
+    lax.fori_loop(0, steps, last_rows, 0)
+    o_copy.start()
+    event(1, jnp.int32(steps - 1))
+    event(2, jnp.int32(steps - 2))
+    x2 = dx2_ref[...]
+    out = (x2 + out_acc[...]).astype(BF)
+    out_ref[...] = dot(onehot_rows(src_ref[...]), out).astype(BF)
+    dx, dgain_ref[...] = rms_back(x2, rms(x2), gain_ref[...], dh[...])
+    dx2 = g_low[...].astype(F32) + dx
+    dx2_ref[...] = dx2
+    dyc_ref[...] = dx2.astype(BF)
+    do_ref[...] = dot_nt(dyc_ref[...], wco_ref[...]).astype(BF)
+    o_copy.wait()
+    okeep_ref[...] = add(even[0:8], came[0:8])
+    osend_ref[...] = add(even[8:16], came[8:16])
+    event(2, jnp.int32(steps - 1))
+
+
+def ffn(src, x1, ocross, gain, cot, wco, win, wout):
     rows, width = x1.shape
     steps = win.shape[1] // width
     half = width // 8
-    full = lambda a: pl.BlockSpec(a.shape, lambda i, m: (0,) * len(a.shape))
-    outs = (
-        sds((16, 2 * half, width), BF),
-        sds((16, 2 * half, width), BF),
-        sds((rows, width), F32),
-        sds((rows, width), F32),
-        sds((rows, width), BF),
-        sds((rows, width), BF),
-        sds((rows, width), BF),
-    )
-    ins = (src, x1, ocross, gain, cot, wco)
-    grid_spec = pltpu.PrefetchScalarGridSpec(
-        num_scalar_prefetch=1,
-        grid=(steps,),
-        in_specs=[full(a) for a in ins]
-        + [
-            pl.BlockSpec((width, width), lambda i, m: (0, m[0] ^ i)),
-            pl.BlockSpec((width, width), lambda i, m: (m[0] ^ i, 0)),
+    any_spec = pl.BlockSpec(memory_space=pl.ANY)
+    buf = lambda *n: pltpu.VMEM(n + (half, width), BF)
+    tok = lambda d: pltpu.VMEM((rows, width), d)
+    return pl.pallas_call(
+        ffn_kernel,
+        out_shape=(
+            sds((8, half, width), BF),
+            sds((8, half, width), BF),
+            sds((4, half, width), BF),
+            sds((rows, width), BF),
+            sds((rows, width), BF),
+            sds((rows, width), F32),
+            sds((rows, width), BF),
+            sds((rows, width), BF),
+            sds((1, width), F32),
+        ),
+        in_specs=[VM] * 6 + [any_spec] * 2,
+        out_specs=(VM,) * 9,
+        scratch_shapes=[
+            pltpu.VMEM(win.shape, BF),
+            pltpu.VMEM(wout.shape, BF),
+            tok(BF),
+            pltpu.VMEM((width, rows), BF),
+            tok(BF),
+            tok(F32),
+            tok(F32),
+            pltpu.VMEM((rows, win.shape[1]), BF),
+            buf(steps, 4),
+            buf(steps, 4),
+            buf(steps, 4),
+            buf(steps, 2),
+            buf(steps, 1),
+            buf(16),
+            buf(16),
+            buf(16),
+            pltpu.SemaphoreType.DMA((2, steps)),
+            pltpu.SemaphoreType.DMA((3, steps)),
+            pltpu.SemaphoreType.DMA((3, steps)),
+            pltpu.SemaphoreType.DMA,
+            pltpu.SemaphoreType.DMA,
         ],
-        out_specs=tuple(full(a) for a in outs),
-        scratch_shapes=[
-            pltpu.VMEM((rows, width), BF),
-            pltpu.VMEM((width, rows), BF),
-            pltpu.VMEM((rows, width), F32),
-        ],
-    )
-    return pl.pallas_call(
-        functools.partial(ffn_kernel, last=steps - 1),
-        out_shape=outs,
-        grid_spec=grid_spec,
-        compiler_params=pltpu.CompilerParams(vmem_limit_bytes=LIMIT),
-        cost_estimate=pl.CostEstimate(flops=60 * 10**11, bytes_accessed=30 << 20, transcendentals=0),
+        compiler_params=pltpu.CompilerParams(
+            vmem_limit_bytes=63 << 20, collective_id=1, has_side_effects=True
+        ),
+        cost_estimate=pl.CostEstimate(flops=10**13, bytes_accessed=30 << 20, transcendentals=0),
         name="ffn",
-    )(me, *ins, win, wout)
-
-
-def ffn_back_kernel(x2_ref, dh_ref, g_ref, gain_ref, wco_ref, dx2_ref, dyc_ref, do_ref, dgain_ref):
-    x2 = x2_ref[...]
-    dx, dgain_ref[...] = rms_back(x2, rms(x2), gain_ref[...], dh_ref[...])
-    dx2 = g_ref[...].astype(F32) + dx
-    dx2_ref[...] = dx2
-    dyc_ref[...] = dx2.astype(BF)
-    do_ref[...] = dot_nt(dyc_ref[...], wco_ref[...]).astype(BF)
-
-
-def ffn_back(x2, dh, g, gain, wco):
-    rows, width = x2.shape
-    return call(
-        ffn_back_kernel,
-        "ffn_back",
-        (sds((rows, width), F32), sds((rows, width), BF), sds((rows, width), BF), sds((1, width), F32)),
-        [VM] * 5,
-        (VM,) * 4,
-        [],
-        (x2, dh, g, gain, wco),
-        us=30,
-    )
+    )(src, x1, ocross, gain, cot, wco, win, wout)
 
 
 def cross_back_kernel(
@@ -1260,6 +1366,7 @@
 
         lo = lo_ref[t]
         hi = hi_ref[t]
+        slots = ps.shape[0]
 
         def two(i, _):
             probs(lo + 2 * i, 0)
@@ -1268,6 +1375,17 @@
             grads(lo + 2 * i + 1, 1)
             return 0
 
+        if slots == 4:
+
+            def four(i, _):
+                for k in range(4):
+                    probs(lo + 4 * i + k, k)
+                for k in range(4):
+                    grads(lo + 4 * i + k, k)
+                return 0
+
+            lax.fori_loop(0, (hi - lo) // 4, four, 0)
+            lo = lo + (hi - lo) // 4 * 4
         lax.fori_loop(0, (hi - lo) // 2, two, 0)
 
         @pl.when((hi - lo) % 2 == 1)
@@ -1323,8 +1441,8 @@
             pltpu.VMEM((keys, width), F32),
             pltpu.VMEM((keys, width), F32),
             pltpu.VMEM((nq, 256, 256), F32),
-            pltpu.VMEM((2, nq, 256, 256), BF),
-            pltpu.VMEM((2, nq, 256, 256), BF),
+            pltpu.VMEM((4 if nq == 1 else 2, nq, 256, 256), BF),
+            pltpu.VMEM((4 if nq == 1 else 2, nq, 256, 256), BF),
         ],
         compiler_params=pltpu.CompilerParams(vmem_limit_bytes=LIMIT),
         cost_estimate=pl.CostEstimate(flops=10**13, bytes_accessed=30 << 20, transcendentals=0),
@@ -1389,6 +1507,7 @@
     h2_ref,
     dq0_ref,
     dq1_ref,
+    wpair_any,
     fkeep_ref,
     fsend_any,
     d_ref,
@@ -1500,17 +1619,28 @@
         pl.semaphore_signal(barrier, inc=1, device_id=p, device_id_type=mesh_id)
     pl.semaphore_wait(barrier, 5)
 
-    f_first = remote(fsend_any, frecv, f_send.at[0], f_recv.at[0], 4)
-    f_second = remote(fown, ffn_any.at[1], f_send.at[1], f_recv.at[1], 4)
-    f_third = remote(ffn_any.at[pl.ds(0, 2)], ffn_any.at[pl.ds(2, 2)], f_send.at[2], f_recv.at[2], 3)
-    f_local = local(fown, ffn_any.at[0], 19)
-    f_slices = fown.shape[0] // step_rows
+    f_half = fown.shape[0]
+    w_at, o_at = pl.ds(0, f_half), pl.ds(f_half, f_half)
+    w_local = local(wpair_any, ffn_any.at[pl.ds(0, 2), w_at, :], 28)
+    w_copies = [
+        remote(wpair_any, ffn_any.at[pl.ds(2, 2), w_at, :], f_send.at[0], f_recv.at[0], 3),
+        remote(ffn_any.at[pl.ds(0, 4), w_at, :], ffn_any.at[pl.ds(4, 4), w_at, :], f_send.at[1], f_recv.at[1], 2),
+    ]
+    f_first = remote(fsend_any, frecv, f_send.at[2], f_recv.at[2], 4)
+    f_second = remote(fown, ffn_any.at[1, o_at, :], f_send.at[3], f_recv.at[3], 4)
+    f_third = remote(
+        ffn_any.at[pl.ds(0, 2), o_at, :], ffn_any.at[pl.ds(2, 2), o_at, :], f_send.at[4], f_recv.at[4], 3
+    )
+    f_local = local(fown, ffn_any.at[0, o_at, :], 19)
+    f_slices = f_half // step_rows
+    w_copies[0].start()
     f_first.start()
+    w_local.start()
 
     def f_copy(i):
-        at = pl.ds(pl.multiple_of(i * step_rows, step_rows), step_rows)
+        at = pl.ds(pl.multiple_of(f_half + i * step_rows, step_rows), step_rows)
         src, dst = ffn_any.at[pl.ds(0, 4), at, :], ffn_any.at[pl.ds(4, 4), at, :]
-        return remote(src, dst, f_send.at[3 + i], f_recv.at[3 + i], 2)
+        return remote(src, dst, f_send.at[5 + i], f_recv.at[5 + i], 2)
 
     enc_copy = remote(enc_out, came_any, x_send, x_recv, 1)
 
@@ -1584,6 +1714,9 @@
         event(0, jnp.int32(j))
     put(jnp.concatenate([dq0_ref[...], dq1_ref[...]], axis=1), 1)
     step(0)
+    w_local.wait()
+    w_copies[0].wait()
+    w_copies[1].start()
     held_in[0].wait()
     held_in[1].wait()
     left_t[...] = oself_ref[...].T
@@ -1621,7 +1754,7 @@
     wqkv_in.start()
 
     projs[0:64, :] = jnp.zeros((64, 3 * width), BF)
-    fill_bias(brow_ref, bias, nq)
+    fill_bias_all(brow_ref, bias, nq)
     dka[...] = jnp.zeros_like(dka)
     dva[...] = jnp.zeros_like(dva)
     dsum[...] = jnp.zeros_like(dsum)
@@ -1746,15 +1879,14 @@
     small_copy(0).start()
     f_third.wait()
     f_copy(0).start()
-    f_copy(1).start()
     step(done)
     hot_rows = onehot_rows(src_ref[...])
     d_ref[...] = dot(hot_rows, both[:rows, :width]) + dot(hot_rows, both[:rows, width:])
     for k in range(5):
         small_sum(k)
         for i in range(2):
-            f_copy(2 + 2 * k + i).start()
             step(done + 1 + 2 * k + i)
+        f_copy(1 + k).start()
 
     def rest(t, _):
         step(t)
@@ -1767,12 +1899,13 @@
         return 0
 
     lax.fori_loop(0, f_slices, f_end, 0)
+    w_copies[1].wait()
     enc_copy.wait()
 
 
 def late(
     start, size, bucket, brow, proj, do, lse, h1, oself, dy1, src, x0, gain, dx1, wqkv, dg2, dg3,
-    keep0, came0, keep1, came1, enc0, enc2, wkv, oc, dyc, h2, dq0, dq1, fkeep, fsend, scale,
+    keep0, came0, keep1, came1, enc0, enc2, wkv, oc, dyc, h2, dq0, dq1, wpair, fkeep, fsend, scale,
 ):
     rows, width = do.shape
     nq = width // 256
@@ -1792,15 +1925,15 @@
             sds((count, 8, step_rows, wide), BF),
             sds((n, width), F32),
             sds((n, width), BF),
-            sds((8,) + fkeep.shape, BF),
+            sds((8, 2 * fkeep.shape[0], width), BF),
         ),
         in_specs=[VM, VM, SM, VM, any_spec, any_spec, VM]
         + [any_spec] * 3
         + [VM, any_spec, VM, any_spec]
         + [any_spec, VM, VM]
         + [any_spec] * 7
-        + [VM] * 6
-        + [any_spec],
+        + [VM] * 5
+        + [any_spec, VM, any_spec],
         out_specs=(VM,) * 4 + (any_spec, any_spec),
         scratch_shapes=[
             pltpu.VMEM((rows + 64, 3 * width), BF),
@@ -1835,9 +1968,9 @@
             pltpu.SemaphoreType.DMA((5,)),
             pltpu.SemaphoreType.DMA,
             pltpu.SemaphoreType.DMA,
-            pltpu.SemaphoreType.DMA((15,)),
-            pltpu.SemaphoreType.DMA((15,)),
-            pltpu.SemaphoreType.DMA((28,)),
+            pltpu.SemaphoreType.DMA((11,)),
+            pltpu.SemaphoreType.DMA((11,)),
+            pltpu.SemaphoreType.DMA((29,)),
         ],
         compiler_params=pltpu.CompilerParams(
             vmem_limit_bytes=63 << 20, collective_id=0, has_side_effects=True
@@ -1846,7 +1979,7 @@
         name="late",
     )(
         start, size, bucket, brow, proj, do, lse, h1, oself, dy1, src, x0, gain, dx1, wqkv, dg2, dg3,
-        keep0, came0, keep1, came1, enc0, enc2, wkv, oc, dyc, h2, dq0, dq1, fkeep, fsend,
+        keep0, came0, keep1, came1, enc0, enc2, wkv, oc, dyc, h2, dq0, dq1, wpair, fkeep, fsend,
     )
 
 
@@ -1964,56 +2097,35 @@
     k, v, kt, ocross, lse = kv_cross(
         me, lo, hi, cstart, csize, qc, (encodings, enc1, enc2, enc3), w_cross_kv
     )
-    f_keep, f_send, x2, dh3, g_low, oc, layer_out = ffn(
-        me, src, x1, ocross, g3, cotangent, w_cross_out, w_in, w_out
-    )
-    f_came = hop(f_send, core=1)
-    dx2, dyc, do, dgain3 = ffn_back(x2, dh3, g_low, g3, w_cross_out)
-    f_came = after(f_came, do)
-    half = width // 8
-    i_keep, i_send, o_keep, o_send = (
-        total(f_keep[n : n + 8, rows_], f_came[n : n + 8, rows_])
-        for rows_ in (slice(0, half), slice(half, 2 * half))
-        for n in (0, 8)
-    )
-    do, o_send, i_send = lax.optimization_barrier((do, o_send, i_send))
-    i_came, o_came = hop(i_send, yb=1), hop(o_send, xb=1)
+    o_keep, o_send, w_part, oc, layer_out, dx2, dyc, do, dgain3 = ffn(
+        src, x1, ocross, g3, cotangent, w_cross_out, w_in, w_out
+    )
+    do, o_send, w_part = lax.optimization_barrier((do, o_send, w_part))
+    o_came = hop(o_send, xb=1)
+    w_came = hop(w_part[2:], z1=1)
     dq0, keep0, send0 = cross_back(
         me, lo, hi, cstart, csize, qc, do, ocross, lse, k, v, kt, scale, 0, 2
     )
     came0 = hop(send0, core=1)
-    i_came, o_came, dq0 = lax.optimization_barrier((i_came, o_came, dq0))
-    i_q = [total(i_keep[2 * j : 2 * j + 2], i_came[2 * j : 2 * j + 2]) for j in range(4)]
+    o_came, w_came, dq0 = lax.optimization_barrier((o_came, w_came, dq0))
     o_q = [total(o_keep[2 * j : 2 * j + 2], o_came[2 * j : 2 * j + 2]) for j in range(4)]
-    z_send = jnp.concatenate([i_q[1], o_q[1]], axis=1)
-    do1, z_send, i_q[2], i_q[3], o_q[2], o_q[3] = lax.optimization_barrier(
-        (do, z_send, i_q[2], i_q[3], o_q[2], o_q[3])
-    )
-    z_came = hop(z_send, z1=1)
-    ix, ixz = hop(i_q[2], xb=1), hop(i_q[3], xb=1, z1=1)
-    oy, oyz = hop(o_q[2], yb=1), hop(o_q[3], yb=1, z1=1)
+    w_two = total(w_part[:2], w_came)
+    do1, o_q[1], o_q[2], o_q[3], w_two = lax.optimization_barrier((do, o_q[1], o_q[2], o_q[3], w_two))
+    oz, oy, oyz = hop(o_q[1], z1=1), hop(o_q[2], yb=1), hop(o_q[3], yb=1, z1=1)
+    w_came = hop(w_two, z2=1)
     dq1, keep1, send1 = cross_back(
         me, lo, hi, cstart, csize, qc, do1, ocross, lse, k, v, kt, scale, 2, 1
     )
     came1 = hop(send1, core=1)
-    z_came, ix, ixz, oy, oyz, dq1 = lax.optimization_barrier((z_came, ix, ixz, oy, oyz, dq1))
-
-    def line(n):
-        return jnp.concatenate(
-            [
-                total(i_q[0][n], z_came[n, :half], ix[n], ixz[n]),
-                total(o_q[0][n], z_came[n, half:], oy[n], oyz[n]),
-            ],
-            axis=0,
-        )
-
-    f_keep, f_send = line(0), line(1)
+    oz, oy, oyz, w_came, dq1 = lax.optimization_barrier((oz, oy, oyz, w_came, dq1))
+    w_pair = total(w_two, w_came[::-1])
+    f_keep, f_send = (total(o_q[0][n], oz[n], oy[n], oyz[n]) for n in range(2))
     dx1, dy1, dos, dgain2 = cross_in(dq0, dq1, x1, dx2, g2, w_cross_q, w_self_out)
     came0, came1, dos = lax.optimization_barrier((came0, came1, dos))
     d_dec_in, small, gathered, enc_own, enc_came, f_all = late(
         sstart, ssize, bucket_table, brow, proj, dos, lse_self, h1, oself, dy1, src, x0, g1, dx1, w_qkv,
         dgain2, dgain3, keep0, came0, keep1, came1, encodings, enc2, w_cross_kv, oc, dyc, h2, dq0, dq1,
-        f_keep, f_send, scale,
+        w_pair, f_keep, f_send, scale,
     )
     (
         o_win, o_wout, o_wco, o_wcq, o_wckv, o_wqkv, o_wso, d_encodings, g_self, g_cross, g_ffn, g_rel,

time: 353 us -> 330 us (0.935)
  Pallas kernels: 309 us -> 287 us
  other arithmetic: 13.9 us -> 8.67 us
  starting transfers between devices: 15.9 us -> 20.5 us
  local copies, waits for them, and re-layouts: 5.12 us -> 8.69 us
    pallas_call x6 -> x5, Pallas kernels: 79.6 us -> 65.3 us  [call(): pl.pallas_call(kernel, out_shape=out_shape, in_specs=in_specs, out_specs=...]
    pallas_call x2, Pallas kernels: 55.5 us -> 48.3 us  [cross_back(): pl.pallas_call(functools.partial(cross_back_kernel, scale=scale), grid=(1...]
    ppermute x13 -> x11, starting transfers between devices: 15.9 us -> 20.5 us  [hop(): return lax.ppermute(x, ('grp', 'blk'), pairs)]
    pallas_call x1, Pallas kernels: 125 us -> 121 us  [late(): pl.pallas_call(functools.partial(late_kernel, scale=scale), out_shape=(sd...]
    convert_element_type x2 -> x3, other arithmetic: 9.12 us -> 6 us  [total(): return out.astype(BF)]
  transfers between devices with their start and end apart: 13 -> 11, of which waited for: 1 -> 0; matrix products, arithmetic and copies ran while one was open for 2% -> 4% of each run, Pallas kernels for 27% -> 23%
where the time goes in v5:
time: 330 us; the launch traced here: 326 us
  Pallas kernels  287 us (87%)
  starting transfers between devices  20.5 us (6%)
  local copies, waits for them, and re-layouts  8.69 us (3%)
  other arithmetic  8.67 us (3%)
    pallas_call x1, Pallas kernels, late(): pl.pallas_call(functools.partial(late_kernel, scale=scale), out_shape=(sd...  121 us
    pallas_call x5, Pallas kernels, call(): pl.pallas_call(kernel, out_shape=out_shape, in_specs=in_specs, out_specs=...  65.3 us
    pallas_call x1, Pallas kernels, ffn(): pl.pallas_call(ffn_kernel, out_shape=(sds((8, half, width), BF), sds((8,...  51.7 us
    pallas_call x2, Pallas kernels, cross_back(): pl.pallas_call(functools.partial(cross_back_kernel, scale=scale), grid=(1...  48.3 us
    ppermute x11, starting transfers between devices, hop(): return lax.ppermute(x, ('grp', 'blk'), pairs)  20.5 us
  transfers between devices with their start and end apart: 11, of which 0 were waited for; matrix products, arithmetic and copies ran while one was open for 4% of the time, Pallas kernels for 23%

profile of v5, /device:TPU:0, one launch (start us, length us, event | category | flops | bytes accessed | tf_op | source)
XLA Modules:
  0.0 325.5 jit_solution(17203625990123416750)
XLA Ops:
  0.6 0.5 collective-permute-start.1
  1.2 2.6 collective-permute-start
  3.7 1.3 reshape.62.gain1_ref.gain_ref
  5.0 1.4 copy.32.rel_ref
  6.4 0.6 pad_add_fusion.me_ref
  7.0 0.0 copy-start.5
  7.0 0.0 copy-start.6
  7.0 14.8 %pre.1 = (s32[1,640]{1,0:T(1,128)}, s32[10,256]{1,0:T(8,128)}, s32[10,256]{1,0:T(8,128)}, s32[10,256]{1,0:T(8,128)}, s32[10,256]{1,0:T(8,128)}, /*index=5*/s32[1...) custom-call(s32[2]{0:T(128)} %pad_add_fusion.me_ref, ...), custom_call_target="tpu_custom_call" | custom-call | flops 3999999983616 | bytes 10561336 | tf_op jit(solution)/shard_map/pre/pallas_call | solution.py:895
  21.8 0.0 copy-done.5
  21.8 0.6 reshape.63.gain2_ref.gain_ref
  22.4 0.0 copy-done.6
  22.4 0.6 reshape.64.gain_ref
  23.0 0.0 collective-permute-done.rest_2_.enc2_any
  23.0 0.2 collective-permute-start.2
  23.1 5.5 %mid.1 = (f32[640,768]{1,0:T(8,128)}, bf16[640,768]{1,0:T(8,128)(2,1)}, bf16[640,768]{1,0:T(8,128)(2,1)}) custom-call(bf16[640,768]{1,0:T(8,128)(2,1)} %get-tuple-element.95.x0_ref.x0_any, bf16[640,768]{1,0:T(8,128)(2,1)} %get-tuple-element.97.oself_ref.oself_any, bf16[768,768]{1,0:T(8,128)(2,1)} %wso_ref.3, f32[1,768]{1,0:T(1,128)} %reshape.63.gain2_ref.gain_ref, ...), custom_call_target="tpu_custom_call" | custom-call | flops 799999983616 | bytes 8260608 | tf_op jit(solution)/shard_map/mid/pallas_call | solution.py:895
  28.6 0.0 collective-permute-done.1.rest_1_
  28.6 0.0 collective-permute-done.2.rest_3_
  28.6 29.9 %kv_cross.1 = (bf16[2048,768]{1,0:T(8,128)(2,1)}, bf16[2048,768]{1,0:T(8,128)(2,1)}, bf16[768,2048]{1,0:T(8,128)(2,1)}, f32[640,768]{1,0:T(8,128)}, f32[10,3,1,256]{3,2,1,0:T(1,128)}) custom-call(s32[2]{0:T(128)} %pad_add_fusion.me_ref, s32[10]{0:T(128)} %get-tuple-element.99.lo_ref, s32[10]{0:T(128)} %get-tuple-element.100.hi_ref, ...), custom_call_target="tpu_custom_call" | custom-call | flops 7999999967232 | bytes 17942616 | tf_op jit(solution)/shard_map/kv_cross/pallas_call | solution.py:895
  58.5 51.7 %ffn.1 = (bf16[8,96,768]{2,1,0:T(8,128)(2,1)}, bf16[8,96,768]{2,1,0:T(8,128)(2,1)}, bf16[4,96,768]{2,1,0:T(8,128)(2,1)}, bf16[640,768]{1,0:T(8,128)(2,1)}, bf16[...) custom-call(s32[1,640]{1,0:T(1,128)} %get-tuple-element.94.src_ref, ...), custom_call_target="tpu_custom_call" | custom-call | flops 9999999827968 | bytes 31457280 | tf_op jit(solution)/shard_map/ffn/pallas_call | solution.py:1253
  110.2 1.7 slice.55
  111.9 3.0 collective-permute-start.5
  114.9 1.0 collective-permute-start.4
  115.9 0.0 copy-start.4
  115.9 0.0 copy-start.1
  115.9 28.8 %cross_back.2 = (bf16[640,512]{1,0:T(8,128)(2,1)}, bf16[2,512,1024]{2,1,0:T(8,128)(2,1)}, bf16[2,512,1024]{2,1,0:T(8,128)(2,1)}) custom-call(s32[2]{0:T(128)} %pad_add_fusion.me_ref, s32[10]{0:T(128)} %get-tuple-element.99.lo_ref, s32[10]{0:T(128)} %get-tuple-element.100.hi_ref, s32[10,256]{1,0:T(8,128)} %get-tuple-element.101.start_ref, ...), custom_call_target="tpu_custom_call" | custom-call | flops 9999999827968 | bytes 31457280 | tf_op jit(solution)/shard_map/cross_back/pallas_call | solution.py:1419
  144.6 0.4 collective-permute-start.3
  145.0 0.0 collective-permute-done.5
  145.0 0.0 collective-permute-done.4
  145.0 0.0 copy-done.4
  145.0 1.7 add_convert_fusion.2
  146.8 0.0 copy-done.1
  146.8 2.4 add_convert_fusion
  149.2 3.4 %collective-permute-start.7 = (bf16[2,96,768]{2,1,0:T(8,128)(2,1)}, bf16[2,96,768]{2,1,0:T(8,128)(2,1)}, u32[]{:S(2)}, u32[]{:S(2)}) collective-permute-start(bf16[2,96,768]{2,1,0:T(8,128)(2,1)} %get-tuple-element.130), channel_id=1, source_target_pairs={{0,8},{1,9},{2,10},{3,11},{4,12},{5,13},{6,14},{7,15},{8,0},{9,1},... | collective-permute-start | bytes 884744 | tf_op jit(solution)/shard_map/ppermute | solution.py:2047
  152.6 2.0 collective-permute-start.8
  154.6 0.0 collective-permute-start.9
  154.6 6.9 %collective-permute-start.10 = (bf16[2,96,768]{2,1,0:T(8,128)(2,1)}, bf16[2,96,768]{2,1,0:T(8,128)(2,1)}, u32[]{:S(2)}, u32[]{:S(2)}) collective-permute-start(bf16[2,96,768]{2,1,0:T(8,128)(2,1)} %add_convert_fusion.2), channel_id=1, source_target_pairs={{0,16},{1,17},{2,18},{3,19},{4,20},{5,21},{6,22},{7,23},{8,24},{9,... | collective-permute-start | bytes 884744 | tf_op jit(solution)/shard_map/ppermute | solution.py:2047
  161.6 19.6 %cross_back.3 = (bf16[640,256]{1,0:T(8,128)(2,1)}, bf16[2,512,512]{2,1,0:T(8,128)(2,1)}, bf16[2,512,512]{2,1,0:T(8,128)(2,1)}) custom-call(s32[2]{0:T(128)} %pad_add_fusion.me_ref, s32[10]{0:T(128)} %get-tuple-element.99.lo_ref, s32[10]{0:T(128)} %get-tuple-element.100.hi_ref, s32[10,256]{1,0:T(8,128)} %get-tuple-element.101.start_ref, ...), custom_call_target="tpu_custom_call" | custom-call | flops 9999999827968 | bytes 31457280 | tf_op jit(solution)/shard_map/cross_back/pallas_call | solution.py:1419
  181.1 0.0 collective-permute-done.7
  181.1 0.5 collective-permute-start.6
  181.7 0.0 collective-permute-done.8
  181.7 0.0 collective-permute-done.9
  181.7 0.0 collective-permute-done.10
  181.7 0.0 copy-start.2
  181.7 7.0 %cross_in.1 = (f32[640,768]{1,0:T(8,128)}, bf16[640,768]{1,0:T(8,128)(2,1)}, bf16[640,768]{1,0:T(8,128)(2,1)}, f32[1,768]{1,0:T(1,128)}) custom-call(bf16[640,512]{1,0:T(8,128)(2,1)} %get-tuple-element.129.dq0_ref, bf16[640,256]{1,0:T(8,128)(2,1)} %get-tuple-element.135.dq1_ref, f32[640,768]{1,0:T(8,128)} %get-tuple-element.98.x1_ref, ...), custom_call_target="tpu_custom_call" | custom-call | flops 6000000106496 | bytes 11212800 | tf_op jit(solution)/shard_map/cross_in/pallas_call | solution.py:895
  188.7 1.8 add_convert_fusion.1.wpair_any
  190.5 0.0 copy-done.2
  190.5 2.1 fusion.1
  192.6 0.0 collective-permute-done.3.came0_any
  192.6 0.0 collective-permute-done.6.came1_any
  192.6 121.4 %late.1 = (f32[640,768]{1,0:T(8,128)}, f32[56,128]{1,0:T(8,128)}, bf16[24,8,16,384]{3,2,1,0:T(8,128)(2,1)}, f32[512,768]{1,0:T(8,128)}, bf16[512,768]{1,0:T(8,128)(2,1)}, /*index=5*/bf16[8,192,768]{2,1,0:T(8,128)(2,1)}) custom-call(s32[10,256]{1,0:T(8,128)} %get-tuple-element.108.start_ref, s32[10,256]{1,0:T(8,128)} %get-tuple-element.109.size_ref, ...), custom_call_target="tpu_custom_call" | custom-call | flops 9999999827968 | bytes 31457280 | tf_op jit(solution)/shard_map/late/pallas_call | solution.py:1920
  314.0 0.0 copy-start.3
  314.0 8.1 %last.1 = (f32[192,3072]{1,0:T(8,128)}, f32[768,768]{1,0:T(8,128)}, f32[192,768]{1,0:T(8,128)}, f32[192,768]{1,0:T(8,128)}, f32[192,1536]{1,0:T(8,128)}, /*index...) custom-call(s32[2]{0:T(128)} %pad_add_fusion.me_ref, ...), custom_call_target="tpu_custom_call" | custom-call | flops 799999983616 | bytes 18119304 | tf_op jit(solution)/shard_map/last/pallas_call | solution.py:895
  322.1 0.0 copy-start
  322.1 0.0 copy-done.3
  322.1 0.9 copy.35
  323.1 0.9 copy-done
  324.0 1.3 copy.36
Async XLA Ops:
  0.6 27.9 %collective-permute-start.1 = (bf16[512,768]{1,0:T(8,128)(2,1)}, bf16[512,768]{1,0:T(8,128)(2,1)}, u32[]{:S(2)}, u32[]{:S(2)}) collective-permute-start(bf16[512,768]{1,0:T(8,128)(2,1)} %enc0_any.1), channel_id=1, source_target_pairs={{0,1},{1,0},{2,3},{3,2},{4,5},{5,4},{6,7},{7,6},{8,9},{9,8},{10,11... | collective-permute-start | bytes 2359304 | tf_op jit(solution)/shard_map/ppermute | solution.py:2047
  1.2 21.8 %collective-permute-start = (bf16[512,768]{1,0:T(8,128)(2,1)}, bf16[512,768]{1,0:T(8,128)(2,1)}, u32[]{:S(2)}, u32[]{:S(2)}) collective-permute-start(bf16[512,768]{1,0:T(8,128)(2,1)} %enc0_any.1), channel_id=1, source_target_pairs={{0,2},{1,3},{2,0},{3,1},{4,6},{5,7},{6,4},{7,5},{8,10},{9,11},{10,... | collective-permute-start | bytes 2359304 | tf_op jit(solution)/shard_map/ppermute | solution.py:2047
  7.0 14.8 %copy-start.5 = (f32[768]{0:T(1024)S(1)}, f32[768]{0:T(1024)}, u32[]{:S(2)}) copy-start(f32[768]{0:T(1024)} %param.28) | copy-start | bytes 9220
  7.0 15.4 %copy-start.6 = (f32[768]{0:T(1024)S(1)}, f32[768]{0:T(1024)}, u32[]{:S(2)}) copy-start(f32[768]{0:T(1024)} %param.32) | copy-start | bytes 9220
  23.0 5.6 %collective-permute-start.2 = (bf16[512,768]{1,0:T(8,128)(2,1)}, bf16[512,768]{1,0:T(8,128)(2,1)}, u32[]{:S(2)}, u32[]{:S(2)}) collective-permute-start(bf16[512,768]{1,0:T(8,128)(2,1)} %collective-permute-done.rest_2_.enc2_any), channel_id=1, source_target_pairs={{0,1},{1,0},{2,3},{3,2},{4,5},{5,4},{6,7},{7,6},{8,9},{9,8},{10,11... | collective-permute-start | bytes 2359304 | tf_op jit(solution)/shard_map/ppermute | solution.py:2047
  111.9 33.1 %collective-permute-start.5 = (bf16[2,96,768]{2,1,0:T(8,128)(2,1)}, bf16[2,96,768]{2,1,0:T(8,128)(2,1)}, u32[]{:S(2)}, u32[]{:S(2)}) collective-permute-start(bf16[2,96,768]{2,1,0:T(8,128)(2,1)} %slice.55), channel_id=1, source_target_pairs={{0,8},{1,9},{2,10},{3,11},{4,12},{5,13},{6,14},{7,15},{8,0},{9,1},... | collective-permute-start | bytes 884744 | tf_op jit(solution)/shard_map/ppermute | solution.py:2047
  114.9 30.1 %collective-permute-start.4 = (bf16[8,96,768]{2,1,0:T(8,128)(2,1)}, bf16[8,96,768]{2,1,0:T(8,128)(2,1)}, u32[]{:S(2)}, u32[]{:S(2)}) collective-permute-start(bf16[8,96,768]{2,1,0:T(8,128)(2,1)} %get-tuple-element.122), channel_id=1, source_target_pairs={{0,2},{1,3},{2,0},{3,1},{4,6},{5,7},{6,4},{7,5},{8,10},{9,11},{10,... | collective-permute-start | bytes 3538952 | tf_op jit(solution)/shard_map/ppermute | solution.py:2047
  115.9 29.2 %copy-start.4 = (bf16[4,96,768]{2,1,0:T(8,128)(2,1)S(1)}, bf16[4,96,768]{2,1,0:T(8,128)(2,1)}, u32[]{:S(2)}) copy-start(bf16[4,96,768]{2,1,0:T(8,128)(2,1)} %get-tuple-element.123) | copy-start | bytes 1769476
  115.9 30.9 %copy-start.1 = (bf16[8,96,768]{2,1,0:T(8,128)(2,1)S(1)}, bf16[8,96,768]{2,1,0:T(8,128)(2,1)}, u32[]{:S(2)}) copy-start(bf16[8,96,768]{2,1,0:T(8,128)(2,1)} %get-tuple-element.121) | copy-start | bytes 3538948
  144.6 48.0 %collective-permute-start.3 = (bf16[2,512,1024]{2,1,0:T(8,128)(2,1)}, bf16[2,512,1024]{2,1,0:T(8,128)(2,1)}, u32[]{:S(2)}, u32[]{:S(2)}) collective-permute-start(bf16[2,512,1024]{2,1,0:T(8,128)(2,1)} %get-tuple-element.120), channel_id=1, source_target_pairs={{0,1},{1,0},{2,3},{3,2},{4,5},{5,4},{6,7},{7,6},{8,9},{9,8},{10,11... | collective-permute-start | bytes 6291464 | tf_op jit(solution)/shard_map/ppermute | solution.py:2047
  149.2 31.9 %collective-permute-start.7 = (bf16[2,96,768]{2,1,0:T(8,128)(2,1)}, bf16[2,96,768]{2,1,0:T(8,128)(2,1)}, u32[]{:S(2)}, u32[]{:S(2)}) collective-permute-start(bf16[2,96,768]{2,1,0:T(8,128)(2,1)} %get-tuple-element.130), channel_id=1, source_target_pairs={{0,8},{1,9},{2,10},{3,11},{4,12},{5,13},{6,14},{7,15},{8,0},{9,1},... | collective-permute-start | bytes 884744 | tf_op jit(solution)/shard_map/ppermute | solution.py:2047
  152.6 29.0 %collective-permute-start.8 = (bf16[2,96,768]{2,1,0:T(8,128)(2,1)}, bf16[2,96,768]{2,1,0:T(8,128)(2,1)}, u32[]{:S(2)}, u32[]{:S(2)}) collective-permute-start(bf16[2,96,768]{2,1,0:T(8,128)(2,1)} %get-tuple-element.131), channel_id=1, source_target_pairs={{0,4},{1,5},{2,6},{3,7},{4,0},{5,1},{6,2},{7,3},{8,12},{9,13},{10,... | collective-permute-start | bytes 884744 | tf_op jit(solution)/shard_map/ppermute | solution.py:2047
  154.6 27.0 %collective-permute-start.9 = (bf16[2,96,768]{2,1,0:T(8,128)(2,1)}, bf16[2,96,768]{2,1,0:T(8,128)(2,1)}, u32[]{:S(2)}, u32[]{:S(2)}) collective-permute-start(bf16[2,96,768]{2,1,0:T(8,128)(2,1)} %get-tuple-element.132), channel_id=1, source_target_pairs={{0,12},{1,13},{2,14},{3,15},{4,8},{5,9},{6,10},{7,11},{8,4},{9,5},... | collective-permute-start | bytes 884744 | tf_op jit(solution)/shard_map/ppermute | solution.py:2047
  154.6 27.0 %collective-permute-start.10 = (bf16[2,96,768]{2,1,0:T(8,128)(2,1)}, bf16[2,96,768]{2,1,0:T(8,128)(2,1)}, u32[]{:S(2)}, u32[]{:S(2)}) collective-permute-start(bf16[2,96,768]{2,1,0:T(8,128)(2,1)} %add_convert_fusion.2), channel_id=1, source_target_pairs={{0,16},{1,17},{2,18},{3,19},{4,20},{5,21},{6,22},{7,23},{8,24},{9,... | collective-permute-start | bytes 884744 | tf_op jit(solution)/shard_map/ppermute | solution.py:2047
  181.1 11.5 %collective-permute-start.6 = (bf16[2,512,512]{2,1,0:T(8,128)(2,1)}, bf16[2,512,512]{2,1,0:T(8,128)(2,1)}, u32[]{:S(2)}, u32[]{:S(2)}) collective-permute-start(bf16[2,512,512]{2,1,0:T(8,128)(2,1)} %get-tuple-element.128), channel_id=1, source_target_pairs={{0,1},{1,0},{2,3},{3,2},{4,5},{5,4},{6,7},{7,6},{8,9},{9,8},{10,11... | collective-permute-start | bytes 3145736 | tf_op jit(solution)/shard_map/ppermute | solution.py:2047
  181.7 8.8 %copy-start.2 = (bf16[2,96,768]{2,1,0:T(8,128)(2,1)S(1)}, bf16[2,96,768]{2,1,0:T(8,128)(2,1)}, u32[]{:S(2)}) copy-start(bf16[2,96,768]{2,1,0:T(8,128)(2,1)} %get-tuple-element.174) | copy-start | bytes 884740
  314.0 8.2 %copy-start.3 = (bf16[640,768]{1,0:T(8,128)(2,1)S(1)}, bf16[640,768]{1,0:T(8,128)(2,1)}, u32[]{:S(2)}) copy-start(bf16[640,768]{1,0:T(8,128)(2,1)} %get-tuple-element.194) | copy-start | bytes 2949124
  322.1 1.9 copy-start

commit v6 on v5

--- a/solution.py
+++ b/solution.py
@@ -828,7 +828,7 @@
 
     x0 = dot_tn(onehot_rows(src), dec_ref[...])
     x0_ref[...] = x0.astype(BF)
-    h1_ref[...] = (x0 * rms(x0) * gain1_ref[...]).astype(BF)
+    h1_ref[...] = (x0 * rms(x0) * gain1_ref[0:1, :]).astype(BF)
     for i in range(3):
         cs = slice(i * width, (i + 1) * width)
         proj_ref[:, cs] = dot(h1_ref[...], wqkv_ref[:, cs]).astype(BF)
@@ -871,7 +871,7 @@
 def mid_kernel(x0_ref, oself_ref, wso_ref, gain2_ref, wcq_ref, x1_ref, h2_ref, qc_ref, *, scale):
     x1 = x0_ref[...].astype(F32) + dot(oself_ref[...], wso_ref[...])
     x1_ref[...] = x1
-    h2_ref[...] = (x1 * rms(x1) * gain2_ref[...]).astype(BF)
+    h2_ref[...] = (x1 * rms(x1) * gain2_ref[1:2, :]).astype(BF)
     qc_ref[...] = dot(h2_ref[...], wcq_ref[...]).astype(BF) * jnp.asarray(scale, BF)
 
 
@@ -1089,6 +1089,7 @@
     okeep_ref,
     osend_ref,
     wi_ref,
+    wj_ref,
     oc_ref,
     out_ref,
     dx2_ref,
@@ -1170,7 +1171,16 @@
                 ik[f, 0:2] = add(ik[f, 0:2], iy[f])
             else:
                 rel = (g >> 1) ^ f
-                wi_ref[(rel & 1) * 2 + (rel >> 1)] = add(ik[f, 0], ix[f, 0])
+                whole = add(ik[f, 0], ix[f, 0])
+
+                @pl.when((rel & 1) == 0)
+                def _():
+                    wi_ref[rel >> 1] = whole
+
+                @pl.when((rel & 1) == 1)
+                def _():
+                    wj_ref[rel >> 1] = whole
+
             if k < 2:
                 remote(k + 1, f).start()
 
@@ -1179,7 +1189,7 @@
     oc_ref[...] = ocross_ref[...].astype(BF)
     x2 = x1_ref[...] + dot(oc_ref[...], wco_ref[...])
     dx2_ref[...] = x2
-    n = (x2 * rms(x2) * gain_ref[...]).astype(BF)
+    n = (x2 * rms(x2) * gain_ref[2:3, :]).astype(BF)
     h3[...] = n
     h3t[...] = n.T
     out_acc[...] = jnp.zeros_like(out_acc)
@@ -1197,8 +1207,8 @@
             dwi = dot(left, da).astype(BF)
             target = ss if r & 1 else ik
             for i in range(2):
-                y = (g ^ (2 * f + i)) & 1
-                target[f, y * 2 + (r >> 1)] = dwi[i * half : (i + 1) * half]
+                y, x = (g ^ (2 * f + i)) & 1, r >> 1
+                target[f, 2 * y + x] = dwi[i * half : (i + 1) * half]
         remote(0, f).start()
         out_acc[...] += dot(u, wout[part(f), :])
         event(0, f)
@@ -1232,7 +1242,7 @@
     x2 = dx2_ref[...]
     out = (x2 + out_acc[...]).astype(BF)
     out_ref[...] = dot(onehot_rows(src_ref[...]), out).astype(BF)
-    dx, dgain_ref[...] = rms_back(x2, rms(x2), gain_ref[...], dh[...])
+    dx, dgain_ref[...] = rms_back(x2, rms(x2), gain_ref[2:3, :], dh[...])
     dx2 = g_low[...].astype(F32) + dx
     dx2_ref[...] = dx2
     dyc_ref[...] = dx2.astype(BF)
@@ -1255,7 +1265,8 @@
         out_shape=(
             sds((8, half, width), BF),
             sds((8, half, width), BF),
-            sds((4, half, width), BF),
+            sds((2, half, width), BF),
+            sds((2, half, width), BF),
             sds((rows, width), BF),
             sds((rows, width), BF),
             sds((rows, width), F32),
@@ -1264,7 +1275,7 @@
             sds((1, width), F32),
         ),
         in_specs=[VM] * 6 + [any_spec] * 2,
-        out_specs=(VM,) * 9,
+        out_specs=(VM,) * 10,
         scratch_shapes=[
             pltpu.VMEM(win.shape, BF),
             pltpu.VMEM(wout.shape, BF),
@@ -1451,28 +1462,41 @@
 
 
 def cross_in_kernel(
-    dq0_ref, dq1_ref, x1_ref, dx2_ref, gain_ref, wcq_ref, wso_ref, dx1_ref, dy1_ref, dos_ref, dgain_ref
+    dq0_ref, dq1_ref, x1_ref, dx2_ref, gain_ref, wcq_ref, wso_ref, own_ref, oz_ref, oy_ref, oyz_ref, two_ref, came_ref,
+    dx1_ref, dy1_ref, dos_ref, dgain_ref, pair_ref, keep_ref, send_ref,
 ):
     x1 = x1_ref[...]
     cut = dq0_ref.shape[1]
     back = dot_nt(dq0_ref[...], wcq_ref[:, :cut]) + dot_nt(dq1_ref[...], wcq_ref[:, cut:])
-    dx, dgain_ref[...] = rms_back(x1, rms(x1), gain_ref[...], back)
+    dx, dgain_ref[...] = rms_back(x1, rms(x1), gain_ref[1:2, :], back)
     dx1 = dx2_ref[...] + dx
     dx1_ref[...] = dx1
     dy1_ref[...] = dx1.astype(BF)
     dos_ref[...] = dot_nt(dy1_ref[...], wso_ref[...]).astype(BF)
-
-
-def cross_in(dq0, dq1, x1, dx2, gain, wcq, wso):
+    for n, ref in ((0, keep_ref), (1, send_ref)):
+        parts = [r[n].astype(F32) for r in (own_ref, oz_ref, oy_ref, oyz_ref)]
+        ref[...] = (parts[0] + parts[1] + parts[2] + parts[3]).astype(BF)
+        pair_ref[n] = (two_ref[n].astype(F32) + came_ref[1 - n].astype(F32)).astype(BF)
+
+
+def cross_in(dq0, dq1, x1, dx2, gain, wcq, wso, own, oz, oy, oyz, two, came):
     rows, width = x1.shape
     return call(
         cross_in_kernel,
         "cross_in",
-        (sds((rows, width), F32), sds((rows, width), BF), sds((rows, width), BF), sds((1, width), F32)),
-        [VM] * 7,
-        (VM,) * 4,
+        (
+            sds((rows, width), F32),
+            sds((rows, width), BF),
+            sds((rows, width), BF),
+            sds((1, width), F32),
+            sds(two.shape, BF),
+            sds(two.shape[1:], BF),
+            sds(two.shape[1:], BF),
+        ),
+        [VM] * 13,
+        (VM,) * 7,
         [],
-        (dq0, dq1, x1, dx2, gain, wcq, wso),
+        (dq0, dq1, x1, dx2, gain, wcq, wso, own, oz, oy, oyz, two, came),
         us=60,
     )
 
@@ -1624,7 +1648,6 @@
     w_local = local(wpair_any, ffn_any.at[pl.ds(0, 2), w_at, :], 28)
     w_copies = [
         remote(wpair_any, ffn_any.at[pl.ds(2, 2), w_at, :], f_send.at[0], f_recv.at[0], 3),
-        remote(ffn_any.at[pl.ds(0, 4), w_at, :], ffn_any.at[pl.ds(4, 4), w_at, :], f_send.at[1], f_recv.at[1], 2),
     ]
     f_first = remote(fsend_any, frecv, f_send.at[2], f_recv.at[2], 4)
     f_second = remote(fown, ffn_any.at[1, o_at, :], f_send.at[3], f_recv.at[3], 4)
@@ -1636,6 +1659,11 @@
     w_copies[0].start()
     f_first.start()
     w_local.start()
+
+    def w_copy(i):
+        at = pl.ds(pl.multiple_of(i * step_rows, step_rows), step_rows)
+        src, dst = ffn_any.at[pl.ds(0, 4), at, :], ffn_any.at[pl.ds(4, 4), at, :]
+        return remote(src, dst, f_send.at[11 + i], f_recv.at[11 + i], 2)
 
     def f_copy(i):
         at = pl.ds(pl.multiple_of(f_half + i * step_rows, step_rows), step_rows)
@@ -1716,7 +1744,7 @@
     step(0)
     w_local.wait()
     w_copies[0].wait()
-    w_copies[1].start()
+    w_copy(0).start()
     held_in[0].wait()
     held_in[1].wait()
     left_t[...] = oself_ref[...].T
@@ -1733,6 +1761,7 @@
     f_local.start()
     f_second.start()
     step(1)
+    w_copy(1).start()
 
     held_in[2].wait()
     held_in[3].wait()
@@ -1748,6 +1777,7 @@
             spread(dot(part, both[:, i * width : (i + 1) * width]).astype(BF), r, 3 + i)
         start_core(3 + i)
         step(2 + i)
+        w_copy(2 + i).start()
     wkv_in.wait()
     enc_out[...] = dot_nt(both[n:, :], wbuf[:, : 2 * width]).astype(BF)
     own_ref[...] = dot_nt(both[:n, :], wbuf[:, : 2 * width])
@@ -1786,6 +1816,11 @@
     def tile_and_step(t, _):
         tile(t)
         step(t + 4)
+
+        @pl.when(t < f_slices - 4)
+        def _():
+            w_copy(t + 4).start()
+
         return 0
 
     lax.fori_loop(0, tiles - 2, tile_and_step, 0)
@@ -1798,45 +1833,6 @@
     f_second.wait()
     f_local.wait()
     f_third.start()
-    done = tiles + 2
-    projs[64:, width : 2 * width] = dka[64:, :].astype(BF)
-    projs[64:, 2 * width : 3 * width] = dva[64:, :].astype(BF)
-    held_in[5].wait()
-    left_t[...] = h1_ref[...].T
-    for i in range(3):
-        put(projs[64:, i * width : (i + 1) * width], 5 + i)
-        step(done)
-        step(done + 1)
-        done += 2
-
-    dgain[...] = jnp.zeros_like(dgain)
-    parts = 5
-    block = rows // parts
-    wqkv_in.wait()
-    held_in[6].wait()
-    held_in[7].wait()
-
-    def self_in(i, _):
-        at = pl.ds(pl.multiple_of(i * block, block), block)
-        held = pl.ds(pl.multiple_of(i * block + 64, 64), block)
-        x0 = x0_ref[at, :].astype(F32)
-        dx, part = rms_back(x0, rms(x0), gain_ref[...], dot_nt(projs[held, :], wbuf[...]))
-        dgain[...] += part
-        dx0 = dx1_ref[at, :] + dx
-        top = dx0.astype(BF)
-        both[at, :width] = top
-        both[at, width:] = (dx0 - top.astype(F32)).astype(BF)
-        step(done + i)
-
-        @pl.when(i == 2)
-        def _():
-            enc_copy.start()
-
-        return 0
-
-    lax.fori_loop(0, parts, self_in, 0)
-    done += parts
-
     dist = distances()
     for c in range(nq):
         cols = slice(c * 256, (c + 1) * 256)
@@ -1859,6 +1855,45 @@
     by_bucket = jnp.dot(hot, drow[...], preferred_element_type=F32, precision=lax.Precision.HIGHEST)
     small_ref[...] = jnp.zeros_like(small_ref)
     small_ref[24:, :] = jnp.dot(by_bucket, head, preferred_element_type=F32, precision=lax.Precision.HIGHEST)
+    done = tiles + 2
+    projs[64:, width : 2 * width] = dka[64:, :].astype(BF)
+    projs[64:, 2 * width : 3 * width] = dva[64:, :].astype(BF)
+    held_in[5].wait()
+    left_t[...] = h1_ref[...].T
+    for i in range(3):
+        put(projs[64:, i * width : (i + 1) * width], 5 + i)
+        step(done)
+        step(done + 1)
+        done += 2
+
+    dgain[...] = jnp.zeros_like(dgain)
+    parts = 5
+    block = rows // parts
+    wqkv_in.wait()
+    held_in[6].wait()
+    held_in[7].wait()
+
+    def self_in(i, _):
+        at = pl.ds(pl.multiple_of(i * block, block), block)
+        held = pl.ds(pl.multiple_of(i * block + 64, 64), block)
+        x0 = x0_ref[at, :].astype(F32)
+        dx, part = rms_back(x0, rms(x0), gain_ref[0:1, :], dot_nt(projs[held, :], wbuf[...]))
+        dgain[...] += part
+        dx0 = dx1_ref[at, :] + dx
+        top = dx0.astype(BF)
+        both[at, :width] = top
+        both[at, width:] = (dx0 - top.astype(F32)).astype(BF)
+        step(done + i)
+
+        @pl.when(i == 2)
+        def _():
+            enc_copy.start()
+
+        return 0
+
+    lax.fori_loop(0, parts, self_in, 0)
+    done += parts
+
     for i, ref in enumerate((dgain, dg2_ref, dg3_ref)):
         for k in range(6):
             small_ref[6 * i + k : 6 * i + k + 1, :] = ref[0:1, k * 128 : (k + 1) * 128]
@@ -1880,10 +1915,11 @@
     f_third.wait()
     f_copy(0).start()
     step(done)
-    hot_rows = onehot_rows(src_ref[...])
-    d_ref[...] = dot(hot_rows, both[:rows, :width]) + dot(hot_rows, both[:rows, width:])
+    chunk = rows // 5
     for k in range(5):
         small_sum(k)
+        hot_rows = (lax.broadcasted_iota(jnp.int32, (chunk, rows), 0) + k * chunk == src_ref[...]).astype(F32).astype(BF)
+        d_ref[k * chunk : (k + 1) * chunk, :] = dot(hot_rows, both[:rows, :width]) + dot(hot_rows, both[:rows, width:])
         for i in range(2):
             step(done + 1 + 2 * k + i)
         f_copy(1 + k).start()
@@ -1899,7 +1935,12 @@
         return 0
 
     lax.fori_loop(0, f_slices, f_end, 0)
-    w_copies[1].wait()
+
+    def w_end(i, _):
+        w_copy(i).wait()
+        return 0
+
+    lax.fori_loop(0, f_slices, w_end, 0)
     enc_copy.wait()
 
 
@@ -1968,8 +2009,8 @@
             pltpu.SemaphoreType.DMA((5,)),
             pltpu.SemaphoreType.DMA,
             pltpu.SemaphoreType.DMA,
-            pltpu.SemaphoreType.DMA((11,)),
-            pltpu.SemaphoreType.DMA((11,)),
+            pltpu.SemaphoreType.DMA((17,)),
+            pltpu.SemaphoreType.DMA((17,)),
             pltpu.SemaphoreType.DMA((29,)),
         ],
         compiler_params=pltpu.CompilerParams(
@@ -1984,8 +2025,27 @@
 
 
 def last_kernel(
-    me_ref, small_ref, ffn_ref, f_ref, own_ref, came_ref, win_ref, wout_ref, co_ref, cq_ref, ckv_ref, qkv_ref, so_ref, enc_ref, g1_ref, g2_ref, g3_ref, rel_ref
+    me_ref, small_ref, ffn_any, f_any, own_any, came_any,
+    win_any, wout_any, co_any, cq_any, ckv_any, qkv_any, so_any, enc_any,
+    g1_ref, g2_ref, g3_ref, rel_ref,
+    ffn_ref, f_ref, own_ref, came_ref, win_ref, wout_ref, co_ref, cq_ref, ckv_ref, qkv_ref, so_ref, enc_ref, sem,
 ):
+    def move(src, dst, k):
+        return pltpu.make_async_copy(src, dst, sem.at[k])
+
+    arriving = [
+        move(a, b, i)
+        for i, (a, b) in enumerate(
+            ((ffn_any, ffn_ref), (own_any, own_ref), (came_any, came_ref), (f_any, f_ref))
+        )
+    ]
+    outs = ((win_ref, win_any), (wout_ref, wout_any), (enc_ref, enc_any), (co_ref, co_any), (cq_ref, cq_any))
+    outs = outs + ((so_ref, so_any), (ckv_ref, ckv_any), (qkv_ref, qkv_any))
+    leaving = [move(a, b, 4 + i) for i, (a, b) in enumerate(outs)]
+    for c in arriving:
+        c.start()
+
+    arriving[0].wait()
     half = ffn_ref.shape[1] // 2
     for slot in range(8):
         s = me_ref[1] ^ ((slot >> 2) + (slot & 2) + 4 * (slot & 1))
@@ -1993,22 +2053,30 @@
         cols = pl.ds(pl.multiple_of((s >> 1) * 768, 768), 768)
         win_ref[rows, cols] = ffn_ref[slot, :half].astype(F32)
         wout_ref[pl.ds(pl.multiple_of(s * half, half), half), :] = ffn_ref[slot, half:].astype(F32)
+    leaving[0].start()
+    leaving[1].start()
+    arriving[1].wait()
+    arriving[2].wait()
+    enc_ref[...] = own_ref[...] + came_ref[...].astype(F32)
+    leaving[2].start()
+    arriving[3].wait()
     count, _, step_rows, wide = f_ref.shape
     width = 2 * wide
     places = (
-        (co_ref, 0), (cq_ref, 0), (so_ref, 0), (ckv_ref, 0), (ckv_ref, width),
-        (qkv_ref, 0), (qkv_ref, width), (qkv_ref, 2 * width),
+        (co_ref, 0, 3), (cq_ref, 0, 4), (so_ref, 0, 5), (ckv_ref, 0, None), (ckv_ref, width, 6),
+        (qkv_ref, 0, None), (qkv_ref, width, None), (qkv_ref, 2 * width, 7),
     )
     each = count // 8
     tall = each * step_rows
-    for slot in range(8):
-        s = me_ref[1] ^ ((slot >> 2) + (slot & 2) + 4 * (slot & 1))
-        for n, (out, col) in enumerate(places):
+    for n, (out, col, done) in enumerate(places):
+        for slot in range(8):
+            s = me_ref[1] ^ ((slot >> 2) + (slot & 2) + 4 * (slot & 1))
             for k in range(each):
                 at = pl.ds(pl.multiple_of((s >> 1) * tall + k * step_rows, step_rows), step_rows)
                 cols = pl.ds(pl.multiple_of(col + (s & 1) * wide, 128), wide)
                 out[at, cols] = f_ref[n * each + k, slot].astype(F32)
-    enc_ref[...] = own_ref[...] + came_ref[...].astype(F32)
+        if done is not None:
+            leaving[done].start()
     quarter = g1_ref.shape[1]
     for i, ref in enumerate((g1_ref, g2_ref, g3_ref)):
         whole = jnp.concatenate([small_ref[6 * i + k : 6 * i + k + 1, :] for k in range(6)], axis=1)
@@ -2020,21 +2088,26 @@
 
     part, heads = rel_ref.shape
     rel_ref[...] = small_ref[pl.ds(pl.multiple_of(24 + me_ref[0] * part, 8), part), :heads]
+    for c in leaving:
+        c.wait()
 
 
 def last(me, small, ffn, f, own, came, buckets, heads):
     width = own.shape[1]
     quarter = width // 4
     cols = lambda n: sds((quarter, n * width), F32)
+    any_spec = pl.BlockSpec(memory_space=pl.ANY)
+    big = (cols(4), sds((width, width), F32), cols(1), cols(1), cols(2), cols(3), cols(1), sds(own.shape, F32))
+    held = (ffn, f, own, came) + big
     return call(
         last_kernel,
         "last",
-        (cols(4), sds((width, width), F32), cols(1), cols(1), cols(2), cols(3), cols(1), sds(own.shape, F32))
+        big
         + (sds((1, quarter), F32),) * 3
         + (sds((buckets // 4, heads), F32),),
-        [SM] + [VM] * 5,
-        (VM,) * 12,
-        [],
+        [SM, VM] + [any_spec] * 4,
+        (any_spec,) * 8 + (VM,) * 4,
+        [pltpu.VMEM(a.shape, a.dtype) for a in held] + [pltpu.SemaphoreType.DMA((12,))],
         (me, small, ffn, f, own, came),
         us=8,
     )
@@ -2083,7 +2156,9 @@
     scale = 1.0 / math.sqrt(width // heads)
     me_b, me_g = lax.axis_index("blk"), lax.axis_index("grp")
     me = jnp.stack([me_b, me_g]).astype(jnp.int32)
-    g1, g2, g3 = (g.reshape(1, width) for g in (gain_self, gain_cross, gain_ffn))
+    row = lax.broadcasted_iota(jnp.int32, (3, width), 0)
+    gains = jnp.where(row == 0, gain_self[None], jnp.where(row == 1, gain_cross[None], gain_ffn[None]))
+    g1, g2, g3 = gains, gains, gains
 
     enc2 = hop(encodings, xb=1)
     enc1 = hop(encodings, core=1)
@@ -2097,19 +2172,19 @@
     k, v, kt, ocross, lse = kv_cross(
         me, lo, hi, cstart, csize, qc, (encodings, enc1, enc2, enc3), w_cross_kv
     )
-    o_keep, o_send, w_part, oc, layer_out, dx2, dyc, do, dgain3 = ffn(
+    o_keep, o_send, w_keep, w_send, oc, layer_out, dx2, dyc, do, dgain3 = ffn(
         src, x1, ocross, g3, cotangent, w_cross_out, w_in, w_out
     )
-    do, o_send, w_part = lax.optimization_barrier((do, o_send, w_part))
+    do, o_send, w_send = lax.optimization_barrier((do, o_send, w_send))
     o_came = hop(o_send, xb=1)
-    w_came = hop(w_part[2:], z1=1)
+    w_came = hop(w_send, z1=1)
     dq0, keep0, send0 = cross_back(
         me, lo, hi, cstart, csize, qc, do, ocross, lse, k, v, kt, scale, 0, 2
     )
     came0 = hop(send0, core=1)
     o_came, w_came, dq0 = lax.optimization_barrier((o_came, w_came, dq0))
     o_q = [total(o_keep[2 * j : 2 * j + 2], o_came[2 * j : 2 * j + 2]) for j in range(4)]
-    w_two = total(w_part[:2], w_came)
+    w_two = total(w_keep, w_came)
     do1, o_q[1], o_q[2], o_q[3], w_two = lax.optimization_barrier((do, o_q[1], o_q[2], o_q[3], w_two))
     oz, oy, oyz = hop(o_q[1], z1=1), hop(o_q[2], yb=1), hop(o_q[3], yb=1, z1=1)
     w_came = hop(w_two, z2=1)
@@ -2118,9 +2193,9 @@
     )
     came1 = hop(send1, core=1)
     oz, oy, oyz, w_came, dq1 = lax.optimization_barrier((oz, oy, oyz, w_came, dq1))
-    w_pair = total(w_two, w_came[::-1])
-    f_keep, f_send = (total(o_q[0][n], oz[n], oy[n], oyz[n]) for n in range(2))
-    dx1, dy1, dos, dgain2 = cross_in(dq0, dq1, x1, dx2, g2, w_cross_q, w_self_out)
+    dx1, dy1, dos, dgain2, w_pair, f_keep, f_send = cross_in(
+        dq0, dq1, x1, dx2, g2, w_cross_q, w_self_out, o_q[0], oz, oy, oyz, w_two, w_came
+    )
     came0, came1, dos = lax.optimization_barrier((came0, came1, dos))
     d_dec_in, small, gathered, enc_own, enc_came, f_all = late(
         sstart, ssize, bucket_table, brow, proj, dos, lse_self, h1, oself, dy1, src, x0, g1, dx1, w_qkv,

time: 330 us -> 323 us (0.979)
  local copies, waits for them, and re-layouts: 8.69 us -> 4.54 us
    pallas_call x1, Pallas kernels: 121 us -> 117 us  [late(): pl.pallas_call(functools.partial(late_kernel, scale=scale), out_shape=(sd...]
  transfers between devices with their start and end apart: 11 -> 11, of which waited for: 0 -> 1; matrix products, arithmetic and copies ran while one was open for 4% -> 2% of each run, Pallas kernels for 23% -> 25%
where the time goes in v6:
time: 323 us; the launch traced here: 321 us
  Pallas kernels  288 us (89%)
  starting transfers between devices  21.4 us (7%)
  other arithmetic  6.28 us (2%)
  local copies, waits for them, and re-layouts  4.54 us (1%)
    pallas_call x1, Pallas kernels, late(): pl.pallas_call(functools.partial(late_kernel, scale=scale), out_shape=(sd...  117 us
    pallas_call x5, Pallas kernels, call(): pl.pallas_call(kernel, out_shape=out_shape, in_specs=in_specs, out_specs=...  67.1 us
    pallas_call x1, Pallas kernels, ffn(): pl.pallas_call(ffn_kernel, out_shape=(sds((8, half, width), BF), sds((8,...  52.9 us
    pallas_call x2, Pallas kernels, cross_back(): pl.pallas_call(functools.partial(cross_back_kernel, scale=scale), grid=(1...  50.8 us
    ppermute x11, starting transfers between devices, hop(): return lax.ppermute(x, ('grp', 'blk'), pairs)  21.4 us
  transfers between devices with their start and end apart: 11, of which 1 were waited for; matrix products, arithmetic and copies ran while one was open for 2% of the time, Pallas kernels for 25%

profile of v6, /device:TPU:0, one launch (start us, length us, event | category | flops | bytes accessed | tf_op | source)
XLA Modules:
  0.0 321.5 jit_solution(13405103437627742583)
XLA Ops:
  0.6 0.5 collective-permute-start.1
  1.2 2.6 collective-permute-start
  3.7 1.4 copy.32.rel_ref
  5.1 0.7 pad_add_fusion.me_ref
  5.8 1.4 select_select_fusion.gain1_ref.gain2_ref.gain_ref
  7.2 14.8 %pre.1 = (s32[1,640]{1,0:T(1,128)}, s32[10,256]{1,0:T(8,128)}, s32[10,256]{1,0:T(8,128)}, s32[10,256]{1,0:T(8,128)}, s32[10,256]{1,0:T(8,128)}, /*index=5*/s32[1...) custom-call(s32[2]{0:T(128)} %pad_add_fusion.me_ref, ...), custom_call_target="tpu_custom_call" | custom-call | flops 3999999983616 | bytes 10567480 | tf_op jit(solution)/shard_map/pre/pallas_call | solution.py:895
  22.0 0.2 collective-permute-done.rest_2_.enc2_any
  22.2 0.0 collective-permute-start.2
  22.2 5.5 %mid.1 = (f32[640,768]{1,0:T(8,128)}, bf16[640,768]{1,0:T(8,128)(2,1)}, bf16[640,768]{1,0:T(8,128)(2,1)}) custom-call(bf16[640,768]{1,0:T(8,128)(2,1)} %get-tuple-element.99.x0_ref.x0_any, bf16[640,768]{1,0:T(8,128)(2,1)} %get-tuple-element.101.oself_ref.oself_any, bf16[768,768]{1,0:T(8,128)(2,1)} %wso_ref.3, ...), custom_call_target="tpu_custom_call" | custom-call | flops 799999983616 | bytes 8266752 | tf_op jit(solution)/shard_map/mid/pallas_call | solution.py:895
  27.7 0.0 collective-permute-done.1.rest_1_
  27.7 0.0 collective-permute-done.2.rest_3_
  27.7 31.5 %kv_cross.1 = (bf16[2048,768]{1,0:T(8,128)(2,1)}, bf16[2048,768]{1,0:T(8,128)(2,1)}, bf16[768,2048]{1,0:T(8,128)(2,1)}, f32[640,768]{1,0:T(8,128)}, f32[10,3,1,256]{3,2,1,0:T(1,128)}) custom-call(s32[2]{0:T(128)} %pad_add_fusion.me_ref, s32[10]{0:T(128)} %get-tuple-element.103.lo_ref, s32[10]{0:T(128)} %get-tuple-element.104.hi_ref, ...), custom_call_target="tpu_custom_call" | custom-call | flops 7999999967232 | bytes 17942616 | tf_op jit(solution)/shard_map/kv_cross/pallas_call | solution.py:895
  59.2 52.9 %ffn.1 = (bf16[8,96,768]{2,1,0:T(8,128)(2,1)}, bf16[8,96,768]{2,1,0:T(8,128)(2,1)}, bf16[2,96,768]{2,1,0:T(8,128)(2,1)}, bf16[2,96,768]{2,1,0:T(8,128)(2,1)}, bf...) custom-call(s32[1,640]{1,0:T(1,128)} %get-tuple-element.98.src_ref, ...), custom_call_target="tpu_custom_call" | custom-call | flops 9999999827968 | bytes 31457280 | tf_op jit(solution)/shard_map/ffn/pallas_call | solution.py:1263
  112.0 0.5 collective-permute-start.5
  112.6 1.5 collective-permute-start.4
  114.0 0.0 copy-start.1
  114.0 30.3 %cross_back.2 = (bf16[640,512]{1,0:T(8,128)(2,1)}, bf16[2,512,1024]{2,1,0:T(8,128)(2,1)}, bf16[2,512,1024]{2,1,0:T(8,128)(2,1)}) custom-call(s32[2]{0:T(128)} %pad_add_fusion.me_ref, s32[10]{0:T(128)} %get-tuple-element.103.lo_ref, s32[10]{0:T(128)} %get-tuple-element.104.hi_ref, s32[10,256]{1,0:T(8,128)} %get-tuple-element.105.start_ref, ...), custom_call_target="tpu_custom_call" | custom-call | flops 9999999827968 | bytes 31457280 | tf_op jit(solution)/shard_map/cross_back/pallas_call | solution.py:1430
  144.4 0.0 copy-start.3
  144.4 0.0 collective-permute-start.3
  144.4 0.0 collective-permute-done.5
  144.4 0.0 collective-permute-done.4
  144.4 0.0 copy-done.1
  144.4 2.5 add_convert_fusion
  146.9 0.0 copy-done.3
  146.9 1.8 add_convert_fusion.1.two_ref
  148.6 4.2 %collective-permute-start.7 = (bf16[2,96,768]{2,1,0:T(8,128)(2,1)}, bf16[2,96,768]{2,1,0:T(8,128)(2,1)}, u32[]{:S(2)}, u32[]{:S(2)}) collective-permute-start(bf16[2,96,768]{2,1,0:T(8,128)(2,1)} %get-tuple-element.135), channel_id=1, source_target_pairs={{0,8},{1,9},{2,10},{3,11},{4,12},{5,13},{6,14},{7,15},{8,0},{9,1},... | collective-permute-start | bytes 884744 | tf_op jit(solution)/shard_map/ppermute | solution.py:2120
  152.8 1.1 collective-permute-start.8
  153.9 1.5 collective-permute-start.9
  155.4 9.6 %collective-permute-start.10 = (bf16[2,96,768]{2,1,0:T(8,128)(2,1)}, bf16[2,96,768]{2,1,0:T(8,128)(2,1)}, u32[]{:S(2)}, u32[]{:S(2)}) collective-permute-start(bf16[2,96,768]{2,1,0:T(8,128)(2,1)} %add_convert_fusion.1.two_ref), channel_id=1, source_target_pairs={{0,16},{1,17},{2,18},{3,19},{4,20},{5,21},{6,22},{7,23},{8,24},{9,... | collective-permute-start | bytes 884744 | tf_op jit(solution)/shard_map/ppermute | solution.py:2120
  164.9 20.5 %cross_back.3 = (bf16[640,256]{1,0:T(8,128)(2,1)}, bf16[2,512,512]{2,1,0:T(8,128)(2,1)}, bf16[2,512,512]{2,1,0:T(8,128)(2,1)}) custom-call(s32[2]{0:T(128)} %pad_add_fusion.me_ref, s32[10]{0:T(128)} %get-tuple-element.103.lo_ref, s32[10]{0:T(128)} %get-tuple-element.104.hi_ref, s32[10,256]{1,0:T(8,128)} %get-tuple-element.105.start_ref, ...), custom_call_target="tpu_custom_call" | custom-call | flops 9999999827968 | bytes 31457280 | tf_op jit(solution)/shard_map/cross_back/pallas_call | solution.py:1430
  185.4 0.0 collective-permute-done.7.oz_ref
  185.4 0.0 collective-permute-start.6
  185.4 0.0 collective-permute-done.8.oy_ref
  185.5 0.0 collective-permute-done.9.oyz_ref
  185.5 0.0 collective-permute-done.10.came_ref
  185.5 7.7 %cross_in.1 = (f32[640,768]{1,0:T(8,128)}, bf16[640,768]{1,0:T(8,128)(2,1)}, bf16[640,768]{1,0:T(8,128)(2,1)}, f32[1,768]{1,0:T(1,128)}, bf16[2,96,768]{2,1,0:T(...) custom-call(bf16[640,512]{1,0:T(8,128)(2,1)} %get-tuple-element.134.dq0_ref, ...), custom_call_target="tpu_custom_call" | custom-call | flops 6000000106496 | bytes 13578240 | tf_op jit(solution)/shard_map/cross_in/pallas_call | solution.py:895
  193.2 0.0 collective-permute-done.3.came0_any
  193.2 0.0 collective-permute-done.6.came1_any
  193.2 117.2 %late.1 = (f32[640,768]{1,0:T(8,128)}, f32[56,128]{1,0:T(8,128)}, bf16[24,8,16,384]{3,2,1,0:T(8,128)(2,1)}, f32[512,768]{1,0:T(8,128)}, bf16[512,768]{1,0:T(8,128)(2,1)}, /*index=5*/bf16[8,192,768]{2,1,0:T(8,128)(2,1)}) custom-call(s32[10,256]{1,0:T(8,128)} %get-tuple-element.112.start_ref, s32[10,256]{1,0:T(8,128)} %get-tuple-element.113.size_ref, ...), custom_call_target="tpu_custom_call" | custom-call | flops 9999999827968 | bytes 31457280 | tf_op jit(solution)/shard_map/late/pallas_call | solution.py:1961
  310.4 0.0 copy-start.2
  310.5 7.6 %last.1 = (f32[192,3072]{1,0:T(8,128)}, f32[768,768]{1,0:T(8,128)}, f32[192,768]{1,0:T(8,128)}, f32[192,768]{1,0:T(8,128)}, f32[192,1536]{1,0:T(8,128)}, /*index...) custom-call(s32[2]{0:T(128)} %pad_add_fusion.me_ref, ...), custom_call_target="tpu_custom_call" | custom-call | flops 799999983616 | bytes 18119304 | tf_op jit(solution)/shard_map/last/pallas_call | solution.py:895
  318.1 0.0 copy-start
  318.1 0.0 copy-done.2
  318.1 0.9 copy.35
  319.1 0.9 copy-done
  320.0 1.3 copy.36
  (1 shorter events, 0.0 us)
Async XLA Ops:
  0.6 27.0 %collective-permute-start.1 = (bf16[512,768]{1,0:T(8,128)(2,1)}, bf16[512,768]{1,0:T(8,128)(2,1)}, u32[]{:S(2)}, u32[]{:S(2)}) collective-permute-start(bf16[512,768]{1,0:T(8,128)(2,1)} %enc0_any.1), channel_id=1, source_target_pairs={{0,1},{1,0},{2,3},{3,2},{4,5},{5,4},{6,7},{7,6},{8,9},{9,8},{10,11... | collective-permute-start | bytes 2359304 | tf_op jit(solution)/shard_map/ppermute | solution.py:2120
  1.2 21.0 %collective-permute-start = (bf16[512,768]{1,0:T(8,128)(2,1)}, bf16[512,768]{1,0:T(8,128)(2,1)}, u32[]{:S(2)}, u32[]{:S(2)}) collective-permute-start(bf16[512,768]{1,0:T(8,128)(2,1)} %enc0_any.1), channel_id=1, source_target_pairs={{0,2},{1,3},{2,0},{3,1},{4,6},{5,7},{6,4},{7,5},{8,10},{9,11},{10,... | collective-permute-start | bytes 2359304 | tf_op jit(solution)/shard_map/ppermute | solution.py:2120
  22.2 5.5 %collective-permute-start.2 = (bf16[512,768]{1,0:T(8,128)(2,1)}, bf16[512,768]{1,0:T(8,128)(2,1)}, u32[]{:S(2)}, u32[]{:S(2)}) collective-permute-start(bf16[512,768]{1,0:T(8,128)(2,1)} %collective-permute-done.rest_2_.enc2_any), channel_id=1, source_target_pairs={{0,1},{1,0},{2,3},{3,2},{4,5},{5,4},{6,7},{7,6},{8,9},{9,8},{10,11... | collective-permute-start | bytes 2359304 | tf_op jit(solution)/shard_map/ppermute | solution.py:2120
  112.0 32.3 %collective-permute-start.5 = (bf16[2,96,768]{2,1,0:T(8,128)(2,1)}, bf16[2,96,768]{2,1,0:T(8,128)(2,1)}, u32[]{:S(2)}, u32[]{:S(2)}) collective-permute-start(bf16[2,96,768]{2,1,0:T(8,128)(2,1)} %get-tuple-element.127), channel_id=1, source_target_pairs={{0,8},{1,9},{2,10},{3,11},{4,12},{5,13},{6,14},{7,15},{8,0},{9,1},... | collective-permute-start | bytes 884744 | tf_op jit(solution)/shard_map/ppermute | solution.py:2120
  112.6 31.8 %collective-permute-start.4 = (bf16[8,96,768]{2,1,0:T(8,128)(2,1)}, bf16[8,96,768]{2,1,0:T(8,128)(2,1)}, u32[]{:S(2)}, u32[]{:S(2)}) collective-permute-start(bf16[8,96,768]{2,1,0:T(8,128)(2,1)} %get-tuple-element.126), channel_id=1, source_target_pairs={{0,2},{1,3},{2,0},{3,1},{4,6},{5,7},{6,4},{7,5},{8,10},{9,11},{10,... | collective-permute-start | bytes 3538952 | tf_op jit(solution)/shard_map/ppermute | solution.py:2120
  114.0 30.4 %copy-start.1 = (bf16[8,96,768]{2,1,0:T(8,128)(2,1)S(1)}, bf16[8,96,768]{2,1,0:T(8,128)(2,1)}, u32[]{:S(2)}) copy-start(bf16[8,96,768]{2,1,0:T(8,128)(2,1)} %get-tuple-element.125) | copy-start | bytes 3538948
  144.4 2.5 copy-start.3
  144.4 48.8 %collective-permute-start.3 = (bf16[2,512,1024]{2,1,0:T(8,128)(2,1)}, bf16[2,512,1024]{2,1,0:T(8,128)(2,1)}, u32[]{:S(2)}, u32[]{:S(2)}) collective-permute-start(bf16[2,512,1024]{2,1,0:T(8,128)(2,1)} %get-tuple-element.124), channel_id=1, source_target_pairs={{0,1},{1,0},{2,3},{3,2},{4,5},{5,4},{6,7},{7,6},{8,9},{9,8},{10,11... | collective-permute-start | bytes 6291464 | tf_op jit(solution)/shard_map/ppermute | solution.py:2120
  148.6 36.8 %collective-permute-start.7 = (bf16[2,96,768]{2,1,0:T(8,128)(2,1)}, bf16[2,96,768]{2,1,0:T(8,128)(2,1)}, u32[]{:S(2)}, u32[]{:S(2)}) collective-permute-start(bf16[2,96,768]{2,1,0:T(8,128)(2,1)} %get-tuple-element.135), channel_id=1, source_target_pairs={{0,8},{1,9},{2,10},{3,11},{4,12},{5,13},{6,14},{7,15},{8,0},{9,1},... | collective-permute-start | bytes 884744 | tf_op jit(solution)/shard_map/ppermute | solution.py:2120
  152.8 32.6 %collective-permute-start.8 = (bf16[2,96,768]{2,1,0:T(8,128)(2,1)}, bf16[2,96,768]{2,1,0:T(8,128)(2,1)}, u32[]{:S(2)}, u32[]{:S(2)}) collective-permute-start(bf16[2,96,768]{2,1,0:T(8,128)(2,1)} %get-tuple-element.136), channel_id=1, source_target_pairs={{0,4},{1,5},{2,6},{3,7},{4,0},{5,1},{6,2},{7,3},{8,12},{9,13},{10,... | collective-permute-start | bytes 884744 | tf_op jit(solution)/shard_map/ppermute | solution.py:2120
  153.9 31.5 %collective-permute-start.9 = (bf16[2,96,768]{2,1,0:T(8,128)(2,1)}, bf16[2,96,768]{2,1,0:T(8,128)(2,1)}, u32[]{:S(2)}, u32[]{:S(2)}) collective-permute-start(bf16[2,96,768]{2,1,0:T(8,128)(2,1)} %get-tuple-element.137), channel_id=1, source_target_pairs={{0,12},{1,13},{2,14},{3,15},{4,8},{5,9},{6,10},{7,11},{8,4},{9,5},... | collective-permute-start | bytes 884744 | tf_op jit(solution)/shard_map/ppermute | solution.py:2120
  155.4 30.1 %collective-permute-start.10 = (bf16[2,96,768]{2,1,0:T(8,128)(2,1)}, bf16[2,96,768]{2,1,0:T(8,128)(2,1)}, u32[]{:S(2)}, u32[]{:S(2)}) collective-permute-start(bf16[2,96,768]{2,1,0:T(8,128)(2,1)} %add_convert_fusion.1.two_ref), channel_id=1, source_target_pairs={{0,16},{1,17},{2,18},{3,19},{4,20},{5,21},{6,22},{7,23},{8,24},{9,... | collective-permute-start | bytes 884744 | tf_op jit(solution)/shard_map/ppermute | solution.py:2120
  185.4 7.7 %collective-permute-start.6 = (bf16[2,512,512]{2,1,0:T(8,128)(2,1)}, bf16[2,512,512]{2,1,0:T(8,128)(2,1)}, u32[]{:S(2)}, u32[]{:S(2)}) collective-permute-start(bf16[2,512,512]{2,1,0:T(8,128)(2,1)} %get-tuple-element.133), channel_id=1, source_target_pairs={{0,1},{1,0},{2,3},{3,2},{4,5},{5,4},{6,7},{7,6},{8,9},{9,8},{10,11... | collective-permute-start | bytes 3145736 | tf_op jit(solution)/shard_map/ppermute | solution.py:2120
  310.4 7.7 %copy-start.2 = (bf16[640,768]{1,0:T(8,128)(2,1)S(1)}, bf16[640,768]{1,0:T(8,128)(2,1)}, u32[]{:S(2)}) copy-start(bf16[640,768]{1,0:T(8,128)(2,1)} %get-tuple-element.202) | copy-start | bytes 2949124
  318.1 1.9 copy-start

commit v7 on v6

--- a/solution.py
+++ b/solution.py
@@ -2120,15 +2120,21 @@
     return lax.ppermute(x, ("grp", "blk"), pairs)
 
 
-def total(*parts):
-    out = parts[0].astype(F32)
-    for p in parts[1:]:
-        out = out + p.astype(F32)
-    return out.astype(BF)
-
-
 def after(x, *deps):
     return lax.optimization_barrier((x,) + deps)[0]
+
+
+def split_kernel(okeep_ref, ocame_ref, wkeep_ref, wcame_ref, q0_ref, q1_ref, q2_ref, q3_ref, two_ref):
+    for j, ref in enumerate((q0_ref, q1_ref, q2_ref, q3_ref)):
+        ref[...] = (okeep_ref[2 * j : 2 * j + 2].astype(F32) + ocame_ref[2 * j : 2 * j + 2].astype(F32)).astype(BF)
+    two_ref[...] = (wkeep_ref[...].astype(F32) + wcame_ref[...].astype(F32)).astype(BF)
+
+
+def split(okeep, ocame, wkeep, wcame):
+    part = sds(wkeep.shape, BF)
+    return call(
+        split_kernel, "split", (part,) * 5, [VM] * 4, (VM,) * 5, [], (okeep, ocame, wkeep, wcame), us=4
+    )
 
 
 def fused_body(
@@ -2183,8 +2189,7 @@
     )
     came0 = hop(send0, core=1)
     o_came, w_came, dq0 = lax.optimization_barrier((o_came, w_came, dq0))
-    o_q = [total(o_keep[2 * j : 2 * j + 2], o_came[2 * j : 2 * j + 2]) for j in range(4)]
-    w_two = total(w_keep, w_came)
+    *o_q, w_two = split(o_keep, o_came, w_keep, w_came)
     do1, o_q[1], o_q[2], o_q[3], w_two = lax.optimization_barrier((do, o_q[1], o_q[2], o_q[3], w_two))
     oz, oy, oyz = hop(o_q[1], z1=1), hop(o_q[2], yb=1), hop(o_q[3], yb=1, z1=1)
     w_came = hop(w_two, z2=1)

time: 323 us -> 320 us (level); the launches traced: 321 us -> 315 us
  starting transfers between devices: 21.4 us -> 14.4 us
  other arithmetic: 6.28 us -> 1.99 us
  Pallas kernels: 288 us -> 292 us
    ppermute x11, starting transfers between devices: 21.4 us -> 14.4 us  [hop(): return lax.ppermute(x, ('grp', 'blk'), pairs)]
    pallas_call x5 -> x6, Pallas kernels: 67.1 us -> 72.8 us  [call(): pl.pallas_call(kernel, out_shape=out_shape, in_specs=in_specs, out_specs=...]
    convert_element_type x2 -> x0, other arithmetic: 4.22 us -> none  [total(): return out.astype(BF)]
    pallas_call x2, Pallas kernels: 50.8 us -> 55 us  [cross_back(): pl.pallas_call(functools.partial(cross_back_kernel, scale=scale), grid=(1...]
    pallas_call x1, Pallas kernels: 117 us -> 113 us  [late(): pl.pallas_call(functools.partial(late_kernel, scale=scale), out_shape=(sd...]
  transfers between devices with their start and end apart: 11 -> 11, of which waited for: 1 -> 1; matrix products, arithmetic and copies ran while one was open for 2% -> 1% of each run, Pallas kernels for 25% -> 27%
where the time goes in v7:
time: 320 us; the launch traced here: 315 us
  Pallas kernels  292 us (91%)
  starting transfers between devices  14.4 us (4%)
  local copies, waits for them, and re-layouts  4.54 us (1%)
    pallas_call x1, Pallas kernels, late(): pl.pallas_call(functools.partial(late_kernel, scale=scale), out_shape=(sd...  113 us
    pallas_call x6, Pallas kernels, call(): pl.pallas_call(kernel, out_shape=out_shape, in_specs=in_specs, out_specs=...  72.8 us
    pallas_call x2, Pallas kernels, cross_back(): pl.pallas_call(functools.partial(cross_back_kernel, scale=scale), grid=(1...  55 us
    pallas_call x1, Pallas kernels, ffn(): pl.pallas_call(ffn_kernel, out_shape=(sds((8, half, width), BF), sds((8,...  51.2 us
    ppermute x11, starting transfers between devices, hop(): return lax.ppermute(x, ('grp', 'blk'), pairs)  14.4 us
  transfers between devices with their start and end apart: 11, of which 1 were waited for; matrix products, arithmetic and copies ran while one was open for 1% of the time, Pallas kernels for 27%

profile of v7, /device:TPU:0, one launch (start us, length us, event | category | flops | bytes accessed | tf_op | source)
XLA Modules:
  0.0 314.6 jit_solution(11007492401921713970)
XLA Ops:
  0.6 0.5 collective-permute-start.1
  1.2 2.6 collective-permute-start
  3.7 1.4 copy.32.rel_ref
  5.1 0.6 pad_add_fusion.me_ref
  5.7 1.4 select_select_fusion.gain1_ref.gain2_ref.gain_ref
  7.1 14.8 %pre.1 = (s32[1,640]{1,0:T(1,128)}, s32[10,256]{1,0:T(8,128)}, s32[10,256]{1,0:T(8,128)}, s32[10,256]{1,0:T(8,128)}, s32[10,256]{1,0:T(8,128)}, /*index=5*/s32[1...) custom-call(s32[2]{0:T(128)} %pad_add_fusion.me_ref, ...), custom_call_target="tpu_custom_call" | custom-call | flops 3999999983616 | bytes 10567480 | tf_op jit(solution)/shard_map/pre/pallas_call | solution.py:895
  21.9 0.3 collective-permute-done.rest_2_.enc2_any
  22.2 0.0 collective-permute-start.2
  22.2 5.5 %mid.1 = (f32[640,768]{1,0:T(8,128)}, bf16[640,768]{1,0:T(8,128)(2,1)}, bf16[640,768]{1,0:T(8,128)(2,1)}) custom-call(bf16[640,768]{1,0:T(8,128)(2,1)} %get-tuple-element.104.x0_ref.x0_any, bf16[640,768]{1,0:T(8,128)(2,1)} %get-tuple-element.106.oself_ref.oself_any, bf16[768,768]{1,0:T(8,128)(2,1)} %wso_ref.3, ...), custom_call_target="tpu_custom_call" | custom-call | flops 799999983616 | bytes 8266752 | tf_op jit(solution)/shard_map/mid/pallas_call | solution.py:895
  27.6 0.0 collective-permute-done.1.rest_1_
  27.7 0.0 collective-permute-done.2.rest_3_
  27.7 34.3 %kv_cross.1 = (bf16[2048,768]{1,0:T(8,128)(2,1)}, bf16[2048,768]{1,0:T(8,128)(2,1)}, bf16[768,2048]{1,0:T(8,128)(2,1)}, f32[640,768]{1,0:T(8,128)}, f32[10,3,1,256]{3,2,1,0:T(1,128)}) custom-call(s32[2]{0:T(128)} %pad_add_fusion.me_ref, s32[10]{0:T(128)} %get-tuple-element.108.lo_ref, s32[10]{0:T(128)} %get-tuple-element.109.hi_ref, ...), custom_call_target="tpu_custom_call" | custom-call | flops 7999999967232 | bytes 17942616 | tf_op jit(solution)/shard_map/kv_cross/pallas_call | solution.py:895
  61.9 51.2 %ffn.1 = (bf16[8,96,768]{2,1,0:T(8,128)(2,1)}, bf16[8,96,768]{2,1,0:T(8,128)(2,1)}, bf16[2,96,768]{2,1,0:T(8,128)(2,1)}, bf16[2,96,768]{2,1,0:T(8,128)(2,1)}, bf...) custom-call(s32[1,640]{1,0:T(1,128)} %get-tuple-element.103.src_ref,, ...), custom_call_target="tpu_custom_call" | custom-call | flops 9999999827968 | bytes 31457280 | tf_op jit(solution)/shard_map/ffn/pallas_call | solution.py:1263
  113.1 1.1 collective-permute-start.5
  114.2 1.5 collective-permute-start.4
  115.8 33.0 %cross_back.2 = (bf16[640,512]{1,0:T(8,128)(2,1)}, bf16[2,512,1024]{2,1,0:T(8,128)(2,1)}, bf16[2,512,1024]{2,1,0:T(8,128)(2,1)}) custom-call(s32[2]{0:T(128)} %pad_add_fusion.me_ref, s32[10]{0:T(128)} %get-tuple-element.108.lo_ref, s32[10]{0:T(128)} %get-tuple-element.109.hi_ref, s32[10,256]{1,0:T(8,128)} %get-tuple-element.110.start_ref, ...), custom_call_target="tpu_custom_call" | custom-call | flops 9999999827968 | bytes 31457280 | tf_op jit(solution)/shard_map/cross_back/pallas_call | solution.py:1430
  148.8 0.0 collective-permute-start.3
  148.8 0.0 collective-permute-done.5.wcame_ref
  148.8 0.0 collective-permute-done.4.ocame_ref
  148.8 2.9 split.1
  151.7 0.9 collective-permute-start.7
  152.7 3.3 %collective-permute-start.8 = (bf16[2,96,768]{2,1,0:T(8,128)(2,1)}, bf16[2,96,768]{2,1,0:T(8,128)(2,1)}, u32[]{:S(2)}, u32[]{:S(2)}) collective-permute-start(bf16[2,96,768]{2,1,0:T(8,128)(2,1)} %get-tuple-element.145), channel_id=1, source_target_pairs={{0,4},{1,5},{2,6},{3,7},{4,0},{5,1},{6,2},{7,3},{8,12},{9,13},{10,... | collective-permute-start | bytes 884744 | tf_op jit(solution)/shard_map/ppermute | solution.py:2120
  156.0 0.1 collective-permute-start.9
  156.1 4.3 %collective-permute-start.10 = (bf16[2,96,768]{2,1,0:T(8,128)(2,1)}, bf16[2,96,768]{2,1,0:T(8,128)(2,1)}, u32[]{:S(2)}, u32[]{:S(2)}) collective-permute-start(bf16[2,96,768]{2,1,0:T(8,128)(2,1)} %get-tuple-element.147.two_ref), channel_id=1, source_target_pairs={{0,16},{1,17},{2,18},{3,19},{4,20},{5,21},{6,22},{7,23},{8,24},{9,... | collective-permute-start | bytes 884744 | tf_op jit(solution)/shard_map/ppermute | solution.py:2120
  160.4 21.9 %cross_back.3 = (bf16[640,256]{1,0:T(8,128)(2,1)}, bf16[2,512,512]{2,1,0:T(8,128)(2,1)}, bf16[2,512,512]{2,1,0:T(8,128)(2,1)}) custom-call(s32[2]{0:T(128)} %pad_add_fusion.me_ref, s32[10]{0:T(128)} %get-tuple-element.108.lo_ref, s32[10]{0:T(128)} %get-tuple-element.109.hi_ref, s32[10,256]{1,0:T(8,128)} %get-tuple-element.110.start_ref, ...), custom_call_target="tpu_custom_call" | custom-call | flops 9999999827968 | bytes 31457280 | tf_op jit(solution)/shard_map/cross_back/pallas_call | solution.py:1430
  182.4 0.0 collective-permute-done.7.oz_ref
  182.4 0.0 collective-permute-start.6
  182.4 0.0 collective-permute-done.8.oy_ref
  182.4 0.0 collective-permute-done.9.oyz_ref
  182.4 0.0 collective-permute-done.10.came_ref
  182.4 7.7 %cross_in.1 = (f32[640,768]{1,0:T(8,128)}, bf16[640,768]{1,0:T(8,128)(2,1)}, bf16[640,768]{1,0:T(8,128)(2,1)}, f32[1,768]{1,0:T(1,128)}, bf16[2,96,768]{2,1,0:T(...) custom-call(bf16[640,512]{1,0:T(8,128)(2,1)} %get-tuple-element.143.dq0_ref, ...), custom_call_target="tpu_custom_call" | custom-call | flops 6000000106496 | bytes 13578240 | tf_op jit(solution)/shard_map/cross_in/pallas_call | solution.py:895
  190.1 0.0 collective-permute-done.3.came0_any
  190.1 0.0 collective-permute-done.6.came1_any
  190.1 113.5 %late.1 = (f32[640,768]{1,0:T(8,128)}, f32[56,128]{1,0:T(8,128)}, bf16[24,8,16,384]{3,2,1,0:T(8,128)(2,1)}, f32[512,768]{1,0:T(8,128)}, bf16[512,768]{1,0:T(8,128)(2,1)}, /*index=5*/bf16[8,192,768]{2,1,0:T(8,128)(2,1)}) custom-call(s32[10,256]{1,0:T(8,128)} %get-tuple-element.117.start_ref, s32[10,256]{1,0:T(8,128)} %get-tuple-element.118.size_ref, ...), custom_call_target="tpu_custom_call" | custom-call | flops 9999999827968 | bytes 31457280 | tf_op jit(solution)/shard_map/late/pallas_call | solution.py:1961
  303.6 0.0 copy-start.1
  303.6 7.6 %last.1 = (f32[192,3072]{1,0:T(8,128)}, f32[768,768]{1,0:T(8,128)}, f32[192,768]{1,0:T(8,128)}, f32[192,768]{1,0:T(8,128)}, f32[192,1536]{1,0:T(8,128)}, /*index...) custom-call(s32[2]{0:T(128)} %pad_add_fusion.me_ref, ...), custom_call_target="tpu_custom_call" | custom-call | flops 799999983616 | bytes 18119304 | tf_op jit(solution)/shard_map/last/pallas_call | solution.py:895
  311.2 0.0 copy-start
  311.2 0.0 copy-done.1
  311.3 0.9 copy.35
  312.2 0.9 copy-done
  313.1 1.3 copy.36
  (1 shorter events, 0.0 us)
Async XLA Ops:
  0.6 27.0 %collective-permute-start.1 = (bf16[512,768]{1,0:T(8,128)(2,1)}, bf16[512,768]{1,0:T(8,128)(2,1)}, u32[]{:S(2)}, u32[]{:S(2)}) collective-permute-start(bf16[512,768]{1,0:T(8,128)(2,1)} %enc0_any.1), channel_id=1, source_target_pairs={{0,1},{1,0},{2,3},{3,2},{4,5},{5,4},{6,7},{7,6},{8,9},{9,8},{10,11... | collective-permute-start | bytes 2359304 | tf_op jit(solution)/shard_map/ppermute | solution.py:2120
  1.2 21.0 %collective-permute-start = (bf16[512,768]{1,0:T(8,128)(2,1)}, bf16[512,768]{1,0:T(8,128)(2,1)}, u32[]{:S(2)}, u32[]{:S(2)}) collective-permute-start(bf16[512,768]{1,0:T(8,128)(2,1)} %enc0_any.1), channel_id=1, source_target_pairs={{0,2},{1,3},{2,0},{3,1},{4,6},{5,7},{6,4},{7,5},{8,10},{9,11},{10,... | collective-permute-start | bytes 2359304 | tf_op jit(solution)/shard_map/ppermute | solution.py:2120
  22.2 5.5 %collective-permute-start.2 = (bf16[512,768]{1,0:T(8,128)(2,1)}, bf16[512,768]{1,0:T(8,128)(2,1)}, u32[]{:S(2)}, u32[]{:S(2)}) collective-permute-start(bf16[512,768]{1,0:T(8,128)(2,1)} %collective-permute-done.rest_2_.enc2_any), channel_id=1, source_target_pairs={{0,1},{1,0},{2,3},{3,2},{4,5},{5,4},{6,7},{7,6},{8,9},{9,8},{10,11... | collective-permute-start | bytes 2359304 | tf_op jit(solution)/shard_map/ppermute | solution.py:2120
  113.1 35.7 %collective-permute-start.5 = (bf16[2,96,768]{2,1,0:T(8,128)(2,1)}, bf16[2,96,768]{2,1,0:T(8,128)(2,1)}, u32[]{:S(2)}, u32[]{:S(2)}) collective-permute-start(bf16[2,96,768]{2,1,0:T(8,128)(2,1)} %get-tuple-element.132), channel_id=1, source_target_pairs={{0,8},{1,9},{2,10},{3,11},{4,12},{5,13},{6,14},{7,15},{8,0},{9,1},... | collective-permute-start | bytes 884744 | tf_op jit(solution)/shard_map/ppermute | solution.py:2120
  114.2 34.6 %collective-permute-start.4 = (bf16[8,96,768]{2,1,0:T(8,128)(2,1)}, bf16[8,96,768]{2,1,0:T(8,128)(2,1)}, u32[]{:S(2)}, u32[]{:S(2)}) collective-permute-start(bf16[8,96,768]{2,1,0:T(8,128)(2,1)} %get-tuple-element.131), channel_id=1, source_target_pairs={{0,2},{1,3},{2,0},{3,1},{4,6},{5,7},{6,4},{7,5},{8,10},{9,11},{10,... | collective-permute-start | bytes 3538952 | tf_op jit(solution)/shard_map/ppermute | solution.py:2120
  148.8 41.3 %collective-permute-start.3 = (bf16[2,512,1024]{2,1,0:T(8,128)(2,1)}, bf16[2,512,1024]{2,1,0:T(8,128)(2,1)}, u32[]{:S(2)}, u32[]{:S(2)}) collective-permute-start(bf16[2,512,1024]{2,1,0:T(8,128)(2,1)} %get-tuple-element.129), channel_id=1, source_target_pairs={{0,1},{1,0},{2,3},{3,2},{4,5},{5,4},{6,7},{7,6},{8,9},{9,8},{10,11... | collective-permute-start | bytes 6291464 | tf_op jit(solution)/shard_map/ppermute | solution.py:2120
  151.7 30.6 %collective-permute-start.7 = (bf16[2,96,768]{2,1,0:T(8,128)(2,1)}, bf16[2,96,768]{2,1,0:T(8,128)(2,1)}, u32[]{:S(2)}, u32[]{:S(2)}) collective-permute-start(bf16[2,96,768]{2,1,0:T(8,128)(2,1)} %get-tuple-element.144), channel_id=1, source_target_pairs={{0,8},{1,9},{2,10},{3,11},{4,12},{5,13},{6,14},{7,15},{8,0},{9,1},... | collective-permute-start | bytes 884744 | tf_op jit(solution)/shard_map/ppermute | solution.py:2120
  152.7 29.7 %collective-permute-start.8 = (bf16[2,96,768]{2,1,0:T(8,128)(2,1)}, bf16[2,96,768]{2,1,0:T(8,128)(2,1)}, u32[]{:S(2)}, u32[]{:S(2)}) collective-permute-start(bf16[2,96,768]{2,1,0:T(8,128)(2,1)} %get-tuple-element.145), channel_id=1, source_target_pairs={{0,4},{1,5},{2,6},{3,7},{4,0},{5,1},{6,2},{7,3},{8,12},{9,13},{10,... | collective-permute-start | bytes 884744 | tf_op jit(solution)/shard_map/ppermute | solution.py:2120
  156.0 26.4 %collective-permute-start.9 = (bf16[2,96,768]{2,1,0:T(8,128)(2,1)}, bf16[2,96,768]{2,1,0:T(8,128)(2,1)}, u32[]{:S(2)}, u32[]{:S(2)}) collective-permute-start(bf16[2,96,768]{2,1,0:T(8,128)(2,1)} %get-tuple-element.146), channel_id=1, source_target_pairs={{0,12},{1,13},{2,14},{3,15},{4,8},{5,9},{6,10},{7,11},{8,4},{9,5},... | collective-permute-start | bytes 884744 | tf_op jit(solution)/shard_map/ppermute | solution.py:2120
  156.1 26.3 %collective-permute-start.10 = (bf16[2,96,768]{2,1,0:T(8,128)(2,1)}, bf16[2,96,768]{2,1,0:T(8,128)(2,1)}, u32[]{:S(2)}, u32[]{:S(2)}) collective-permute-start(bf16[2,96,768]{2,1,0:T(8,128)(2,1)} %get-tuple-element.147.two_ref), channel_id=1, source_target_pairs={{0,16},{1,17},{2,18},{3,19},{4,20},{5,21},{6,22},{7,23},{8,24},{9,... | collective-permute-start | bytes 884744 | tf_op jit(solution)/shard_map/ppermute | solution.py:2120
  182.4 7.7 %collective-permute-start.6 = (bf16[2,512,512]{2,1,0:T(8,128)(2,1)}, bf16[2,512,512]{2,1,0:T(8,128)(2,1)}, u32[]{:S(2)}, u32[]{:S(2)}) collective-permute-start(bf16[2,512,512]{2,1,0:T(8,128)(2,1)} %get-tuple-element.142), channel_id=1, source_target_pairs={{0,1},{1,0},{2,3},{3,2},{4,5},{5,4},{6,7},{7,6},{8,9},{9,8},{10,11... | collective-permute-start | bytes 3145736 | tf_op jit(solution)/shard_map/ppermute | solution.py:2120
  303.6 7.7 %copy-start.1 = (bf16[640,768]{1,0:T(8,128)(2,1)S(1)}, bf16[640,768]{1,0:T(8,128)(2,1)}, u32[]{:S(2)}) copy-start(bf16[640,768]{1,0:T(8,128)(2,1)} %get-tuple-element.208) | copy-start | bytes 2949124
  311.2 1.9 copy-start
